TPU v7x, 32 devices: a whole 2x2x4 slice. The times are simulated.
32 devices in a mesh: aux: 8 (over z, x), vir: 4 (over y, core).
Axes of the slice: x: 2, y: 2, z: 4, core: 2. Of those that a mesh axis runs over, the one named last changes fastest.
Arguments:
- factors: bfloat16 [2048, 1024, 128], P('aux', 'vir'), may hold values from -0.125 to 0.125
- trials: float32 [1, 1024, 128], P(None, 'vir', 'aux'), may hold values from -6 to 6
- occ_energy: float32 [128], replicated, may hold values from -3 to -0.5
- vir_energy: float32 [1024], P('vir'), may hold values from 0.5 to 3
Outputs:
- trial_out: float32 [1, 1024, 128], P(None, 'vir', 'aux')
- shifts: float32 [2, 1], replicated
All inputs are finite; a program needn't handle non-finite values.
Results may differ from a plain program's by a relative error of at most 0.0075.
Values may be sent and summed in bfloat16 or wider, within the bound.
No kernel may reach another device: no remote copies, remote signals or barrier semaphores. Data moves between devices by JAX's collectives and lax.ppermute only.
A program may use at most 128 MiB of HBM per device.

v0:
```python
import jax
import jax.numpy as jnp
from jax import lax
from jax.sharding import PartitionSpec as P

OCC = 128
VIR = 1024
ITERS = 2


def local(factors, trials, occ_energy, vir_energy):
    aux_count = lax.axis_size("aux")
    occ_count = factors.shape[2]
    row_share = occ_count // aux_count
    row_start = lax.axis_index("aux") * row_share
    gap_full = vir_energy[:, None] - occ_energy[None, :]
    gap_share = lax.dynamic_slice_in_dim(gap_full, row_start, row_share, 1)
    trial = lax.all_gather(trials, "aux", axis=2, tiled=True)
    shift_list = []
    for iteration in range(ITERS):
        rounded = trial.astype(jnp.bfloat16)
        whole_trial = lax.all_gather(rounded, "vir", axis=1, tiled=True)
        local_density = jnp.einsum(
            "pai,nai->np", factors, rounded, preferred_element_type=jnp.float32
        )
        density = lax.psum(local_density, "vir").astype(jnp.bfloat16)
        full_factors = lax.all_gather(factors, "vir", axis=1, tiled=True)
        pairs = jnp.einsum(
            "pai,naj->npij", full_factors, whole_trial, preferred_element_type=jnp.float32
        ).astype(jnp.bfloat16)
        exchange_term = jnp.einsum(
            "paj,npij->nai", factors, pairs, preferred_element_type=jnp.float32
        )
        partial_value = (
            2.0 * jnp.einsum("pai,np->nai", factors, density, preferred_element_type=jnp.float32)
            - exchange_term
        )
        coupling = lax.psum(partial_value, "aux")
        response = gap_full[None] * rounded.astype(jnp.float32) + coupling
        trial_share = lax.dynamic_slice_in_dim(trial, row_start, row_share, 2)
        response_share = lax.dynamic_slice_in_dim(response, row_start, row_share, 2)
        scaled_diff = trial_share - response_share / gap_share[None]
        scaled_trial = trial_share / gap_share[None]
        cross_sum, self_sum, diff_sum, mixed_sum, scaled_sum = lax.psum(
            (
                jnp.sum(trial_share * response_share, axis=(1, 2)),
                jnp.sum(trial_share * trial_share, axis=(1, 2)),
                jnp.sum(scaled_diff * scaled_diff, axis=(1, 2)),
                jnp.sum(scaled_diff * scaled_trial, axis=(1, 2)),
                jnp.sum(scaled_trial * scaled_trial, axis=(1, 2)),
            ),
            ("aux", "vir"),
        )
        shift_now = cross_sum / self_sum
        update = trial - (response - shift_now[:, None, None] * trial) / gap_full[None]
        length_sq = diff_sum + 2.0 * shift_now * mixed_sum + shift_now * shift_now * scaled_sum
        mean_square = length_sq / (OCC * VIR)
        trial = update * lax.rsqrt(mean_square + 1e-06)[:, None, None]
        shift_list.append(shift_now)
    result = lax.dynamic_slice_in_dim(trial, row_start, row_share, 2)
    return (result, jnp.stack(shift_list))


def solution(mesh):
    placed = (P("aux", "vir", None), P(None, "vir", "aux"), P(), P("vir"))
    return jax.shard_map(
        local, mesh=mesh, in_specs=placed, out_specs=(P(None, "vir", "aux"), P()), check_vma=False
    )
```

profile of v0, /device:TPU:0, one launch (start us, length us, event | category | flops | bytes accessed | tf_op | source)
XLA Modules:
  0.0 739.8 jit_solution(10210970792558156459)
XLA Ops:
  7.2 0.7 all-gather.2.cloned.1.call-update
  8.0 32.3 %all_gather.13 = f32[1,256,128]{1,2,0:T(8,128)S(1)} all-gather(f32[1,256,16]{1,2,0:T(8,128)S(1)} %copy-done.1), channel_id=1, replica_groups=mesh['aux'=8,'vir'=4] {'aux'}, dimensions={2}, use_global_device_ids=true | all-gather | bytes 147456 | tf_op jit(solution)/shard_map/all_gather | solution.py:18
  40.4 12.1 %fusion = f32[256]{0:T(256)S(1)} fusion(f32[256,128]{1,0:T(8,128)S(1)} %copy.25, bf16[256,256,128]{2,1,0:T(8,128)(2,1)} %param.4), kind=kLoop, calls=%fused_computation.2 | loop fusion | flops 25165568 | bytes 16909312 | tf_op jit(solution)/shard_map/pai,nai->np/dot_general | solution.py:23
  52.5 6.4 psum.98
  58.9 15.6 %fusion.4 = f32[1,256,128]{2,0,1:T(1,128)S(1)} fusion(bf16[256,256,128]{2,1,0:T(8,128)(2,1)} %param.4, bf16[1,256]{1,0:T(2,128)(2,1)S(1)} %psum.98), kind=kOutput, calls=%fused_computation.6 | convolution fusion | flops 16777216 | bytes 16908800 | tf_op jit(solution)/shard_map/pai,np->nai/dot_general | solution.py:35
  74.6 7.8 %all_gather.14 = bf16[1,1024,128]{1,2,0:T(8,128)(2,1)S(1)} all-gather(bf16[1,256,128]{1,2,0:T(8,128)(2,1)S(1)} %get-tuple-element.26), channel_id=1, replica_groups=mesh['aux'=8,'vir'=4] {'vir'}, dimensions={1}, use_global_device_ids=true | all-gather | bytes 327680 | tf_op jit(solution)/shard_map/all_gather | solution.py:22
  82.4 324.3 %all-gather.2.cloned.1.call-done = bf16[256,1024,128]{2,1,0:T(8,128)(2,1)} async-done(((bf16[256,256,128]{2,1,0:T(8,128)(2,1)}), bf16[256,1024,128]{2,1,0:T(8,128)(2,1)}) %all-gather.2.cloned.1.call-update) | async-done | bytes 67108880 | tf_op jit(solution)/shard_map/all_gather | solution.py:27
  406.7 29.4 %fusion.21 = f32[1,256,128]{1,2,0:T(8,128)} fusion(bf16[256,256,128]{2,1,0:T(8,128)(2,1)} %param.4, bf16[256,1024,128]{2,1,0:T(8,128)(2,1)} %all-gather.2.cloned.1.call-done, bf16[1,1024,128]{1,2,0:T(8,128)(2,1)S(1)} %all_gather.14, f32[1,256,128]{1,2,0:T(8,128)S(1)} %copy.15), kind=kOutput, calls=%fused_computation.17 | convolution fusion | flops 10741678080 | bytes 84410368 | tf_op jit(solution)/shard_map/paj,npij->nai/dot_general | solution.py:31
  436.3 69.7 %all-reduce.5.cloned.1.call-done = f32[1,256,128]{1,2,0:T(8,128)} async-done(((f32[1,256,128]{1,2,0:T(8,128)}), f32[1,256,128]{1,2,0:T(8,128)}) %all-reduce.5.cloned.1.call-update) | async-done | bytes 131088 | tf_op jit(solution)/shard_map/psum | solution.py:38
  506.0 1.0 fusion.32
  507.0 0.8 multiply_reduce_fusion.5
  507.8 40.0 %all-reduce.1 = (f32[1]{0:T(128)}, f32[1]{0:T(128)}, f32[1]{0:T(128)}, f32[1]{0:T(128)}, f32[1]{0:T(128)}) all-reduce(f32[1]{0:T(128)} %bitcast.18, f32[1]{0:T(128)} %bitcast.14, f32[1]{0:T(128)} %bitcast.15, f32[1]{0:T(128)} %bitcast.19, f32[1]{0:T(128)} %bitcast.20), channel_id=1, replica_groups=mesh['aux'=8,'vir'=4] {'aux','vir'}, use_global_device_ids=true, to_apply=%region_7.0 | all-reduce | flops 5 | bytes 40 | tf_op jit(solution)/shard_map/psum | solution.py:44
  551.0 0.1 bitcast_convert_fusion
  551.2 10.0 %fusion.1 = f32[256]{0:T(256)S(1)} fusion(f32[256,128]{1,0:T(8,128)S(1)} %copy.26, bf16[256,256,128]{2,1,0:T(8,128)(2,1)} %param.4), kind=kLoop, calls=%fused_computation.3 | loop fusion | flops 25165568 | bytes 16909312 | tf_op jit(solution)/shard_map/pai,nai->np/dot_general | solution.py:23
  561.2 6.1 psum.105
  567.4 14.6 %fusion.2 = f32[1,256,128]{2,0,1:T(1,128)S(1)} fusion(bf16[256,256,128]{2,1,0:T(8,128)(2,1)} %param.4, bf16[1,256]{1,0:T(2,128)(2,1)S(1)} %psum.105), kind=kOutput, calls=%fused_computation.4 | convolution fusion | flops 16777216 | bytes 16908800 | tf_op jit(solution)/shard_map/pai,np->nai/dot_general | solution.py:35
  582.1 6.7 all_gather.16
  588.8 29.5 %fusion.18 = f32[1,256,128]{1,2,0:T(8,128)} fusion(bf16[256,256,128]{2,1,0:T(8,128)(2,1)} %param.4, bf16[256,1024,128]{2,1,0:T(8,128)(2,1)} %all-gather.2.cloned.1.call-done, bf16[1,1024,128]{1,2,0:T(8,128)(2,1)S(1)} %all_gather.16, f32[1,256,128]{1,2,0:T(8,128)S(1)} %copy.22), kind=kOutput, calls=%fused_computation.16 | convolution fusion | flops 10741678080 | bytes 84410368 | tf_op jit(solution)/shard_map/paj,npij->nai/dot_general | solution.py:31
  618.3 68.8 %all-reduce.7.cloned.1.call-done = f32[1,256,128]{1,2,0:T(8,128)} async-done(((f32[1,256,128]{1,2,0:T(8,128)}), f32[1,256,128]{1,2,0:T(8,128)}) %all-reduce.7.cloned.1.call-update) | async-done | bytes 131088 | tf_op jit(solution)/shard_map/psum | solution.py:38
  687.1 1.0 fusion.35
  688.1 0.8 multiply_reduce_fusion
  688.8 40.0 %all-reduce = (f32[1]{0:T(128)}, f32[1]{0:T(128)}, f32[1]{0:T(128)}, f32[1]{0:T(128)}, f32[1]{0:T(128)}) all-reduce(f32[1]{0:T(128)} %bitcast.37, f32[1]{0:T(128)} %bitcast.34, f32[1]{0:T(128)} %bitcast.35, f32[1]{0:T(128)} %bitcast.38, f32[1]{0:T(128)} %bitcast.39), channel_id=1, replica_groups=mesh['aux'=8,'vir'=4] {'aux','vir'}, use_global_device_ids=true, to_apply=%region_19.0 | all-reduce | flops 5 | bytes 40 | tf_op jit(solution)/shard_map/psum | solution.py:44
  732.1 0.6 pad_maximum_fusion
  732.7 0.6 fusion.37
  (17 shorter events, 0.6 us)
Async XLA Ops:
  7.2 0.8 copy-start.1
  7.2 399.5 %all-gather.2.cloned.1.call-start = ((), (), s32[]{:S(2)}) async-start(), calls=%async_computation | async-start | bytes 83886080 | tf_op jit(solution)/shard_map/all_gather | solution.py:27
  7.9 498.1 %all-reduce.5.cloned.1.call-start = ((), (), s32[]{:S(2)}) async-start(), calls=%async_computation.1 | async-start | bytes 262144 | tf_op jit(solution)/shard_map/psum | solution.py:38
  82.4 353.8 %copy-start.2 = (f32[128]{0:T(128)S(1)}, f32[128]{0:T(128)}, u32[]{:S(2)}) copy-start(f32[128]{0:T(128)} %param.6) | copy-start | bytes 1540
  82.4 423.6 %copy-start = (f32[256]{0:T(256)S(1)}, f32[256]{0:T(256)}, u32[]{:S(2)}) copy-start(f32[256]{0:T(256)} %param.7) | copy-start | bytes 3076
  436.2 250.9 %all-reduce.7.cloned.1.call-start = ((), (), s32[]{:S(2)}) async-start(), calls=%async_computation.2 | async-start | bytes 262144 | tf_op jit(solution)/shard_map/psum | solution.py:38
Sparse Core Ops, SparseCore 0:
  9.6 397.0 all-gather.1
  436.3 69.6 all-reduce.4
  618.4 68.6 all-reduce.6
where the time goes:
time: 740 us
  waiting for transfers between devices  463 us (63%)
  blocking collectives  139 us (19%)
  matrix products  89.1 us (12%)
  other arithmetic  26.9 us (4%)
  between operations  20.4 us (3%)
    all_gather x1, waiting for transfers between devices, local(): full_factors = lax.all_gather(factors, 'vir', axis=1, tiled=True)  324 us
    psum x2, waiting for transfers between devices, local(): coupling = lax.psum(partial_value, 'aux')  138 us
    psum x2, blocking collectives, local(): lax.psum((jnp.sum(trial_share * response_share, axis=(1, 2)), jnp.sum(tri...  80 us
    dot_general x2, matrix products, local(): jnp.einsum('paj,npij->nai', factors, pairs, preferred_element_type=jnp.fl...  58.9 us
    all_gather x1, blocking collectives, local(): trial = lax.all_gather(trials, 'aux', axis=2, tiled=True)  32.3 us
    dot_general x2, matrix products, local(): jnp.einsum('pai,np->nai', factors, density, preferred_element_type=jnp.fl...  30.2 us
    dot_general x2, other arithmetic, local(): jnp.einsum('pai,nai->np', factors, rounded, preferred_element_type=jnp.fl...  22.1 us
  transfers between devices with their start and end apart: 3, of which 3 were waited for; matrix products, arithmetic and copies ran while one was open for 4% of the time, Pallas kernels for 0%

commit v1 on v0

v1 whole, which is shorter than its diff:
```python
import functools

import jax
import jax.numpy as jnp
from jax import lax
from jax.experimental import pallas as pl
from jax.experimental.pallas import tpu as pltpu
from jax.sharding import PartitionSpec as P

ITERS = 2
EVERY = ("aux", "vir")


def contract_body(nv, counts, block, group, order_ref, xt_ref, *refs):
    f_refs, out_ref, acc_ref = refs[:-2], refs[-2], refs[-1]
    step = pl.program_id(0)
    occ, width = xt_ref.shape[1:]
    share = out_ref.shape[2]

    @pl.when(step == 0)
    def _():
        acc_ref[...] = jnp.zeros_like(acc_ref)

    xt = jnp.concatenate([xt_ref[order_ref[k]] for k in range(nv)], axis=1)
    eye = lax.broadcasted_iota(jnp.int32, (occ, occ), 0) == lax.broadcasted_iota(
        jnp.int32, (occ, occ), 1
    )

    def work(blocks):
        for first in range(0, block, group):
            tall = jnp.concatenate(
                [
                    jnp.concatenate([blocks[k][first + q] for q in range(group)], axis=1)
                    for k in range(nv)
                ],
                axis=0,
            )
            pairs = jnp.dot(xt, tall, preferred_element_type=jnp.float32)
            mixes = []
            for q in range(group):
                pair = pairs[:, q * occ : (q + 1) * occ]
                density = jnp.sum(jnp.where(eye, pair, 0.0), keepdims=True)
                density = density.astype(jnp.bfloat16).astype(jnp.float32)
                pair = pair.astype(jnp.bfloat16).astype(jnp.float32)
                mixes.append((jnp.where(eye, 2.0 * density, 0.0) - pair).astype(jnp.bfloat16))
            mix = jnp.concatenate(mixes, axis=0)
            acc_ref[...] += jnp.dot(tall, mix, preferred_element_type=jnp.float32)

    start = 0
    for c, n in enumerate(counts):

        @pl.when((step >= start) & (step < start + n))
        def _(c=c):
            work(f_refs[c * nv : (c + 1) * nv])

        start += n

    @pl.when(step == start - 1)
    def _():
        for k in range(nv):
            turned = acc_ref[k * width : (k + 1) * width, :].T
            for r in range(occ // share):
                out_ref[r, order_ref[k]] = turned[r * share : (r + 1) * share, :].astype(out_ref.dtype)


def contract(order, xt, chunks, aux_count, block, group):
    nv, occ, width = xt.shape
    counts = [chunk[0].shape[0] // block for chunk in chunks]
    specs = [
        pl.BlockSpec(memory_space=pltpu.SMEM),
        pl.BlockSpec((nv, occ, width), lambda g: (0, 0, 0)),
    ]
    start = 0
    for n in counts:
        place = functools.partial(lambda s, m, g: (jnp.clip(g - s, 0, m - 1), 0, 0), start, n)
        specs += [pl.BlockSpec((block, width, occ), place)] * nv
        start += n
    shape = (aux_count, nv, occ // aux_count, width)
    pairs_total = start * block
    return pl.pallas_call(
        functools.partial(contract_body, nv, counts, block, group),
        grid=(start,),
        in_specs=specs,
        out_specs=pl.BlockSpec(shape, lambda g: (0, 0, 0, 0)),
        out_shape=jax.ShapeDtypeStruct(shape, jnp.float32),
        scratch_shapes=[pltpu.VMEM((nv * width, occ), jnp.float32)],
        compiler_params=pltpu.CompilerParams(vmem_limit_bytes=48 * 2**20),
        cost_estimate=pl.CostEstimate(
            flops=4 * pairs_total * nv * width * occ * occ,
            bytes_accessed=2 * pairs_total * nv * width * occ,
            transcendentals=0,
        ),
    )(order, xt, *[part for chunk in chunks for part in chunk])


def spread(share, count):
    copies = jnp.broadcast_to(share[None], (count,) + share.shape)
    return lax.all_to_all(copies, EVERY, 0, 0, tiled=True)


def local(factors, trials, occ_energy, vir_energy):
    na, nv = lax.axis_size("aux"), lax.axis_size("vir")
    count = na * nv
    aux_at, vir_at = lax.axis_index("aux"), lax.axis_index("vir")
    p_count, width, occ = factors.shape
    own = p_count // nv
    share = occ // na
    total = occ * width * nv
    paired = nv & (nv - 1) == 0

    def partner(at, k):
        return at ^ k if paired else (at + k) % nv

    def source(at, k):
        return at ^ k if paired else (at - k) % nv

    block = next(n for n in (8, 4, 2, 1) if own % n == 0)
    tail = max(block, own // 4 // block * block)
    cuts = [(0, own - tail), (own - tail, own)] if own > tail else [(0, own)]

    chunks = []
    for low, high in cuts:
        parts = []
        for k in range(nv):
            piece = lax.dynamic_slice_in_dim(factors, partner(vir_at, k) * own + low, high - low, 0)
            if k:
                piece = lax.ppermute(piece, "vir", [(at, partner(at, k)) for at in range(nv)])
            parts.append(piece)
        chunks.append(parts)
    order = jnp.stack([source(vir_at, k) for k in range(nv)]).astype(jnp.int32)

    trial_own = trials[0].T
    begin = spread(jnp.concatenate([trial_own, vir_energy[None]], axis=0), count)
    begin = begin.reshape(na, nv, share + 1, width)
    trial = begin[:, :, :share]
    gap = begin[:, :, share:] - occ_energy.reshape(na, 1, share, 1)
    gap_own = vir_energy[None, :] - lax.dynamic_slice_in_dim(occ_energy, aux_at * share, share)[:, None]

    def reduce_to_share(partial):
        terms = lax.all_to_all(
            partial.astype(jnp.bfloat16).reshape(count, share, width), EVERY, 0, 0, tiled=True
        )
        return jnp.sum(terms.astype(jnp.float32), axis=0)

    shift_list = []
    for iteration in range(ITERS):
        rounded = trial.astype(jnp.bfloat16)
        xt = rounded.transpose(1, 0, 2, 3).reshape(nv, occ, width)
        if iteration == 0:
            partial = None
            for chunk in chunks:
                part = contract(order, xt, [chunk], na, block, block)
                partial = part if partial is None else partial + part
        else:
            partial = contract(order, xt, chunks, na, block, block)
        coupling = reduce_to_share(partial)
        last = iteration == ITERS - 1
        if last:
            trial_now = lax.dynamic_slice(
                trial, (aux_at, vir_at, 0, 0), (1, 1, share, width)
            ).reshape(share, width)
            gap_now = gap_own
        else:
            trial_now, gap_now = trial, gap
            coupling = spread(coupling.astype(jnp.bfloat16), count).astype(jnp.float32)
            coupling = coupling.reshape(na, nv, share, width)
        image = gap_now * trial_now.astype(jnp.bfloat16).astype(jnp.float32) + coupling
        scaled_trial = trial_now / gap_now
        scaled_diff = trial_now - image / gap_now
        sums = jnp.stack(
            [
                jnp.sum(trial_now * image),
                jnp.sum(trial_now * trial_now),
                jnp.sum(scaled_diff * scaled_diff),
                jnp.sum(scaled_diff * scaled_trial),
                jnp.sum(scaled_trial * scaled_trial),
            ]
        )
        if last:
            sums = jnp.sum(spread(jnp.pad(sums, (0, 3)), count), axis=0)
        shift = sums[0] / sums[1]
        mean_square = (sums[2] + 2.0 * shift * sums[3] + shift * shift * sums[4]) / total
        trial = (scaled_diff + shift * scaled_trial) * lax.rsqrt(mean_square + 1e-06)
        shift_list.append(shift)
    return (trial.T[None], jnp.stack(shift_list)[:, None])


def solution(mesh):
    placed = (P("aux", "vir", None), P(None, "vir", "aux"), P(), P("vir"))
    return jax.shard_map(
        local, mesh=mesh, in_specs=placed, out_specs=(P(None, "vir", "aux"), P()), check_vma=False
    )
```

time: 740 us -> 300 us (0.41)
  waiting for transfers between devices: 463 us -> 193 us
  blocking collectives: 139 us -> 25.5 us
  matrix products: 89.1 us -> 0 us
  Pallas kernels: 0 us -> 26.2 us
  local copies, waits for them, and re-layouts: 0.45 us -> 23.8 us
  other arithmetic: 26.9 us -> 6.05 us
  starting transfers between devices: 0.12 us -> 16.6 us
  between operations: 20.4 us -> 7.44 us
    all_gather x1 -> x0, waiting for transfers between devices: 324 us -> none  [local(): full_factors = lax.all_gather(factors, 'vir', axis=1, tiled=True)]
    all_to_all x0 -> x3, waiting for transfers between devices: none -> 150 us  [the longest x2 140 us: spread(): return lax.all_to_all(copies, EVERY, 0, 0, tiled=True)]
    psum x2 -> x0, waiting for transfers between devices: 138 us -> none  [local(): coupling = lax.psum(partial_value, 'aux')]
    psum x4 -> x0, blocking collectives: 92.6 us -> none  [the longest x2 80 us: local(): lax.psum((jnp.sum(trial_share * response_share, axis=(1, 2)), jnp.sum(tri...]
    dot_general x4 -> x0, matrix products: 89.1 us -> none  [the longest x2 58.9 us: local(): jnp.einsum('paj,npij->nai', factors, pairs, preferred_element_type=jnp.fl...]
    all_gather x3 -> x0, blocking collectives: 46.9 us -> none  [the longest x1 32.3 us: local(): trial = lax.all_gather(trials, 'aux', axis=2, tiled=True)]
    ppermute x0 -> x6, waiting for transfers between devices: none -> 43.4 us  [local(): lax.ppermute(piece, 'vir', [(at, partner(at, k)) for at in range(nv)])]
    pallas_call x0 -> x3, Pallas kernels: none -> 26.2 us  [contract(): pl.pallas_call(functools.partial(contract_body, nv, counts, block, group)...]
  transfers between devices with their start and end apart: 3 -> 9, of which waited for: 3 -> 5; matrix products, arithmetic and copies ran while one was open for 4% -> 3% of each run, Pallas kernels for 0% -> 1%
where the time goes in v1:
time: 300 us; the launch traced here: 299 us
  waiting for transfers between devices  193 us (64%)
  Pallas kernels  26.2 us (9%)
  blocking collectives  25.5 us (8%)
  local copies, waits for them, and re-layouts  23.8 us (8%)
  starting transfers between devices  16.6 us (6%)
  between operations  7.44 us (2%)
  other arithmetic  6.05 us (2%)
    all_to_all x2, waiting for transfers between devices, spread(): return lax.all_to_all(copies, EVERY, 0, 0, tiled=True)  140 us
    ppermute x6, waiting for transfers between devices, local(): lax.ppermute(piece, 'vir', [(at, partner(at, k)) for at in range(nv)])  43.4 us
    pallas_call x3, Pallas kernels, contract(): pl.pallas_call(functools.partial(contract_body, nv, counts, block, group)...  26.2 us
    all_to_all x1, blocking collectives, reduce_to_share(): lax.all_to_all(partial.astype(jnp.bfloat16).reshape(count, share, width),...  16.3 us
    dynamic_slice x2, local copies, waits for them, and re-layouts, local(): lax.dynamic_slice_in_dim(factors, partner(vir_at, k) * own + low, high -...  13.1 us
    all_to_all x1, waiting for transfers between devices, reduce_to_share(): lax.all_to_all(partial.astype(jnp.bfloat16).reshape(count, share, width),...  9.66 us
    all_to_all x1, blocking collectives, spread(): return lax.all_to_all(copies, EVERY, 0, 0, tiled=True)  9.26 us
    all_to_all x2, starting transfers between devices, spread(): return lax.all_to_all(copies, EVERY, 0, 0, tiled=True)  8.96 us
  transfers between devices with their start and end apart: 9, of which 5 were waited for; matrix products, arithmetic and copies ran while one was open for 3% of the time, Pallas kernels for 1%

profile of v1, /device:TPU:0, one launch (start us, length us, event | category | flops | bytes accessed | tf_op | source)
XLA Modules:
  0.0 298.7 jit_solution(8720701319847797959)
XLA Ops:
  0.7 8.7 %constant_dynamic-slice_fusion.5 = (bf16[48,256,128]{2,1,0:T(8,128)(2,1)}, bf16[48,256,128]{2,1,0:T(8,128)(2,1)}, bf16[48,256,128]{2,1,0:T(8,128)(2,1)}, bf16[48,256,128]{2,1,0:T(8,128)(2,1)S(1)}) fusion(bf16[256,256,128]{2,1,0:T(8,128)(2,1)} %param.4, s32[]{:T(128)S(6)} %select_n.36, s32[]{:T(128)S(6)} %select_n.35, s32[]{:T(128)S(6)} %select_n.34, ...), kind=kLoop, calls=%fused_computation.37 | loop fusion | bytes 25165840 | tf_op jit(solution)/shard_map/dynamic_slice | solution.py:125
  9.8 2.6 collective-permute-start.1
  12.5 4.4 %constant_dynamic-slice_fusion.1 = (bf16[16,256,128]{2,1,0:T(8,128)(2,1)}, bf16[16,256,128]{2,1,0:T(8,128)(2,1)}, bf16[16,256,128]{2,1,0:T(8,128)(2,1)}, bf16[16,256,128]{2,1,0:T(8,128)(2,1)}) fusion(bf16[256,256,128]{2,1,0:T(8,128)(2,1)} %param.4, s32[]{:T(128)S(6)} %select_n.40, s32[]{:T(128)S(6)} %select_n.38, s32[]{:T(128)S(6)} %select_n.37, s32[]{:T(128)S(6)} %select_n.39), kind=kLoop, calls=%fused_computation.33 | loop fusion | bytes 8388624 | tf_op jit(solution)/shard_map/dynamic_slice | solution.py:125
  17.1 1.0 broadcast_in_dim.13
  18.0 6.4 %all-to-all-start = ((f32[32,17,256]{2,1,0:T(8,128)}), f32[32,17,256]{2,1,0:T(8,128)}, u32[]{:S(2)}, u32[]{:S(2)}) async-start(f32[32,17,256]{2,1,0:T(8,128)} %broadcast_in_dim.13), calls=%async_computation | async-start | bytes 1572864 | tf_op jit(solution)/shard_map/all_to_all | solution.py:98
  24.4 1.8 collective-permute-start.4
  26.3 130.7 %all-to-all-done = f32[32,17,256]{2,1,0:T(8,128)} async-done(((f32[32,17,256]{2,1,0:T(8,128)}), f32[32,17,256]{2,1,0:T(8,128)}, u32[]{:S(2)}, u32[]{:S(2)}) %all-to-all-start) | async-done | bytes 557088 | tf_op jit(solution)/shard_map/all_to_all | solution.py:98
  157.0 1.1 slice.28
  158.6 21.4 %collective-permute-done.4.refs_2_.refs_6_ = bf16[16,256,128]{2,1,0:T(8,128)(2,1)} collective-permute-done((bf16[16,256,128]{2,1,0:T(8,128)(2,1)}, bf16[16,256,128]{2,1,0:T(8,128)(2,1)}, u32[]{:S(2)}, u32[]{:S(2)}) %collective-permute-start.4) | collective-permute-done | bytes 1048608 | tf_op jit(solution)/shard_map/ppermute | solution.py:127
  180.0 21.9 %collective-permute-done.5.refs_3_.refs_7_ = bf16[16,256,128]{2,1,0:T(8,128)(2,1)} collective-permute-done((bf16[16,256,128]{2,1,0:T(8,128)(2,1)}, bf16[16,256,128]{2,1,0:T(8,128)(2,1)}, u32[]{:S(2)}, u32[]{:S(2)}) %collective-permute-start.5) | collective-permute-done | bytes 1048608 | tf_op jit(solution)/shard_map/ppermute | solution.py:127
  201.9 1.2 copy-done.1
  203.2 4.0 %shard_map.60 = f32[8,4,16,256]{3,2,1,0:T(8,128)S(1)} custom-call(s32[4]{0:T(128)S(1)} %pad_add_fusion.order_ref, bf16[4,128,256]{2,1,0:T(8,128)(2,1)S(1)} %bitcast.61, bf16[16,256,128]{2,1,0:T(8,128)(2,1)S(1)} %copy-done.1, bf16[16,256,128]{2,1,0:T(8,128)(2,1)} %collective-permute-done.3.refs_1_.refs_5_, ...), custom_call_target="tpu_custom_call" | custom-call | flops 1073741824 | bytes 4194304 | tf_op jit(solution)/shard_map/pallas_call | solution.py:80
  207.3 9.2 %shard_map.59 = f32[8,4,16,256]{3,2,1,0:T(8,128)S(1)} custom-call(s32[4]{0:T(128)S(1)} %pad_add_fusion.order_ref, bf16[4,128,256]{2,1,0:T(8,128)(2,1)S(1)} %bitcast.62, bf16[48,256,128]{2,1,0:T(8,128)(2,1)S(1)} %get-tuple-element.24.refs_0_, bf16[48,256,128]{2,1,0:T(8,128)(2,1)} %collective-permute-done.refs_1_, ...), custom_call_target="tpu_custom_call" | custom-call | flops 3221225472 | bytes 12582912 | tf_op jit(solution)/shard_map/pallas_call | solution.py:80
  216.6 16.3 %all_to_all.26 = bf16[32,16,256]{2,1,0:T(8,128)(2,1)S(1)} all-to-all(bf16[32,16,256]{2,1,0:T(8,128)(2,1)S(1)} %bitcast.64), channel_id=1, replica_groups=mesh['aux'=8,'vir'=4] {'aux','vir'}, dimensions={0} | all-to-all | bytes 524288 | tf_op jit(solution)/shard_map/all_to_all | solution.py:140
  233.7 2.6 all-to-all-start.2
  236.4 1.0 slice.29
  237.4 9.4 %all-to-all-done.2 = bf16[32,16,256]{2,1,0:T(8,128)(2,1)S(1)} async-done(((bf16[32,16,256]{2,1,0:T(8,128)(2,1)}), bf16[32,16,256]{2,1,0:T(8,128)(2,1)S(1)}, u32[]{:S(2)}, u32[]{:S(2)}) %all-to-all-start.2) | async-done | bytes 262176 | tf_op jit(solution)/shard_map/all_to_all | solution.py:98
  246.9 1.8 multiply_reduce_fusion.3
  252.1 1.1 convert_bitcast_fusion
  253.3 12.9 %shard_map.61 = f32[8,4,16,256]{3,2,1,0:T(8,128)S(1)} custom-call(s32[4]{0:T(128)S(1)} %pad_add_fusion.order_ref, bf16[4,128,256]{2,1,0:T(8,128)(2,1)S(1)} %bitcast.63, bf16[48,256,128]{2,1,0:T(8,128)(2,1)} %copy-done, bf16[48,256,128]{2,1,0:T(8,128)(2,1)} %collective-permute-done.refs_1_, bf16[48,256,128]{2,1,0:T(8,128)(2,1)} %collective-permute-done.1.refs_2_, ...), custom_call_target="tpu_custom_call" | custom-call | flops 4294967296 | bytes 16777216 | tf_op jit(solution)/shard_map/pallas_call | solution.py:80
  266.9 2.6 all-to-all-start.3
  270.5 9.7 %all-to-all-done.3 = bf16[32,16,256]{2,1,0:T(8,128)(2,1)S(1)} async-done(((bf16[32,16,256]{2,1,0:T(8,128)(2,1)}), bf16[32,16,256]{2,1,0:T(8,128)(2,1)S(1)}, u32[]{:S(2)}, u32[]{:S(2)}) %all-to-all-start.3) | async-done | bytes 262176 | tf_op jit(solution)/shard_map/all_to_all | solution.py:140
  281.0 3.2 %stack.50 = f32[5]{0:T(128)S(1)} concatenate(f32[1]{0:T(128)} %bitcast.16, f32[1]{0:T(128)} %bitcast.17, f32[1]{0:T(128)} %bitcast.18, f32[1]{0:T(128)} %bitcast.19, f32[1]{0:T(128)} %bitcast.20), dimensions={0} | concatenate | bytes 40 | tf_op jit(solution)/shard_map/stack | solution.py:170
  284.2 9.3 %all_to_all.27 = f32[32,1,8]{2,1,0:T(1,128)S(1)} all-to-all(f32[32,1,8]{2,1,0:T(1,128)S(1)} %broadcast_in_dim.15), channel_id=1, replica_groups=mesh['aux'=8,'vir'=4] {'aux','vir'}, dimensions={0} | all-to-all | bytes 2048 | tf_op jit(solution)/shard_map/all_to_all | solution.py:98
  (46 shorter events, 7.0 us)
Async XLA Ops:
  9.4 197.9 %copy-start = (bf16[48,256,128]{2,1,0:T(8,128)(2,1)}, bf16[48,256,128]{2,1,0:T(8,128)(2,1)S(1)}, u32[]{:S(2)}) copy-start(bf16[48,256,128]{2,1,0:T(8,128)(2,1)S(1)} %get-tuple-element.24.refs_0_) | copy-start | bytes 9437188
  9.4 197.8 %collective-permute-start = (bf16[48,256,128]{2,1,0:T(8,128)(2,1)}, bf16[48,256,128]{2,1,0:T(8,128)(2,1)}, u32[]{:S(2)}, u32[]{:S(2)}) collective-permute-start(bf16[48,256,128]{2,1,0:T(8,128)(2,1)} %get-tuple-element.23), channel_id=1, source_target_pairs={{0,1},{1,0},{2,3},{3,2},{4,5},{5,4},{6,7},{7,6},{8,9},{9,8},{10,11... | collective-permute-start | bytes 9437192 | tf_op jit(solution)/shard_map/ppermute | solution.py:127
  9.8 197.4 %collective-permute-start.1 = (bf16[48,256,128]{2,1,0:T(8,128)(2,1)}, bf16[48,256,128]{2,1,0:T(8,128)(2,1)}, u32[]{:S(2)}, u32[]{:S(2)}) collective-permute-start(bf16[48,256,128]{2,1,0:T(8,128)(2,1)} %get-tuple-element.22), channel_id=1, source_target_pairs={{0,2},{1,3},{2,0},{3,1},{4,6},{5,7},{6,4},{7,5},{8,10},{9,11},{10,... | collective-permute-start | bytes 9437192 | tf_op jit(solution)/shard_map/ppermute | solution.py:127
  12.4 194.8 %collective-permute-start.2 = (bf16[48,256,128]{2,1,0:T(8,128)(2,1)}, bf16[48,256,128]{2,1,0:T(8,128)(2,1)}, u32[]{:S(2)}, u32[]{:S(2)}) collective-permute-start(bf16[48,256,128]{2,1,0:T(8,128)(2,1)} %get-tuple-element.21), channel_id=1, source_target_pairs={{0,3},{1,2},{2,1},{3,0},{4,7},{5,6},{6,5},{7,4},{8,11},{9,10},{10,... | collective-permute-start | bytes 9437192 | tf_op jit(solution)/shard_map/ppermute | solution.py:127
  12.5 4.6 %copy-start.5 = (f32[1,256,16]{1,2,0:T(8,128)S(1)}, f32[1,256,16]{1,2,0:T(8,128)}, u32[]{:S(2)}) copy-start(f32[1,256,16]{1,2,0:T(8,128)} %param.5) | copy-start | bytes 49156
  12.5 4.6 %copy-start.6 = (f32[256]{0:T(256)S(1)}, f32[256]{0:T(256)}, u32[]{:S(2)}) copy-start(f32[256]{0:T(256)} %param.7) | copy-start | bytes 3076
  16.9 9.3 %collective-permute-start.3 = (bf16[16,256,128]{2,1,0:T(8,128)(2,1)}, bf16[16,256,128]{2,1,0:T(8,128)(2,1)}, u32[]{:S(2)}, u32[]{:S(2)}) collective-permute-start(bf16[16,256,128]{2,1,0:T(8,128)(2,1)} %get-tuple-element.18), channel_id=1, source_target_pairs={{0,1},{1,0},{2,3},{3,2},{4,5},{5,4},{6,7},{7,6},{8,9},{9,8},{10,11... | collective-permute-start | bytes 3145736 | tf_op jit(solution)/shard_map/ppermute | solution.py:127
  18.0 139.0 %all-to-all-start = ((f32[32,17,256]{2,1,0:T(8,128)}), f32[32,17,256]{2,1,0:T(8,128)}, u32[]{:S(2)}, u32[]{:S(2)}) async-start(f32[32,17,256]{2,1,0:T(8,128)} %broadcast_in_dim.13), calls=%async_computation | async-start | bytes 1572864 | tf_op jit(solution)/shard_map/all_to_all | solution.py:98
  24.4 155.6 %collective-permute-start.4 = (bf16[16,256,128]{2,1,0:T(8,128)(2,1)}, bf16[16,256,128]{2,1,0:T(8,128)(2,1)}, u32[]{:S(2)}, u32[]{:S(2)}) collective-permute-start(bf16[16,256,128]{2,1,0:T(8,128)(2,1)} %get-tuple-element.20), channel_id=1, source_target_pairs={{0,2},{1,3},{2,0},{3,1},{4,6},{5,7},{6,4},{7,5},{8,10},{9,11},{10,... | collective-permute-start | bytes 3145736 | tf_op jit(solution)/shard_map/ppermute | solution.py:127
  26.2 175.8 %collective-permute-start.5 = (bf16[16,256,128]{2,1,0:T(8,128)(2,1)}, bf16[16,256,128]{2,1,0:T(8,128)(2,1)}, u32[]{:S(2)}, u32[]{:S(2)}) collective-permute-start(bf16[16,256,128]{2,1,0:T(8,128)(2,1)} %get-tuple-element.17), channel_id=1, source_target_pairs={{0,3},{1,2},{2,1},{3,0},{4,7},{5,6},{6,5},{7,4},{8,11},{9,10},{10,... | collective-permute-start | bytes 3145736 | tf_op jit(solution)/shard_map/ppermute | solution.py:127
  158.1 43.9 %copy-start.3 = (f32[8,4,16,256]{3,2,1,0:T(8,128)}, f32[8,4,16,256]{3,2,1,0:T(8,128)S(1)}, u32[]{:S(2)}) copy-start(f32[8,4,16,256]{3,2,1,0:T(8,128)S(1)} %slice.28) | copy-start | bytes 1572868
  201.9 1.2 copy-start.1
  207.2 29.0 %copy-start.7 = (f32[128]{0:T(128)S(1)}, f32[128]{0:T(128)}, u32[]{:S(2)}) copy-start(f32[128]{0:T(128)} %param.6) | copy-start | bytes 1540
  216.5 30.4 %copy-start.4 = (f32[8,4,16,256]{3,2,1,0:T(8,128)S(1)}, f32[8,4,16,256]{3,2,1,0:T(8,128)}, u32[]{:S(2)}) copy-start(f32[8,4,16,256]{3,2,1,0:T(8,128)} %copy-done.3) | copy-start | bytes 1572868
  232.9 20.4 %copy-start.2 = (bf16[16,256,128]{2,1,0:T(8,128)(2,1)S(1)}, bf16[16,256,128]{2,1,0:T(8,128)(2,1)}, u32[]{:S(2)}) copy-start(bf16[16,256,128]{2,1,0:T(8,128)(2,1)} %get-tuple-element.19.refs_0_.refs_4_) | copy-start | bytes 3145732
  233.7 13.2 %all-to-all-start.2 = ((bf16[32,16,256]{2,1,0:T(8,128)(2,1)}), bf16[32,16,256]{2,1,0:T(8,128)(2,1)S(1)}, u32[]{:S(2)}, u32[]{:S(2)}) async-start(bf16[32,16,256]{2,1,0:T(8,128)(2,1)} %broadcast_in_dim.14), calls=%async_computation.2 | async-start | bytes 524288 | tf_op jit(solution)/shard_map/all_to_all | solution.py:98
  266.9 13.2 %all-to-all-start.3 = ((bf16[32,16,256]{2,1,0:T(8,128)(2,1)}), bf16[32,16,256]{2,1,0:T(8,128)(2,1)S(1)}, u32[]{:S(2)}, u32[]{:S(2)}) async-start(bf16[32,16,256]{2,1,0:T(8,128)(2,1)} %bitcast.15), calls=%async_computation.3 | async-start | bytes 524288 | tf_op jit(solution)/shard_map/all_to_all | solution.py:140

commit v2 on v1

v2 whole, which is shorter than its diff:
```python
import functools

import jax
import jax.numpy as jnp
from jax import lax
from jax.experimental import pallas as pl
from jax.experimental.pallas import tpu as pltpu
from jax.sharding import PartitionSpec as P

ITERS = 2
EVERY = ("aux", "vir")


def contract_body(nv, counts, block, group, order_ref, xt_ref, carry_ref, *refs):
    f_refs, out_ref, acc_ref = refs[:-2], refs[-2], refs[-1]
    step = pl.program_id(0)
    occ, width = xt_ref.shape[1:]

    @pl.when(step == 0)
    def _():
        acc_ref[...] = jnp.zeros_like(acc_ref) if carry_ref is None else carry_ref[...]

    xt = jnp.concatenate([xt_ref[order_ref[k]] for k in range(nv)], axis=1)
    eye = lax.broadcasted_iota(jnp.int32, (occ, occ), 0) == lax.broadcasted_iota(
        jnp.int32, (occ, occ), 1
    )

    def work(blocks):
        for first in range(0, block, group):
            tall = jnp.concatenate(
                [
                    jnp.concatenate([blocks[k][first + q] for q in range(group)], axis=1)
                    for k in range(nv)
                ],
                axis=0,
            )
            pairs = jnp.dot(xt, tall, preferred_element_type=jnp.float32)
            mixes = []
            for q in range(group):
                pair = pairs[:, q * occ : (q + 1) * occ]
                density = jnp.sum(jnp.where(eye, pair, 0.0), keepdims=True)
                density = density.astype(jnp.bfloat16).astype(jnp.float32)
                pair = pair.astype(jnp.bfloat16).astype(jnp.float32)
                mixes.append((jnp.where(eye, 2.0 * density, 0.0) - pair).astype(jnp.bfloat16))
            mix = jnp.concatenate(mixes, axis=0)
            acc_ref[...] += jnp.dot(tall, mix, preferred_element_type=jnp.float32)

    start = 0
    for c, n in enumerate(counts):

        @pl.when((step >= start) & (step < start + n))
        def _(c=c):
            work(f_refs[c * nv : (c + 1) * nv])

        start += n

    @pl.when(step == start - 1)
    def _():
        if len(out_ref.shape) == 2:
            out_ref[...] = acc_ref[...]
            return
        share = out_ref.shape[2]
        for k in range(nv):
            turned = acc_ref[k * width : (k + 1) * width, :].T
            for r in range(occ // share):
                rows = turned[r * share : (r + 1) * share, :]
                out_ref[r, order_ref[k]] = rows.astype(out_ref.dtype)


def contract(order, xt, chunks, bounds, block, carry=None, aux_count=None):
    nv, occ, width = xt.shape
    counts = [(high - low) // block for low, high in bounds]
    whole = pl.BlockSpec((nv * width, occ), lambda g, order: (0, 0))
    specs = [pl.BlockSpec((nv, occ, width), lambda g, order: (0, 0, 0))]
    if carry is not None:
        specs.append(whole)
    start = 0
    for n, (low, high) in zip(counts, bounds):

        def near(g, order, s=start, m=n, skip=low // block):
            return (order[nv] + skip + jnp.clip(g - s, 0, m - 1), 0, 0)

        def far(g, order, s=start, m=n):
            return (jnp.clip(g - s, 0, m - 1), 0, 0)

        specs.append(pl.BlockSpec((block, width, occ), near))
        specs += [pl.BlockSpec((block, width, occ), far)] * (nv - 1)
        start += n
    body = functools.partial(contract_body, nv, counts, block, block)
    if carry is None:
        body = functools.partial(lambda f, o, x, *refs: f(o, x, None, *refs), body)
    if aux_count is None:
        out_spec, out = whole, jax.ShapeDtypeStruct((nv * width, occ), jnp.float32)
    else:
        shape = (aux_count, nv, occ // aux_count, width)
        out_spec = pl.BlockSpec(shape, lambda g, order: (0, 0, 0, 0))
        out = jax.ShapeDtypeStruct(shape, jnp.bfloat16)
    return pl.pallas_call(
        body,
        grid_spec=pltpu.PrefetchScalarGridSpec(
            num_scalar_prefetch=1,
            grid=(start,),
            in_specs=specs,
            out_specs=out_spec,
            scratch_shapes=[pltpu.VMEM((nv * width, occ), jnp.float32)],
        ),
        out_shape=out,
        compiler_params=pltpu.CompilerParams(vmem_limit_bytes=48 * 2**20),
        cost_estimate=pl.CostEstimate(
            flops=4 * start * block * nv * width * occ * occ,
            bytes_accessed=2 * start * block * nv * width * occ,
            transcendentals=0,
        ),
    )(order, xt, *([] if carry is None else [carry]), *[part for chunk in chunks for part in chunk])


def five_sums(trial, gap, coupling):
    rounded = trial.astype(jnp.bfloat16).astype(jnp.float32)
    image = gap * rounded + coupling
    scaled_trial = trial / gap
    scaled_diff = trial - image / gap

    def total(values):
        return jnp.sum(values, keepdims=True)

    sums = (
        total(trial * image),
        total(trial * trial),
        total(scaled_diff * scaled_diff),
        total(scaled_diff * scaled_trial),
        total(scaled_trial * scaled_trial),
    )
    return scaled_diff, scaled_trial, sums


def finish(scaled_diff, scaled_trial, sums, count):
    cross_sum, self_sum, diff_sum, mixed_sum, scaled_sum = sums
    shift = cross_sum / self_sum
    mean_square = (diff_sum + 2.0 * shift * mixed_sum + shift * shift * scaled_sum) / count
    return (scaled_diff + shift * scaled_trial) * lax.rsqrt(mean_square + 1e-06), shift


def step_whole(coupling_shares, trial, gap, aux_count):
    nv, occ, width = trial.shape
    share = occ // aux_count

    def body(shares_ref, trial_ref, gap_ref, next_ref, xt_ref, shift_ref, coupling_ref):
        for r in range(aux_count):
            for v in range(nv):
                rows = shares_ref[r * nv + v].astype(jnp.float32)
                coupling_ref[v * occ + r * share : v * occ + (r + 1) * share, :] = rows
        diff, scaled, sums = five_sums(
            trial_ref[...].reshape(nv * occ, width), gap_ref[...].reshape(nv * occ, width), coupling_ref[...]
        )
        fresh, shift = finish(diff, scaled, sums, nv * occ * width)
        fresh = fresh.reshape(nv, occ, width)
        next_ref[...] = fresh
        xt_ref[...] = fresh.astype(jnp.bfloat16)
        shift_ref[...] = jnp.broadcast_to(shift, shift_ref.shape)

    return pl.pallas_call(
        body,
        out_shape=(
            jax.ShapeDtypeStruct(trial.shape, jnp.float32),
            jax.ShapeDtypeStruct(trial.shape, jnp.bfloat16),
            jax.ShapeDtypeStruct((1, 128), jnp.float32),
        ),
        scratch_shapes=[pltpu.VMEM((nv * occ, width), jnp.float32)],
        compiler_params=pltpu.CompilerParams(vmem_limit_bytes=24 * 2**20),
    )(coupling_shares, trial, gap)


def share_sums(terms, trial, gap):
    count = terms.shape[0]

    def body(terms_ref, trial_ref, gap_ref, diff_ref, scaled_ref, sums_ref):
        coupling = jnp.sum(terms_ref[...].astype(jnp.float32), axis=0)
        diff, scaled, sums = five_sums(trial_ref[...], gap_ref[...], coupling)
        diff_ref[...] = diff
        scaled_ref[...] = scaled
        lane = lax.broadcasted_iota(jnp.int32, (1, 128), 1)
        row = jnp.zeros((1, 128), jnp.float32)
        for at, value in enumerate(sums):
            row = jnp.where(lane == at, value, row)
        sums_ref[...] = jnp.broadcast_to(row[None], sums_ref.shape)

    like = jax.ShapeDtypeStruct(trial.shape, jnp.float32)
    return pl.pallas_call(
        body,
        out_shape=(like, like, jax.ShapeDtypeStruct((count, 1, 128), jnp.float32)),
        compiler_params=pltpu.CompilerParams(vmem_limit_bytes=24 * 2**20),
    )(terms, trial, gap)


def step_share(diff, scaled, all_sums, total):
    def body(diff_ref, scaled_ref, sums_ref, next_ref, shift_ref):
        row = jnp.sum(sums_ref[...], axis=0)
        fresh, shift = finish(
            diff_ref[...], scaled_ref[...], [row[:, at : at + 1] for at in range(5)], total
        )
        next_ref[...] = fresh
        shift_ref[...] = jnp.broadcast_to(shift, shift_ref.shape)

    return pl.pallas_call(
        body,
        out_shape=(
            jax.ShapeDtypeStruct(diff.shape, jnp.float32),
            jax.ShapeDtypeStruct((1, 128), jnp.float32),
        ),
    )(diff, scaled, all_sums)


def spread(share, count):
    copies = jnp.broadcast_to(share[None], (count,) + share.shape)
    return lax.all_to_all(copies, EVERY, 0, 0, tiled=True)


def local(factors, trials, occ_energy, vir_energy):
    na, nv = lax.axis_size("aux"), lax.axis_size("vir")
    count = na * nv
    aux_at, vir_at = lax.axis_index("aux"), lax.axis_index("vir")
    p_count, width, occ = factors.shape
    own = p_count // nv
    share = occ // na
    total = occ * width * nv
    paired = nv & (nv - 1) == 0

    def partner(at, k):
        return at ^ k if paired else (at + k) % nv

    def source(at, k):
        return at ^ k if paired else (at - k) % nv

    block = next(n for n in (8, 4, 2, 1) if own % n == 0)
    cuts = [0, own]
    if own >= 8 * block:
        cuts = [0, 2 * block, own - block, own]
    bounds = list(zip(cuts, cuts[1:]))

    message = jnp.concatenate([trials[0].T, vir_energy[None]], axis=0)
    begin = spread(message, count)
    chunks = []
    for at, (low, high) in enumerate(bounds):
        parts = [factors]
        for k in range(1, nv):
            piece = lax.dynamic_slice_in_dim(
                factors, partner(vir_at, k) * own + low, high - low, 0
            )
            if at:
                piece, chunks[-1][k] = lax.optimization_barrier((piece, chunks[-1][k]))
            pairs = [(one, partner(one, k)) for one in range(nv)]
            parts.append(lax.ppermute(piece, "vir", pairs))
        chunks.append(parts)
    order = jnp.stack([source(vir_at, k) for k in range(nv)] + [vir_at * (own // block)])
    order = order.astype(jnp.int32)

    begin = begin.reshape(na, nv, share + 1, width)
    trial = begin[:, :, :share].transpose(1, 0, 2, 3).reshape(nv, occ, width)
    gap = begin[0, :, share:] - occ_energy[None, :, None]
    gap_own = vir_energy[None, :] - lax.dynamic_slice_in_dim(occ_energy, aux_at * share, share)[:, None]
    xt = trial.astype(jnp.bfloat16)

    shift_list = []
    for iteration in range(ITERS):
        if iteration == 0:
            carry = None
            for chunk, bound in zip(chunks[:-1], bounds[:-1]):
                carry = contract(order, xt, [chunk], [bound], block, carry)
            partial = contract(order, xt, chunks[-1:], bounds[-1:], block, carry, na)
        else:
            partial = contract(order, xt, chunks, bounds, block, None, na)
        terms = lax.all_to_all(partial.reshape(count, share, width), EVERY, 0, 0, tiled=True)
        if iteration < ITERS - 1:
            coupling = jnp.sum(terms.astype(jnp.float32), axis=0).astype(jnp.bfloat16)
            trial, xt, shift = step_whole(spread(coupling, count), trial, gap, na)
        else:
            trial_own = lax.dynamic_slice(
                trial, (vir_at, aux_at * share, 0), (1, share, width)
            ).reshape(share, width)
            diff, scaled, sums = share_sums(terms, trial_own, gap_own)
            sums = lax.all_to_all(sums, EVERY, 0, 0, tiled=True)
            fresh, shift = step_share(diff, scaled, sums, total)
        shift_list.append(shift[:, :1])
    return (fresh.T[None], jnp.concatenate(shift_list, axis=0))


def solution(mesh):
    placed = (P("aux", "vir", None), P(None, "vir", "aux"), P(), P("vir"))
    return jax.shard_map(
        local, mesh=mesh, in_specs=placed, out_specs=(P(None, "vir", "aux"), P()), check_vma=False
    )
```

time: 300 us -> 278 us (0.927)
  waiting for transfers between devices: 193 us -> 176 us
  between operations: 7.44 us -> 0.96 us
  Pallas kernels: 26.2 us -> 32.3 us
  other arithmetic: 6.05 us -> 1.75 us
    all_to_all x2, waiting for transfers between devices: 140 us -> 119 us  [spread(): return lax.all_to_all(copies, EVERY, 0, 0, tiled=True)]
    pallas_call x3 -> x7, Pallas kernels: 26.2 us -> 32.3 us  [the longest x4 29.9 us: contract(): pl.pallas_call(body, grid_spec=pltpu.PrefetchScalarGridSpec(num_scalar_pr...]
    unnamed x18 -> x45, local copies, waits for them, and re-layouts: 1.61 us -> 5.61 us
    ppermute x6 -> x9, starting transfers between devices: 5.02 us -> 8.91 us  [local(): parts.append(lax.ppermute(piece, 'vir', pairs))]
    ppermute x6 -> x9, waiting for transfers between devices: 43.4 us -> 46.8 us  [local(): parts.append(lax.ppermute(piece, 'vir', pairs))]
    another operation x1, local copies, waits for them, and re-layouts: 3.24 us -> 0.09 us  [local(): jnp.stack([source(vir_at, k) for k in range(nv)] + [vir_at * (own // bloc...]
    dynamic_slice x2 -> x3, local copies, waits for them, and re-layouts: 13.1 us -> 12.8 us  [local(): lax.dynamic_slice_in_dim(factors, partner(vir_at, k) * own + low, high -...]
  transfers between devices with their start and end apart: 9 -> 12, of which waited for: 5 -> 6; matrix products, arithmetic and copies ran while one was open for 3% -> 5% of each run, Pallas kernels for 1% -> 5%
where the time goes in v2:
time: 278 us; the launch traced here: 277 us
  waiting for transfers between devices  176 us (63%)
  Pallas kernels  32.3 us (12%)
  blocking collectives  25.7 us (9%)
  local copies, waits for them, and re-layouts  22.1 us (8%)
  starting transfers between devices  19 us (7%)
    all_to_all x2, waiting for transfers between devices, spread(): return lax.all_to_all(copies, EVERY, 0, 0, tiled=True)  119 us
    ppermute x9, waiting for transfers between devices, local(): parts.append(lax.ppermute(piece, 'vir', pairs))  46.8 us
    pallas_call x4, Pallas kernels, contract(): pl.pallas_call(body, grid_spec=pltpu.PrefetchScalarGridSpec(num_scalar_pr...  29.9 us
    all_to_all x1, blocking collectives, local(): lax.all_to_all(partial.reshape(count, share, width), EVERY, 0, 0, tiled=T...  16.4 us
    dynamic_slice x3, local copies, waits for them, and re-layouts, local(): lax.dynamic_slice_in_dim(factors, partner(vir_at, k) * own + low, high -...  12.8 us
    all_to_all x1, waiting for transfers between devices, local(): lax.all_to_all(partial.reshape(count, share, width), EVERY, 0, 0, tiled=T...  9.72 us
    all_to_all x1, blocking collectives, local(): sums = lax.all_to_all(sums, EVERY, 0, 0, tiled=True)  9.31 us
    ppermute x9, starting transfers between devices, local(): parts.append(lax.ppermute(piece, 'vir', pairs))  8.91 us
  transfers between devices with their start and end apart: 12, of which 6 were waited for; matrix products, arithmetic and copies ran while one was open for 5% of the time, Pallas kernels for 5%

profile of v2, /device:TPU:0, one launch (start us, length us, event | category | flops | bytes accessed | tf_op | source)
XLA Modules:
  0.0 277.5 jit_solution(10924449383883983451)
XLA Ops:
  0.7 3.5 %constant_dynamic-slice_fusion.3 = (bf16[16,256,128]{2,1,0:T(8,128)(2,1)}, bf16[16,256,128]{2,1,0:T(8,128)(2,1)}, bf16[16,256,128]{2,1,0:T(8,128)(2,1)S(1)}) fusion(bf16[256,256,128]{2,1,0:T(8,128)(2,1)} %refs_8_.1, s32[]{:T(128)S(6)} %select_n.39, s32[]{:T(128)S(6)} %select_n.37, s32[]{:T(128)S(6)} %select_n.35), kind=kLoop, calls=%fused_computation.9 | loop fusion | bytes 6291468 | tf_op jit(solution)/shard_map/dynamic_slice | solution.py:246
  4.6 2.5 collective-permute-start.1
  7.3 6.7 %constant_dynamic-slice_fusion.4 = (bf16[40,256,128]{2,1,0:T(8,128)(2,1)}, bf16[40,256,128]{2,1,0:T(8,128)(2,1)}, bf16[40,256,128]{2,1,0:T(8,128)(2,1)}) fusion(bf16[256,256,128]{2,1,0:T(8,128)(2,1)} %refs_8_.1, s32[]{:T(128)S(6)} %select_n.38, s32[]{:T(128)S(6)} %select_n.36, s32[]{:T(128)S(6)} %select_n.34), kind=kLoop, calls=%fused_computation.10 | loop fusion | bytes 15728652 | tf_op jit(solution)/shard_map/dynamic_slice | solution.py:246
  15.1 16.4 %collective-permute-done.1.refs_2_ = bf16[16,256,128]{2,1,0:T(8,128)(2,1)} collective-permute-done((bf16[16,256,128]{2,1,0:T(8,128)(2,1)}, bf16[16,256,128]{2,1,0:T(8,128)(2,1)}, u32[]{:S(2)}, u32[]{:S(2)}) %collective-permute-start.1) | collective-permute-done | bytes 1048608 | tf_op jit(solution)/shard_map/ppermute | solution.py:252
  31.5 1.9 collective-permute-start.4
  33.4 20.2 %collective-permute-done.2.refs_3_ = bf16[16,256,128]{2,1,0:T(8,128)(2,1)} collective-permute-done((bf16[16,256,128]{2,1,0:T(8,128)(2,1)}, bf16[16,256,128]{2,1,0:T(8,128)(2,1)}, u32[]{:S(2)}, u32[]{:S(2)}) %collective-permute-start.2) | collective-permute-done | bytes 1048608 | tf_op jit(solution)/shard_map/ppermute | solution.py:252
  53.6 1.7 collective-permute-start.5
  56.3 4.9 %all-to-all-start = ((f32[32,17,256]{2,1,0:T(8,128)}), f32[32,17,256]{2,1,0:T(8,128)S(1)}, u32[]{:S(2)}, u32[]{:S(2)}) async-start(f32[32,17,256]{2,1,0:T(8,128)} %broadcast_in_dim.9), calls=%async_computation | async-start | bytes 1572864 | tf_op jit(solution)/shard_map/all_to_all | solution.py:215
  61.3 2.5 constant_dynamic-slice_fusion
  63.8 110.3 %all-to-all-done = f32[32,17,256]{2,1,0:T(8,128)S(1)} async-done(((f32[32,17,256]{2,1,0:T(8,128)}), f32[32,17,256]{2,1,0:T(8,128)S(1)}, u32[]{:S(2)}, u32[]{:S(2)}) %all-to-all-start) | async-done | bytes 557088 | tf_op jit(solution)/shard_map/all_to_all | solution.py:215
  175.6 1.8 collective-permute-start.7
  177.5 4.4 %shard_map.59.carry_ref = f32[1024,128]{1,0:T(8,128)S(1)} custom-call(s32[5]{0:T(128)S(1)} %stack.23.o.order_ref, bf16[4,128,256]{2,1,0:T(8,128)(2,1)S(1)} %bitcast_convert_fusion.x.xt_ref, bf16[256,256,128]{2,1,0:T(8,128)(2,1)} %refs_8_.1, bf16[16,256,128]{2,1,0:T(8,128)(2,1)S(1)} %copy-done.2, bf16[16,256,128]{2,1,0:T(8,128)(2,1)} %collective-permute-done.1.refs_2_, ...), custom_call_target="tpu_custom_call" | custom-call | flops 1073741824 | bytes 4194304 | tf_op jit(solution)/shard_map/pallas_call | solution.py:98
  182.0 8.3 %shard_map.60.carry_ref = f32[1024,128]{1,0:T(8,128)S(1)} custom-call(s32[5]{0:T(128)S(1)} %stack.23.o.order_ref, bf16[4,128,256]{2,1,0:T(8,128)(2,1)S(1)} %bitcast_convert_fusion.x.xt_ref, f32[1024,128]{1,0:T(8,128)S(1)} %shard_map.59.carry_ref, bf16[256,256,128]{2,1,0:T(8,128)(2,1)} %refs_8_.1, ...), custom_call_target="tpu_custom_call" | custom-call | flops 2684354560 | bytes 10485760 | tf_op jit(solution)/shard_map/pallas_call | solution.py:98
  190.4 10.2 %collective-permute-done.8.refs_3_.refs_11_ = bf16[8,256,128]{2,1,0:T(8,128)(2,1)S(1)} collective-permute-done((bf16[8,256,128]{2,1,0:T(8,128)(2,1)S(1)}, bf16[8,256,128]{2,1,0:T(8,128)(2,1)S(1)}, u32[]{:S(2)}, u32[]{:S(2)}) %collective-permute-start.8) | collective-permute-done | bytes 524320 | tf_op jit(solution)/shard_map/ppermute | solution.py:252
  200.6 2.8 %shard_map.61 = bf16[8,4,16,256]{3,2,1,0:T(8,128)(2,1)S(1)} custom-call(s32[5]{0:T(128)S(1)} %stack.23.o.order_ref, bf16[4,128,256]{2,1,0:T(8,128)(2,1)S(1)} %bitcast_convert_fusion.x.xt_ref, f32[1024,128]{1,0:T(8,128)S(1)} %shard_map.60.carry_ref, bf16[256,256,128]{2,1,0:T(8,128)(2,1)} %refs_8_.1, ...), custom_call_target="tpu_custom_call" | custom-call | flops 536870912 | bytes 2097152 | tf_op jit(solution)/shard_map/pallas_call | solution.py:98
  203.5 16.4 %all_to_all.25 = bf16[32,16,256]{2,1,0:T(8,128)(2,1)S(1)} all-to-all(bf16[32,16,256]{2,1,0:T(8,128)(2,1)S(1)} %bitcast.28), channel_id=1, replica_groups=mesh['aux'=8,'vir'=4] {'aux','vir'}, dimensions={0} | all-to-all | bytes 524288 | tf_op jit(solution)/shard_map/all_to_all | solution.py:272
  220.7 2.6 all-to-all-start.2
  225.0 8.9 %all-to-all-done.2.shares_ref = bf16[32,16,256]{2,1,0:T(8,128)(2,1)S(1)} async-done(((bf16[32,16,256]{2,1,0:T(8,128)(2,1)}), bf16[32,16,256]{2,1,0:T(8,128)(2,1)S(1)}, u32[]{:S(2)}, u32[]{:S(2)}) %all-to-all-start.2) | async-done | bytes 262176 | tf_op jit(solution)/shard_map/all_to_all | solution.py:215
  233.9 1.0 copy-done.10
  236.5 14.3 %shard_map.63 = bf16[8,4,16,256]{3,2,1,0:T(8,128)(2,1)} custom-call(s32[5]{0:T(128)S(1)} %stack.23.o.order_ref, bf16[4,128,256]{2,1,0:T(8,128)(2,1)S(1)} %get-tuple-element.34.x, bf16[256,256,128]{2,1,0:T(8,128)(2,1)} %refs_8_.1, bf16[16,256,128]{2,1,0:T(8,128)(2,1)S(1)} %copy-done.3, bf16[16,256,128]{2,1,0:T(8,128)(2,1)} %collective-permute-done.1.refs_2_, ...), custom_call_target="tpu_custom_call" | custom-call | flops 4294967296 | bytes 16777216 | tf_op jit(solution)/shard_map/pallas_call | solution.py:98
  250.7 2.6 all-to-all-start.3
  254.2 9.7 %all-to-all-done.3.terms_ref = bf16[32,16,256]{2,1,0:T(8,128)(2,1)S(1)} async-done(((bf16[32,16,256]{2,1,0:T(8,128)(2,1)}), bf16[32,16,256]{2,1,0:T(8,128)(2,1)S(1)}, u32[]{:S(2)}, u32[]{:S(2)}) %all-to-all-start.3) | async-done | bytes 262176 | tf_op jit(solution)/shard_map/all_to_all | solution.py:272
  265.3 9.3 %all_to_all.26.sums_ref = f32[32,1,128]{2,1,0:T(1,128)} all-to-all(f32[32,1,128]{2,1,0:T(1,128)S(1)} %get-tuple-element.38), channel_id=1, replica_groups=mesh['aux'=8,'vir'=4] {'aux','vir'}, dimensions={0} | all-to-all | bytes 32768 | tf_op jit(solution)/shard_map/all_to_all | solution.py:281
  274.6 1.6 shard_map.65
  (71 shorter events, 11.7 us)
Async XLA Ops:
  4.2 9.9 %collective-permute-start = (bf16[16,256,128]{2,1,0:T(8,128)(2,1)S(1)}, bf16[16,256,128]{2,1,0:T(8,128)(2,1)S(1)}, u32[]{:S(2)}, u32[]{:S(2)}) collective-permute-start(bf16[16,256,128]{2,1,0:T(8,128)(2,1)S(1)} %get-tuple-element.53), channel_id=1, source_target_pairs={{0,1},{1,0},{2,3},{3,2},{4,5},{5,4},{6,7},{7,6},{8,9},{9,8},{10,11... | collective-permute-start | bytes 3145736 | tf_op jit(solution)/shard_map/ppermute | solution.py:252
  4.6 26.8 %collective-permute-start.1 = (bf16[16,256,128]{2,1,0:T(8,128)(2,1)}, bf16[16,256,128]{2,1,0:T(8,128)(2,1)}, u32[]{:S(2)}, u32[]{:S(2)}) collective-permute-start(bf16[16,256,128]{2,1,0:T(8,128)(2,1)} %get-tuple-element.52), channel_id=1, source_target_pairs={{0,2},{1,3},{2,0},{3,1},{4,6},{5,7},{6,4},{7,5},{8,10},{9,11},{10,... | collective-permute-start | bytes 3145736 | tf_op jit(solution)/shard_map/ppermute | solution.py:252
  7.1 46.4 %collective-permute-start.2 = (bf16[16,256,128]{2,1,0:T(8,128)(2,1)}, bf16[16,256,128]{2,1,0:T(8,128)(2,1)}, u32[]{:S(2)}, u32[]{:S(2)}) collective-permute-start(bf16[16,256,128]{2,1,0:T(8,128)(2,1)} %get-tuple-element.51), channel_id=1, source_target_pairs={{0,3},{1,2},{2,1},{3,0},{4,7},{5,6},{6,5},{7,4},{8,11},{9,10},{10,... | collective-permute-start | bytes 3145736 | tf_op jit(solution)/shard_map/ppermute | solution.py:252
  7.3 48.0 %copy-start.18 = (f32[1,256,16]{1,2,0:T(8,128)S(1)}, f32[1,256,16]{1,2,0:T(8,128)}, u32[]{:S(2)}) copy-start(f32[1,256,16]{1,2,0:T(8,128)} %param.5) | copy-start | bytes 49156
  7.3 48.0 %copy-start.19 = (f32[256]{0:T(256)S(1)}, f32[256]{0:T(256)}, u32[]{:S(2)}) copy-start(f32[256]{0:T(256)} %param.7) | copy-start | bytes 3076
  15.0 160.3 %collective-permute-start.3 = (bf16[40,256,128]{2,1,0:T(8,128)(2,1)}, bf16[40,256,128]{2,1,0:T(8,128)(2,1)S(1)}, u32[]{:S(2)}, u32[]{:S(2)}) collective-permute-start(bf16[40,256,128]{2,1,0:T(8,128)(2,1)} %get-tuple-element.25), channel_id=1, source_target_pairs={{0,1},{1,0},{2,3},{3,2},{4,5},{5,4},{6,7},{7,6},{8,9},{9,8},{10,11... | collective-permute-start | bytes 7864328 | tf_op jit(solution)/shard_map/ppermute | solution.py:252
  31.5 144.1 %collective-permute-start.4 = (bf16[40,256,128]{2,1,0:T(8,128)(2,1)}, bf16[40,256,128]{2,1,0:T(8,128)(2,1)}, u32[]{:S(2)}, u32[]{:S(2)}) collective-permute-start(bf16[40,256,128]{2,1,0:T(8,128)(2,1)} %get-tuple-element.27), channel_id=1, source_target_pairs={{0,2},{1,3},{2,0},{3,1},{4,6},{5,7},{6,4},{7,5},{8,10},{9,11},{10,... | collective-permute-start | bytes 7864328 | tf_op jit(solution)/shard_map/ppermute | solution.py:252
  53.6 123.8 %collective-permute-start.5 = (bf16[40,256,128]{2,1,0:T(8,128)(2,1)}, bf16[40,256,128]{2,1,0:T(8,128)(2,1)}, u32[]{:S(2)}, u32[]{:S(2)}) collective-permute-start(bf16[40,256,128]{2,1,0:T(8,128)(2,1)} %get-tuple-element.29), channel_id=1, source_target_pairs={{0,3},{1,2},{2,1},{3,0},{4,7},{5,6},{6,5},{7,4},{8,11},{9,10},{10,... | collective-permute-start | bytes 7864328 | tf_op jit(solution)/shard_map/ppermute | solution.py:252
  56.3 117.8 %all-to-all-start = ((f32[32,17,256]{2,1,0:T(8,128)}), f32[32,17,256]{2,1,0:T(8,128)S(1)}, u32[]{:S(2)}, u32[]{:S(2)}) async-start(f32[32,17,256]{2,1,0:T(8,128)} %broadcast_in_dim.9), calls=%async_computation | async-start | bytes 1572864 | tf_op jit(solution)/shard_map/all_to_all | solution.py:215
  174.1 3.3 %copy-start.15 = (bf16[8,256,128]{2,1,0:T(8,128)(2,1)S(1)}, bf16[8,256,128]{2,1,0:T(8,128)(2,1)}, u32[]{:S(2)}) copy-start(bf16[8,256,128]{2,1,0:T(8,128)(2,1)} %get-tuple-element.33) | copy-start | bytes 1572868
  174.1 3.4 %copy-start.2 = (bf16[16,256,128]{2,1,0:T(8,128)(2,1)S(1)}, bf16[16,256,128]{2,1,0:T(8,128)(2,1)}, u32[]{:S(2)}) copy-start(bf16[16,256,128]{2,1,0:T(8,128)(2,1)} %copy-done.1) | copy-start | bytes 3145732
  175.3 6.6 %copy-start = (bf16[40,256,128]{2,1,0:T(8,128)(2,1)}, bf16[40,256,128]{2,1,0:T(8,128)(2,1)S(1)}, u32[]{:S(2)}) copy-start(bf16[40,256,128]{2,1,0:T(8,128)(2,1)S(1)} %collective-permute-done.3.refs_1_.refs_5_) | copy-start | bytes 7864324
  175.4 14.9 %collective-permute-start.6 = (bf16[8,256,128]{2,1,0:T(8,128)(2,1)S(1)}, bf16[8,256,128]{2,1,0:T(8,128)(2,1)S(1)}, u32[]{:S(2)}, u32[]{:S(2)}) collective-permute-start(bf16[8,256,128]{2,1,0:T(8,128)(2,1)S(1)} %copy-done.17), channel_id=1, source_target_pairs={{0,1},{1,0},{2,3},{3,2},{4,5},{5,4},{6,7},{7,6},{8,9},{9,8},{10,11... | collective-permute-start | bytes 1572872 | tf_op jit(solution)/shard_map/ppermute | solution.py:252
  175.6 14.7 %collective-permute-start.7 = (bf16[8,256,128]{2,1,0:T(8,128)(2,1)S(1)}, bf16[8,256,128]{2,1,0:T(8,128)(2,1)S(1)}, u32[]{:S(2)}, u32[]{:S(2)}) collective-permute-start(bf16[8,256,128]{2,1,0:T(8,128)(2,1)S(1)} %copy-done.16), channel_id=1, source_target_pairs={{0,2},{1,3},{2,0},{3,1},{4,6},{5,7},{6,4},{7,5},{8,10},{9,11},{10,... | collective-permute-start | bytes 1572872 | tf_op jit(solution)/shard_map/ppermute | solution.py:252
  177.4 23.2 %collective-permute-start.8 = (bf16[8,256,128]{2,1,0:T(8,128)(2,1)S(1)}, bf16[8,256,128]{2,1,0:T(8,128)(2,1)S(1)}, u32[]{:S(2)}, u32[]{:S(2)}) collective-permute-start(bf16[8,256,128]{2,1,0:T(8,128)(2,1)S(1)} %copy-done.15), channel_id=1, source_target_pairs={{0,3},{1,2},{2,1},{3,0},{4,7},{5,6},{6,5},{7,4},{8,11},{9,10},{10,... | collective-permute-start | bytes 1572872 | tf_op jit(solution)/shard_map/ppermute | solution.py:252
  190.3 33.8 %copy-start.20 = (f32[128]{0:T(128)S(1)}, f32[128]{0:T(128)}, u32[]{:S(2)}) copy-start(f32[128]{0:T(128)} %param.6) | copy-start | bytes 1540
  190.3 13.1 %copy-start.4 = (bf16[8,256,128]{2,1,0:T(8,128)(2,1)}, bf16[8,256,128]{2,1,0:T(8,128)(2,1)S(1)}, u32[]{:S(2)}) copy-start(bf16[8,256,128]{2,1,0:T(8,128)(2,1)S(1)} %collective-permute-done.6.refs_1_.refs_9_) | copy-start | bytes 1572868
  190.3 13.1 %copy-start.6 = (bf16[8,256,128]{2,1,0:T(8,128)(2,1)}, bf16[8,256,128]{2,1,0:T(8,128)(2,1)S(1)}, u32[]{:S(2)}) copy-start(bf16[8,256,128]{2,1,0:T(8,128)(2,1)S(1)} %collective-permute-done.7.refs_2_.refs_10_) | copy-start | bytes 1572868
  203.5 33.0 %copy-start.3 = (bf16[16,256,128]{2,1,0:T(8,128)(2,1)S(1)}, bf16[16,256,128]{2,1,0:T(8,128)(2,1)}, u32[]{:S(2)}) copy-start(bf16[16,256,128]{2,1,0:T(8,128)(2,1)} %copy-done.1) | copy-start | bytes 3145732
  203.5 33.0 %copy-start.5 = (bf16[8,256,128]{2,1,0:T(8,128)(2,1)S(1)}, bf16[8,256,128]{2,1,0:T(8,128)(2,1)}, u32[]{:S(2)}) copy-start(bf16[8,256,128]{2,1,0:T(8,128)(2,1)} %copy-done.4) | copy-start | bytes 1572868
  203.5 33.0 %copy-start.7 = (bf16[8,256,128]{2,1,0:T(8,128)(2,1)S(1)}, bf16[8,256,128]{2,1,0:T(8,128)(2,1)}, u32[]{:S(2)}) copy-start(bf16[8,256,128]{2,1,0:T(8,128)(2,1)} %copy-done.6) | copy-start | bytes 1572868
  203.5 33.0 %copy-start.9 = (bf16[8,256,128]{2,1,0:T(8,128)(2,1)S(1)}, bf16[8,256,128]{2,1,0:T(8,128)(2,1)}, u32[]{:S(2)}) copy-start(bf16[8,256,128]{2,1,0:T(8,128)(2,1)} %copy-done.8) | copy-start | bytes 1572868
  220.7 13.2 %all-to-all-start.2 = ((bf16[32,16,256]{2,1,0:T(8,128)(2,1)}), bf16[32,16,256]{2,1,0:T(8,128)(2,1)S(1)}, u32[]{:S(2)}, u32[]{:S(2)}) async-start(bf16[32,16,256]{2,1,0:T(8,128)(2,1)} %broadcast_in_dim.10), calls=%async_computation.2 | async-start | bytes 524288 | tf_op jit(solution)/shard_map/all_to_all | solution.py:215
  250.7 13.2 %all-to-all-start.3 = ((bf16[32,16,256]{2,1,0:T(8,128)(2,1)}), bf16[32,16,256]{2,1,0:T(8,128)(2,1)S(1)}, u32[]{:S(2)}, u32[]{:S(2)}) async-start(bf16[32,16,256]{2,1,0:T(8,128)(2,1)} %bitcast.13), calls=%async_computation.3 | async-start | bytes 524288 | tf_op jit(solution)/shard_map/all_to_all | solution.py:272
  (9 other events, 10.6 us)

commit v3 on v2

v3 whole, which is shorter than its diff:
```python
import functools

import jax
import jax.numpy as jnp
from jax import lax
from jax.experimental import pallas as pl
from jax.experimental.pallas import tpu as pltpu
from jax.sharding import PartitionSpec as P

ITERS = 2
EVERY = ("aux", "vir")


def diagonal(occ):
    rows = lax.broadcasted_iota(jnp.int32, (occ, occ), 0)
    return rows == lax.broadcasted_iota(jnp.int32, (occ, occ), 1)


def coulomb_and_exchange(pair, eye):
    density = jnp.sum(jnp.where(eye, pair, 0.0), keepdims=True)
    density = density.astype(jnp.bfloat16).astype(jnp.float32)
    pair = pair.astype(jnp.bfloat16).astype(jnp.float32)
    return (jnp.where(eye, 2.0 * density, 0.0) - pair).astype(jnp.bfloat16)


def side_by_side(blocks, count):
    return jnp.concatenate([blocks[q] for q in range(count)], axis=1)


def contract_body(nv, bounds, own, carried, slots, order_ref, xt_ref, *refs):
    carry_ref = refs[0] if carried else None
    f_refs, (out_ref, acc_ref, held, sems) = refs[carried:-4], refs[-4:]
    occ, width = xt_ref.shape[1:]
    near_start = order_ref[nv] * own

    def copies(step):
        low, high = bounds[step]
        slot = step % slots
        made = []
        for k in range(nv):
            ref = f_refs[step * nv + k]
            if k == 0:
                ref = ref.at[pl.ds(near_start + low, high - low)]
            into = held.at[slot, k, pl.ds(0, high - low)]
            made.append(pltpu.make_async_copy(ref, into, sems.at[slot, k]))
        return made

    for step in range(min(slots, len(bounds))):
        for copy in copies(step):
            copy.start()
    acc_ref[...] = carry_ref[...] if carried else jnp.zeros_like(acc_ref)
    xt = jnp.concatenate([xt_ref[k] for k in range(nv)], axis=1)
    eye = diagonal(occ)
    for step, (low, high) in enumerate(bounds):
        for copy in copies(step):
            copy.wait()
        block = high - low
        tall = jnp.concatenate(
            [side_by_side(held.at[step % slots, k], block) for k in range(nv)], axis=0
        )
        pairs = jnp.dot(xt, tall, preferred_element_type=jnp.float32)
        mix = jnp.concatenate(
            [coulomb_and_exchange(pairs[:, q * occ : (q + 1) * occ], eye) for q in range(block)],
            axis=0,
        )
        acc_ref[...] += jnp.dot(tall, mix, preferred_element_type=jnp.float32)
        if step + slots < len(bounds):
            for copy in copies(step + slots):
                copy.start()
    if len(out_ref.shape) == 2:
        out_ref[...] = acc_ref[...]
        return
    share = out_ref.shape[2]
    for k in range(nv):
        turned = acc_ref[k * width : (k + 1) * width, :].T
        for r in range(occ // share):
            out_ref[r, order_ref[k]] = turned[r * share : (r + 1) * share, :].astype(out_ref.dtype)


def contract(order, xt, chunks, bounds, own, carry=None, aux_count=None):
    nv, occ, width = xt.shape
    carried = carry is not None
    slots = 3
    largest = max(high - low for low, high in bounds)
    count = sum(high - low for low, high in bounds)
    if aux_count is None:
        out = jax.ShapeDtypeStruct((nv * width, occ), jnp.float32)
    else:
        out = jax.ShapeDtypeStruct((aux_count, nv, occ // aux_count, width), jnp.bfloat16)
    in_vmem, anywhere = pl.BlockSpec(memory_space=pltpu.VMEM), pl.BlockSpec(memory_space=pl.ANY)
    return pl.pallas_call(
        functools.partial(contract_body, nv, bounds, own, carried, slots),
        in_specs=[pl.BlockSpec(memory_space=pltpu.SMEM)]
        + [in_vmem] * (1 + carried)
        + [anywhere] * (nv * len(chunks)),
        out_specs=in_vmem,
        out_shape=out,
        scratch_shapes=[
            pltpu.VMEM((nv * width, occ), jnp.float32),
            pltpu.VMEM((slots, nv, largest, width, occ), jnp.bfloat16),
            pltpu.SemaphoreType.DMA((slots, nv)),
        ],
        compiler_params=pltpu.CompilerParams(vmem_limit_bytes=40 * 2**20),
        cost_estimate=pl.CostEstimate(flops=0, bytes_accessed=0, transcendentals=0),
    )(order, xt, *([carry] if carried else []), *[part for chunk in chunks for part in chunk])


def partial_pairs(factors, xt_own, own, kept, unit):
    p_count, width, occ = factors.shape
    nv, per = p_count // own, kept // unit

    def body(xt_ref, f_ref, out_ref):
        wide = side_by_side(f_ref, unit)
        pairs = jnp.dot(xt_ref[...], wide, preferred_element_type=jnp.float32)
        for q in range(unit):
            out_ref[q] = pairs[:, q * occ : (q + 1) * occ].astype(jnp.bfloat16)

    return pl.pallas_call(
        body,
        grid=(nv, per),
        in_specs=[
            pl.BlockSpec((occ, width), lambda b, t: (0, 0)),
            pl.BlockSpec((unit, width, occ), lambda b, t: (b * (own // unit) + (own - kept) // unit + t, 0, 0)),
        ],
        out_specs=pl.BlockSpec((unit, occ, occ), lambda b, t: (b * per + t, 0, 0)),
        out_shape=jax.ShapeDtypeStruct((nv * kept, occ, occ), jnp.bfloat16),
        cost_estimate=pl.CostEstimate(flops=0, bytes_accessed=0, transcendentals=0),
    )(xt_own, factors)


def contract_pairs(order, factors, mine, other, carry, own, kept, unit):
    p_count, width, occ = factors.shape
    nv, per = p_count // own, kept // unit
    half = nv * per // 2

    def body(order_ref, mine_ref, other_ref, f_ref, carry_ref, out_ref):
        step = pl.program_id(0)

        @pl.when(step == 0)
        def _():
            out_ref[...] = carry_ref[...]

        eye = diagonal(occ)
        is_mine = step < half
        mix = jnp.concatenate(
            [
                coulomb_and_exchange(
                    jnp.where(is_mine, mine_ref[q].astype(jnp.float32), other_ref[q].astype(jnp.float32)), eye
                )
                for q in range(unit)
            ],
            axis=0,
        )
        wide = side_by_side(f_ref, unit)
        out_ref[0:width, :] += jnp.dot(wide, mix, preferred_element_type=jnp.float32)

    def place(g, order):
        core = order[nv + 1]
        at = jnp.where(g < half, core * half + g, (1 - core) * half + g - half)
        return (lax.div(at, per) * (own // unit) + (own - kept) // unit + lax.rem(at, per), 0, 0)

    whole = pl.BlockSpec((nv * width, occ), lambda g, order: (0, 0))
    return pl.pallas_call(
        body,
        grid_spec=pltpu.PrefetchScalarGridSpec(
            num_scalar_prefetch=1,
            grid=(2 * half,),
            in_specs=[
                pl.BlockSpec((unit, occ, occ), lambda g, order: (jnp.minimum(g, half - 1), 0, 0)),
                pl.BlockSpec((unit, occ, occ), lambda g, order: (jnp.maximum(g - half, 0), 0, 0)),
                pl.BlockSpec((unit, width, occ), place),
                whole,
            ],
            out_specs=whole,
        ),
        out_shape=jax.ShapeDtypeStruct((nv * width, occ), jnp.float32),
        cost_estimate=pl.CostEstimate(flops=0, bytes_accessed=0, transcendentals=0),
    )(order, mine, other, factors, carry)


def five_sums(trial, gap, coupling):
    rounded = trial.astype(jnp.bfloat16).astype(jnp.float32)
    image = gap * rounded + coupling
    scaled_trial = trial / gap
    scaled_diff = trial - image / gap

    def total(values):
        return jnp.sum(values, keepdims=True)

    sums = (
        total(trial * image),
        total(trial * trial),
        total(scaled_diff * scaled_diff),
        total(scaled_diff * scaled_trial),
        total(scaled_trial * scaled_trial),
    )
    return scaled_diff, scaled_trial, sums


def finish(scaled_diff, scaled_trial, sums, count):
    cross_sum, self_sum, diff_sum, mixed_sum, scaled_sum = sums
    shift = cross_sum / self_sum
    mean_square = (diff_sum + 2.0 * shift * mixed_sum + shift * shift * scaled_sum) / count
    return (scaled_diff + shift * scaled_trial) * lax.rsqrt(mean_square + 1e-06), shift


def step_whole(order, coupling_shares, trial, gap, aux_count):
    nv, occ, width = trial.shape
    share = occ // aux_count

    def body(order_ref, shares_ref, trial_ref, gap_ref, next_ref, xt_ref, shift_ref, coupling_ref):
        for r in range(aux_count):
            for v in range(nv):
                rows = shares_ref[r * nv + order_ref[v]].astype(jnp.float32)
                coupling_ref[v * occ + r * share : v * occ + (r + 1) * share, :] = rows
        diff, scaled, sums = five_sums(
            trial_ref[...].reshape(nv * occ, width), gap_ref[...].reshape(nv * occ, width), coupling_ref[...]
        )
        fresh, shift = finish(diff, scaled, sums, nv * occ * width)
        fresh = fresh.reshape(nv, occ, width)
        next_ref[...] = fresh
        xt_ref[...] = fresh.astype(jnp.bfloat16)
        shift_ref[...] = jnp.broadcast_to(shift, shift_ref.shape)

    return pl.pallas_call(
        body,
        out_shape=(
            jax.ShapeDtypeStruct(trial.shape, jnp.float32),
            jax.ShapeDtypeStruct(trial.shape, jnp.bfloat16),
            jax.ShapeDtypeStruct((1, 128), jnp.float32),
        ),
        in_specs=[pl.BlockSpec(memory_space=pltpu.SMEM)] + [pl.BlockSpec(memory_space=pltpu.VMEM)] * 3,
        scratch_shapes=[pltpu.VMEM((nv * occ, width), jnp.float32)],
        compiler_params=pltpu.CompilerParams(vmem_limit_bytes=24 * 2**20),
    )(order, coupling_shares, trial, gap)


def share_sums(terms, trial, gap):
    count = terms.shape[0]

    def body(terms_ref, trial_ref, gap_ref, diff_ref, scaled_ref, sums_ref):
        coupling = jnp.sum(terms_ref[...].astype(jnp.float32), axis=0)
        diff, scaled, sums = five_sums(trial_ref[...], gap_ref[...], coupling)
        diff_ref[...] = diff
        scaled_ref[...] = scaled
        lane = lax.broadcasted_iota(jnp.int32, (1, 128), 1)
        row = jnp.zeros((1, 128), jnp.float32)
        for at, value in enumerate(sums):
            row = jnp.where(lane == at, value, row)
        sums_ref[...] = jnp.broadcast_to(row[None], sums_ref.shape)

    like = jax.ShapeDtypeStruct(trial.shape, jnp.float32)
    return pl.pallas_call(
        body,
        out_shape=(like, like, jax.ShapeDtypeStruct((count, 1, 128), jnp.float32)),
        compiler_params=pltpu.CompilerParams(vmem_limit_bytes=24 * 2**20),
    )(terms, trial, gap)


def step_share(diff, scaled, all_sums, total):
    def body(diff_ref, scaled_ref, sums_ref, next_ref, shift_ref):
        row = jnp.sum(sums_ref[...], axis=0)
        fresh, shift = finish(
            diff_ref[...], scaled_ref[...], [row[:, at : at + 1] for at in range(5)], total
        )
        next_ref[...] = fresh
        shift_ref[...] = jnp.broadcast_to(shift, shift_ref.shape)

    return pl.pallas_call(
        body,
        out_shape=(
            jax.ShapeDtypeStruct(diff.shape, jnp.float32),
            jax.ShapeDtypeStruct((1, 128), jnp.float32),
        ),
    )(diff, scaled, all_sums)


def spread(share, count, axes=EVERY):
    copies = jnp.broadcast_to(share[None], (count,) + share.shape)
    return lax.all_to_all(copies, axes, 0, 0, tiled=True)


def local(factors, trials, occ_energy, vir_energy):
    na, nv = lax.axis_size("aux"), lax.axis_size("vir")
    count = na * nv
    aux_at, vir_at = lax.axis_index("aux"), lax.axis_index("vir")
    p_count, width, occ = factors.shape
    own = p_count // nv
    share = occ // na
    total = occ * width * nv
    paired = nv & (nv - 1) == 0

    def partner(at, k):
        return at ^ k if paired else (at + k) % nv

    def source(at, k):
        return at ^ k if paired else (at - k) % nv

    def send(value, k):
        return lax.ppermute(value, "vir", [(one, partner(one, k)) for one in range(nv)])

    order = [source(vir_at, k) for k in range(nv)] + [vir_at, vir_at & 1]
    order = jnp.stack(order).astype(jnp.int32)

    early, late = [(0, own)], []
    unit = own // 16
    if paired and nv >= 4 and own % 16 == 0 and unit >= 4:
        cuts = [0, 2 * unit, 6 * unit, 10 * unit, 12 * unit, 13 * unit, 14 * unit, own]
        bounds = list(zip(cuts, cuts[1:]))
        early, late = bounds[:-2], bounds[-2:]
    kept = own - early[-1][1]

    def pieces_of(bound, after):
        low, high = bound
        pieces = []
        for k in range(1, nv):
            place = partner(vir_at, k) * own + low
            pieces.append(lax.dynamic_slice_in_dim(after, place, high - low, 0))
        return pieces

    def send_pieces(pieces):
        return [factors] + [send(piece, k) for k, piece in enumerate(pieces, 1)]

    chunks = [send_pieces(pieces_of(early[0], factors))]
    later_factors = factors
    if kept:
        later_factors, trials, chunks[0][1] = lax.optimization_barrier(
            (factors, trials, chunks[0][1])
        )

    gathered = spread(trials[0].T, na, "aux").reshape(occ, width)
    gathered = jnp.concatenate([gathered, vir_energy[None]], axis=0)
    if paired:
        state = {0: gathered}
        bit = nv // 2
        while bit:
            names = sorted(state)
            if kept and bit in (1, 2):
                at = 4 - bit if bit == 1 else bit
                state[0], chunks[0][at] = lax.optimization_barrier((state[0], chunks[0][at]))
            came = send(jnp.stack([state[k] for k in names]), bit)
            state.update({k ^ bit: came[at] for at, k in enumerate(names)})
            bit //= 2
    else:
        state = {k: send(gathered, k) if k else gathered for k in range(nv)}
    state = jnp.stack([state[k] for k in range(nv)])
    trial = state[:, :occ]
    gap = state[:, occ:] - occ_energy[None, :, None]
    gap_own = vir_energy[None, :] - lax.dynamic_slice_in_dim(occ_energy, aux_at * share, share)[:, None]
    xt = trial.astype(jnp.bfloat16)

    carry, carried = None, 0
    for at in range(1, len(early)):
        pieces = pieces_of(early[at], later_factors)
        if at == len(early) - 1:
            while carried < at - 1:
                carry = contract(order, xt, [chunks[carried]], [early[carried]], own, carry)
                carried += 1
            pieces, carry = lax.optimization_barrier((pieces, carry))
        pieces, chunks[-1][2] = lax.optimization_barrier((pieces, chunks[-1][2]))
        chunks.append(send_pieces(pieces))

    if kept:
        half = nv * kept // 2
        core = vir_at & 1
        sums = partial_pairs(factors, xt[0], own, kept, unit)
        mine = lax.dynamic_slice_in_dim(sums, core * half, half, 0)
        other = lax.dynamic_slice_in_dim(sums, (1 - core) * half, half, 0)

        def add(one, two):
            return (one.astype(jnp.float32) + two.astype(jnp.float32)).astype(jnp.bfloat16)

        mine = add(mine, send(other, 1))
        bit = 2
        while bit < nv:
            mine = add(mine, send(mine, bit))
            bit *= 2
        other = send(mine, 1)

    shift_list = []
    for iteration in range(ITERS):
        last = iteration == ITERS - 1
        if iteration == 0:
            while carried < len(early) - 1:
                carry = contract(order, xt, [chunks[carried]], [early[carried]], own, carry)
                carried += 1
            if kept:
                carry = contract_pairs(order, factors, mine, other, carry, own, kept, unit)
            partial = contract(order, xt, chunks[-1:], early[-1:], own, carry, na)
        else:
            bounds = early + late
            if late:
                carry = contract(order, xt, chunks[:-1], bounds[:-1], own)
                partial = contract(order, xt, chunks[-1:], bounds[-1:], own, carry, na)
            else:
                partial = contract(order, xt, chunks, bounds, own, None, na)
        if iteration == 0 and late:
            pieces, partial = lax.optimization_barrier((pieces_of(late[0], later_factors), partial))
            parts = send_pieces(pieces)
        terms = lax.all_to_all(partial.reshape(count, share, width), EVERY, 0, 0, tiled=True)
        if not last:
            coupling = jnp.sum(terms.astype(jnp.float32), axis=0).astype(jnp.bfloat16)
            if iteration == 0 and late:
                parts[1:], coupling = lax.optimization_barrier((parts[1:], coupling))
                chunks.append(parts)
                pieces, coupling = lax.optimization_barrier(
                    (pieces_of(late[1], later_factors), coupling)
                )
                chunks.append(send_pieces(pieces))
            trial, xt, shift = step_whole(order, spread(coupling, count), trial, gap, na)
        else:
            trial_own = lax.dynamic_slice_in_dim(trial[0], aux_at * share, share, 0)
            diff, scaled, sums = share_sums(terms, trial_own, gap_own)
            sums = lax.all_to_all(sums, EVERY, 0, 0, tiled=True)
            fresh, shift = step_share(diff, scaled, sums, total)
        shift_list.append(shift[:, :1])
    return (fresh.T[None], jnp.concatenate(shift_list, axis=0))


def solution(mesh):
    placed = (P("aux", "vir", None), P(None, "vir", "aux"), P(), P("vir"))
    return jax.shard_map(
        local, mesh=mesh, in_specs=placed, out_specs=(P(None, "vir", "aux"), P()), check_vma=False
    )
```

time: 278 us -> 296 us (1.065)
  waiting for transfers between devices: 176 us -> 137 us
  Pallas kernels: 32.3 us -> 56.4 us
  starting transfers between devices: 19 us -> 35.9 us
  other arithmetic: 1.75 us -> 10.6 us
  local copies, waits for them, and re-layouts: 22.1 us -> 30.9 us
  blocking collectives: 25.7 us -> 22.7 us
    all_to_all x2 -> x1, waiting for transfers between devices: 119 us -> 16.2 us  [spread(): return lax.all_to_all(copies, axes, 0, 0, tiled=True)]
    ppermute x9 -> x26, waiting for transfers between devices: 46.8 us -> 102 us  [send(): lax.ppermute(value, 'vir', [(one, partner(one, k)) for one in range(nv)])]
    pallas_call x4 -> x9, Pallas kernels: 29.9 us -> 53.3 us  [the longest x7 33.8 us: contract(): pl.pallas_call(functools.partial(contract_body, nv, bounds, own, carried,...]
    ppermute x9 -> x26, starting transfers between devices: 8.91 us -> 20.3 us  [send(): lax.ppermute(value, 'vir', [(one, partner(one, k)) for one in range(nv)])]
    all_to_all x1 -> x2, waiting for transfers between devices: 9.72 us -> 18.2 us  [local(): lax.all_to_all(partial.reshape(count, share, width), EVERY, 0, 0, tiled=T...]
    all_to_all x1 -> x2, starting transfers between devices: 2.58 us -> 10.9 us  [local(): lax.all_to_all(partial.reshape(count, share, width), EVERY, 0, 0, tiled=T...]
    convert_element_type x1 -> x2, other arithmetic: 0.03 us -> 5.12 us  [add(): (one.astype(jnp.float32) + two.astype(jnp.float32)).astype(jnp.bfloat16)]
    unnamed x45 -> x56, local copies, waits for them, and re-layouts: 5.61 us -> 9.65 us
  transfers between devices with their start and end apart: 12 -> 29, of which waited for: 6 -> 13; matrix products, arithmetic and copies ran while one was open for 5% -> 10% of each run, Pallas kernels for 5% -> 16%
where the time goes in v3:
time: 296 us; the launch traced here: 295 us
  waiting for transfers between devices  137 us (46%)
  Pallas kernels  56.4 us (19%)
  starting transfers between devices  35.9 us (12%)
  local copies, waits for them, and re-layouts  30.9 us (10%)
  blocking collectives  22.7 us (8%)
  other arithmetic  10.6 us (4%)
    ppermute x26, waiting for transfers between devices, send(): lax.ppermute(value, 'vir', [(one, partner(one, k)) for one in range(nv)])  102 us
    pallas_call x7, Pallas kernels, contract(): pl.pallas_call(functools.partial(contract_body, nv, bounds, own, carried,...  33.8 us
    ppermute x26, starting transfers between devices, send(): lax.ppermute(value, 'vir', [(one, partner(one, k)) for one in range(nv)])  20.3 us
    all_to_all x2, waiting for transfers between devices, local(): lax.all_to_all(partial.reshape(count, share, width), EVERY, 0, 0, tiled=T...  18.2 us
    all_to_all x1, waiting for transfers between devices, spread(): return lax.all_to_all(copies, axes, 0, 0, tiled=True)  16.2 us
    all_to_all x1, blocking collectives, spread(): return lax.all_to_all(copies, axes, 0, 0, tiled=True)  13.3 us
    dynamic_slice x4, local copies, waits for them, and re-layouts, pieces_of(): pieces.append(lax.dynamic_slice_in_dim(after, place, high - low, 0))  13 us
    pallas_call x1, Pallas kernels, contract_pairs(): pl.pallas_call(body, grid_spec=pltpu.PrefetchScalarGridSpec(num_scalar_pr...  11 us
  transfers between devices with their start and end apart: 29, of which 13 were waited for; matrix products, arithmetic and copies ran while one was open for 10% of the time, Pallas kernels for 16%

profile of v3, /device:TPU:0, one launch (start us, length us, event | category | flops | bytes accessed | tf_op | source)
XLA Modules:
  0.0 294.5 jit_solution(566265023212243320)
XLA Ops:
  6.2 13.3 %all_to_all.25 = f32[8,16,256]{2,1,0:T(8,128)S(1)} all-to-all(f32[8,16,256]{2,1,0:T(8,128)S(1)} %broadcast_in_dim.8), channel_id=1, replica_groups=mesh['aux'=8,'vir'=4] {'aux'}, dimensions={0} | all-to-all | bytes 262144 | tf_op jit(solution)/shard_map/all_to_all | solution.py:280
  21.8 6.9 %collective-permute-done.2.refs_3_ = bf16[8,256,128]{2,1,0:T(8,128)(2,1)S(1)} collective-permute-done((bf16[8,256,128]{2,1,0:T(8,128)(2,1)S(1)}, bf16[8,256,128]{2,1,0:T(8,128)(2,1)S(1)}, u32[]{:S(2)}, u32[]{:S(2)}) %collective-permute-start.2) | collective-permute-done | bytes 524320 | tf_op jit(solution)/shard_map/ppermute | solution.py:300
  32.1 5.4 %constant_dynamic-slice_fusion.3 = (bf16[16,256,128]{2,1,0:T(8,128)(2,1)}, bf16[16,256,128]{2,1,0:T(8,128)(2,1)}, bf16[16,256,128]{2,1,0:T(8,128)(2,1)}, bf16[16...) fusion(bf16[256,256,128]{2,1,0:T(8,128)(2,1)} %refs_1_.9, ...), kind=kLoop, calls=%fused_computation.12 | loop fusion | bytes 12582936 | tf_op jit(solution)/shard_map/dynamic_slice | solution.py:318
  41.9 8.5 %shard_map.59 = bf16[48,128,128]{2,1,0:T(8,128)(2,1)} custom-call(bf16[128,256]{1,0:T(8,128)(2,1)} %slice_bitcast_fusion.xt_ref, bf16[256,256,128]{2,1,0:T(8,128)(2,1)} %refs_1_.9), custom_call_target="tpu_custom_call" | custom-call | tf_op jit(solution)/shard_map/pallas_call | solution.py:118
  52.7 10.4 %collective-permute-done.9.refs_3_.refs_6_ = bf16[16,256,128]{2,1,0:T(8,128)(2,1)S(1)} collective-permute-done((bf16[16,256,128]{2,1,0:T(8,128)(2,1)S(1)}, bf16[16,256,128]{2,1,0:T(8,128)(2,1)S(1)}, u32[]{:S(2)}, u32[]{:S(2)}) %collective-permute-start.9) | collective-permute-done | bytes 1048608 | tf_op jit(solution)/shard_map/ppermute | solution.py:300
  69.5 19.8 %collective-permute-done.12.refs_3_.refs_10_ = bf16[16,256,128]{2,1,0:T(8,128)(2,1)S(1)} collective-permute-done((bf16[16,256,128]{2,1,0:T(8,128)(2,1)}, bf16[16,256,128]{2,1,0:T(8,128)(2,1)S(1)}, u32[]{:S(2)}, u32[]{:S(2)}) %collective-permute-start.12) | collective-permute-done | bytes 1048608 | tf_op jit(solution)/shard_map/ppermute | solution.py:300
  92.8 13.5 %collective-permute-done.6 = bf16[24,128,128]{2,1,0:T(8,128)(2,1)} collective-permute-done((bf16[24,128,128]{2,1,0:T(8,128)(2,1)}, bf16[24,128,128]{2,1,0:T(8,128)(2,1)}, u32[]{:S(2)}, u32[]{:S(2)}) %collective-permute-start.6) | collective-permute-done | bytes 786464 | tf_op jit(solution)/shard_map/ppermute | solution.py:300
  110.6 17.4 %collective-permute-done.10.refs_4_.refs_7_ = bf16[16,256,128]{2,1,0:T(8,128)(2,1)} collective-permute-done((bf16[16,256,128]{2,1,0:T(8,128)(2,1)}, bf16[16,256,128]{2,1,0:T(8,128)(2,1)}, u32[]{:S(2)}, u32[]{:S(2)}) %collective-permute-start.10) | collective-permute-done | bytes 1048608 | tf_op jit(solution)/shard_map/ppermute | solution.py:300
  136.0 4.1 %shard_map.61.refs_0_ = f32[1024,128]{1,0:T(8,128)S(1)} custom-call(s32[6]{0:T(128)S(1)} %stack.37.order_ref, bf16[4,128,256]{2,1,0:T(8,128)(2,1)S(1)} %slice.38.xt_ref, f32[1024,128]{1,0:T(8,128)S(1)} %shard_map.60.refs_0_, bf16[256,256,128]{2,1,0:T(8,128)(2,1)} %refs_1_.9, bf16[16,256,128]{2,1,0:T(8,128)(2,1)S(1)} %collective-permute-done.8.refs_2_.refs_5_, ...), custom_call_target="tpu_custom_call" | custom-call | tf_op jit(solution)/shard_map/pallas_call | solution.py:91
  140.1 10.4 %collective-permute-done.13.refs_4_.refs_11_ = bf16[16,256,128]{2,1,0:T(8,128)(2,1)} collective-permute-done((bf16[16,256,128]{2,1,0:T(8,128)(2,1)}, bf16[16,256,128]{2,1,0:T(8,128)(2,1)}, u32[]{:S(2)}, u32[]{:S(2)}) %collective-permute-start.13) | collective-permute-done | bytes 1048608 | tf_op jit(solution)/shard_map/ppermute | solution.py:300
  150.5 4.4 %shard_map.62.refs_0_ = f32[1024,128]{1,0:T(8,128)S(1)} custom-call(s32[6]{0:T(128)S(1)} %stack.37.order_ref, bf16[4,128,256]{2,1,0:T(8,128)(2,1)S(1)} %slice.38.xt_ref, f32[1024,128]{1,0:T(8,128)S(1)} %shard_map.61.refs_0_, bf16[256,256,128]{2,1,0:T(8,128)(2,1)} %refs_1_.9, bf16[16,256,128]{2,1,0:T(8,128)(2,1)} %collective-permute-done.11.refs_2_.refs_9_, ...), custom_call_target="tpu_custom_call" | custom-call | tf_op jit(solution)/shard_map/pallas_call | solution.py:91
  154.9 7.6 %collective-permute-done.15.refs_3_.refs_14_ = bf16[8,256,128]{2,1,0:T(8,128)(2,1)} collective-permute-done((bf16[8,256,128]{2,1,0:T(8,128)(2,1)}, bf16[8,256,128]{2,1,0:T(8,128)(2,1)}, u32[]{:S(2)}, u32[]{:S(2)}) %collective-permute-start.15) | collective-permute-done | bytes 524320 | tf_op jit(solution)/shard_map/ppermute | solution.py:300
  164.3 8.6 %collective-permute-done.16.refs_4_.refs_15_ = bf16[8,256,128]{2,1,0:T(8,128)(2,1)} collective-permute-done((bf16[8,256,128]{2,1,0:T(8,128)(2,1)}, bf16[8,256,128]{2,1,0:T(8,128)(2,1)}, u32[]{:S(2)}, u32[]{:S(2)}) %collective-permute-start.16) | collective-permute-done | bytes 524320 | tf_op jit(solution)/shard_map/ppermute | solution.py:300
  177.1 11.0 %shard_map.64.refs_0_ = f32[1024,128]{1,0:T(8,128)} custom-call(s32[6]{0:T(128)} %copy-done.16, bf16[24,128,128]{2,1,0:T(8,128)(2,1)} %add_convert_fusion.mine_ref, bf16[24,128,128]{2,1,0:T(8,128)(2,1)} %collective-permute-done.7.other_ref, bf16[256,256,128]{2,1,0:T(8,128)(2,1)} %refs_1_.9, f32[1024,128]{1,0:T(8,128)} %copy-done.10), custom_call_target="tpu_custom_call" | custom-call | tf_op jit(solution)/shard_map/pallas_call | solution.py:163
  192.7 6.4 %all-to-all-start.1 = ((bf16[32,16,256]{2,1,0:T(8,128)(2,1)}), bf16[32,16,256]{2,1,0:T(8,128)(2,1)}, u32[]{:S(2)}, u32[]{:S(2)}) async-start(bf16[32,16,256]{2,1,0:T(8,128)(2,1)} %bitcast.26), calls=%async_computation.1 | async-start | bytes 524288 | tf_op jit(solution)/shard_map/all_to_all | solution.py:400
  201.0 8.7 %all-to-all-done.1 = bf16[32,16,256]{2,1,0:T(8,128)(2,1)} async-done(((bf16[32,16,256]{2,1,0:T(8,128)(2,1)}), bf16[32,16,256]{2,1,0:T(8,128)(2,1)}, u32[]{:S(2)}, u32[]{:S(2)}) %all-to-all-start.1) | async-done | bytes 262176 | tf_op jit(solution)/shard_map/all_to_all | solution.py:400
  211.3 4.7 %collective-permute-done.22.refs_23_ = bf16[4,256,128]{2,1,0:T(8,128)(2,1)} collective-permute-done((bf16[4,256,128]{2,1,0:T(8,128)(2,1)}, bf16[4,256,128]{2,1,0:T(8,128)(2,1)}, u32[]{:S(2)}, u32[]{:S(2)}) %collective-permute-start.22) | collective-permute-done | bytes 262176 | tf_op jit(solution)/shard_map/ppermute | solution.py:300
  219.3 4.7 %all-to-all-start.2 = ((bf16[32,16,256]{2,1,0:T(8,128)(2,1)}), bf16[32,16,256]{2,1,0:T(8,128)(2,1)S(1)}, u32[]{:S(2)}, u32[]{:S(2)}) async-start(bf16[32,16,256]{2,1,0:T(8,128)(2,1)} %broadcast_in_dim.10), calls=%async_computation.2 | async-start | bytes 524288 | tf_op jit(solution)/shard_map/all_to_all | solution.py:280
  228.2 16.2 %all-to-all-done.2.shares_ref = bf16[32,16,256]{2,1,0:T(8,128)(2,1)S(1)} async-done(((bf16[32,16,256]{2,1,0:T(8,128)(2,1)}), bf16[32,16,256]{2,1,0:T(8,128)(2,1)S(1)}, u32[]{:S(2)}, u32[]{:S(2)}) %all-to-all-start.2) | async-done | bytes 262176 | tf_op jit(solution)/shard_map/all_to_all | solution.py:280
  250.6 12.1 %shard_map.67.refs_0_ = f32[1024,128]{1,0:T(8,128)S(1)} custom-call(s32[6]{0:T(128)S(1)} %copy-done.17, bf16[4,128,256]{2,1,0:T(8,128)(2,1)S(1)} %get-tuple-element.82.xt_ref, bf16[256,256,128]{2,1,0:T(8,128)(2,1)} %refs_1_.9, bf16[8,256,128]{2,1,0:T(8,128)(2,1)S(1)} %copy-done.2, bf16[8,256,128]{2,1,0:T(8,128)(2,1)S(1)} %copy-done.5, ...), custom_call_target="tpu_custom_call" | custom-call | tf_op jit(solution)/shard_map/pallas_call | solution.py:91
  262.7 4.1 %shard_map.68 = bf16[8,4,16,256]{3,2,1,0:T(8,128)(2,1)} custom-call(s32[6]{0:T(128)S(1)} %copy-done.17, bf16[4,128,256]{2,1,0:T(8,128)(2,1)S(1)} %get-tuple-element.82.xt_ref, f32[1024,128]{1,0:T(8,128)S(1)} %shard_map.67.refs_0_, bf16[256,256,128]{2,1,0:T(8,128)(2,1)} %refs_1_.9, bf16[8,256,128]{2,1,0:T(8,128)(2,1)} %collective-permute-done.23.refs_2_, ...), custom_call_target="tpu_custom_call" | custom-call | tf_op jit(solution)/shard_map/pallas_call | solution.py:91
  266.9 4.5 %all-to-all-start.3 = ((bf16[32,16,256]{2,1,0:T(8,128)(2,1)}), bf16[32,16,256]{2,1,0:T(8,128)(2,1)S(1)}, u32[]{:S(2)}, u32[]{:S(2)}) async-start(bf16[32,16,256]{2,1,0:T(8,128)(2,1)} %bitcast.13), calls=%async_computation.3 | async-start | bytes 524288 | tf_op jit(solution)/shard_map/all_to_all | solution.py:400
  272.5 9.5 %all-to-all-done.3.terms_ref = bf16[32,16,256]{2,1,0:T(8,128)(2,1)S(1)} async-done(((bf16[32,16,256]{2,1,0:T(8,128)(2,1)}), bf16[32,16,256]{2,1,0:T(8,128)(2,1)S(1)}, u32[]{:S(2)}, u32[]{:S(2)}) %all-to-all-start.3) | async-done | bytes 262176 | tf_op jit(solution)/shard_map/all_to_all | solution.py:400
  282.2 9.4 %all_to_all.26.sums_ref = f32[32,1,128]{2,1,0:T(1,128)} all-to-all(f32[32,1,128]{2,1,0:T(1,128)S(1)} %get-tuple-element.92), channel_id=1, replica_groups=mesh['aux'=8,'vir'=4] {'aux','vir'}, dimensions={0} | all-to-all | bytes 32768 | tf_op jit(solution)/shard_map/all_to_all | solution.py:414
  (129 shorter events, 71.9 us)
Async XLA Ops:
  2.7 16.8 %collective-permute-start.1 = (bf16[8,256,128]{2,1,0:T(8,128)(2,1)S(1)}, bf16[8,256,128]{2,1,0:T(8,128)(2,1)S(1)}, u32[]{:S(2)}, u32[]{:S(2)}) collective-permute-start(bf16[8,256,128]{2,1,0:T(8,128)(2,1)S(1)} %get-tuple-element.117), channel_id=1, source_target_pairs={{0,2},{1,3},{2,0},{3,1},{4,6},{5,7},{6,4},{7,5},{8,10},{9,11},{10,... | collective-permute-start | bytes 1572872 | tf_op jit(solution)/shard_map/ppermute | solution.py:300
  5.3 23.5 %collective-permute-start.2 = (bf16[8,256,128]{2,1,0:T(8,128)(2,1)S(1)}, bf16[8,256,128]{2,1,0:T(8,128)(2,1)S(1)}, u32[]{:S(2)}, u32[]{:S(2)}) collective-permute-start(bf16[8,256,128]{2,1,0:T(8,128)(2,1)S(1)} %get-tuple-element.116), channel_id=1, source_target_pairs={{0,3},{1,2},{2,1},{3,0},{4,7},{5,6},{6,5},{7,4},{8,11},{9,10},{10,... | collective-permute-start | bytes 1572872 | tf_op jit(solution)/shard_map/ppermute | solution.py:300
  37.5 25.6 %collective-permute-start.9 = (bf16[16,256,128]{2,1,0:T(8,128)(2,1)S(1)}, bf16[16,256,128]{2,1,0:T(8,128)(2,1)S(1)}, u32[]{:S(2)}, u32[]{:S(2)}) collective-permute-start(bf16[16,256,128]{2,1,0:T(8,128)(2,1)S(1)} %get-tuple-element.58), channel_id=1, source_target_pairs={{0,2},{1,3},{2,0},{3,1},{4,6},{5,7},{6,4},{7,5},{8,10},{9,11},{10,... | collective-permute-start | bytes 3145736 | tf_op jit(solution)/shard_map/ppermute | solution.py:300
  52.5 12.3 %collective-permute-start.5 = (bf16[24,128,128]{2,1,0:T(8,128)(2,1)}, bf16[24,128,128]{2,1,0:T(8,128)(2,1)}, u32[]{:S(2)}, u32[]{:S(2)}) collective-permute-start(bf16[24,128,128]{2,1,0:T(8,128)(2,1)} %constant_dynamic-slice_fusion.12), channel_id=1, source_target_pairs={{0,1},{1,0},{2,3},{3,2},{4,5},{5,4},{6,7},{7,6},{8,9},{9,8},{10,11... | collective-permute-start | bytes 2359304 | tf_op jit(solution)/shard_map/ppermute | solution.py:300
  63.0 26.3 %collective-permute-start.12 = (bf16[16,256,128]{2,1,0:T(8,128)(2,1)}, bf16[16,256,128]{2,1,0:T(8,128)(2,1)S(1)}, u32[]{:S(2)}, u32[]{:S(2)}) collective-permute-start(bf16[16,256,128]{2,1,0:T(8,128)(2,1)} %get-tuple-element.62), channel_id=1, source_target_pairs={{0,2},{1,3},{2,0},{3,1},{4,6},{5,7},{6,4},{7,5},{8,10},{9,11},{10,... | collective-permute-start | bytes 3145736 | tf_op jit(solution)/shard_map/ppermute | solution.py:300
  67.3 38.9 %collective-permute-start.6 = (bf16[24,128,128]{2,1,0:T(8,128)(2,1)}, bf16[24,128,128]{2,1,0:T(8,128)(2,1)}, u32[]{:S(2)}, u32[]{:S(2)}) collective-permute-start(bf16[24,128,128]{2,1,0:T(8,128)(2,1)} %add_convert_fusion.1), channel_id=1, source_target_pairs={{0,2},{1,3},{2,0},{3,1},{4,6},{5,7},{6,4},{7,5},{8,10},{9,11},{10,... | collective-permute-start | bytes 2359304 | tf_op jit(solution)/shard_map/ppermute | solution.py:300
  67.6 43.0 %collective-permute-start.8 = (bf16[16,256,128]{2,1,0:T(8,128)(2,1)}, bf16[16,256,128]{2,1,0:T(8,128)(2,1)S(1)}, u32[]{:S(2)}, u32[]{:S(2)}) collective-permute-start(bf16[16,256,128]{2,1,0:T(8,128)(2,1)} %get-tuple-element.57), channel_id=1, source_target_pairs={{0,1},{1,0},{2,3},{3,2},{4,5},{5,4},{6,7},{7,6},{8,9},{9,8},{10,11... | collective-permute-start | bytes 3145736 | tf_op jit(solution)/shard_map/ppermute | solution.py:300
  67.6 60.4 %collective-permute-start.10 = (bf16[16,256,128]{2,1,0:T(8,128)(2,1)}, bf16[16,256,128]{2,1,0:T(8,128)(2,1)}, u32[]{:S(2)}, u32[]{:S(2)}) collective-permute-start(bf16[16,256,128]{2,1,0:T(8,128)(2,1)} %get-tuple-element.60), channel_id=1, source_target_pairs={{0,3},{1,2},{2,1},{3,0},{4,7},{5,6},{6,5},{7,4},{8,11},{9,10},{10,... | collective-permute-start | bytes 3145736 | tf_op jit(solution)/shard_map/ppermute | solution.py:300
  69.5 59.4 %collective-permute-start.11 = (bf16[16,256,128]{2,1,0:T(8,128)(2,1)}, bf16[16,256,128]{2,1,0:T(8,128)(2,1)}, u32[]{:S(2)}, u32[]{:S(2)}) collective-permute-start(bf16[16,256,128]{2,1,0:T(8,128)(2,1)} %get-tuple-element.61), channel_id=1, source_target_pairs={{0,1},{1,0},{2,3},{3,2},{4,5},{5,4},{6,7},{7,6},{8,9},{9,8},{10,11... | collective-permute-start | bytes 3145736 | tf_op jit(solution)/shard_map/ppermute | solution.py:300
  89.3 61.2 %collective-permute-start.13 = (bf16[16,256,128]{2,1,0:T(8,128)(2,1)}, bf16[16,256,128]{2,1,0:T(8,128)(2,1)}, u32[]{:S(2)}, u32[]{:S(2)}) collective-permute-start(bf16[16,256,128]{2,1,0:T(8,128)(2,1)} %get-tuple-element.64), channel_id=1, source_target_pairs={{0,3},{1,2},{2,1},{3,0},{4,7},{5,6},{6,5},{7,4},{8,11},{9,10},{10,... | collective-permute-start | bytes 3145736 | tf_op jit(solution)/shard_map/ppermute | solution.py:300
  106.3 56.2 %collective-permute-start.15 = (bf16[8,256,128]{2,1,0:T(8,128)(2,1)}, bf16[8,256,128]{2,1,0:T(8,128)(2,1)}, u32[]{:S(2)}, u32[]{:S(2)}) collective-permute-start(bf16[8,256,128]{2,1,0:T(8,128)(2,1)} %get-tuple-element.70), channel_id=1, source_target_pairs={{0,2},{1,3},{2,0},{3,1},{4,6},{5,7},{6,4},{7,5},{8,10},{9,11},{10,... | collective-permute-start | bytes 1572872 | tf_op jit(solution)/shard_map/ppermute | solution.py:300
  110.6 66.5 %collective-permute-start.7 = (bf16[24,128,128]{2,1,0:T(8,128)(2,1)}, bf16[24,128,128]{2,1,0:T(8,128)(2,1)}, u32[]{:S(2)}, u32[]{:S(2)}) collective-permute-start(bf16[24,128,128]{2,1,0:T(8,128)(2,1)} %add_convert_fusion.mine_ref), channel_id=1, source_target_pairs={{0,1},{1,0},{2,3},{3,2},{4,5},{5,4},{6,7},{7,6},{8,9},{9,8},{10,11... | collective-permute-start | bytes 2359304 | tf_op jit(solution)/shard_map/ppermute | solution.py:300
  128.0 36.2 %collective-permute-start.14 = (bf16[8,256,128]{2,1,0:T(8,128)(2,1)}, bf16[8,256,128]{2,1,0:T(8,128)(2,1)}, u32[]{:S(2)}, u32[]{:S(2)}) collective-permute-start(bf16[8,256,128]{2,1,0:T(8,128)(2,1)} %get-tuple-element.66), channel_id=1, source_target_pairs={{0,1},{1,0},{2,3},{3,2},{4,5},{5,4},{6,7},{7,6},{8,9},{9,8},{10,11... | collective-permute-start | bytes 1572872 | tf_op jit(solution)/shard_map/ppermute | solution.py:300
  128.9 44.1 %collective-permute-start.16 = (bf16[8,256,128]{2,1,0:T(8,128)(2,1)}, bf16[8,256,128]{2,1,0:T(8,128)(2,1)}, u32[]{:S(2)}, u32[]{:S(2)}) collective-permute-start(bf16[8,256,128]{2,1,0:T(8,128)(2,1)} %get-tuple-element.72), channel_id=1, source_target_pairs={{0,3},{1,2},{2,1},{3,0},{4,7},{5,6},{6,5},{7,4},{8,11},{9,10},{10,... | collective-permute-start | bytes 1572872 | tf_op jit(solution)/shard_map/ppermute | solution.py:300
  162.4 25.7 %collective-permute-start.17 = (bf16[4,256,128]{2,1,0:T(8,128)(2,1)}, bf16[4,256,128]{2,1,0:T(8,128)(2,1)}, u32[]{:S(2)}, u32[]{:S(2)}) collective-permute-start(bf16[4,256,128]{2,1,0:T(8,128)(2,1)} %get-tuple-element.73), channel_id=1, source_target_pairs={{0,1},{1,0},{2,3},{3,2},{4,5},{5,4},{6,7},{7,6},{8,9},{9,8},{10,11... | collective-permute-start | bytes 786440 | tf_op jit(solution)/shard_map/ppermute | solution.py:300
  162.4 25.7 %collective-permute-start.18 = (bf16[4,256,128]{2,1,0:T(8,128)(2,1)}, bf16[4,256,128]{2,1,0:T(8,128)(2,1)}, u32[]{:S(2)}, u32[]{:S(2)}) collective-permute-start(bf16[4,256,128]{2,1,0:T(8,128)(2,1)} %get-tuple-element.74), channel_id=1, source_target_pairs={{0,2},{1,3},{2,0},{3,1},{4,6},{5,7},{6,4},{7,5},{8,10},{9,11},{10,... | collective-permute-start | bytes 786440 | tf_op jit(solution)/shard_map/ppermute | solution.py:300
  164.2 23.9 %collective-permute-start.19 = (bf16[4,256,128]{2,1,0:T(8,128)(2,1)}, bf16[4,256,128]{2,1,0:T(8,128)(2,1)}, u32[]{:S(2)}, u32[]{:S(2)}) collective-permute-start(bf16[4,256,128]{2,1,0:T(8,128)(2,1)} %get-tuple-element.75), channel_id=1, source_target_pairs={{0,3},{1,2},{2,1},{3,0},{4,7},{5,6},{6,5},{7,4},{8,11},{9,10},{10,... | collective-permute-start | bytes 786440 | tf_op jit(solution)/shard_map/ppermute | solution.py:300
  192.7 17.1 %all-to-all-start.1 = ((bf16[32,16,256]{2,1,0:T(8,128)(2,1)}), bf16[32,16,256]{2,1,0:T(8,128)(2,1)}, u32[]{:S(2)}, u32[]{:S(2)}) async-start(bf16[32,16,256]{2,1,0:T(8,128)(2,1)} %bitcast.26), calls=%async_computation.1 | async-start | bytes 524288 | tf_op jit(solution)/shard_map/all_to_all | solution.py:400
  201.0 15.0 %collective-permute-start.22 = (bf16[4,256,128]{2,1,0:T(8,128)(2,1)}, bf16[4,256,128]{2,1,0:T(8,128)(2,1)}, u32[]{:S(2)}, u32[]{:S(2)}) collective-permute-start(bf16[4,256,128]{2,1,0:T(8,128)(2,1)} %get-tuple-element.78), channel_id=1, source_target_pairs={{0,3},{1,2},{2,1},{3,0},{4,7},{5,6},{6,5},{7,4},{8,11},{9,10},{10,... | collective-permute-start | bytes 786440 | tf_op jit(solution)/shard_map/ppermute | solution.py:300
  216.0 46.7 %collective-permute-start.23 = (bf16[8,256,128]{2,1,0:T(8,128)(2,1)}, bf16[8,256,128]{2,1,0:T(8,128)(2,1)}, u32[]{:S(2)}, u32[]{:S(2)}) collective-permute-start(bf16[8,256,128]{2,1,0:T(8,128)(2,1)} %get-tuple-element.86), channel_id=1, source_target_pairs={{0,1},{1,0},{2,3},{3,2},{4,5},{5,4},{6,7},{7,6},{8,9},{9,8},{10,11... | collective-permute-start | bytes 1572872 | tf_op jit(solution)/shard_map/ppermute | solution.py:300
  216.1 46.6 %collective-permute-start.24 = (bf16[8,256,128]{2,1,0:T(8,128)(2,1)}, bf16[8,256,128]{2,1,0:T(8,128)(2,1)}, u32[]{:S(2)}, u32[]{:S(2)}) collective-permute-start(bf16[8,256,128]{2,1,0:T(8,128)(2,1)} %get-tuple-element.87), channel_id=1, source_target_pairs={{0,2},{1,3},{2,0},{3,1},{4,6},{5,7},{6,4},{7,5},{8,10},{9,11},{10,... | collective-permute-start | bytes 1572872 | tf_op jit(solution)/shard_map/ppermute | solution.py:300
  217.3 45.4 %collective-permute-start.25 = (bf16[8,256,128]{2,1,0:T(8,128)(2,1)}, bf16[8,256,128]{2,1,0:T(8,128)(2,1)}, u32[]{:S(2)}, u32[]{:S(2)}) collective-permute-start(bf16[8,256,128]{2,1,0:T(8,128)(2,1)} %get-tuple-element.88), channel_id=1, source_target_pairs={{0,3},{1,2},{2,1},{3,0},{4,7},{5,6},{6,5},{7,4},{8,11},{9,10},{10,... | collective-permute-start | bytes 1572872 | tf_op jit(solution)/shard_map/ppermute | solution.py:300
  219.3 25.2 %all-to-all-start.2 = ((bf16[32,16,256]{2,1,0:T(8,128)(2,1)}), bf16[32,16,256]{2,1,0:T(8,128)(2,1)S(1)}, u32[]{:S(2)}, u32[]{:S(2)}) async-start(bf16[32,16,256]{2,1,0:T(8,128)(2,1)} %broadcast_in_dim.10), calls=%async_computation.2 | async-start | bytes 524288 | tf_op jit(solution)/shard_map/all_to_all | solution.py:280
  266.9 15.1 %all-to-all-start.3 = ((bf16[32,16,256]{2,1,0:T(8,128)(2,1)}), bf16[32,16,256]{2,1,0:T(8,128)(2,1)S(1)}, u32[]{:S(2)}, u32[]{:S(2)}) async-start(bf16[32,16,256]{2,1,0:T(8,128)(2,1)} %bitcast.13), calls=%async_computation.3 | async-start | bytes 524288 | tf_op jit(solution)/shard_map/all_to_all | solution.py:400
  (32 other events, 219.2 us)

commit v4 on v3

v4 whole, which is shorter than its diff:
```python
import functools

import jax
import jax.numpy as jnp
from jax import lax
from jax.experimental import pallas as pl
from jax.experimental.pallas import tpu as pltpu
from jax.sharding import PartitionSpec as P

ITERS = 2
EVERY = ("aux", "vir")


def diagonal(occ):
    rows = lax.broadcasted_iota(jnp.int32, (occ, occ), 0)
    return rows == lax.broadcasted_iota(jnp.int32, (occ, occ), 1)


def coulomb_and_exchange(pair, eye):
    density = jnp.sum(jnp.where(eye, pair, 0.0), keepdims=True)
    density = density.astype(jnp.bfloat16).astype(jnp.float32)
    pair = pair.astype(jnp.bfloat16).astype(jnp.float32)
    return (jnp.where(eye, 2.0 * density, 0.0) - pair).astype(jnp.bfloat16)


def side_by_side(blocks, count):
    return jnp.concatenate([blocks[q] for q in range(count)], axis=1)


def contract_body(nv, steps, own, carried, slots, order_ref, xt_ref, *refs):
    carry_ref = refs[0] if carried else None
    f_refs, (out_ref, acc_ref, held, sems) = refs[carried:-4], refs[-4:]
    occ, width = xt_ref.shape[1:]
    near_start = order_ref[nv] * own

    def copies(step):
        low, high, places = steps[step]
        slot = step % slots
        made = []
        for k, (at, offset) in enumerate(places):
            first = near_start + low if k == 0 else offset
            part = f_refs[at].at[pl.ds(first, high - low)]
            into = held.at[slot, k, pl.ds(0, high - low)]
            made.append(pltpu.make_async_copy(part, into, sems.at[slot, k]))
        return made

    for step in range(min(slots, len(steps))):
        for copy in copies(step):
            copy.start()
    acc_ref[...] = carry_ref[...] if carried else jnp.zeros_like(acc_ref)
    xt = jnp.concatenate([xt_ref[k] for k in range(nv)], axis=1)
    eye = diagonal(occ)
    for step, (low, high, places) in enumerate(steps):
        for copy in copies(step):
            copy.wait()
        block = high - low
        tall = jnp.concatenate(
            [side_by_side(held.at[step % slots, k], block) for k in range(nv)], axis=0
        )
        pairs = jnp.dot(xt, tall, preferred_element_type=jnp.float32)
        mix = jnp.concatenate(
            [coulomb_and_exchange(pairs[:, q * occ : (q + 1) * occ], eye) for q in range(block)],
            axis=0,
        )
        acc_ref[...] += jnp.dot(tall, mix, preferred_element_type=jnp.float32)
        if step + slots < len(steps):
            for copy in copies(step + slots):
                copy.start()
    if len(out_ref.shape) == 2:
        out_ref[...] = acc_ref[...]
        return
    share = out_ref.shape[2]
    for k in range(nv):
        turned = acc_ref[k * width : (k + 1) * width, :].T
        for r in range(occ // share):
            out_ref[r, order_ref[k]] = turned[r * share : (r + 1) * share, :].astype(out_ref.dtype)


def contract(order, xt, factors, sources, bounds, own, carry=None, aux_count=None):
    nv, occ, width = xt.shape
    carried = carry is not None
    slots = 3
    largest = max(high - low for low, high in bounds)
    count = sum(high - low for low, high in bounds)
    arrays, steps = [factors], []
    for low, high in bounds:
        places = [(0, 0)]
        for k in range(1, nv):
            start, array = next((a, x) for a, b, x in sources[k] if a <= low and high <= b)
            at = next((n for n, x in enumerate(arrays) if x is array), len(arrays))
            if at == len(arrays):
                arrays.append(array)
            places.append((at, low - start))
        steps.append((low, high, places))
    if aux_count is None:
        out = jax.ShapeDtypeStruct((nv * width, occ), jnp.float32)
    else:
        out = jax.ShapeDtypeStruct((aux_count, nv, occ // aux_count, width), jnp.bfloat16)
    in_vmem, anywhere = pl.BlockSpec(memory_space=pltpu.VMEM), pl.BlockSpec(memory_space=pl.ANY)
    return pl.pallas_call(
        functools.partial(contract_body, nv, steps, own, carried, slots),
        in_specs=[pl.BlockSpec(memory_space=pltpu.SMEM)]
        + [in_vmem] * (1 + carried)
        + [anywhere] * len(arrays),
        out_specs=in_vmem,
        out_shape=out,
        scratch_shapes=[
            pltpu.VMEM((nv * width, occ), jnp.float32),
            pltpu.VMEM((slots, nv, largest, width, occ), jnp.bfloat16),
            pltpu.SemaphoreType.DMA((slots, nv)),
        ],
        compiler_params=pltpu.CompilerParams(vmem_limit_bytes=40 * 2**20),
        cost_estimate=pl.CostEstimate(flops=0, bytes_accessed=0, transcendentals=0),
    )(order, xt, *([carry] if carried else []), *arrays)


def five_sums(trial, gap, coupling):
    rounded = trial.astype(jnp.bfloat16).astype(jnp.float32)
    image = gap * rounded + coupling
    scaled_trial = trial / gap
    scaled_diff = trial - image / gap

    def total(values):
        return jnp.sum(values, keepdims=True)

    sums = (
        total(trial * image),
        total(trial * trial),
        total(scaled_diff * scaled_diff),
        total(scaled_diff * scaled_trial),
        total(scaled_trial * scaled_trial),
    )
    return scaled_diff, scaled_trial, sums


def finish(scaled_diff, scaled_trial, sums, count):
    cross_sum, self_sum, diff_sum, mixed_sum, scaled_sum = sums
    shift = cross_sum / self_sum
    mean_square = (diff_sum + 2.0 * shift * mixed_sum + shift * shift * scaled_sum) / count
    return (scaled_diff + shift * scaled_trial) * lax.rsqrt(mean_square + 1e-06), shift


def step_whole(order, coupling_shares, trial, gap, aux_count):
    nv, occ, width = trial.shape
    share = occ // aux_count

    def body(order_ref, shares_ref, trial_ref, gap_ref, next_ref, xt_ref, shift_ref, coupling_ref):
        for r in range(aux_count):
            for v in range(nv):
                rows = shares_ref[r * nv + order_ref[v]].astype(jnp.float32)
                coupling_ref[v * occ + r * share : v * occ + (r + 1) * share, :] = rows
        diff, scaled, sums = five_sums(
            trial_ref[...].reshape(nv * occ, width), gap_ref[...].reshape(nv * occ, width), coupling_ref[...]
        )
        fresh, shift = finish(diff, scaled, sums, nv * occ * width)
        fresh = fresh.reshape(nv, occ, width)
        next_ref[...] = fresh
        xt_ref[...] = fresh.astype(jnp.bfloat16)
        shift_ref[...] = jnp.broadcast_to(shift, shift_ref.shape)

    return pl.pallas_call(
        body,
        out_shape=(
            jax.ShapeDtypeStruct(trial.shape, jnp.float32),
            jax.ShapeDtypeStruct(trial.shape, jnp.bfloat16),
            jax.ShapeDtypeStruct((1, 128), jnp.float32),
        ),
        in_specs=[pl.BlockSpec(memory_space=pltpu.SMEM)] + [pl.BlockSpec(memory_space=pltpu.VMEM)] * 3,
        scratch_shapes=[pltpu.VMEM((nv * occ, width), jnp.float32)],
        compiler_params=pltpu.CompilerParams(vmem_limit_bytes=24 * 2**20),
    )(order, coupling_shares, trial, gap)


def share_sums(terms, trial, gap):
    count = terms.shape[0]

    def body(terms_ref, trial_ref, gap_ref, diff_ref, scaled_ref, sums_ref):
        coupling = jnp.sum(terms_ref[...].astype(jnp.float32), axis=0)
        diff, scaled, sums = five_sums(trial_ref[...], gap_ref[...], coupling)
        diff_ref[...] = diff
        scaled_ref[...] = scaled
        lane = lax.broadcasted_iota(jnp.int32, (1, 128), 1)
        row = jnp.zeros((1, 128), jnp.float32)
        for at, value in enumerate(sums):
            row = jnp.where(lane == at, value, row)
        sums_ref[...] = jnp.broadcast_to(row[None], sums_ref.shape)

    like = jax.ShapeDtypeStruct(trial.shape, jnp.float32)
    return pl.pallas_call(
        body,
        out_shape=(like, like, jax.ShapeDtypeStruct((count, 1, 128), jnp.float32)),
        compiler_params=pltpu.CompilerParams(vmem_limit_bytes=24 * 2**20),
    )(terms, trial, gap)


def step_share(diff, scaled, all_sums, total):
    def body(diff_ref, scaled_ref, sums_ref, next_ref, shift_ref):
        row = jnp.sum(sums_ref[...], axis=0)
        fresh, shift = finish(
            diff_ref[...], scaled_ref[...], [row[:, at : at + 1] for at in range(5)], total
        )
        next_ref[...] = fresh
        shift_ref[...] = jnp.broadcast_to(shift, shift_ref.shape)

    return pl.pallas_call(
        body,
        out_shape=(
            jax.ShapeDtypeStruct(diff.shape, jnp.float32),
            jax.ShapeDtypeStruct((1, 128), jnp.float32),
        ),
    )(diff, scaled, all_sums)


def spread(share, count, axes=EVERY):
    copies = jnp.broadcast_to(share[None], (count,) + share.shape)
    return lax.all_to_all(copies, axes, 0, 0, tiled=True)


def local(factors, trials, occ_energy, vir_energy):
    na, nv = lax.axis_size("aux"), lax.axis_size("vir")
    count = na * nv
    aux_at, vir_at = lax.axis_index("aux"), lax.axis_index("vir")
    p_count, width, occ = factors.shape
    own = p_count // nv
    share = occ // na
    total = occ * width * nv
    paired = nv & (nv - 1) == 0

    def partner(at, k):
        return at ^ k if paired else (at + k) % nv

    def source(at, k):
        return at ^ k if paired else (at - k) % nv

    def send(value, k):
        return lax.ppermute(value, "vir", [(one, partner(one, k)) for one in range(nv)])

    order = [source(vir_at, k) for k in range(nv)] + [vir_at]
    order = jnp.stack(order).astype(jnp.int32)

    unit = own // 16
    cut_up = unit >= 4 and own % 16 == 0
    sources = {k: [] for k in range(1, nv)}

    def piece(k, low, high, whole=factors):
        return lax.dynamic_slice_in_dim(whole, partner(vir_at, k) * own + low, high - low, 0)

    def exchange(k, low, high, part):
        sources[k].append((low, high, send(part, k)))

    def after_newest(k, *values):
        low, high, array = sources[k][-1]
        *values, array = lax.optimization_barrier((*values, array))
        sources[k][-1] = (low, high, array)
        return values

    marks = [0, own]
    if cut_up:
        marks = [0, 3 * unit, 15 * unit, own]
    for k in range(1, nv):
        exchange(k, 0, marks[1], piece(k, 0, marks[1]))
    later_factors = factors
    if cut_up:
        later_factors, trials = after_newest(1, factors, trials)

    gathered = spread(trials[0].T, na, "aux").reshape(occ, width)
    gathered = jnp.concatenate([gathered, vir_energy[None]], axis=0)
    if paired:
        state = {0: gathered}
        bit = nv // 2
        while bit:
            names = sorted(state)
            if cut_up and bit <= 2:
                state[0], = after_newest(4 - bit if bit == 1 else bit, state[0])
            came = send(jnp.stack([state[k] for k in names]), bit)
            if cut_up and bit == 2:
                large = [piece(k, *marks[1:3], later_factors) for k in range(1, nv)]
                large, came = lax.optimization_barrier((large, came))
            state.update({k ^ bit: came[at] for at, k in enumerate(names)})
            bit //= 2
    else:
        state = {k: send(gathered, k) if k else gathered for k in range(nv)}
    state = jnp.stack([state[k] for k in range(nv)])
    trial = state[:, :occ]
    gap_own = vir_energy[None, :] - lax.dynamic_slice_in_dim(occ_energy, aux_at * share, share)[:, None]
    xt = trial.astype(jnp.bfloat16)

    for low, high in zip(marks[1:], marks[2:]):
        for k in range(nv - 1, 0, -1):
            if low == marks[1]:
                exchange(k, low, high, large[k - 1])
            else:
                cut = piece(k, low, high, later_factors)
                exchange(k, low, high, *after_newest(min(k, 2), cut))

    early, ending = [], [(0, own)]
    if cut_up:
        steps = [0, 3 * unit, 7 * unit, 11 * unit, 15 * unit]
        early, ending = list(zip(steps, steps[1:])), [(15 * unit, own)]

    shift_list = []
    for iteration in range(ITERS):
        last = iteration == ITERS - 1
        call = functools.partial(contract, order, xt, factors, sources)
        if early and iteration == 0:
            partial = call(ending, own, call(early, own), na)
        else:
            partial = call(early + ending, own, None, na)
        if not last:
            energy, partial = lax.optimization_barrier((occ_energy, partial))
            gap = state[:, occ:] - energy[None, :, None]
        terms = lax.all_to_all(partial.reshape(count, share, width), EVERY, 0, 0, tiled=True)
        if not last:
            coupling = jnp.sum(terms.astype(jnp.float32), axis=0).astype(jnp.bfloat16)
            coupling, gap = lax.optimization_barrier((coupling, gap))
            trial, xt, shift = step_whole(order, spread(coupling, count), trial, gap, na)
        else:
            trial_own = lax.dynamic_slice_in_dim(trial[0], aux_at * share, share, 0)
            diff, scaled, sums = share_sums(terms, trial_own, gap_own)
            sums = lax.all_to_all(sums, EVERY, 0, 0, tiled=True)
            fresh, shift = step_share(diff, scaled, sums, total)
        shift_list.append(shift[:, :1])
    return (fresh.T[None], jnp.concatenate(shift_list, axis=0))


def solution(mesh):
    placed = (P("aux", "vir", None), P(None, "vir", "aux"), P(), P("vir"))
    return jax.shard_map(
        local, mesh=mesh, in_specs=placed, out_specs=(P(None, "vir", "aux"), P()), check_vma=False
    )
```

time: 296 us -> 295 us (level)
  waiting for transfers between devices: 137 us -> 186 us
  Pallas kernels: 56.4 us -> 30.8 us
  blocking collectives: 22.7 us -> 9.43 us
  starting transfers between devices: 35.9 us -> 28.5 us
  other arithmetic: 10.6 us -> 5.72 us
    ppermute x26 -> x11, waiting for transfers between devices: 102 us -> 153 us  [send(): lax.ppermute(value, 'vir', [(one, partner(one, k)) for one in range(nv)])]
    pallas_call x9 -> x3, Pallas kernels: 53.3 us -> 27.4 us  [contract(): pl.pallas_call(functools.partial(contract_body, nv, steps, own, carried,...]
    all_to_all x1 -> x0, blocking collectives: 13.3 us -> none  [spread(): return lax.all_to_all(copies, axes, 0, 0, tiled=True)]
    ppermute x26 -> x11, starting transfers between devices: 20.3 us -> 10.6 us  [send(): lax.ppermute(value, 'vir', [(one, partner(one, k)) for one in range(nv)])]
    all_to_all x1 -> x2, starting transfers between devices: 4.75 us -> 10.1 us  [spread(): return lax.all_to_all(copies, axes, 0, 0, tiled=True)]
    convert_element_type x2 -> x0, other arithmetic: 5.12 us -> none  [add(): (one.astype(jnp.float32) + two.astype(jnp.float32)).astype(jnp.bfloat16)]
    unnamed x56 -> x58, local copies, waits for them, and re-layouts: 9.65 us -> 14.6 us
    dynamic_slice x5 -> x3, local copies, waits for them, and re-layouts: 15.1 us -> 11.7 us  [piece(): lax.dynamic_slice_in_dim(whole, partner(vir_at, k) * own + low, high - lo...]
  transfers between devices with their start and end apart: 29 -> 15, of which waited for: 13 -> 6; matrix products, arithmetic and copies ran while one was open for 10% -> 6% of each run, Pallas kernels for 16% -> 4%
where the time goes in v4:
time: 295 us; the launch traced here: 294 us
  waiting for transfers between devices  186 us (63%)
  local copies, waits for them, and re-layouts  31.7 us (11%)
  Pallas kernels  30.8 us (10%)
  starting transfers between devices  28.5 us (10%)
  blocking collectives  9.43 us (3%)
  other arithmetic  5.72 us (2%)
    ppermute x11, waiting for transfers between devices, send(): lax.ppermute(value, 'vir', [(one, partner(one, k)) for one in range(nv)])  153 us
    pallas_call x3, Pallas kernels, contract(): pl.pallas_call(functools.partial(contract_body, nv, steps, own, carried,...  27.4 us
    all_to_all x2, waiting for transfers between devices, local(): lax.all_to_all(partial.reshape(count, share, width), EVERY, 0, 0, tiled=T...  17.8 us
    all_to_all x2, waiting for transfers between devices, spread(): return lax.all_to_all(copies, axes, 0, 0, tiled=True)  15.9 us
    unnamed x58, local copies, waits for them, and re-layouts  14.6 us
    dynamic_slice x3, local copies, waits for them, and re-layouts, piece(): lax.dynamic_slice_in_dim(whole, partner(vir_at, k) * own + low, high - lo...  11.7 us
    ppermute x11, starting transfers between devices, send(): lax.ppermute(value, 'vir', [(one, partner(one, k)) for one in range(nv)])  10.6 us
    all_to_all x2, starting transfers between devices, spread(): return lax.all_to_all(copies, axes, 0, 0, tiled=True)  10.1 us
  transfers between devices with their start and end apart: 15, of which 6 were waited for; matrix products, arithmetic and copies ran while one was open for 6% of the time, Pallas kernels for 4%

profile of v4, /device:TPU:0, one launch (start us, length us, event | category | flops | bytes accessed | tf_op | source)
XLA Modules:
  0.0 293.6 jit_solution(5923859787705450158)
XLA Ops:
  0.7 2.7 constant_dynamic-slice_fusion.6
  3.8 2.5 collective-permute-start.1
  7.9 6.6 %all-to-all-start = ((f32[8,16,256]{2,1,0:T(8,128)}), f32[8,16,256]{2,1,0:T(8,128)S(1)}, u32[]{:S(2)}, u32[]{:S(2)}) async-start(f32[8,16,256]{2,1,0:T(8,128)} %broadcast_in_dim.8), calls=%async_computation | async-start | bytes 262144 | tf_op jit(solution)/shard_map/all_to_all | solution.py:216
  14.5 7.3 %all-to-all-done = f32[8,16,256]{2,1,0:T(8,128)S(1)} async-done(((f32[8,16,256]{2,1,0:T(8,128)}), f32[8,16,256]{2,1,0:T(8,128)S(1)}, u32[]{:S(2)}, u32[]{:S(2)}) %all-to-all-start) | async-done | bytes 131104 | tf_op jit(solution)/shard_map/all_to_all | solution.py:216
  21.8 2.7 collective-permute-done.1.refs_2_
  24.6 1.7 collective-permute-start.3
  26.3 7.7 %constant_dynamic-slice_fusion.3 = (bf16[48,256,128]{2,1,0:T(8,128)(2,1)}, bf16[48,256,128]{2,1,0:T(8,128)(2,1)}, bf16[48,256,128]{2,1,0:T(8,128)(2,1)}) fusion(bf16[256,256,128]{2,1,0:T(8,128)(2,1)} %refs_0_.3, s32[]{:T(128)S(6)} %select_n.36, s32[]{:T(128)S(6)} %select_n.35, s32[]{:T(128)S(6)} %select_n.34), kind=kLoop, calls=%fused_computation.11 | loop fusion | bytes 18874380 | tf_op jit(solution)/shard_map/dynamic_slice | solution.py:246
  34.6 1.6 collective-permute-start.7
  36.3 150.1 %collective-permute-done.2.refs_3_ = bf16[12,256,128]{2,1,0:T(8,128)(2,1)S(1)} collective-permute-done((bf16[12,256,128]{2,1,0:T(8,128)(2,1)S(1)}, bf16[12,256,128]{2,1,0:T(8,128)(2,1)S(1)}, u32[]{:S(2)}, u32[]{:S(2)}) %collective-permute-start.2) | collective-permute-done | bytes 786464 | tf_op jit(solution)/shard_map/ppermute | solution.py:236
  188.0 1.4 collective-permute-start.4
  196.6 11.9 %shard_map.59.refs_0_ = f32[1024,128]{1,0:T(8,128)S(1)} custom-call(s32[5]{0:T(128)S(1)} %stack.33.order_ref, bf16[4,128,256]{2,1,0:T(8,128)(2,1)S(1)} %slice.32.xt_ref, bf16[256,256,128]{2,1,0:T(8,128)(2,1)} %refs_0_.3, bf16[12,256,128]{2,1,0:T(8,128)(2,1)S(1)} %copy-done.1, bf16[12,256,128]{2,1,0:T(8,128)(2,1)S(1)} %copy-done.4, ...), custom_call_target="tpu_custom_call" | custom-call | tf_op jit(solution)/shard_map/pallas_call | solution.py:100
  208.5 2.5 shard_map.60
  211.8 5.2 %all-to-all-start.1 = ((bf16[32,16,256]{2,1,0:T(8,128)(2,1)}), bf16[32,16,256]{2,1,0:T(8,128)(2,1)}, u32[]{:S(2)}, u32[]{:S(2)}) async-start(bf16[32,16,256]{2,1,0:T(8,128)(2,1)} %bitcast.24), calls=%async_computation.1 | async-start | bytes 524288 | tf_op jit(solution)/shard_map/all_to_all | solution.py:312
  217.8 1.5 broadcast_subtract_fusion.gap_ref
  219.3 8.3 %all-to-all-done.1 = bf16[32,16,256]{2,1,0:T(8,128)(2,1)} async-done(((bf16[32,16,256]{2,1,0:T(8,128)(2,1)}), bf16[32,16,256]{2,1,0:T(8,128)(2,1)}, u32[]{:S(2)}, u32[]{:S(2)}) %all-to-all-start.1) | async-done | bytes 262176 | tf_op jit(solution)/shard_map/all_to_all | solution.py:312
  229.3 3.5 %all-to-all-start.2 = ((bf16[32,16,256]{2,1,0:T(8,128)(2,1)}), bf16[32,16,256]{2,1,0:T(8,128)(2,1)}, u32[]{:S(2)}, u32[]{:S(2)}) async-start(bf16[32,16,256]{2,1,0:T(8,128)(2,1)} %broadcast_in_dim.10), calls=%async_computation.2 | async-start | bytes 524288 | tf_op jit(solution)/shard_map/all_to_all | solution.py:216
  232.8 1.9 slice.30.trial_ref
  234.7 8.5 %all-to-all-done.2.shares_ref = bf16[32,16,256]{2,1,0:T(8,128)(2,1)} async-done(((bf16[32,16,256]{2,1,0:T(8,128)(2,1)}), bf16[32,16,256]{2,1,0:T(8,128)(2,1)}, u32[]{:S(2)}, u32[]{:S(2)}) %all-to-all-start.2) | async-done | bytes 262176 | tf_op jit(solution)/shard_map/all_to_all | solution.py:216
  245.3 1.6 shard_map.61
  253.0 13.0 %shard_map.62 = bf16[8,4,16,256]{3,2,1,0:T(8,128)(2,1)S(1)} custom-call(s32[5]{0:T(128)S(1)} %stack.33.order_ref, bf16[4,128,256]{2,1,0:T(8,128)(2,1)S(1)} %get-tuple-element.52.xt_ref, bf16[256,256,128]{2,1,0:T(8,128)(2,1)} %refs_0_.3, bf16[12,256,128]{2,1,0:T(8,128)(2,1)S(1)} %copy-done.2, bf16[12,256,128]{2,1,0:T(8,128)(2,1)S(1)} %copy-done.5, ...), custom_call_target="tpu_custom_call" | custom-call | tf_op jit(solution)/shard_map/pallas_call | solution.py:100
  266.7 2.6 all-to-all-start.3
  270.4 9.5 %all-to-all-done.3.terms_ref = bf16[32,16,256]{2,1,0:T(8,128)(2,1)S(1)} async-done(((bf16[32,16,256]{2,1,0:T(8,128)(2,1)}), bf16[32,16,256]{2,1,0:T(8,128)(2,1)S(1)}, u32[]{:S(2)}, u32[]{:S(2)}) %all-to-all-start.3) | async-done | bytes 262176 | tf_op jit(solution)/shard_map/all_to_all | solution.py:312
  281.3 9.4 %all_to_all.25.sums_ref = f32[32,1,128]{2,1,0:T(1,128)} all-to-all(f32[32,1,128]{2,1,0:T(1,128)S(1)} %get-tuple-element.56), channel_id=1, replica_groups=mesh['aux'=8,'vir'=4] {'aux','vir'}, dimensions={0} | all-to-all | bytes 32768 | tf_op jit(solution)/shard_map/all_to_all | solution.py:320
  290.7 1.6 shard_map.64
  (91 shorter events, 27.1 us)
Async XLA Ops:
  0.6 6.6 %copy-start.25 = (f32[1,256,16]{1,2,0:T(8,128)S(1)}, f32[1,256,16]{1,2,0:T(8,128)}, u32[]{:S(2)}) copy-start(f32[1,256,16]{1,2,0:T(8,128)} %param.5) | copy-start | bytes 49156
  0.6 21.2 %copy-start.26 = (f32[256]{0:T(256)S(1)}, f32[256]{0:T(256)}, u32[]{:S(2)}) copy-start(f32[256]{0:T(256)} %param.7) | copy-start | bytes 3076
  3.4 3.0 %collective-permute-start = (bf16[12,256,128]{2,1,0:T(8,128)(2,1)S(1)}, bf16[12,256,128]{2,1,0:T(8,128)(2,1)S(1)}, u32[]{:S(2)}, u32[]{:S(2)}) collective-permute-start(bf16[12,256,128]{2,1,0:T(8,128)(2,1)S(1)} %get-tuple-element.67), channel_id=1, source_target_pairs={{0,1},{1,0},{2,3},{3,2},{4,5},{5,4},{6,7},{7,6},{8,9},{9,8},{10,11... | collective-permute-start | bytes 2359304 | tf_op jit(solution)/shard_map/ppermute | solution.py:236
  3.8 20.7 %collective-permute-start.1 = (bf16[12,256,128]{2,1,0:T(8,128)(2,1)S(1)}, bf16[12,256,128]{2,1,0:T(8,128)(2,1)S(1)}, u32[]{:S(2)}, u32[]{:S(2)}) collective-permute-start(bf16[12,256,128]{2,1,0:T(8,128)(2,1)S(1)} %get-tuple-element.66), channel_id=1, source_target_pairs={{0,2},{1,3},{2,0},{3,1},{4,6},{5,7},{6,4},{7,5},{8,10},{9,11},{10,... | collective-permute-start | bytes 2359304 | tf_op jit(solution)/shard_map/ppermute | solution.py:236
  7.9 13.9 %all-to-all-start = ((f32[8,16,256]{2,1,0:T(8,128)}), f32[8,16,256]{2,1,0:T(8,128)S(1)}, u32[]{:S(2)}, u32[]{:S(2)}) async-start(f32[8,16,256]{2,1,0:T(8,128)} %broadcast_in_dim.8), calls=%async_computation | async-start | bytes 262144 | tf_op jit(solution)/shard_map/all_to_all | solution.py:216
  24.6 9.4 %copy-start.3 = (bf16[12,256,128]{2,1,0:T(8,128)(2,1)}, bf16[12,256,128]{2,1,0:T(8,128)(2,1)S(1)}, u32[]{:S(2)}) copy-start(bf16[12,256,128]{2,1,0:T(8,128)(2,1)S(1)} %collective-permute-done.1.refs_2_) | copy-start | bytes 2359300
  24.6 11.6 %copy-start.24 = (bf16[12,256,128]{2,1,0:T(8,128)(2,1)S(1)}, bf16[12,256,128]{2,1,0:T(8,128)(2,1)}, u32[]{:S(2)}) copy-start(bf16[12,256,128]{2,1,0:T(8,128)(2,1)} %get-tuple-element.65) | copy-start | bytes 2359300
  24.6 9.4 %collective-permute-start.3 = (f32[1,129,256]{2,1,0:T(8,128)S(1)}, f32[1,129,256]{2,1,0:T(8,128)S(1)}, u32[]{:S(2)}, u32[]{:S(2)}) collective-permute-start(f32[1,129,256]{2,1,0:T(8,128)S(1)} %bitcast.26), channel_id=1, source_target_pairs={{0,2},{1,3},{2,0},{3,1},{4,6},{5,7},{6,4},{7,5},{8,10},{9,11},{10,... | collective-permute-start | bytes 396296 | tf_op jit(solution)/shard_map/ppermute | solution.py:236
  34.0 155.5 %copy-start.21 = (f32[1,129,256]{2,1,0:T(8,128)}, f32[1,129,256]{2,1,0:T(8,128)S(1)}, u32[]{:S(2)}) copy-start(f32[1,129,256]{2,1,0:T(8,128)S(1)} %collective-permute-done.3) | copy-start | bytes 396292
  34.0 156.9 %collective-permute-start.6 = (bf16[48,256,128]{2,1,0:T(8,128)(2,1)}, bf16[48,256,128]{2,1,0:T(8,128)(2,1)S(1)}, u32[]{:S(2)}, u32[]{:S(2)}) collective-permute-start(bf16[48,256,128]{2,1,0:T(8,128)(2,1)} %get-tuple-element.41), channel_id=1, source_target_pairs={{0,2},{1,3},{2,0},{3,1},{4,6},{5,7},{6,4},{7,5},{8,10},{9,11},{10,... | collective-permute-start | bytes 9437192 | tf_op jit(solution)/shard_map/ppermute | solution.py:236
  34.6 156.3 %collective-permute-start.5 = (bf16[48,256,128]{2,1,0:T(8,128)(2,1)}, bf16[48,256,128]{2,1,0:T(8,128)(2,1)}, u32[]{:S(2)}, u32[]{:S(2)}) collective-permute-start(bf16[48,256,128]{2,1,0:T(8,128)(2,1)} %get-tuple-element.39), channel_id=1, source_target_pairs={{0,1},{1,0},{2,3},{3,2},{4,5},{5,4},{6,7},{7,6},{8,9},{9,8},{10,11... | collective-permute-start | bytes 9437192 | tf_op jit(solution)/shard_map/ppermute | solution.py:236
  34.6 162.0 %collective-permute-start.7 = (bf16[48,256,128]{2,1,0:T(8,128)(2,1)}, bf16[48,256,128]{2,1,0:T(8,128)(2,1)}, u32[]{:S(2)}, u32[]{:S(2)}) collective-permute-start(bf16[48,256,128]{2,1,0:T(8,128)(2,1)} %get-tuple-element.44), channel_id=1, source_target_pairs={{0,3},{1,2},{2,1},{3,0},{4,7},{5,6},{6,5},{7,4},{8,11},{9,10},{10,... | collective-permute-start | bytes 9437192 | tf_op jit(solution)/shard_map/ppermute | solution.py:236
  36.2 150.2 %collective-permute-start.2 = (bf16[12,256,128]{2,1,0:T(8,128)(2,1)S(1)}, bf16[12,256,128]{2,1,0:T(8,128)(2,1)S(1)}, u32[]{:S(2)}, u32[]{:S(2)}) collective-permute-start(bf16[12,256,128]{2,1,0:T(8,128)(2,1)S(1)} %copy-done.24), channel_id=1, source_target_pairs={{0,3},{1,2},{2,1},{3,0},{4,7},{5,6},{6,5},{7,4},{8,11},{9,10},{10,... | collective-permute-start | bytes 2359304 | tf_op jit(solution)/shard_map/ppermute | solution.py:236
  188.0 5.1 %collective-permute-start.4 = (f32[2,129,256]{2,1,0:T(8,128)}, f32[2,129,256]{2,1,0:T(8,128)}, u32[]{:S(2)}, u32[]{:S(2)}) collective-permute-start(f32[2,129,256]{2,1,0:T(8,128)} %pad_maximum_fusion.1), channel_id=1, source_target_pairs={{0,1},{1,0},{2,3},{3,2},{4,5},{5,4},{6,7},{7,6},{8,9},{9,8},{10,11... | collective-permute-start | bytes 792584 | tf_op jit(solution)/shard_map/ppermute | solution.py:236
  189.5 7.0 %copy-start.1 = (bf16[12,256,128]{2,1,0:T(8,128)(2,1)S(1)}, bf16[12,256,128]{2,1,0:T(8,128)(2,1)}, u32[]{:S(2)}) copy-start(bf16[12,256,128]{2,1,0:T(8,128)(2,1)} %copy-done) | copy-start | bytes 2359300
  189.6 7.0 %copy-start.4 = (bf16[12,256,128]{2,1,0:T(8,128)(2,1)S(1)}, bf16[12,256,128]{2,1,0:T(8,128)(2,1)}, u32[]{:S(2)}) copy-start(bf16[12,256,128]{2,1,0:T(8,128)(2,1)} %copy-done.3) | copy-start | bytes 2359300
  189.6 7.0 %copy-start.7 = (bf16[12,256,128]{2,1,0:T(8,128)(2,1)S(1)}, bf16[12,256,128]{2,1,0:T(8,128)(2,1)}, u32[]{:S(2)}) copy-start(bf16[12,256,128]{2,1,0:T(8,128)(2,1)} %copy-done.6) | copy-start | bytes 2359300
  190.9 17.5 %collective-permute-start.9 = (bf16[4,256,128]{2,1,0:T(8,128)(2,1)S(1)}, bf16[4,256,128]{2,1,0:T(8,128)(2,1)S(1)}, u32[]{:S(2)}, u32[]{:S(2)}) collective-permute-start(bf16[4,256,128]{2,1,0:T(8,128)(2,1)S(1)} %get-tuple-element.46), channel_id=1, source_target_pairs={{0,2},{1,3},{2,0},{3,1},{4,6},{5,7},{6,4},{7,5},{8,10},{9,11},{10,... | collective-permute-start | bytes 786440 | tf_op jit(solution)/shard_map/ppermute | solution.py:236
  191.7 16.7 %collective-permute-start.10 = (bf16[4,256,128]{2,1,0:T(8,128)(2,1)S(1)}, bf16[4,256,128]{2,1,0:T(8,128)(2,1)S(1)}, u32[]{:S(2)}, u32[]{:S(2)}) collective-permute-start(bf16[4,256,128]{2,1,0:T(8,128)(2,1)S(1)} %get-tuple-element.47), channel_id=1, source_target_pairs={{0,3},{1,2},{2,1},{3,0},{4,7},{5,6},{6,5},{7,4},{8,11},{9,10},{10,... | collective-permute-start | bytes 786440 | tf_op jit(solution)/shard_map/ppermute | solution.py:236
  192.3 16.1 %collective-permute-start.8 = (bf16[4,256,128]{2,1,0:T(8,128)(2,1)S(1)}, bf16[4,256,128]{2,1,0:T(8,128)(2,1)S(1)}, u32[]{:S(2)}, u32[]{:S(2)}) collective-permute-start(bf16[4,256,128]{2,1,0:T(8,128)(2,1)S(1)} %get-tuple-element.45), channel_id=1, source_target_pairs={{0,1},{1,0},{2,3},{3,2},{4,5},{5,4},{6,7},{7,6},{8,9},{9,8},{10,11... | collective-permute-start | bytes 786440 | tf_op jit(solution)/shard_map/ppermute | solution.py:236
  211.8 15.8 %all-to-all-start.1 = ((bf16[32,16,256]{2,1,0:T(8,128)(2,1)}), bf16[32,16,256]{2,1,0:T(8,128)(2,1)}, u32[]{:S(2)}, u32[]{:S(2)}) async-start(bf16[32,16,256]{2,1,0:T(8,128)(2,1)} %bitcast.24), calls=%async_computation.1 | async-start | bytes 524288 | tf_op jit(solution)/shard_map/all_to_all | solution.py:312
  229.3 13.9 %all-to-all-start.2 = ((bf16[32,16,256]{2,1,0:T(8,128)(2,1)}), bf16[32,16,256]{2,1,0:T(8,128)(2,1)}, u32[]{:S(2)}, u32[]{:S(2)}) async-start(bf16[32,16,256]{2,1,0:T(8,128)(2,1)} %broadcast_in_dim.10), calls=%async_computation.2 | async-start | bytes 524288 | tf_op jit(solution)/shard_map/all_to_all | solution.py:216
  253.0 16.3 %copy-start.27 = (f32[128]{0:T(128)S(1)}, f32[128]{0:T(128)}, u32[]{:S(2)}) copy-start(f32[128]{0:T(128)} %param.6) | copy-start | bytes 1540
  266.7 13.2 %all-to-all-start.3 = ((bf16[32,16,256]{2,1,0:T(8,128)(2,1)}), bf16[32,16,256]{2,1,0:T(8,128)(2,1)S(1)}, u32[]{:S(2)}, u32[]{:S(2)}) async-start(bf16[32,16,256]{2,1,0:T(8,128)(2,1)} %bitcast.23), calls=%async_computation.3 | async-start | bytes 524288 | tf_op jit(solution)/shard_map/all_to_all | solution.py:312
  (19 other events, 20.9 us)

commit v5 on v4

--- a/solution.py
+++ b/solution.py
@@ -96,12 +96,12 @@
         out = jax.ShapeDtypeStruct((nv * width, occ), jnp.float32)
     else:
         out = jax.ShapeDtypeStruct((aux_count, nv, occ // aux_count, width), jnp.bfloat16)
-    in_vmem, anywhere = pl.BlockSpec(memory_space=pltpu.VMEM), pl.BlockSpec(memory_space=pl.ANY)
+    in_vmem, in_hbm = pl.BlockSpec(memory_space=pltpu.VMEM), pl.BlockSpec(memory_space=pltpu.HBM)
     return pl.pallas_call(
         functools.partial(contract_body, nv, steps, own, carried, slots),
         in_specs=[pl.BlockSpec(memory_space=pltpu.SMEM)]
         + [in_vmem] * (1 + carried)
-        + [anywhere] * len(arrays),
+        + [in_hbm] * len(arrays),
         out_specs=in_vmem,
         out_shape=out,
         scratch_shapes=[
@@ -256,12 +256,17 @@
 
     marks = [0, own]
     if cut_up:
-        marks = [0, 3 * unit, 15 * unit, own]
-    for k in range(1, nv):
-        exchange(k, 0, marks[1], piece(k, 0, marks[1]))
+        marks = [0, 12 * unit, 15 * unit, own]
+    far = [k for k in range(nv) if k > 1] + [1]
     later_factors = factors
+    for n, k in enumerate(far):
+        cut = piece(k, *marks[:2], later_factors)
+        if cut_up and n == 0:
+            later_factors, cut = lax.optimization_barrier((factors, cut))
+        exchange(k, *marks[:2], cut)
     if cut_up:
-        later_factors, trials = after_newest(1, factors, trials)
+        later = [[piece(k, low, high, later_factors) for k in far] for low, high in zip(marks[1:], marks[2:])]
+        later, trials = lax.optimization_barrier((later, *after_newest(2, trials)))
 
     gathered = spread(trials[0].T, na, "aux").reshape(occ, width)
     gathered = jnp.concatenate([gathered, vir_energy[None]], axis=0)
@@ -270,12 +275,7 @@
         bit = nv // 2
         while bit:
             names = sorted(state)
-            if cut_up and bit <= 2:
-                state[0], = after_newest(4 - bit if bit == 1 else bit, state[0])
             came = send(jnp.stack([state[k] for k in names]), bit)
-            if cut_up and bit == 2:
-                large = [piece(k, *marks[1:3], later_factors) for k in range(1, nv)]
-                large, came = lax.optimization_barrier((large, came))
             state.update({k ^ bit: came[at] for at, k in enumerate(names)})
             bit //= 2
     else:
@@ -285,27 +285,27 @@
     gap_own = vir_energy[None, :] - lax.dynamic_slice_in_dim(occ_energy, aux_at * share, share)[:, None]
     xt = trial.astype(jnp.bfloat16)
 
-    for low, high in zip(marks[1:], marks[2:]):
-        for k in range(nv - 1, 0, -1):
-            if low == marks[1]:
-                exchange(k, low, high, large[k - 1])
-            else:
-                cut = piece(k, low, high, later_factors)
-                exchange(k, low, high, *after_newest(min(k, 2), cut))
-
-    early, ending = [], [(0, own)]
+    call = functools.partial(contract, order, xt, factors, sources)
+    groups = [[(0, own)]]
     if cut_up:
-        steps = [0, 3 * unit, 7 * unit, 11 * unit, 15 * unit]
-        early, ending = list(zip(steps, steps[1:])), [(15 * unit, own)]
+        low, high, end = marks[1:]
+        for k, cut in enumerate(later[0]):
+            exchange(far[k], low, high, cut)
+        groups = [[(n * 4 * unit, (n + 1) * 4 * unit) for n in range(3)], [(low, high)], [(high, end)]]
+        carry = call(groups[0], own)
+        cuts, carry = lax.optimization_barrier((later[1], carry))
+        for k, cut in zip(far, cuts):
+            exchange(k, high, end, cut)
+        carry = call(groups[1], own, carry)
 
     shift_list = []
     for iteration in range(ITERS):
         last = iteration == ITERS - 1
         call = functools.partial(contract, order, xt, factors, sources)
-        if early and iteration == 0:
-            partial = call(ending, own, call(early, own), na)
+        if cut_up and iteration == 0:
+            partial = call(groups[-1], own, carry, na)
         else:
-            partial = call(early + ending, own, None, na)
+            partial = call(sum(groups, []), own, None, na)
         if not last:
             energy, partial = lax.optimization_barrier((occ_energy, partial))
             gap = state[:, occ:] - energy[None, :, None]

time: 295 us -> 277 us (0.939)
  waiting for transfers between devices: 186 us -> 164 us
  blocking collectives: 9.43 us -> 22.9 us
  starting transfers between devices: 28.5 us -> 22.1 us
  local copies, waits for them, and re-layouts: 31.7 us -> 27.7 us
  Pallas kernels: 30.8 us -> 34.8 us
    ppermute x11, waiting for transfers between devices: 153 us -> 138 us  [send(): lax.ppermute(value, 'vir', [(one, partner(one, k)) for one in range(nv)])]
    all_to_all x0 -> x1, blocking collectives: none -> 13.5 us  [spread(): return lax.all_to_all(copies, axes, 0, 0, tiled=True)]
    all_to_all x2 -> x1, waiting for transfers between devices: 15.9 us -> 8.52 us  [spread(): return lax.all_to_all(copies, axes, 0, 0, tiled=True)]
    unnamed x58 -> x48, local copies, waits for them, and re-layouts: 14.6 us -> 7.6 us
    all_to_all x2 -> x1, starting transfers between devices: 10.1 us -> 3.49 us  [spread(): return lax.all_to_all(copies, axes, 0, 0, tiled=True)]
    pallas_call x3 -> x4, Pallas kernels: 27.4 us -> 31.3 us  [contract(): pl.pallas_call(functools.partial(contract_body, nv, steps, own, carried,...]
    dynamic_slice x3 -> x4, local copies, waits for them, and re-layouts: 11.7 us -> 15.3 us  [piece(): lax.dynamic_slice_in_dim(whole, partner(vir_at, k) * own + low, high - lo...]
  transfers between devices with their start and end apart: 15 -> 14, of which waited for: 6 -> 9; matrix products, arithmetic and copies ran while one was open for 6% -> 6% of each run, Pallas kernels for 4% -> 5%
where the time goes in v5:
time: 277 us
  waiting for transfers between devices  164 us (59%)
  Pallas kernels  34.8 us (13%)
  local copies, waits for them, and re-layouts  27.7 us (10%)
  blocking collectives  22.9 us (8%)
  starting transfers between devices  22.1 us (8%)
  other arithmetic  4.08 us (1%)
    ppermute x11, waiting for transfers between devices, send(): lax.ppermute(value, 'vir', [(one, partner(one, k)) for one in range(nv)])  138 us
    pallas_call x4, Pallas kernels, contract(): pl.pallas_call(functools.partial(contract_body, nv, steps, own, carried,...  31.3 us
    all_to_all x2, waiting for transfers between devices, local(): lax.all_to_all(partial.reshape(count, share, width), EVERY, 0, 0, tiled=T...  17.8 us
    dynamic_slice x4, local copies, waits for them, and re-layouts, piece(): lax.dynamic_slice_in_dim(whole, partner(vir_at, k) * own + low, high - lo...  15.3 us
    all_to_all x1, blocking collectives, spread(): return lax.all_to_all(copies, axes, 0, 0, tiled=True)  13.5 us
    ppermute x11, starting transfers between devices, send(): lax.ppermute(value, 'vir', [(one, partner(one, k)) for one in range(nv)])  9.69 us
    all_to_all x1, blocking collectives, local(): sums = lax.all_to_all(sums, EVERY, 0, 0, tiled=True)  9.43 us
    all_to_all x2, starting transfers between devices, local(): lax.all_to_all(partial.reshape(count, share, width), EVERY, 0, 0, tiled=T...  8.95 us
  transfers between devices with their start and end apart: 14, of which 9 were waited for; matrix products, arithmetic and copies ran while one was open for 6% of the time, Pallas kernels for 5%

profile of v5, /device:TPU:0, one launch (start us, length us, event | category | flops | bytes accessed | tf_op | source)
XLA Modules:
  0.0 276.5 jit_solution(13443649803204314701)
XLA Ops:
  0.6 3.9 %constant_dynamic-slice_fusion.8 = bf16[48,256,128]{2,1,0:T(8,128)(2,1)} fusion(bf16[256,256,128]{2,1,0:T(8,128)(2,1)} %refs_0_.3, s32[]{:T(128)S(6)} %select_n.31), kind=kLoop, calls=%fused_computation.16 | loop fusion | bytes 6291460 | tf_op jit(solution)/shard_map/dynamic_slice | solution.py:246
  4.5 3.0 %collective-permute-start = (bf16[48,256,128]{2,1,0:T(8,128)(2,1)}, bf16[48,256,128]{2,1,0:T(8,128)(2,1)S(1)}, u32[]{:S(2)}, u32[]{:S(2)}) collective-permute-start(bf16[48,256,128]{2,1,0:T(8,128)(2,1)} %constant_dynamic-slice_fusion.8), channel_id=1, source_target_pairs={{0,2},{1,3},{2,0},{3,1},{4,6},{5,7},{6,4},{7,5},{8,10},{9,11},{10,... | collective-permute-start | bytes 9437192 | tf_op jit(solution)/shard_map/ppermute | solution.py:236
  7.5 6.3 %constant_dynamic-slice_fusion = (bf16[48,256,128]{2,1,0:T(8,128)(2,1)}, bf16[48,256,128]{2,1,0:T(8,128)(2,1)}) fusion(bf16[256,256,128]{2,1,0:T(8,128)(2,1)} %refs_0_.3, s32[]{:T(128)S(6)} %select_n.39, s32[]{:T(128)S(6)} %select_n.38), kind=kLoop, calls=%fused_computation.8 | loop fusion | bytes 12582920 | tf_op jit(solution)/shard_map/dynamic_slice | solution.py:246
  13.9 2.1 constant_dynamic-slice_fusion.2
  16.0 3.1 %constant_dynamic-slice_fusion.5 = (bf16[12,256,128]{2,1,0:T(8,128)(2,1)}, bf16[12,256,128]{2,1,0:T(8,128)(2,1)}, bf16[12,256,128]{2,1,0:T(8,128)(2,1)}) fusion(bf16[256,256,128]{2,1,0:T(8,128)(2,1)} %refs_0_.3, s32[]{:T(128)S(6)} %select_n.34, s32[]{:T(128)S(6)} %select_n.33, s32[]{:T(128)S(6)} %select_n.32), kind=kLoop, calls=%fused_computation.13 | loop fusion | bytes 4718604 | tf_op jit(solution)/shard_map/dynamic_slice | solution.py:246
  19.1 57.6 %collective-permute-done.refs_2_ = bf16[48,256,128]{2,1,0:T(8,128)(2,1)S(1)} collective-permute-done((bf16[48,256,128]{2,1,0:T(8,128)(2,1)}, bf16[48,256,128]{2,1,0:T(8,128)(2,1)S(1)}, u32[]{:S(2)}, u32[]{:S(2)}) %collective-permute-start) | collective-permute-done | bytes 3145760 | tf_op jit(solution)/shard_map/ppermute | solution.py:236
  76.7 13.5 %all_to_all.25 = f32[8,16,256]{2,1,0:T(8,128)S(1)} all-to-all(f32[8,16,256]{2,1,0:T(8,128)S(1)} %broadcast_in_dim.8), channel_id=1, replica_groups=mesh['aux'=8,'vir'=4] {'aux'}, dimensions={0} | all-to-all | bytes 262144 | tf_op jit(solution)/shard_map/all_to_all | solution.py:216
  91.7 54.5 %collective-permute-done.1 = f32[1,129,256]{2,1,0:T(8,128)S(1)} collective-permute-done((f32[1,129,256]{2,1,0:T(8,128)S(1)}, f32[1,129,256]{2,1,0:T(8,128)S(1)}, u32[]{:S(2)}, u32[]{:S(2)}) %collective-permute-start.1) | collective-permute-done | bytes 132128 | tf_op jit(solution)/shard_map/ppermute | solution.py:236
  151.4 10.9 %shard_map.59.refs_0_ = f32[1024,128]{1,0:T(8,128)S(1)} custom-call(s32[5]{0:T(128)S(1)} %stack.31.order_ref, bf16[4,128,256]{2,1,0:T(8,128)(2,1)S(1)} %slice.32.xt_ref, bf16[256,256,128]{2,1,0:T(8,128)(2,1)} %refs_0_.3, bf16[48,256,128]{2,1,0:T(8,128)(2,1)} %collective-permute-done.3.refs_1_, bf16[48,256,128]{2,1,0:T(8,128)(2,1)S(1)} %collective-permute-done.refs_2_, ...), custom_call_target="tpu_custom_call" | custom-call | tf_op jit(solution)/shard_map/pallas_call | solution.py:100
  164.3 3.2 %collective-permute-done.6.refs_3_.refs_5_ = bf16[12,256,128]{2,1,0:T(8,128)(2,1)} collective-permute-done((bf16[12,256,128]{2,1,0:T(8,128)(2,1)}, bf16[12,256,128]{2,1,0:T(8,128)(2,1)}, u32[]{:S(2)}, u32[]{:S(2)}) %collective-permute-start.6) | collective-permute-done | bytes 786464 | tf_op jit(solution)/shard_map/ppermute | solution.py:236
  167.5 16.1 %collective-permute-done.7.refs_4_.refs_6_ = bf16[12,256,128]{2,1,0:T(8,128)(2,1)} collective-permute-done((bf16[12,256,128]{2,1,0:T(8,128)(2,1)}, bf16[12,256,128]{2,1,0:T(8,128)(2,1)}, u32[]{:S(2)}, u32[]{:S(2)}) %collective-permute-start.7) | collective-permute-done | bytes 786464 | tf_op jit(solution)/shard_map/ppermute | solution.py:236
  183.6 3.9 %shard_map.60.refs_0_ = f32[1024,128]{1,0:T(8,128)S(1)} custom-call(s32[5]{0:T(128)S(1)} %stack.31.order_ref, bf16[4,128,256]{2,1,0:T(8,128)(2,1)S(1)} %slice.32.xt_ref, f32[1024,128]{1,0:T(8,128)S(1)} %shard_map.59.refs_0_, bf16[256,256,128]{2,1,0:T(8,128)(2,1)} %refs_0_.3, bf16[12,256,128]{2,1,0:T(8,128)(2,1)} %collective-permute-done.5.refs_2_.refs_4_, ...), custom_call_target="tpu_custom_call" | custom-call | tf_op jit(solution)/shard_map/pallas_call | solution.py:100
  187.6 2.3 collective-permute-done.9.refs_3_.refs_8_
  189.9 4.0 %collective-permute-done.10.refs_4_.refs_9_ = bf16[4,256,128]{2,1,0:T(8,128)(2,1)S(1)} collective-permute-done((bf16[4,256,128]{2,1,0:T(8,128)(2,1)S(1)}, bf16[4,256,128]{2,1,0:T(8,128)(2,1)S(1)}, u32[]{:S(2)}, u32[]{:S(2)}) %collective-permute-start.10) | collective-permute-done | bytes 262176 | tf_op jit(solution)/shard_map/ppermute | solution.py:236
  193.9 2.5 shard_map.61
  197.2 6.4 %all-to-all-start.1 = ((bf16[32,16,256]{2,1,0:T(8,128)(2,1)}), bf16[32,16,256]{2,1,0:T(8,128)(2,1)}, u32[]{:S(2)}, u32[]{:S(2)}) async-start(bf16[32,16,256]{2,1,0:T(8,128)(2,1)} %bitcast.24), calls=%async_computation.1 | async-start | bytes 524288 | tf_op jit(solution)/shard_map/all_to_all | solution.py:312
  205.8 8.3 %all-to-all-done.1 = bf16[32,16,256]{2,1,0:T(8,128)(2,1)} async-done(((bf16[32,16,256]{2,1,0:T(8,128)(2,1)}), bf16[32,16,256]{2,1,0:T(8,128)(2,1)}, u32[]{:S(2)}, u32[]{:S(2)}) %all-to-all-start.1) | async-done | bytes 262176 | tf_op jit(solution)/shard_map/all_to_all | solution.py:312
  215.9 3.5 %all-to-all-start.2 = ((bf16[32,16,256]{2,1,0:T(8,128)(2,1)}), bf16[32,16,256]{2,1,0:T(8,128)(2,1)}, u32[]{:S(2)}, u32[]{:S(2)}) async-start(bf16[32,16,256]{2,1,0:T(8,128)(2,1)} %broadcast_in_dim.10), calls=%async_computation.2 | async-start | bytes 524288 | tf_op jit(solution)/shard_map/all_to_all | solution.py:216
  219.4 1.9 slice.30.trial_ref
  221.3 8.5 %all-to-all-done.2.shares_ref = bf16[32,16,256]{2,1,0:T(8,128)(2,1)} async-done(((bf16[32,16,256]{2,1,0:T(8,128)(2,1)}), bf16[32,16,256]{2,1,0:T(8,128)(2,1)}, u32[]{:S(2)}, u32[]{:S(2)}) %all-to-all-start.2) | async-done | bytes 262176 | tf_op jit(solution)/shard_map/all_to_all | solution.py:216
  236.2 13.9 %shard_map.63 = bf16[8,4,16,256]{3,2,1,0:T(8,128)(2,1)S(1)} custom-call(s32[5]{0:T(128)S(1)} %stack.31.order_ref, bf16[4,128,256]{2,1,0:T(8,128)(2,1)S(1)} %get-tuple-element.48.xt_ref, bf16[256,256,128]{2,1,0:T(8,128)(2,1)} %refs_0_.3, bf16[48,256,128]{2,1,0:T(8,128)(2,1)} %collective-permute-done.3.refs_1_, ...), custom_call_target="tpu_custom_call" | custom-call | tf_op jit(solution)/shard_map/pallas_call | solution.py:100
  250.8 2.6 all-to-all-start.3
  254.5 9.5 %all-to-all-done.3.terms_ref = bf16[32,16,256]{2,1,0:T(8,128)(2,1)S(1)} async-done(((bf16[32,16,256]{2,1,0:T(8,128)(2,1)}), bf16[32,16,256]{2,1,0:T(8,128)(2,1)S(1)}, u32[]{:S(2)}, u32[]{:S(2)}) %all-to-all-start.3) | async-done | bytes 262176 | tf_op jit(solution)/shard_map/all_to_all | solution.py:312
  264.2 9.4 %all_to_all.26.sums_ref = f32[32,1,128]{2,1,0:T(1,128)} all-to-all(f32[32,1,128]{2,1,0:T(1,128)S(1)} %get-tuple-element.52), channel_id=1, replica_groups=mesh['aux'=8,'vir'=4] {'aux','vir'}, dimensions={0} | all-to-all | bytes 32768 | tf_op jit(solution)/shard_map/all_to_all | solution.py:320
  (82 shorter events, 24.8 us)
Async XLA Ops:
  4.5 72.1 %collective-permute-start = (bf16[48,256,128]{2,1,0:T(8,128)(2,1)}, bf16[48,256,128]{2,1,0:T(8,128)(2,1)S(1)}, u32[]{:S(2)}, u32[]{:S(2)}) collective-permute-start(bf16[48,256,128]{2,1,0:T(8,128)(2,1)} %constant_dynamic-slice_fusion.8), channel_id=1, source_target_pairs={{0,2},{1,3},{2,0},{3,1},{4,6},{5,7},{6,4},{7,5},{8,10},{9,11},{10,... | collective-permute-start | bytes 9437192 | tf_op jit(solution)/shard_map/ppermute | solution.py:236
  13.8 136.8 %collective-permute-start.4 = (bf16[48,256,128]{2,1,0:T(8,128)(2,1)}, bf16[48,256,128]{2,1,0:T(8,128)(2,1)}, u32[]{:S(2)}, u32[]{:S(2)}) collective-permute-start(bf16[48,256,128]{2,1,0:T(8,128)(2,1)} %get-tuple-element.58), channel_id=1, source_target_pairs={{0,3},{1,2},{2,1},{3,0},{4,7},{5,6},{6,5},{7,4},{8,11},{9,10},{10,... | collective-permute-start | bytes 9437192 | tf_op jit(solution)/shard_map/ppermute | solution.py:236
  13.8 137.6 %collective-permute-start.3 = (bf16[48,256,128]{2,1,0:T(8,128)(2,1)}, bf16[48,256,128]{2,1,0:T(8,128)(2,1)}, u32[]{:S(2)}, u32[]{:S(2)}) collective-permute-start(bf16[48,256,128]{2,1,0:T(8,128)(2,1)} %get-tuple-element.59), channel_id=1, source_target_pairs={{0,1},{1,0},{2,3},{3,2},{4,5},{5,4},{6,7},{7,6},{8,9},{9,8},{10,11... | collective-permute-start | bytes 9437192 | tf_op jit(solution)/shard_map/ppermute | solution.py:236
  13.9 62.7 %copy-start.19 = (f32[1,256,16]{1,2,0:T(8,128)S(1)}, f32[1,256,16]{1,2,0:T(8,128)}, u32[]{:S(2)}) copy-start(f32[1,256,16]{1,2,0:T(8,128)} %param.5) | copy-start | bytes 49156
  13.9 76.2 %copy-start.20 = (f32[256]{0:T(256)S(1)}, f32[256]{0:T(256)}, u32[]{:S(2)}) copy-start(f32[256]{0:T(256)} %param.7) | copy-start | bytes 3076
  90.2 56.0 %collective-permute-start.1 = (f32[1,129,256]{2,1,0:T(8,128)S(1)}, f32[1,129,256]{2,1,0:T(8,128)S(1)}, u32[]{:S(2)}, u32[]{:S(2)}) collective-permute-start(f32[1,129,256]{2,1,0:T(8,128)S(1)} %maximum_bitcast_fusion), channel_id=1, source_target_pairs={{0,2},{1,3},{2,0},{3,1},{4,6},{5,7},{6,4},{7,5},{8,10},{9,11},{10,... | collective-permute-start | bytes 396296 | tf_op jit(solution)/shard_map/ppermute | solution.py:236
  146.2 2.3 collective-permute-start.2
  146.3 17.5 %collective-permute-start.5 = (bf16[12,256,128]{2,1,0:T(8,128)(2,1)}, bf16[12,256,128]{2,1,0:T(8,128)(2,1)}, u32[]{:S(2)}, u32[]{:S(2)}) collective-permute-start(bf16[12,256,128]{2,1,0:T(8,128)(2,1)} %get-tuple-element.38), channel_id=1, source_target_pairs={{0,1},{1,0},{2,3},{3,2},{4,5},{5,4},{6,7},{7,6},{8,9},{9,8},{10,11... | collective-permute-start | bytes 2359304 | tf_op jit(solution)/shard_map/ppermute | solution.py:236
  146.8 20.7 %collective-permute-start.6 = (bf16[12,256,128]{2,1,0:T(8,128)(2,1)}, bf16[12,256,128]{2,1,0:T(8,128)(2,1)}, u32[]{:S(2)}, u32[]{:S(2)}) collective-permute-start(bf16[12,256,128]{2,1,0:T(8,128)(2,1)} %get-tuple-element.39), channel_id=1, source_target_pairs={{0,2},{1,3},{2,0},{3,1},{4,6},{5,7},{6,4},{7,5},{8,10},{9,11},{10,... | collective-permute-start | bytes 2359304 | tf_op jit(solution)/shard_map/ppermute | solution.py:236
  148.6 35.1 %collective-permute-start.7 = (bf16[12,256,128]{2,1,0:T(8,128)(2,1)}, bf16[12,256,128]{2,1,0:T(8,128)(2,1)}, u32[]{:S(2)}, u32[]{:S(2)}) collective-permute-start(bf16[12,256,128]{2,1,0:T(8,128)(2,1)} %get-tuple-element.40), channel_id=1, source_target_pairs={{0,3},{1,2},{2,1},{3,0},{4,7},{5,6},{6,5},{7,4},{8,11},{9,10},{10,... | collective-permute-start | bytes 2359304 | tf_op jit(solution)/shard_map/ppermute | solution.py:236
  150.5 11.8 %copy-start.18 = (bf16[4,256,128]{2,1,0:T(8,128)(2,1)S(1)}, bf16[4,256,128]{2,1,0:T(8,128)(2,1)}, u32[]{:S(2)}) copy-start(bf16[4,256,128]{2,1,0:T(8,128)(2,1)} %get-tuple-element.41) | copy-start | bytes 786436
  150.6 12.2 %copy-start.17 = (bf16[4,256,128]{2,1,0:T(8,128)(2,1)S(1)}, bf16[4,256,128]{2,1,0:T(8,128)(2,1)}, u32[]{:S(2)}) copy-start(bf16[4,256,128]{2,1,0:T(8,128)(2,1)} %get-tuple-element.42) | copy-start | bytes 786436
  150.6 13.2 %copy-start.16 = (bf16[4,256,128]{2,1,0:T(8,128)(2,1)S(1)}, bf16[4,256,128]{2,1,0:T(8,128)(2,1)}, u32[]{:S(2)}) copy-start(bf16[4,256,128]{2,1,0:T(8,128)(2,1)} %get-tuple-element.43) | copy-start | bytes 786436
  162.4 25.2 %collective-permute-start.8 = (bf16[4,256,128]{2,1,0:T(8,128)(2,1)S(1)}, bf16[4,256,128]{2,1,0:T(8,128)(2,1)S(1)}, u32[]{:S(2)}, u32[]{:S(2)}) collective-permute-start(bf16[4,256,128]{2,1,0:T(8,128)(2,1)S(1)} %copy-done.18), channel_id=1, source_target_pairs={{0,1},{1,0},{2,3},{3,2},{4,5},{5,4},{6,7},{7,6},{8,9},{9,8},{10,11... | collective-permute-start | bytes 786440 | tf_op jit(solution)/shard_map/ppermute | solution.py:236
  162.8 27.1 %collective-permute-start.9 = (bf16[4,256,128]{2,1,0:T(8,128)(2,1)S(1)}, bf16[4,256,128]{2,1,0:T(8,128)(2,1)S(1)}, u32[]{:S(2)}, u32[]{:S(2)}) collective-permute-start(bf16[4,256,128]{2,1,0:T(8,128)(2,1)S(1)} %copy-done.17), channel_id=1, source_target_pairs={{0,2},{1,3},{2,0},{3,1},{4,6},{5,7},{6,4},{7,5},{8,10},{9,11},{10,... | collective-permute-start | bytes 786440 | tf_op jit(solution)/shard_map/ppermute | solution.py:236
  163.8 30.1 %collective-permute-start.10 = (bf16[4,256,128]{2,1,0:T(8,128)(2,1)S(1)}, bf16[4,256,128]{2,1,0:T(8,128)(2,1)S(1)}, u32[]{:S(2)}, u32[]{:S(2)}) collective-permute-start(bf16[4,256,128]{2,1,0:T(8,128)(2,1)S(1)} %copy-done.16), channel_id=1, source_target_pairs={{0,3},{1,2},{2,1},{3,0},{4,7},{5,6},{6,5},{7,4},{8,11},{9,10},{10,... | collective-permute-start | bytes 786440 | tf_op jit(solution)/shard_map/ppermute | solution.py:236
  189.9 6.6 %copy-start.2 = (bf16[4,256,128]{2,1,0:T(8,128)(2,1)}, bf16[4,256,128]{2,1,0:T(8,128)(2,1)S(1)}, u32[]{:S(2)}) copy-start(bf16[4,256,128]{2,1,0:T(8,128)(2,1)S(1)} %collective-permute-done.9.refs_3_.refs_8_) | copy-start | bytes 786436
  197.2 16.9 %all-to-all-start.1 = ((bf16[32,16,256]{2,1,0:T(8,128)(2,1)}), bf16[32,16,256]{2,1,0:T(8,128)(2,1)}, u32[]{:S(2)}, u32[]{:S(2)}) async-start(bf16[32,16,256]{2,1,0:T(8,128)(2,1)} %bitcast.24), calls=%async_computation.1 | async-start | bytes 524288 | tf_op jit(solution)/shard_map/all_to_all | solution.py:312
  215.9 13.9 %all-to-all-start.2 = ((bf16[32,16,256]{2,1,0:T(8,128)(2,1)}), bf16[32,16,256]{2,1,0:T(8,128)(2,1)}, u32[]{:S(2)}, u32[]{:S(2)}) async-start(bf16[32,16,256]{2,1,0:T(8,128)(2,1)} %broadcast_in_dim.10), calls=%async_computation.2 | async-start | bytes 524288 | tf_op jit(solution)/shard_map/all_to_all | solution.py:216
  236.2 17.2 %copy-start.22 = (f32[128]{0:T(128)S(1)}, f32[128]{0:T(128)}, u32[]{:S(2)}) copy-start(f32[128]{0:T(128)} %param.6) | copy-start | bytes 1540
  236.2 17.3 %copy-start.21 = (f32[256]{0:T(256)S(1)}, f32[256]{0:T(256)}, u32[]{:S(2)}) copy-start(f32[256]{0:T(256)} %param.7) | copy-start | bytes 3076
  250.8 13.2 %all-to-all-start.3 = ((bf16[32,16,256]{2,1,0:T(8,128)(2,1)}), bf16[32,16,256]{2,1,0:T(8,128)(2,1)S(1)}, u32[]{:S(2)}, u32[]{:S(2)}) async-start(bf16[32,16,256]{2,1,0:T(8,128)(2,1)} %bitcast.23), calls=%async_computation.3 | async-start | bytes 524288 | tf_op jit(solution)/shard_map/all_to_all | solution.py:312
  264.2 9.4 %copy-start.9 = (f32[16,256]{1,0:T(8,128)}, f32[16,256]{1,0:T(8,128)S(1)}, u32[]{:S(2)}) copy-start(f32[16,256]{1,0:T(8,128)S(1)} %get-tuple-element.50.diff_ref) | copy-start | bytes 49156
  264.2 9.4 %copy-start.10 = (f32[16,256]{1,0:T(8,128)}, f32[16,256]{1,0:T(8,128)S(1)}, u32[]{:S(2)}) copy-start(f32[16,256]{1,0:T(8,128)S(1)} %get-tuple-element.51.scaled_ref) | copy-start | bytes 49156
  (13 other events, 17.0 us)

commit v6 on v5

v6 whole, which is shorter than its diff:
```python
import functools

import jax
import jax.numpy as jnp
from jax import lax
from jax.experimental import pallas as pl
from jax.experimental.pallas import tpu as pltpu
from jax.sharding import PartitionSpec as P

EVERY = ("aux", "vir")


def diagonal(occ):
    rows = lax.broadcasted_iota(jnp.int32, (occ, occ), 0)
    return rows == lax.broadcasted_iota(jnp.int32, (occ, occ), 1)


def coulomb_and_exchange(pair, eye):
    density = jnp.sum(jnp.where(eye, pair, 0.0), keepdims=True)
    density = density.astype(jnp.bfloat16).astype(jnp.float32)
    pair = pair.astype(jnp.bfloat16).astype(jnp.float32)
    return (jnp.where(eye, 2.0 * density, 0.0) - pair).astype(jnp.bfloat16)


def side_by_side(blocks, count):
    return jnp.concatenate([blocks[q] for q in range(count)], axis=1)


def five_sums(trial, gap, coupling):
    rounded = trial.astype(jnp.bfloat16).astype(jnp.float32)
    image = gap * rounded + coupling
    scaled_trial = trial / gap
    scaled_diff = trial - image / gap

    def total(values):
        return jnp.sum(values, keepdims=True)

    sums = (
        total(trial * image),
        total(trial * trial),
        total(scaled_diff * scaled_diff),
        total(scaled_diff * scaled_trial),
        total(scaled_trial * scaled_trial),
    )
    return scaled_diff, scaled_trial, sums


def finish(scaled_diff, scaled_trial, sums, count):
    cross_sum, self_sum, diff_sum, mixed_sum, scaled_sum = sums
    shift = cross_sum / self_sum
    mean_square = (diff_sum + 2.0 * shift * mixed_sum + shift * shift * scaled_sum) / count
    return (scaled_diff + shift * scaled_trial) * lax.rsqrt(mean_square + 1e-06), shift


def contract_body(nv, blocks, size, own, carried, stepping, total, order_ref, *refs):
    first_refs, refs = refs[: 4 if stepping else 1], refs[4 if stepping else 1 :]
    carry_ref, f_refs = (refs[0], refs[1:]) if carried else (None, refs)
    f_count = 1 + max(at for block in blocks for _, _, places in block for at, _ in places)
    f_refs, refs = f_refs[:f_count], f_refs[f_count:]
    out_refs, (acc_ref, xt_ref, held, sems) = refs[:-4], refs[-4:]
    out_ref = out_refs[0]
    width, occ = held.shape[3:]
    near_start = order_ref[nv] * own

    for at, block in enumerate(blocks):
        for k in range(nv):
            into_at = 0
            for low, high, places in block:
                array, offset = places[k]
                start = near_start + low if k == 0 else offset
                count = high - low
                pltpu.make_async_copy(
                    f_refs[array].at[pl.ds(start, count)],
                    held.at[at, k, pl.ds(into_at, count)],
                    sems.at[at, k],
                ).start()
                into_at += count

    acc_ref[...] = carry_ref[...] if carried else jnp.zeros_like(acc_ref)
    if stepping:
        shares_ref, trial_ref, vir_ref, occ_ref = first_refs
        own_ref, shift_ref = out_refs[1:]
        share = own_ref.shape[0]
        coupling = jnp.concatenate(
            [
                shares_ref[r * nv + order_ref[k]].astype(jnp.float32)
                for k in range(nv)
                for r in range(occ // share)
            ],
            axis=0,
        )
        gap = jnp.concatenate([vir_ref[k] - occ_ref[...] for k in range(nv)], axis=0)
        diff, scaled, sums = five_sums(trial_ref[...].reshape(nv * occ, width), gap, coupling)
        fresh, shift = finish(diff, scaled, sums, total)
        shift_ref[...] = jnp.broadcast_to(shift, shift_ref.shape)
        for k in range(nv):
            rows = fresh[k * occ : (k + 1) * occ]
            xt_ref[:, k * width : (k + 1) * width] = rows.astype(jnp.bfloat16)
        mine = fresh[:share]
        for r in range(1, occ // share):
            rows = fresh[r * share : (r + 1) * share]
            mine = jnp.where(order_ref[nv + 1] == r, rows, mine)
        own_ref[...] = mine
    else:
        for k in range(nv):
            xt_ref[:, k * width : (k + 1) * width] = first_refs[0][k]
    eye = lax.broadcasted_iota(jnp.int32, (occ, occ), 0) == lax.broadcasted_iota(
        jnp.int32, (occ, occ), 1
    )

    def work(at, _):
        for k in range(nv):
            pltpu.make_async_copy(held.at[at, k], held.at[at, k], sems.at[at, k]).wait()
        tall = jnp.concatenate(
            [
                jnp.concatenate([held[at, k, q] for q in range(size)], axis=1)
                for k in range(nv)
            ],
            axis=0,
        )
        pairs = jnp.dot(xt_ref[...], tall, preferred_element_type=jnp.float32)
        mixes = []
        for q in range(size):
            pair = pairs[:, q * occ : (q + 1) * occ]
            density = jnp.sum(jnp.where(eye, pair, 0.0), keepdims=True)
            density = density.astype(jnp.bfloat16).astype(jnp.float32)
            pair = pair.astype(jnp.bfloat16).astype(jnp.float32)
            mixes.append((jnp.where(eye, 2.0 * density, 0.0) - pair).astype(jnp.bfloat16))
        mix = jnp.concatenate(mixes, axis=0)
        acc_ref[...] += jnp.dot(tall, mix, preferred_element_type=jnp.float32)
        return _

    lax.fori_loop(0, len(blocks), work, 0)
    if len(out_ref.shape) == 2:
        out_ref[...] = acc_ref[...]
        return
    share = out_ref.shape[2]
    for k in range(nv):
        turned = acc_ref[k * width : (k + 1) * width, :].T
        for r in range(occ // share):
            out_ref[r, order_ref[k]] = turned[r * share : (r + 1) * share, :].astype(out_ref.dtype)


def contract(order, first, factors, sources, blocks, own, carry=None, aux_count=None):
    p_count, width, occ = factors.shape
    nv = p_count // own
    carried, stepping = carry is not None, len(first) > 1
    size = sum(high - low for low, high in blocks[0])
    arrays, placed = [factors], []
    for block in blocks:
        placed.append([])
        for low, high in block:
            places = [(0, 0)]
            for k in range(1, nv):
                start, array = next((a, x) for a, b, x in sources[k] if a <= low and high <= b)
                at = next((n for n, x in enumerate(arrays) if x is array), len(arrays))
                if at == len(arrays):
                    arrays.append(array)
                places.append((at, low - start))
            placed[-1].append((low, high, places))
    if aux_count is None:
        out = [jax.ShapeDtypeStruct((nv * width, occ), jnp.float32)]
    else:
        out = [jax.ShapeDtypeStruct((aux_count, nv, occ // aux_count, width), jnp.bfloat16)]
    if stepping:
        out.append(jax.ShapeDtypeStruct((occ // aux_count, width), jnp.float32))
        out.append(jax.ShapeDtypeStruct((1, 128), jnp.float32))
    in_vmem, in_hbm = pl.BlockSpec(memory_space=pltpu.VMEM), pl.BlockSpec(memory_space=pltpu.HBM)
    body = functools.partial(
        contract_body, nv, placed, size, own, carried, stepping, nv * width * occ
    )
    return pl.pallas_call(
        body,
        in_specs=[pl.BlockSpec(memory_space=pltpu.SMEM)]
        + [in_vmem] * (len(first) + carried)
        + [in_hbm] * len(arrays),
        out_specs=[in_vmem] * len(out),
        out_shape=out,
        scratch_shapes=[
            pltpu.VMEM((nv * width, occ), jnp.float32),
            pltpu.VMEM((occ, nv * width), jnp.bfloat16),
            pltpu.VMEM((len(blocks), nv, size, width, occ), jnp.bfloat16),
            pltpu.SemaphoreType.DMA((len(blocks), nv)),
        ],
        compiler_params=pltpu.CompilerParams(vmem_limit_bytes=40 * 2**20),
        cost_estimate=pl.CostEstimate(flops=0, bytes_accessed=0, transcendentals=0),
    )(order, *first, *([carry] if carried else []), *arrays)


def share_sums(terms, trial, gap):
    count = terms.shape[0]

    def body(terms_ref, trial_ref, gap_ref, diff_ref, scaled_ref, sums_ref):
        coupling = jnp.sum(terms_ref[...].astype(jnp.float32), axis=0)
        diff, scaled, sums = five_sums(trial_ref[...], gap_ref[...], coupling)
        diff_ref[...] = diff
        scaled_ref[...] = scaled
        lane = lax.broadcasted_iota(jnp.int32, (1, 128), 1)
        row = jnp.zeros((1, 128), jnp.float32)
        for at, value in enumerate(sums):
            row = jnp.where(lane == at, value, row)
        sums_ref[...] = jnp.broadcast_to(row[None], sums_ref.shape)

    like = jax.ShapeDtypeStruct(trial.shape, jnp.float32)
    return pl.pallas_call(
        body,
        out_shape=(like, like, jax.ShapeDtypeStruct((count, 1, 128), jnp.float32)),
        compiler_params=pltpu.CompilerParams(vmem_limit_bytes=24 * 2**20),
    )(terms, trial, gap)


def step_share(diff, scaled, all_sums, before, total):
    def body(diff_ref, scaled_ref, sums_ref, before_ref, next_ref, shifts_ref):
        row = jnp.sum(sums_ref[...], axis=0)
        fresh, shift = finish(
            diff_ref[...], scaled_ref[...], [row[:, at : at + 1] for at in range(5)], total
        )
        next_ref[...] = fresh
        shifts_ref[...] = jnp.concatenate([before_ref[:, :1], shift], axis=1)

    return pl.pallas_call(
        body,
        out_shape=(
            jax.ShapeDtypeStruct(diff.shape, jnp.float32),
            jax.ShapeDtypeStruct((1, 2), jnp.float32),
        ),
    )(diff, scaled, all_sums, before)


def spread(share, count, axes=EVERY):
    copies = jnp.broadcast_to(share[None], (count,) + share.shape)
    return lax.all_to_all(copies, axes, 0, 0, tiled=True)


def local(factors, trials, occ_energy, vir_energy):
    na, nv = lax.axis_size("aux"), lax.axis_size("vir")
    count = na * nv
    aux_at, vir_at = lax.axis_index("aux"), lax.axis_index("vir")
    p_count, width, occ = factors.shape
    own = p_count // nv
    share = occ // na
    total = occ * width * nv
    paired = nv & (nv - 1) == 0

    def partner(at, k):
        return at ^ k if paired else (at + k) % nv

    def source(at, k):
        return at ^ k if paired else (at - k) % nv

    def send(value, k):
        return lax.ppermute(value, "vir", [(one, partner(one, k)) for one in range(nv)])

    order = [source(vir_at, k) for k in range(nv)] + [vir_at, aux_at]
    order = jnp.stack(order).astype(jnp.int32)

    unit = own // 16
    cut_up = unit >= 4 and own % 16 == 0
    sources = {k: [] for k in range(1, nv)}

    def piece(k, low, high, whole=factors):
        return lax.dynamic_slice_in_dim(whole, partner(vir_at, k) * own + low, high - low, 0)

    def exchange(k, low, high, part):
        sources[k].append((low, high, send(part, k)))

    def after_newest(k, *values):
        low, high, array = sources[k][-1]
        *values, array = lax.optimization_barrier((*values, array))
        sources[k][-1] = (low, high, array)
        return values

    marks = [0, own]
    if cut_up:
        marks = [0, 12 * unit, 15 * unit, own]
    far = [k for k in range(nv) if k > 1] + [1]
    later_factors = factors
    for n, k in enumerate(far):
        cut = piece(k, *marks[:2], later_factors)
        if cut_up and n == 0:
            later_factors, cut = lax.optimization_barrier((factors, cut))
        exchange(k, *marks[:2], cut)
    if cut_up:
        later = [[piece(k, low, high, later_factors) for k in far] for low, high in zip(marks[1:], marks[2:])]
        later, trials = lax.optimization_barrier((later, *after_newest(2, trials)))

    gathered = spread(trials[0].T, na, "aux").reshape(occ, width)
    gathered = jnp.concatenate([gathered, vir_energy[None]], axis=0)
    if paired:
        state = {0: gathered}
        bit = nv // 2
        while bit:
            names = sorted(state)
            came = send(jnp.stack([state[k] for k in names]), bit)
            state.update({k ^ bit: came[at] for at, k in enumerate(names)})
            bit //= 2
    else:
        state = {k: send(gathered, k) if k else gathered for k in range(nv)}
    state = jnp.stack([state[k] for k in range(nv)])
    trial = state[:, :occ]
    gap_own = vir_energy[None, :] - lax.dynamic_slice_in_dim(occ_energy, aux_at * share, share)[:, None]
    xt = trial.astype(jnp.bfloat16)

    def call(first, blocks, carry=None, aux_count=None):
        return contract(order, first, factors, sources, blocks, own, carry, aux_count)

    carry = None
    blocks = last_block = [[(0, own)]]
    if cut_up:
        low, high, end = marks[1:]
        for k, cut in enumerate(later[0]):
            exchange(far[k], low, high, cut)
        blocks = [[(n * 4 * unit, (n + 1) * 4 * unit)] for n in range(3)]
        last_block = [[(high, end)]]
        (carry,) = call([xt], blocks)
        cuts, carry = lax.optimization_barrier((later[1], carry))
        for k, cut in zip(far, cuts):
            exchange(k, high, end, cut)
        (carry,) = call([xt], [[(low, high)]], carry)
        blocks.append([(low, high), (high, end)])

    def sum_terms(partial):
        return lax.all_to_all(partial.reshape(count, share, width), EVERY, 0, 0, tiled=True)

    (partial,) = call([xt], last_block, carry, na)
    coupling = jnp.sum(sum_terms(partial).astype(jnp.float32), axis=0).astype(jnp.bfloat16)
    first = [spread(coupling, count), trial, state[:, occ:], occ_energy[:, None]]
    partial, trial_own, before = call(first, blocks, None, na)
    diff, scaled, sums = share_sums(sum_terms(partial), trial_own, gap_own)
    sums = lax.all_to_all(sums, EVERY, 0, 0, tiled=True)
    fresh, shifts = step_share(diff, scaled, sums, before, total)
    return (fresh.T[None], shifts.T)


def solution(mesh):
    placed = (P("aux", "vir", None), P(None, "vir", "aux"), P(), P("vir"))
    return jax.shard_map(
        local, mesh=mesh, in_specs=placed, out_specs=(P(None, "vir", "aux"), P()), check_vma=False
    )
```

time: 277 us -> 269 us (0.971)
  blocking collectives: 22.9 us -> 39.4 us
  Pallas kernels: 34.8 us -> 26.9 us
  starting transfers between devices: 22.1 us -> 16 us
  waiting for transfers between devices: 164 us -> 159 us
  local copies, waits for them, and re-layouts: 27.7 us -> 24.2 us
    all_to_all x0 -> x1, blocking collectives: none -> 16.6 us  [sum_terms(): lax.all_to_all(partial.reshape(count, share, width), EVERY, 0, 0, tiled=T...]
    pallas_call x5 -> x4, Pallas kernels: 32.9 us -> 25 us  [contract(): pl.pallas_call(body, in_specs=[pl.BlockSpec(memory_space=pltpu.SMEM)] + [...]
    all_to_all x2 -> x1, waiting for transfers between devices: 17.8 us -> 10.4 us  [sum_terms(): lax.all_to_all(partial.reshape(count, share, width), EVERY, 0, 0, tiled=T...]
    all_to_all x2 -> x1, starting transfers between devices: 8.95 us -> 2.58 us  [sum_terms(): lax.all_to_all(partial.reshape(count, share, width), EVERY, 0, 0, tiled=T...]
    ppermute x11, waiting for transfers between devices: 138 us -> 141 us  [send(): lax.ppermute(value, 'vir', [(one, partner(one, k)) for one in range(nv)])]
    unnamed x48 -> x40, local copies, waits for them, and re-layouts: 7.6 us -> 5.01 us
  transfers between devices with their start and end apart: 14 -> 13, of which waited for: 9 -> 8; matrix products, arithmetic and copies ran while one was open for 6% -> 6% of each run, Pallas kernels for 5% -> 4%
where the time goes in v6:
time: 269 us; the launch traced here: 268 us
  waiting for transfers between devices  159 us (59%)
  blocking collectives  39.4 us (15%)
  Pallas kernels  26.9 us (10%)
  local copies, waits for them, and re-layouts  24.2 us (9%)
  starting transfers between devices  16 us (6%)
    ppermute x11, waiting for transfers between devices, send(): lax.ppermute(value, 'vir', [(one, partner(one, k)) for one in range(nv)])  141 us
    pallas_call x4, Pallas kernels, contract(): pl.pallas_call(body, in_specs=[pl.BlockSpec(memory_space=pltpu.SMEM)] + [...  25 us
    all_to_all x1, blocking collectives, sum_terms(): lax.all_to_all(partial.reshape(count, share, width), EVERY, 0, 0, tiled=T...  16.6 us
    dynamic_slice x4, local copies, waits for them, and re-layouts, piece(): lax.dynamic_slice_in_dim(whole, partner(vir_at, k) * own + low, high - lo...  15.2 us
    all_to_all x1, blocking collectives, spread(): return lax.all_to_all(copies, axes, 0, 0, tiled=True)  13.5 us
    all_to_all x1, waiting for transfers between devices, sum_terms(): lax.all_to_all(partial.reshape(count, share, width), EVERY, 0, 0, tiled=T...  10.4 us
    ppermute x11, starting transfers between devices, send(): lax.ppermute(value, 'vir', [(one, partner(one, k)) for one in range(nv)])  10.1 us
    all_to_all x1, blocking collectives, local(): sums = lax.all_to_all(sums, EVERY, 0, 0, tiled=True)  9.33 us
  transfers between devices with their start and end apart: 13, of which 8 were waited for; matrix products, arithmetic and copies ran while one was open for 6% of the time, Pallas kernels for 4%

profile of v6, /device:TPU:0, one launch (start us, length us, event | category | flops | bytes accessed | tf_op | source)
XLA Modules:
  0.0 268.5 jit_solution(10093128781687730940)
XLA Ops:
  0.6 3.9 %constant_dynamic-slice_fusion.8 = bf16[48,256,128]{2,1,0:T(8,128)(2,1)} fusion(bf16[256,256,128]{2,1,0:T(8,128)(2,1)} %refs_4_.1, s32[]{:T(128)S(6)} %select_n.30), kind=kLoop, calls=%fused_computation.13 | loop fusion | bytes 6291460 | tf_op jit(solution)/shard_map/dynamic_slice | solution.py:262
  4.5 3.0 %collective-permute-start = (bf16[48,256,128]{2,1,0:T(8,128)(2,1)}, bf16[48,256,128]{2,1,0:T(8,128)(2,1)S(1)}, u32[]{:S(2)}, u32[]{:S(2)}) collective-permute-start(bf16[48,256,128]{2,1,0:T(8,128)(2,1)} %constant_dynamic-slice_fusion.8), channel_id=1, source_target_pairs={{0,2},{1,3},{2,0},{3,1},{4,6},{5,7},{6,4},{7,5},{8,10},{9,11},{10,... | collective-permute-start | bytes 9437192 | tf_op jit(solution)/shard_map/ppermute | solution.py:252
  7.5 6.3 %constant_dynamic-slice_fusion = (bf16[48,256,128]{2,1,0:T(8,128)(2,1)}, bf16[48,256,128]{2,1,0:T(8,128)(2,1)}) fusion(bf16[256,256,128]{2,1,0:T(8,128)(2,1)} %refs_4_.1, s32[]{:T(128)S(6)} %select_n.38, s32[]{:T(128)S(6)} %select_n.37), kind=kLoop, calls=%fused_computation.5 | loop fusion | bytes 12582920 | tf_op jit(solution)/shard_map/dynamic_slice | solution.py:262
  13.9 2.0 constant_dynamic-slice_fusion.2
  15.9 3.1 %constant_dynamic-slice_fusion.5 = (bf16[12,256,128]{2,1,0:T(8,128)(2,1)}, bf16[12,256,128]{2,1,0:T(8,128)(2,1)}, bf16[12,256,128]{2,1,0:T(8,128)(2,1)}) fusion(bf16[256,256,128]{2,1,0:T(8,128)(2,1)} %refs_4_.1, s32[]{:T(128)S(6)} %select_n.33, s32[]{:T(128)S(6)} %select_n.32, s32[]{:T(128)S(6)} %select_n.31), kind=kLoop, calls=%fused_computation.10 | loop fusion | bytes 4718604 | tf_op jit(solution)/shard_map/dynamic_slice | solution.py:262
  19.0 57.6 %collective-permute-done.refs_3_.refs_6_ = bf16[48,256,128]{2,1,0:T(8,128)(2,1)S(1)} collective-permute-done((bf16[48,256,128]{2,1,0:T(8,128)(2,1)}, bf16[48,256,128]{2,1,0:T(8,128)(2,1)S(1)}, u32[]{:S(2)}, u32[]{:S(2)}) %collective-permute-start) | collective-permute-done | bytes 3145760 | tf_op jit(solution)/shard_map/ppermute | solution.py:252
  76.6 13.5 %all_to_all.25 = f32[8,16,256]{2,1,0:T(8,128)S(1)} all-to-all(f32[8,16,256]{2,1,0:T(8,128)S(1)} %broadcast_in_dim.10), channel_id=1, replica_groups=mesh['aux'=8,'vir'=4] {'aux'}, dimensions={0} | all-to-all | bytes 262144 | tf_op jit(solution)/shard_map/all_to_all | solution.py:232
  91.7 54.5 %collective-permute-done.1 = f32[1,129,256]{2,1,0:T(8,128)S(1)} collective-permute-done((f32[1,129,256]{2,1,0:T(8,128)S(1)}, f32[1,129,256]{2,1,0:T(8,128)S(1)}, u32[]{:S(2)}, u32[]{:S(2)}) %collective-permute-start.1) | collective-permute-done | bytes 132128 | tf_op jit(solution)/shard_map/ppermute | solution.py:252
  146.8 1.7 collective-permute-start.6
  151.5 8.1 %shard_map.59.refs_1_ = f32[1024,128]{1,0:T(8,128)S(1)} custom-call(s32[6]{0:T(128)S(1)} %stack.35.order_ref, bf16[4,128,256]{2,1,0:T(8,128)(2,1)S(1)} %slice.20.refs_0_, bf16[256,256,128]{2,1,0:T(8,128)(2,1)} %refs_4_.1, bf16[48,256,128]{2,1,0:T(8,128)(2,1)} %collective-permute-done.3.refs_2_.refs_5_, ...), custom_call_target="tpu_custom_call" | custom-call | tf_op jit(solution)/shard_map/pallas_call | solution.py:172
  161.9 5.6 %collective-permute-done.6.refs_4_.refs_9_ = bf16[12,256,128]{2,1,0:T(8,128)(2,1)} collective-permute-done((bf16[12,256,128]{2,1,0:T(8,128)(2,1)}, bf16[12,256,128]{2,1,0:T(8,128)(2,1)}, u32[]{:S(2)}, u32[]{:S(2)}) %collective-permute-start.6) | collective-permute-done | bytes 786464 | tf_op jit(solution)/shard_map/ppermute | solution.py:252
  167.5 16.1 %collective-permute-done.7.refs_5_.refs_10_ = bf16[12,256,128]{2,1,0:T(8,128)(2,1)} collective-permute-done((bf16[12,256,128]{2,1,0:T(8,128)(2,1)}, bf16[12,256,128]{2,1,0:T(8,128)(2,1)}, u32[]{:S(2)}, u32[]{:S(2)}) %collective-permute-start.7) | collective-permute-done | bytes 786464 | tf_op jit(solution)/shard_map/ppermute | solution.py:252
  183.6 3.9 %shard_map.60.refs_1_ = f32[1024,128]{1,0:T(8,128)S(1)} custom-call(s32[6]{0:T(128)S(1)} %stack.35.order_ref, bf16[4,128,256]{2,1,0:T(8,128)(2,1)S(1)} %slice.20.refs_0_, f32[1024,128]{1,0:T(8,128)S(1)} %shard_map.59.refs_1_, bf16[256,256,128]{2,1,0:T(8,128)(2,1)} %refs_4_.1, bf16[12,256,128]{2,1,0:T(8,128)(2,1)} %collective-permute-done.5.refs_3_.refs_8_, ...), custom_call_target="tpu_custom_call" | custom-call | tf_op jit(solution)/shard_map/pallas_call | solution.py:172
  189.1 5.5 %collective-permute-done.9.refs_4_.refs_12_ = bf16[4,256,128]{2,1,0:T(8,128)(2,1)S(1)} collective-permute-done((bf16[4,256,128]{2,1,0:T(8,128)(2,1)S(1)}, bf16[4,256,128]{2,1,0:T(8,128)(2,1)S(1)}, u32[]{:S(2)}, u32[]{:S(2)}) %collective-permute-start.9) | collective-permute-done | bytes 262176 | tf_op jit(solution)/shard_map/ppermute | solution.py:252
  194.6 2.5 shard_map.61
  197.1 16.6 %all_to_all.26 = bf16[32,16,256]{2,1,0:T(8,128)(2,1)} all-to-all(bf16[32,16,256]{2,1,0:T(8,128)(2,1)S(1)} %bitcast.19), channel_id=1, replica_groups=mesh['aux'=8,'vir'=4] {'aux','vir'}, dimensions={0} | all-to-all | bytes 524288 | tf_op jit(solution)/shard_map/all_to_all | solution.py:323
  215.5 3.3 %all-to-all-start.2 = ((bf16[32,16,256]{2,1,0:T(8,128)(2,1)}), bf16[32,16,256]{2,1,0:T(8,128)(2,1)}, u32[]{:S(2)}, u32[]{:S(2)}) async-start(bf16[32,16,256]{2,1,0:T(8,128)(2,1)} %broadcast_in_dim.12), calls=%async_computation.2 | async-start | bytes 524288 | tf_op jit(solution)/shard_map/all_to_all | solution.py:232
  218.9 1.9 slice.18.refs_1_
  221.5 7.8 %all-to-all-done.2.refs_0_ = bf16[32,16,256]{2,1,0:T(8,128)(2,1)} async-done(((bf16[32,16,256]{2,1,0:T(8,128)(2,1)}), bf16[32,16,256]{2,1,0:T(8,128)(2,1)}, u32[]{:S(2)}, u32[]{:S(2)}) %all-to-all-start.2) | async-done | bytes 262176 | tf_op jit(solution)/shard_map/all_to_all | solution.py:232
  232.3 10.6 %shard_map.62 = (bf16[8,4,16,256]{3,2,1,0:T(8,128)(2,1)S(1)}, f32[16,256]{1,0:T(8,128)S(1)}, f32[1,128]{1,0:T(1,128)S(1)}) custom-call(s32[6]{0:T(128)S(1)} %stack.35.order_ref, bf16[32,16,256]{2,1,0:T(8,128)(2,1)} %all-to-all-done.2.refs_0_, f32[4,128,256]{2,1,0:T(8,128)S(1)} %copy-done, f32[4,1,256]{2,1,0:T(1,128)S(1)} %pad_maximum_fusion.2.refs_2_, ...), custom_call_target="tpu_custom_call" | custom-call | tf_op jit(solution)/shard_map/pallas_call | solution.py:172
  244.1 2.6 all-to-all-start.3
  246.9 10.4 %all-to-all-done.3.terms_ref = bf16[32,16,256]{2,1,0:T(8,128)(2,1)S(1)} async-done(((bf16[32,16,256]{2,1,0:T(8,128)(2,1)}), bf16[32,16,256]{2,1,0:T(8,128)(2,1)S(1)}, u32[]{:S(2)}, u32[]{:S(2)}) %all-to-all-start.3) | async-done | bytes 262176 | tf_op jit(solution)/shard_map/all_to_all | solution.py:323
  257.5 9.3 %all_to_all.27.sums_ref = f32[32,1,128]{2,1,0:T(1,128)} all-to-all(f32[32,1,128]{2,1,0:T(1,128)S(1)} %get-tuple-element.44), channel_id=1, replica_groups=mesh['aux'=8,'vir'=4] {'aux','vir'}, dimensions={0} | all-to-all | bytes 32768 | tf_op jit(solution)/shard_map/all_to_all | solution.py:330
  266.8 1.7 shard_map.64
  (69 shorter events, 16.2 us)
Async XLA Ops:
  4.5 72.1 %collective-permute-start = (bf16[48,256,128]{2,1,0:T(8,128)(2,1)}, bf16[48,256,128]{2,1,0:T(8,128)(2,1)S(1)}, u32[]{:S(2)}, u32[]{:S(2)}) collective-permute-start(bf16[48,256,128]{2,1,0:T(8,128)(2,1)} %constant_dynamic-slice_fusion.8), channel_id=1, source_target_pairs={{0,2},{1,3},{2,0},{3,1},{4,6},{5,7},{6,4},{7,5},{8,10},{9,11},{10,... | collective-permute-start | bytes 9437192 | tf_op jit(solution)/shard_map/ppermute | solution.py:252
  13.8 136.9 %collective-permute-start.3 = (bf16[48,256,128]{2,1,0:T(8,128)(2,1)}, bf16[48,256,128]{2,1,0:T(8,128)(2,1)}, u32[]{:S(2)}, u32[]{:S(2)}) collective-permute-start(bf16[48,256,128]{2,1,0:T(8,128)(2,1)} %get-tuple-element.49), channel_id=1, source_target_pairs={{0,1},{1,0},{2,3},{3,2},{4,5},{5,4},{6,7},{7,6},{8,9},{9,8},{10,11... | collective-permute-start | bytes 9437192 | tf_op jit(solution)/shard_map/ppermute | solution.py:252
  13.8 137.7 %collective-permute-start.4 = (bf16[48,256,128]{2,1,0:T(8,128)(2,1)}, bf16[48,256,128]{2,1,0:T(8,128)(2,1)}, u32[]{:S(2)}, u32[]{:S(2)}) collective-permute-start(bf16[48,256,128]{2,1,0:T(8,128)(2,1)} %get-tuple-element.48), channel_id=1, source_target_pairs={{0,3},{1,2},{2,1},{3,0},{4,7},{5,6},{6,5},{7,4},{8,11},{9,10},{10,... | collective-permute-start | bytes 9437192 | tf_op jit(solution)/shard_map/ppermute | solution.py:252
  13.9 62.7 %copy-start.17 = (f32[1,256,16]{1,2,0:T(8,128)S(1)}, f32[1,256,16]{1,2,0:T(8,128)}, u32[]{:S(2)}) copy-start(f32[1,256,16]{1,2,0:T(8,128)} %param.5) | copy-start | bytes 49156
  13.9 76.2 %copy-start.18 = (f32[256]{0:T(256)S(1)}, f32[256]{0:T(256)}, u32[]{:S(2)}) copy-start(f32[256]{0:T(256)} %param.7) | copy-start | bytes 3076
  90.1 61.3 %copy-start.10 = (f32[1,129,256]{2,1,0:T(8,128)}, f32[1,129,256]{2,1,0:T(8,128)S(1)}, u32[]{:S(2)}) copy-start(f32[1,129,256]{2,1,0:T(8,128)S(1)} %maximum_bitcast_fusion) | copy-start | bytes 396292
  90.2 56.0 %collective-permute-start.1 = (f32[1,129,256]{2,1,0:T(8,128)S(1)}, f32[1,129,256]{2,1,0:T(8,128)S(1)}, u32[]{:S(2)}, u32[]{:S(2)}) collective-permute-start(f32[1,129,256]{2,1,0:T(8,128)S(1)} %maximum_bitcast_fusion), channel_id=1, source_target_pairs={{0,2},{1,3},{2,0},{3,1},{4,6},{5,7},{6,4},{7,5},{8,10},{9,11},{10,... | collective-permute-start | bytes 396296 | tf_op jit(solution)/shard_map/ppermute | solution.py:252
  146.2 5.3 %copy-start.11 = (f32[1,129,256]{2,1,0:T(8,128)}, f32[1,129,256]{2,1,0:T(8,128)S(1)}, u32[]{:S(2)}) copy-start(f32[1,129,256]{2,1,0:T(8,128)S(1)} %collective-permute-done.1) | copy-start | bytes 396292
  146.2 2.3 collective-permute-start.2
  146.3 14.3 %collective-permute-start.5 = (bf16[12,256,128]{2,1,0:T(8,128)(2,1)}, bf16[12,256,128]{2,1,0:T(8,128)(2,1)}, u32[]{:S(2)}, u32[]{:S(2)}) collective-permute-start(bf16[12,256,128]{2,1,0:T(8,128)(2,1)} %get-tuple-element.34), channel_id=1, source_target_pairs={{0,1},{1,0},{2,3},{3,2},{4,5},{5,4},{6,7},{7,6},{8,9},{9,8},{10,11... | collective-permute-start | bytes 2359304 | tf_op jit(solution)/shard_map/ppermute | solution.py:252
  146.8 20.7 %collective-permute-start.6 = (bf16[12,256,128]{2,1,0:T(8,128)(2,1)}, bf16[12,256,128]{2,1,0:T(8,128)(2,1)}, u32[]{:S(2)}, u32[]{:S(2)}) collective-permute-start(bf16[12,256,128]{2,1,0:T(8,128)(2,1)} %get-tuple-element.35), channel_id=1, source_target_pairs={{0,2},{1,3},{2,0},{3,1},{4,6},{5,7},{6,4},{7,5},{8,10},{9,11},{10,... | collective-permute-start | bytes 2359304 | tf_op jit(solution)/shard_map/ppermute | solution.py:252
  148.5 35.1 %collective-permute-start.7 = (bf16[12,256,128]{2,1,0:T(8,128)(2,1)}, bf16[12,256,128]{2,1,0:T(8,128)(2,1)}, u32[]{:S(2)}, u32[]{:S(2)}) collective-permute-start(bf16[12,256,128]{2,1,0:T(8,128)(2,1)} %get-tuple-element.36), channel_id=1, source_target_pairs={{0,3},{1,2},{2,1},{3,0},{4,7},{5,6},{6,5},{7,4},{8,11},{9,10},{10,... | collective-permute-start | bytes 2359304 | tf_op jit(solution)/shard_map/ppermute | solution.py:252
  150.7 9.0 %copy-start.16 = (bf16[4,256,128]{2,1,0:T(8,128)(2,1)S(1)}, bf16[4,256,128]{2,1,0:T(8,128)(2,1)}, u32[]{:S(2)}) copy-start(bf16[4,256,128]{2,1,0:T(8,128)(2,1)} %get-tuple-element.39) | copy-start | bytes 786436
  150.7 9.9 %copy-start.15 = (bf16[4,256,128]{2,1,0:T(8,128)(2,1)S(1)}, bf16[4,256,128]{2,1,0:T(8,128)(2,1)}, u32[]{:S(2)}) copy-start(bf16[4,256,128]{2,1,0:T(8,128)(2,1)} %get-tuple-element.37) | copy-start | bytes 786436
  150.7 9.9 %copy-start.14 = (bf16[4,256,128]{2,1,0:T(8,128)(2,1)S(1)}, bf16[4,256,128]{2,1,0:T(8,128)(2,1)}, u32[]{:S(2)}) copy-start(bf16[4,256,128]{2,1,0:T(8,128)(2,1)} %get-tuple-element.38) | copy-start | bytes 786436
  159.7 29.5 %collective-permute-start.10 = (bf16[4,256,128]{2,1,0:T(8,128)(2,1)S(1)}, bf16[4,256,128]{2,1,0:T(8,128)(2,1)S(1)}, u32[]{:S(2)}, u32[]{:S(2)}) collective-permute-start(bf16[4,256,128]{2,1,0:T(8,128)(2,1)S(1)} %copy-done.16), channel_id=1, source_target_pairs={{0,3},{1,2},{2,1},{3,0},{4,7},{5,6},{6,5},{7,4},{8,11},{9,10},{10,... | collective-permute-start | bytes 786440 | tf_op jit(solution)/shard_map/ppermute | solution.py:252
  160.6 28.6 %collective-permute-start.8 = (bf16[4,256,128]{2,1,0:T(8,128)(2,1)S(1)}, bf16[4,256,128]{2,1,0:T(8,128)(2,1)S(1)}, u32[]{:S(2)}, u32[]{:S(2)}) collective-permute-start(bf16[4,256,128]{2,1,0:T(8,128)(2,1)S(1)} %copy-done.15), channel_id=1, source_target_pairs={{0,1},{1,0},{2,3},{3,2},{4,5},{5,4},{6,7},{7,6},{8,9},{9,8},{10,11... | collective-permute-start | bytes 786440 | tf_op jit(solution)/shard_map/ppermute | solution.py:252
  160.6 34.0 %collective-permute-start.9 = (bf16[4,256,128]{2,1,0:T(8,128)(2,1)S(1)}, bf16[4,256,128]{2,1,0:T(8,128)(2,1)S(1)}, u32[]{:S(2)}, u32[]{:S(2)}) collective-permute-start(bf16[4,256,128]{2,1,0:T(8,128)(2,1)S(1)} %copy-done.14), channel_id=1, source_target_pairs={{0,2},{1,3},{2,0},{3,1},{4,6},{5,7},{6,4},{7,5},{8,10},{9,11},{10,... | collective-permute-start | bytes 786440 | tf_op jit(solution)/shard_map/ppermute | solution.py:252
  187.5 31.3 %copy-start.19 = (f32[128]{0:T(128)S(1)}, f32[128]{0:T(128)}, u32[]{:S(2)}) copy-start(f32[128]{0:T(128)} %param.6) | copy-start | bytes 1540
  189.1 8.0 %copy-start.1 = (bf16[4,256,128]{2,1,0:T(8,128)(2,1)}, bf16[4,256,128]{2,1,0:T(8,128)(2,1)S(1)}, u32[]{:S(2)}) copy-start(bf16[4,256,128]{2,1,0:T(8,128)(2,1)S(1)} %collective-permute-done.8.refs_3_.refs_11_) | copy-start | bytes 786436
  215.5 13.9 %all-to-all-start.2 = ((bf16[32,16,256]{2,1,0:T(8,128)(2,1)}), bf16[32,16,256]{2,1,0:T(8,128)(2,1)}, u32[]{:S(2)}, u32[]{:S(2)}) async-start(bf16[32,16,256]{2,1,0:T(8,128)(2,1)} %broadcast_in_dim.12), calls=%async_computation.2 | async-start | bytes 524288 | tf_op jit(solution)/shard_map/all_to_all | solution.py:232
  244.1 13.2 %all-to-all-start.3 = ((bf16[32,16,256]{2,1,0:T(8,128)(2,1)}), bf16[32,16,256]{2,1,0:T(8,128)(2,1)S(1)}, u32[]{:S(2)}, u32[]{:S(2)}) async-start(bf16[32,16,256]{2,1,0:T(8,128)(2,1)} %bitcast.20), calls=%async_computation.3 | async-start | bytes 524288 | tf_op jit(solution)/shard_map/all_to_all | solution.py:323
  257.5 9.4 %copy-start.6 = (f32[16,256]{1,0:T(8,128)}, f32[16,256]{1,0:T(8,128)S(1)}, u32[]{:S(2)}) copy-start(f32[16,256]{1,0:T(8,128)S(1)} %get-tuple-element.42.diff_ref) | copy-start | bytes 49156
  257.5 9.3 %copy-start.7 = (f32[16,256]{1,0:T(8,128)}, f32[16,256]{1,0:T(8,128)S(1)}, u32[]{:S(2)}) copy-start(f32[16,256]{1,0:T(8,128)S(1)} %get-tuple-element.43.scaled_ref) | copy-start | bytes 49156
  (9 other events, 8.9 us)

commit v7 on v6

--- a/solution.py
+++ b/solution.py
@@ -182,7 +182,7 @@
             pltpu.VMEM((len(blocks), nv, size, width, occ), jnp.bfloat16),
             pltpu.SemaphoreType.DMA((len(blocks), nv)),
         ],
-        compiler_params=pltpu.CompilerParams(vmem_limit_bytes=40 * 2**20),
+        compiler_params=pltpu.CompilerParams(vmem_limit_bytes=(58 if stepping else 24) * 2**20),
         cost_estimate=pl.CostEstimate(flops=0, bytes_accessed=0, transcendentals=0),
     )(order, *first, *([carry] if carried else []), *arrays)
 
@@ -225,6 +225,14 @@
             jax.ShapeDtypeStruct((1, 2), jnp.float32),
         ),
     )(diff, scaled, all_sums, before)
+
+
+def share_copies(terms):
+    def body(terms_ref, copies_ref):
+        coupling = jnp.sum(terms_ref[...].astype(jnp.float32), axis=0).astype(jnp.bfloat16)
+        copies_ref[...] = jnp.broadcast_to(coupling[None], copies_ref.shape)
+
+    return pl.pallas_call(body, out_shape=jax.ShapeDtypeStruct(terms.shape, jnp.bfloat16))(terms)
 
 
 def spread(share, count, axes=EVERY):
@@ -323,8 +331,8 @@
         return lax.all_to_all(partial.reshape(count, share, width), EVERY, 0, 0, tiled=True)
 
     (partial,) = call([xt], last_block, carry, na)
-    coupling = jnp.sum(sum_terms(partial).astype(jnp.float32), axis=0).astype(jnp.bfloat16)
-    first = [spread(coupling, count), trial, state[:, occ:], occ_energy[:, None]]
+    copies = share_copies(sum_terms(partial))
+    first = [lax.all_to_all(copies, EVERY, 0, 0, tiled=True), trial, state[:, occ:], occ_energy[:, None]]
     partial, trial_own, before = call(first, blocks, None, na)
     diff, scaled, sums = share_sums(sum_terms(partial), trial_own, gap_own)
     sums = lax.all_to_all(sums, EVERY, 0, 0, tiled=True)

time: 269 us -> 268 us (level)
  waiting for transfers between devices: 159 us -> 155 us
    ppermute x11, waiting for transfers between devices: 141 us -> 136 us  [send(): lax.ppermute(value, 'vir', [(one, partner(one, k)) for one in range(nv)])]
    unnamed x40 -> x48, local copies, waits for them, and re-layouts: 5.01 us -> 8.73 us
where the time goes in v7:
time: 268 us; the launch traced here: 267 us
  waiting for transfers between devices  155 us (58%)
  blocking collectives  39.4 us (15%)
  Pallas kernels  29 us (11%)
  local copies, waits for them, and re-layouts  26.8 us (10%)
  starting transfers between devices  15.3 us (6%)
    ppermute x11, waiting for transfers between devices, send(): lax.ppermute(value, 'vir', [(one, partner(one, k)) for one in range(nv)])  136 us
    pallas_call x4, Pallas kernels, contract(): pl.pallas_call(body, in_specs=[pl.BlockSpec(memory_space=pltpu.SMEM)] + [...  25.5 us
    all_to_all x1, blocking collectives, sum_terms(): lax.all_to_all(partial.reshape(count, share, width), EVERY, 0, 0, tiled=T...  16.6 us
    dynamic_slice x4, local copies, waits for them, and re-layouts, piece(): lax.dynamic_slice_in_dim(whole, partner(vir_at, k) * own + low, high - lo...  15.3 us
    all_to_all x1, blocking collectives, spread(): return lax.all_to_all(copies, axes, 0, 0, tiled=True)  13.5 us
    all_to_all x1, waiting for transfers between devices, sum_terms(): lax.all_to_all(partial.reshape(count, share, width), EVERY, 0, 0, tiled=T...  10.4 us
    ppermute x11, starting transfers between devices, send(): lax.ppermute(value, 'vir', [(one, partner(one, k)) for one in range(nv)])  10.1 us
    all_to_all x1, blocking collectives, local(): sums = lax.all_to_all(sums, EVERY, 0, 0, tiled=True)  9.35 us
  transfers between devices with their start and end apart: 13, of which 8 were waited for; matrix products, arithmetic and copies ran while one was open for 6% of the time, Pallas kernels for 4%

profile of v7, /device:TPU:0, one launch (start us, length us, event | category | flops | bytes accessed | tf_op | source)
XLA Modules:
  0.0 267.1 jit_solution(17989874897455895049)
XLA Ops:
  0.6 3.9 %constant_dynamic-slice_fusion.8 = bf16[48,256,128]{2,1,0:T(8,128)(2,1)} fusion(bf16[256,256,128]{2,1,0:T(8,128)(2,1)} %refs_4_.1, s32[]{:T(128)S(6)} %select_n.30), kind=kLoop, calls=%fused_computation.13 | loop fusion | bytes 6291460 | tf_op jit(solution)/shard_map/dynamic_slice | solution.py:270
  4.6 3.0 %collective-permute-start = (bf16[48,256,128]{2,1,0:T(8,128)(2,1)}, bf16[48,256,128]{2,1,0:T(8,128)(2,1)S(1)}, u32[]{:S(2)}, u32[]{:S(2)}) collective-permute-start(bf16[48,256,128]{2,1,0:T(8,128)(2,1)} %constant_dynamic-slice_fusion.8), channel_id=1, source_target_pairs={{0,2},{1,3},{2,0},{3,1},{4,6},{5,7},{6,4},{7,5},{8,10},{9,11},{10,... | collective-permute-start | bytes 9437192 | tf_op jit(solution)/shard_map/ppermute | solution.py:260
  7.5 6.2 %constant_dynamic-slice_fusion = (bf16[48,256,128]{2,1,0:T(8,128)(2,1)}, bf16[48,256,128]{2,1,0:T(8,128)(2,1)}) fusion(bf16[256,256,128]{2,1,0:T(8,128)(2,1)} %refs_4_.1, s32[]{:T(128)S(6)} %select_n.38, s32[]{:T(128)S(6)} %select_n.37), kind=kLoop, calls=%fused_computation.5 | loop fusion | bytes 12582920 | tf_op jit(solution)/shard_map/dynamic_slice | solution.py:270
  13.9 2.1 constant_dynamic-slice_fusion.2
  16.0 3.0 %constant_dynamic-slice_fusion.5 = (bf16[12,256,128]{2,1,0:T(8,128)(2,1)}, bf16[12,256,128]{2,1,0:T(8,128)(2,1)}, bf16[12,256,128]{2,1,0:T(8,128)(2,1)}) fusion(bf16[256,256,128]{2,1,0:T(8,128)(2,1)} %refs_4_.1, s32[]{:T(128)S(6)} %select_n.33, s32[]{:T(128)S(6)} %select_n.32, s32[]{:T(128)S(6)} %select_n.31), kind=kLoop, calls=%fused_computation.10 | loop fusion | bytes 4718604 | tf_op jit(solution)/shard_map/dynamic_slice | solution.py:270
  19.0 57.7 %collective-permute-done.refs_3_.refs_6_ = bf16[48,256,128]{2,1,0:T(8,128)(2,1)S(1)} collective-permute-done((bf16[48,256,128]{2,1,0:T(8,128)(2,1)}, bf16[48,256,128]{2,1,0:T(8,128)(2,1)S(1)}, u32[]{:S(2)}, u32[]{:S(2)}) %collective-permute-start) | collective-permute-done | bytes 3145760 | tf_op jit(solution)/shard_map/ppermute | solution.py:260
  76.7 13.5 %all_to_all.25 = f32[8,16,256]{2,1,0:T(8,128)S(1)} all-to-all(f32[8,16,256]{2,1,0:T(8,128)S(1)} %broadcast_in_dim.8), channel_id=1, replica_groups=mesh['aux'=8,'vir'=4] {'aux'}, dimensions={0} | all-to-all | bytes 262144 | tf_op jit(solution)/shard_map/all_to_all | solution.py:240
  91.8 54.5 %collective-permute-done.1 = f32[1,129,256]{2,1,0:T(8,128)S(1)} collective-permute-done((f32[1,129,256]{2,1,0:T(8,128)S(1)}, f32[1,129,256]{2,1,0:T(8,128)S(1)}, u32[]{:S(2)}, u32[]{:S(2)}) %collective-permute-start.1) | collective-permute-done | bytes 132128 | tf_op jit(solution)/shard_map/ppermute | solution.py:260
  146.9 1.7 collective-permute-start.6
  150.8 6.0 %copy-done = bf16[256,256,128]{2,1,0:T(8,128)(2,1)S(1)} copy-done((bf16[256,256,128]{2,1,0:T(8,128)(2,1)S(1)}, bf16[256,256,128]{2,1,0:T(8,128)(2,1)}, u32[]{:S(2)}) %copy-start) | copy-done | bytes 16777240
  156.8 7.9 %shard_map.59.refs_1_ = f32[1024,128]{1,0:T(8,128)S(1)} custom-call(s32[6]{0:T(128)S(1)} %stack.35.order_ref, bf16[4,128,256]{2,1,0:T(8,128)(2,1)S(1)} %slice.20.refs_0_, bf16[256,256,128]{2,1,0:T(8,128)(2,1)S(1)} %copy-done, bf16[48,256,128]{2,1,0:T(8,128)(2,1)} %collective-permute-done.3.refs_2_.refs_5_, ...), custom_call_target="tpu_custom_call" | custom-call | tf_op jit(solution)/shard_map/pallas_call | solution.py:172
  167.6 16.1 %collective-permute-done.7.refs_5_.refs_10_ = bf16[12,256,128]{2,1,0:T(8,128)(2,1)} collective-permute-done((bf16[12,256,128]{2,1,0:T(8,128)(2,1)}, bf16[12,256,128]{2,1,0:T(8,128)(2,1)}, u32[]{:S(2)}, u32[]{:S(2)}) %collective-permute-start.7) | collective-permute-done | bytes 786464 | tf_op jit(solution)/shard_map/ppermute | solution.py:260
  183.7 3.7 %shard_map.60.refs_1_ = f32[1024,128]{1,0:T(8,128)S(1)} custom-call(s32[6]{0:T(128)S(1)} %stack.35.order_ref, bf16[4,128,256]{2,1,0:T(8,128)(2,1)S(1)} %slice.20.refs_0_, f32[1024,128]{1,0:T(8,128)S(1)} %shard_map.59.refs_1_, bf16[256,256,128]{2,1,0:T(8,128)(2,1)S(1)} %copy-done, bf16[12,256,128]{2,1,0:T(8,128)(2,1)} %collective-permute-done.5.refs_3_.refs_8_, ...), custom_call_target="tpu_custom_call" | custom-call | tf_op jit(solution)/shard_map/pallas_call | solution.py:172
  187.4 1.8 collective-permute-done.10.refs_5_.refs_13_
  189.2 5.5 %collective-permute-done.9.refs_4_.refs_12_ = bf16[4,256,128]{2,1,0:T(8,128)(2,1)S(1)} collective-permute-done((bf16[4,256,128]{2,1,0:T(8,128)(2,1)S(1)}, bf16[4,256,128]{2,1,0:T(8,128)(2,1)S(1)}, u32[]{:S(2)}, u32[]{:S(2)}) %collective-permute-start.9) | collective-permute-done | bytes 262176 | tf_op jit(solution)/shard_map/ppermute | solution.py:260
  196.4 16.6 %all_to_all.26.terms_ref = bf16[32,16,256]{2,1,0:T(8,128)(2,1)} all-to-all(bf16[32,16,256]{2,1,0:T(8,128)(2,1)S(1)} %bitcast.19), channel_id=1, replica_groups=mesh['aux'=8,'vir'=4] {'aux','vir'}, dimensions={0} | all-to-all | bytes 524288 | tf_op jit(solution)/shard_map/all_to_all | solution.py:331
  213.0 1.7 shard_map.62
  214.7 2.6 all-to-all-start.2
  219.5 8.4 %all-to-all-done.2.refs_0_ = bf16[32,16,256]{2,1,0:T(8,128)(2,1)S(1)} async-done(((bf16[32,16,256]{2,1,0:T(8,128)(2,1)}), bf16[32,16,256]{2,1,0:T(8,128)(2,1)S(1)}, u32[]{:S(2)}, u32[]{:S(2)}) %all-to-all-start.2) | async-done | bytes 262176 | tf_op jit(solution)/shard_map/all_to_all | solution.py:335
  228.6 12.3 %shard_map.63 = (bf16[8,4,16,256]{3,2,1,0:T(8,128)(2,1)}, f32[16,256]{1,0:T(8,128)}, f32[1,128]{1,0:T(1,128)}) custom-call(s32[6]{0:T(128)} %copy-done.8, bf16[32,16,256]{2,1,0:T(8,128)(2,1)} %copy-done.17, f32[4,128,256]{2,1,0:T(8,128)} %slice.18.refs_1_, f32[4,1,256]{2,1,0:T(1,128)} %pad_maximum_fusion.2.refs_2_, f32[128,1]{1,0:T(8,128)} %copy.6.refs_3_, ...), custom_call_target="tpu_custom_call" | custom-call | tf_op jit(solution)/shard_map/pallas_call | solution.py:172
  240.8 2.6 all-to-all-start.3
  243.6 10.4 %all-to-all-done.3.terms_ref = bf16[32,16,256]{2,1,0:T(8,128)(2,1)S(1)} async-done(((bf16[32,16,256]{2,1,0:T(8,128)(2,1)}), bf16[32,16,256]{2,1,0:T(8,128)(2,1)S(1)}, u32[]{:S(2)}, u32[]{:S(2)}) %all-to-all-start.3) | async-done | bytes 262176 | tf_op jit(solution)/shard_map/all_to_all | solution.py:331
  256.1 9.3 %all_to_all.27.sums_ref = f32[32,1,128]{2,1,0:T(1,128)} all-to-all(f32[32,1,128]{2,1,0:T(1,128)S(1)} %get-tuple-element.44), channel_id=1, replica_groups=mesh['aux'=8,'vir'=4] {'aux','vir'}, dimensions={0} | all-to-all | bytes 32768 | tf_op jit(solution)/shard_map/all_to_all | solution.py:338
  265.5 1.7 shard_map.65
  (76 shorter events, 14.0 us)
Async XLA Ops:
  4.6 72.1 %collective-permute-start = (bf16[48,256,128]{2,1,0:T(8,128)(2,1)}, bf16[48,256,128]{2,1,0:T(8,128)(2,1)S(1)}, u32[]{:S(2)}, u32[]{:S(2)}) collective-permute-start(bf16[48,256,128]{2,1,0:T(8,128)(2,1)} %constant_dynamic-slice_fusion.8), channel_id=1, source_target_pairs={{0,2},{1,3},{2,0},{3,1},{4,6},{5,7},{6,4},{7,5},{8,10},{9,11},{10,... | collective-permute-start | bytes 9437192 | tf_op jit(solution)/shard_map/ppermute | solution.py:260
  13.8 137.0 %collective-permute-start.3 = (bf16[48,256,128]{2,1,0:T(8,128)(2,1)}, bf16[48,256,128]{2,1,0:T(8,128)(2,1)}, u32[]{:S(2)}, u32[]{:S(2)}) collective-permute-start(bf16[48,256,128]{2,1,0:T(8,128)(2,1)} %get-tuple-element.49), channel_id=1, source_target_pairs={{0,1},{1,0},{2,3},{3,2},{4,5},{5,4},{6,7},{7,6},{8,9},{9,8},{10,11... | collective-permute-start | bytes 9437192 | tf_op jit(solution)/shard_map/ppermute | solution.py:260
  13.8 137.0 %collective-permute-start.4 = (bf16[48,256,128]{2,1,0:T(8,128)(2,1)}, bf16[48,256,128]{2,1,0:T(8,128)(2,1)}, u32[]{:S(2)}, u32[]{:S(2)}) collective-permute-start(bf16[48,256,128]{2,1,0:T(8,128)(2,1)} %get-tuple-element.48), channel_id=1, source_target_pairs={{0,3},{1,2},{2,1},{3,0},{4,7},{5,6},{6,5},{7,4},{8,11},{9,10},{10,... | collective-permute-start | bytes 9437192 | tf_op jit(solution)/shard_map/ppermute | solution.py:260
  13.9 62.8 %copy-start.21 = (f32[1,256,16]{1,2,0:T(8,128)S(1)}, f32[1,256,16]{1,2,0:T(8,128)}, u32[]{:S(2)}) copy-start(f32[1,256,16]{1,2,0:T(8,128)} %param.5) | copy-start | bytes 49156
  13.9 76.3 %copy-start.22 = (f32[256]{0:T(256)S(1)}, f32[256]{0:T(256)}, u32[]{:S(2)}) copy-start(f32[256]{0:T(256)} %param.7) | copy-start | bytes 3076
  76.7 88.1 %copy-start.1 = (bf16[48,256,128]{2,1,0:T(8,128)(2,1)}, bf16[48,256,128]{2,1,0:T(8,128)(2,1)S(1)}, u32[]{:S(2)}) copy-start(bf16[48,256,128]{2,1,0:T(8,128)(2,1)S(1)} %collective-permute-done.refs_3_.refs_6_) | copy-start | bytes 9437188
  90.2 56.0 %collective-permute-start.1 = (f32[1,129,256]{2,1,0:T(8,128)S(1)}, f32[1,129,256]{2,1,0:T(8,128)S(1)}, u32[]{:S(2)}, u32[]{:S(2)}) collective-permute-start(f32[1,129,256]{2,1,0:T(8,128)S(1)} %maximum_bitcast_fusion), channel_id=1, source_target_pairs={{0,2},{1,3},{2,0},{3,1},{4,6},{5,7},{6,4},{7,5},{8,10},{9,11},{10,... | collective-permute-start | bytes 396296 | tf_op jit(solution)/shard_map/ppermute | solution.py:260
  146.3 2.3 collective-permute-start.2
  146.4 19.3 %collective-permute-start.5 = (bf16[12,256,128]{2,1,0:T(8,128)(2,1)}, bf16[12,256,128]{2,1,0:T(8,128)(2,1)}, u32[]{:S(2)}, u32[]{:S(2)}) collective-permute-start(bf16[12,256,128]{2,1,0:T(8,128)(2,1)} %get-tuple-element.34), channel_id=1, source_target_pairs={{0,1},{1,0},{2,3},{3,2},{4,5},{5,4},{6,7},{7,6},{8,9},{9,8},{10,11... | collective-permute-start | bytes 2359304 | tf_op jit(solution)/shard_map/ppermute | solution.py:260
  146.9 20.7 %collective-permute-start.6 = (bf16[12,256,128]{2,1,0:T(8,128)(2,1)}, bf16[12,256,128]{2,1,0:T(8,128)(2,1)}, u32[]{:S(2)}, u32[]{:S(2)}) collective-permute-start(bf16[12,256,128]{2,1,0:T(8,128)(2,1)} %get-tuple-element.35), channel_id=1, source_target_pairs={{0,2},{1,3},{2,0},{3,1},{4,6},{5,7},{6,4},{7,5},{8,10},{9,11},{10,... | collective-permute-start | bytes 2359304 | tf_op jit(solution)/shard_map/ppermute | solution.py:260
  148.6 35.1 %collective-permute-start.7 = (bf16[12,256,128]{2,1,0:T(8,128)(2,1)}, bf16[12,256,128]{2,1,0:T(8,128)(2,1)}, u32[]{:S(2)}, u32[]{:S(2)}) collective-permute-start(bf16[12,256,128]{2,1,0:T(8,128)(2,1)} %get-tuple-element.36), channel_id=1, source_target_pairs={{0,3},{1,2},{2,1},{3,0},{4,7},{5,6},{6,5},{7,4},{8,11},{9,10},{10,... | collective-permute-start | bytes 2359304 | tf_op jit(solution)/shard_map/ppermute | solution.py:260
  149.6 45.1 %copy-start.8 = (s32[6]{0:T(128)}, s32[6]{0:T(128)S(1)}, u32[]{:S(2)}) copy-start(s32[6]{0:T(128)S(1)} %stack.35.order_ref) | copy-start | bytes 76
  150.7 15.0 %copy-start.19 = (bf16[4,256,128]{2,1,0:T(8,128)(2,1)S(1)}, bf16[4,256,128]{2,1,0:T(8,128)(2,1)}, u32[]{:S(2)}) copy-start(bf16[4,256,128]{2,1,0:T(8,128)(2,1)} %get-tuple-element.37) | copy-start | bytes 786436
  150.7 15.0 %copy-start.18 = (bf16[4,256,128]{2,1,0:T(8,128)(2,1)S(1)}, bf16[4,256,128]{2,1,0:T(8,128)(2,1)}, u32[]{:S(2)}) copy-start(bf16[4,256,128]{2,1,0:T(8,128)(2,1)} %get-tuple-element.38) | copy-start | bytes 786436
  164.8 24.4 %collective-permute-start.10 = (bf16[4,256,128]{2,1,0:T(8,128)(2,1)S(1)}, bf16[4,256,128]{2,1,0:T(8,128)(2,1)S(1)}, u32[]{:S(2)}, u32[]{:S(2)}) collective-permute-start(bf16[4,256,128]{2,1,0:T(8,128)(2,1)S(1)} %copy-done.20), channel_id=1, source_target_pairs={{0,3},{1,2},{2,1},{3,0},{4,7},{5,6},{6,5},{7,4},{8,11},{9,10},{10,... | collective-permute-start | bytes 786440 | tf_op jit(solution)/shard_map/ppermute | solution.py:260
  165.7 23.5 %collective-permute-start.8 = (bf16[4,256,128]{2,1,0:T(8,128)(2,1)S(1)}, bf16[4,256,128]{2,1,0:T(8,128)(2,1)S(1)}, u32[]{:S(2)}, u32[]{:S(2)}) collective-permute-start(bf16[4,256,128]{2,1,0:T(8,128)(2,1)S(1)} %copy-done.19), channel_id=1, source_target_pairs={{0,1},{1,0},{2,3},{3,2},{4,5},{5,4},{6,7},{7,6},{8,9},{9,8},{10,11... | collective-permute-start | bytes 786440 | tf_op jit(solution)/shard_map/ppermute | solution.py:260
  165.7 29.0 %collective-permute-start.9 = (bf16[4,256,128]{2,1,0:T(8,128)(2,1)S(1)}, bf16[4,256,128]{2,1,0:T(8,128)(2,1)S(1)}, u32[]{:S(2)}, u32[]{:S(2)}) collective-permute-start(bf16[4,256,128]{2,1,0:T(8,128)(2,1)S(1)} %copy-done.18), channel_id=1, source_target_pairs={{0,2},{1,3},{2,0},{3,1},{4,6},{5,7},{6,4},{7,5},{8,10},{9,11},{10,... | collective-permute-start | bytes 786440 | tf_op jit(solution)/shard_map/ppermute | solution.py:260
  187.4 29.9 %copy-start.23 = (f32[128]{0:T(128)S(1)}, f32[128]{0:T(128)}, u32[]{:S(2)}) copy-start(f32[128]{0:T(128)} %param.6) | copy-start | bytes 1540
  187.4 30.6 %copy-start.10 = (f32[4,129,256]{2,1,0:T(8,128)S(1)}, f32[4,129,256]{2,1,0:T(8,128)}, u32[]{:S(2)}) copy-start(f32[4,129,256]{2,1,0:T(8,128)} %copy-done.9) | copy-start | bytes 1585156
  187.4 31.5 %copy-start.12 = (f32[1,129,256]{2,1,0:T(8,128)S(1)}, f32[1,129,256]{2,1,0:T(8,128)}, u32[]{:S(2)}) copy-start(f32[1,129,256]{2,1,0:T(8,128)} %copy-done.11) | copy-start | bytes 396292
  187.4 31.4 %copy-start.14 = (f32[1,129,256]{2,1,0:T(8,128)S(1)}, f32[1,129,256]{2,1,0:T(8,128)}, u32[]{:S(2)}) copy-start(f32[1,129,256]{2,1,0:T(8,128)} %copy-done.13) | copy-start | bytes 396292
  187.4 31.4 %copy-start.16 = (f32[1,129,256]{2,1,0:T(8,128)S(1)}, f32[1,129,256]{2,1,0:T(8,128)}, u32[]{:S(2)}) copy-start(f32[1,129,256]{2,1,0:T(8,128)} %copy-done.15) | copy-start | bytes 396292
  214.7 13.2 %all-to-all-start.2 = ((bf16[32,16,256]{2,1,0:T(8,128)(2,1)}), bf16[32,16,256]{2,1,0:T(8,128)(2,1)S(1)}, u32[]{:S(2)}, u32[]{:S(2)}) async-start(bf16[32,16,256]{2,1,0:T(8,128)(2,1)} %shard_map.62), calls=%async_computation.2 | async-start | bytes 524288 | tf_op jit(solution)/shard_map/all_to_all | solution.py:335
  240.8 13.2 %all-to-all-start.3 = ((bf16[32,16,256]{2,1,0:T(8,128)(2,1)}), bf16[32,16,256]{2,1,0:T(8,128)(2,1)S(1)}, u32[]{:S(2)}, u32[]{:S(2)}) async-start(bf16[32,16,256]{2,1,0:T(8,128)(2,1)} %bitcast.21), calls=%async_computation.3 | async-start | bytes 524288 | tf_op jit(solution)/shard_map/all_to_all | solution.py:331
  (13 other events, 79.5 us)

commit v8 on v7

--- a/solution.py
+++ b/solution.py
@@ -50,6 +50,22 @@
     shift = cross_sum / self_sum
     mean_square = (diff_sum + 2.0 * shift * mixed_sum + shift * shift * scaled_sum) / count
     return (scaled_diff + shift * scaled_trial) * lax.rsqrt(mean_square + 1e-06), shift
+
+
+def diagonal(occ):
+    rows = lax.broadcasted_iota(jnp.int32, (occ, occ), 0)
+    return rows == lax.broadcasted_iota(jnp.int32, (occ, occ), 1)
+
+
+def coulomb_and_exchange(pair, eye):
+    density = jnp.sum(jnp.where(eye, pair, 0.0), keepdims=True)
+    density = density.astype(jnp.bfloat16).astype(jnp.float32)
+    pair = pair.astype(jnp.bfloat16).astype(jnp.float32)
+    return (jnp.where(eye, 2.0 * density, 0.0) - pair).astype(jnp.bfloat16)
+
+
+def side_by_side(blocks, count):
+    return jnp.concatenate([blocks[q] for q in range(count)], axis=1)
 
 
 def contract_body(nv, blocks, size, own, carried, stepping, total, order_ref, *refs):
@@ -79,7 +95,7 @@
     acc_ref[...] = carry_ref[...] if carried else jnp.zeros_like(acc_ref)
     if stepping:
         shares_ref, trial_ref, vir_ref, occ_ref = first_refs
-        own_ref, shift_ref = out_refs[1:]
+        own_ref, shift_ref, next_ref = out_refs[1:]
         share = own_ref.shape[0]
         coupling = jnp.concatenate(
             [
@@ -96,6 +112,7 @@
         for k in range(nv):
             rows = fresh[k * occ : (k + 1) * occ]
             xt_ref[:, k * width : (k + 1) * width] = rows.astype(jnp.bfloat16)
+            next_ref[k] = rows.astype(jnp.bfloat16)
         mine = fresh[:share]
         for r in range(1, occ // share):
             rows = fresh[r * share : (r + 1) * share]
@@ -104,9 +121,7 @@
     else:
         for k in range(nv):
             xt_ref[:, k * width : (k + 1) * width] = first_refs[0][k]
-    eye = lax.broadcasted_iota(jnp.int32, (occ, occ), 0) == lax.broadcasted_iota(
-        jnp.int32, (occ, occ), 1
-    )
+    eye = diagonal(occ)
 
     def work(at, _):
         for k in range(nv):
@@ -119,14 +134,10 @@
             axis=0,
         )
         pairs = jnp.dot(xt_ref[...], tall, preferred_element_type=jnp.float32)
-        mixes = []
-        for q in range(size):
-            pair = pairs[:, q * occ : (q + 1) * occ]
-            density = jnp.sum(jnp.where(eye, pair, 0.0), keepdims=True)
-            density = density.astype(jnp.bfloat16).astype(jnp.float32)
-            pair = pair.astype(jnp.bfloat16).astype(jnp.float32)
-            mixes.append((jnp.where(eye, 2.0 * density, 0.0) - pair).astype(jnp.bfloat16))
-        mix = jnp.concatenate(mixes, axis=0)
+        mix = jnp.concatenate(
+            [coulomb_and_exchange(pairs[:, q * occ : (q + 1) * occ], eye) for q in range(size)],
+            axis=0,
+        )
         acc_ref[...] += jnp.dot(tall, mix, preferred_element_type=jnp.float32)
         return _
 
@@ -141,7 +152,7 @@
             out_ref[r, order_ref[k]] = turned[r * share : (r + 1) * share, :].astype(out_ref.dtype)
 
 
-def contract(order, first, factors, sources, blocks, own, carry=None, aux_count=None):
+def contract(order, first, factors, sources, blocks, own, share, carry=None, aux_count=None):
     p_count, width, occ = factors.shape
     nv = p_count // own
     carried, stepping = carry is not None, len(first) > 1
@@ -163,8 +174,9 @@
     else:
         out = [jax.ShapeDtypeStruct((aux_count, nv, occ // aux_count, width), jnp.bfloat16)]
     if stepping:
-        out.append(jax.ShapeDtypeStruct((occ // aux_count, width), jnp.float32))
+        out.append(jax.ShapeDtypeStruct((share, width), jnp.float32))
         out.append(jax.ShapeDtypeStruct((1, 128), jnp.float32))
+        out.append(jax.ShapeDtypeStruct((nv, occ, width), jnp.bfloat16))
     in_vmem, in_hbm = pl.BlockSpec(memory_space=pltpu.VMEM), pl.BlockSpec(memory_space=pltpu.HBM)
     body = functools.partial(
         contract_body, nv, placed, size, own, carried, stepping, nv * width * occ
@@ -183,8 +195,85 @@
             pltpu.SemaphoreType.DMA((len(blocks), nv)),
         ],
         compiler_params=pltpu.CompilerParams(vmem_limit_bytes=(58 if stepping else 24) * 2**20),
+        cost_estimate=pl.CostEstimate(
+            flops=4 * own * nv * width * occ * occ * stepping,
+            bytes_accessed=2 * own * nv * width * occ * stepping,
+            transcendentals=0,
+        ),
+    )(order, *first, *([carry] if carried else []), *arrays)
+
+
+def partial_pairs(factors, xt_own, own, kept, unit):
+    p_count, width, occ = factors.shape
+    nv, per = p_count // own, kept // unit
+
+    def body(xt_ref, f_ref, out_ref):
+        wide = side_by_side(f_ref, unit)
+        pairs = jnp.dot(xt_ref[...], wide, preferred_element_type=jnp.float32)
+        for q in range(unit):
+            out_ref[q] = pairs[:, q * occ : (q + 1) * occ].astype(jnp.bfloat16)
+
+    return pl.pallas_call(
+        body,
+        grid=(nv, per),
+        in_specs=[
+            pl.BlockSpec((occ, width), lambda b, t: (0, 0)),
+            pl.BlockSpec((unit, width, occ), lambda b, t: (b * (own // unit) + (own - kept) // unit + t, 0, 0)),
+        ],
+        out_specs=pl.BlockSpec((unit, occ, occ), lambda b, t: (b * per + t, 0, 0)),
+        out_shape=jax.ShapeDtypeStruct((nv * kept, occ, occ), jnp.bfloat16),
         cost_estimate=pl.CostEstimate(flops=0, bytes_accessed=0, transcendentals=0),
-    )(order, *first, *([carry] if carried else []), *arrays)
+    )(xt_own, factors)
+
+
+def contract_pairs(order, factors, mine, other, carry, own, kept, unit):
+    p_count, width, occ = factors.shape
+    nv, per = p_count // own, kept // unit
+    half = nv * per // 2
+
+    def body(order_ref, mine_ref, other_ref, f_ref, carry_ref, out_ref):
+        step = pl.program_id(0)
+
+        @pl.when(step == 0)
+        def _():
+            out_ref[...] = carry_ref[...]
+
+        eye = diagonal(occ)
+        is_mine = step < half
+        mix = jnp.concatenate(
+            [
+                coulomb_and_exchange(
+                    jnp.where(is_mine, mine_ref[q].astype(jnp.float32), other_ref[q].astype(jnp.float32)), eye
+                )
+                for q in range(unit)
+            ],
+            axis=0,
+        )
+        wide = side_by_side(f_ref, unit)
+        out_ref[0:width, :] += jnp.dot(wide, mix, preferred_element_type=jnp.float32)
+
+    def place(g, order):
+        core = order[nv + 2]
+        at = jnp.where(g < half, core * half + g, (1 - core) * half + g - half)
+        return (lax.div(at, per) * (own // unit) + (own - kept) // unit + lax.rem(at, per), 0, 0)
+
+    whole = pl.BlockSpec((nv * width, occ), lambda g, order: (0, 0))
+    return pl.pallas_call(
+        body,
+        grid_spec=pltpu.PrefetchScalarGridSpec(
+            num_scalar_prefetch=1,
+            grid=(2 * half,),
+            in_specs=[
+                pl.BlockSpec((unit, occ, occ), lambda g, order: (jnp.minimum(g, half - 1), 0, 0)),
+                pl.BlockSpec((unit, occ, occ), lambda g, order: (jnp.maximum(g - half, 0), 0, 0)),
+                pl.BlockSpec((unit, width, occ), place),
+                whole,
+            ],
+            out_specs=whole,
+        ),
+        out_shape=jax.ShapeDtypeStruct((nv * width, occ), jnp.float32),
+        cost_estimate=pl.CostEstimate(flops=0, bytes_accessed=0, transcendentals=0),
+    )(order, mine, other, factors, carry)
 
 
 def share_sums(terms, trial, gap):
@@ -259,11 +348,11 @@
     def send(value, k):
         return lax.ppermute(value, "vir", [(one, partner(one, k)) for one in range(nv)])
 
-    order = [source(vir_at, k) for k in range(nv)] + [vir_at, aux_at]
+    order = [source(vir_at, k) for k in range(nv)] + [vir_at, aux_at, vir_at & 1]
     order = jnp.stack(order).astype(jnp.int32)
 
     unit = own // 16
-    cut_up = unit >= 4 and own % 16 == 0
+    cut_up = paired and nv >= 4 and unit >= 4 and own % 16 == 0
     sources = {k: [] for k in range(1, nv)}
 
     def piece(k, low, high, whole=factors):
@@ -278,19 +367,21 @@
         sources[k][-1] = (low, high, array)
         return values
 
-    marks = [0, own]
+    low, high, end = 11 * unit, 13 * unit, 14 * unit
+    far = [k for k in range(nv) if k > 1] + [1]
+    starts = {k: high if cut_up else own for k in far}
     if cut_up:
-        marks = [0, 12 * unit, 15 * unit, own]
-    far = [k for k in range(nv) if k > 1] + [1]
+        starts[2] = low
     later_factors = factors
     for n, k in enumerate(far):
-        cut = piece(k, *marks[:2], later_factors)
+        cut = piece(k, 0, starts[k], later_factors)
         if cut_up and n == 0:
             later_factors, cut = lax.optimization_barrier((factors, cut))
-        exchange(k, *marks[:2], cut)
+        exchange(k, 0, starts[k], cut)
     if cut_up:
-        later = [[piece(k, low, high, later_factors) for k in far] for low, high in zip(marks[1:], marks[2:])]
-        later, trials = lax.optimization_barrier((later, *after_newest(2, trials)))
+        middle = piece(2, low, high, later_factors)
+        ending = [piece(k, high, end, later_factors) for k in far]
+        middle, ending, trials = lax.optimization_barrier((middle, ending, *after_newest(2, trials)))
 
     gathered = spread(trials[0].T, na, "aux").reshape(occ, width)
     gathered = jnp.concatenate([gathered, vir_energy[None]], axis=0)
@@ -300,6 +391,9 @@
         while bit:
             names = sorted(state)
             came = send(jnp.stack([state[k] for k in names]), bit)
+            if cut_up and bit == 2:
+                middle, came = lax.optimization_barrier((middle, came))
+                exchange(2, low, high, middle)
             state.update({k ^ bit: came[at] for at, k in enumerate(names)})
             bit //= 2
     else:
@@ -310,30 +404,52 @@
     xt = trial.astype(jnp.bfloat16)
 
     def call(first, blocks, carry=None, aux_count=None):
-        return contract(order, first, factors, sources, blocks, own, carry, aux_count)
+        return contract(order, first, factors, sources, blocks, own, share, carry, aux_count)
 
     carry = None
     blocks = last_block = [[(0, own)]]
     if cut_up:
-        low, high, end = marks[1:]
-        for k, cut in enumerate(later[0]):
-            exchange(far[k], low, high, cut)
-        blocks = [[(n * 4 * unit, (n + 1) * 4 * unit)] for n in range(3)]
-        last_block = [[(high, end)]]
-        (carry,) = call([xt], blocks)
-        cuts, carry = lax.optimization_barrier((later[1], carry))
+        kept = own - end
+        half, core = nv * kept // 2, vir_at & 1
+        sums = partial_pairs(factors, xt[0], own, kept, kept)
+        mine = lax.dynamic_slice_in_dim(sums, core * half, half, 0)
+        other = lax.dynamic_slice_in_dim(sums, (1 - core) * half, half, 0)
+
+        def add(one, two):
+            return (one.astype(jnp.float32) + two.astype(jnp.float32)).astype(jnp.bfloat16)
+
+        (carry,) = call([xt], [[(n * low // 4, (n + 1) * low // 4)] for n in range(4)])
+        other, carry = after_newest(2, other, carry)
+        mine = add(mine, send(other, 1))
+        cuts, mine = lax.optimization_barrier((ending, mine))
+        bit = 2
+        while bit < nv:
+            mine = add(mine, send(mine, bit))
+            bit *= 2
         for k, cut in zip(far, cuts):
             exchange(k, high, end, cut)
         (carry,) = call([xt], [[(low, high)]], carry)
-        blocks.append([(low, high), (high, end)])
+        carry = contract_pairs(order, factors, mine, send(mine, 1), carry, own, kept, kept)
+        last_block = [[(high, end)]]
+        size = end // 4
+        blocks = [[(n * size, (n + 1) * size)] for n in range(3)]
+        blocks.append([(3 * size, low), (low, high), (high, end)])
 
     def sum_terms(partial):
         return lax.all_to_all(partial.reshape(count, share, width), EVERY, 0, 0, tiled=True)
 
     (partial,) = call([xt], last_block, carry, na)
     copies = share_copies(sum_terms(partial))
+    if cut_up:
+        whole, copies = lax.optimization_barrier((factors, copies))
+        for k in far:
+            exchange(k, end, own, piece(k, end, own, whole))
     first = [lax.all_to_all(copies, EVERY, 0, 0, tiled=True), trial, state[:, occ:], occ_energy[:, None]]
-    partial, trial_own, before = call(first, blocks, None, na)
+    if cut_up:
+        carry, trial_own, before, xt = call(first, blocks)
+        (partial,) = call([xt], [[(end, own)]], carry, na)
+    else:
+        partial, trial_own, before, xt = call(first, blocks, None, na)
     diff, scaled, sums = share_sums(sum_terms(partial), trial_own, gap_own)
     sums = lax.all_to_all(sums, EVERY, 0, 0, tiled=True)
     fresh, shifts = step_share(diff, scaled, sums, before, total)

time: 268 us -> 312 us (1.16)
  local copies, waits for them, and re-layouts: 26.8 us -> 56.8 us
  Pallas kernels: 29 us -> 41.9 us
  waiting for transfers between devices: 155 us -> 149 us
  starting transfers between devices: 15.3 us -> 19.8 us
    unnamed x48 -> x70, local copies, waits for them, and re-layouts: 8.73 us -> 35.8 us
    pallas_call x0 -> x2, Pallas kernels: none -> 9.68 us  [the longest x1 5.68 us: contract_pairs(): pl.pallas_call(body, grid_spec=pltpu.PrefetchScalarGridSpec(num_scalar_pr...]
    all_to_all x1, waiting for transfers between devices: 8.4 us -> 4.11 us  [local(): lax.all_to_all(copies, EVERY, 0, 0, tiled=True)]
    pallas_call x4 -> x5, Pallas kernels: 25.5 us -> 28.7 us  [contract(): pl.pallas_call(body, in_specs=[pl.BlockSpec(memory_space=pltpu.SMEM)] + [...]
    ppermute x11 -> x15, starting transfers between devices: 10.1 us -> 12.6 us  [send(): lax.ppermute(value, 'vir', [(one, partner(one, k)) for one in range(nv)])]
    ppermute x11 -> x15, waiting for transfers between devices: 136 us -> 134 us  [send(): lax.ppermute(value, 'vir', [(one, partner(one, k)) for one in range(nv)])]
    dynamic_slice x4 -> x5, local copies, waits for them, and re-layouts: 15.3 us -> 16.8 us  [piece(): lax.dynamic_slice_in_dim(whole, partner(vir_at, k) * own + low, high - lo...]
  transfers between devices with their start and end apart: 13 -> 17, of which waited for: 8 -> 7; matrix products, arithmetic and copies ran while one was open for 6% -> 6% of each run, Pallas kernels for 4% -> 11%
where the time goes in v8:
time: 312 us; the launch traced here: 311 us
  waiting for transfers between devices  149 us (48%)
  local copies, waits for them, and re-layouts  56.8 us (18%)
  Pallas kernels  41.9 us (13%)
  blocking collectives  39.4 us (13%)
  starting transfers between devices  19.8 us (6%)
  other arithmetic  3.84 us (1%)
    ppermute x15, waiting for transfers between devices, send(): lax.ppermute(value, 'vir', [(one, partner(one, k)) for one in range(nv)])  134 us
    unnamed x70, local copies, waits for them, and re-layouts  35.8 us
    pallas_call x5, Pallas kernels, contract(): pl.pallas_call(body, in_specs=[pl.BlockSpec(memory_space=pltpu.SMEM)] + [...  28.7 us
    dynamic_slice x5, local copies, waits for them, and re-layouts, piece(): lax.dynamic_slice_in_dim(whole, partner(vir_at, k) * own + low, high - lo...  16.8 us
    all_to_all x1, blocking collectives, sum_terms(): lax.all_to_all(partial.reshape(count, share, width), EVERY, 0, 0, tiled=T...  16.5 us
    all_to_all x1, blocking collectives, spread(): return lax.all_to_all(copies, axes, 0, 0, tiled=True)  13.5 us
    ppermute x15, starting transfers between devices, send(): lax.ppermute(value, 'vir', [(one, partner(one, k)) for one in range(nv)])  12.6 us
    all_to_all x1, waiting for transfers between devices, sum_terms(): lax.all_to_all(partial.reshape(count, share, width), EVERY, 0, 0, tiled=T...  10.4 us
  transfers between devices with their start and end apart: 17, of which 7 were waited for; matrix products, arithmetic and copies ran while one was open for 6% of the time, Pallas kernels for 11%

profile of v8, /device:TPU:0, one launch (start us, length us, event | category | flops | bytes accessed | tf_op | source)
XLA Modules:
  0.0 311.3 jit_solution(15597392965494694498)
XLA Ops:
  0.6 3.7 %constant_dynamic-slice_fusion.10 = bf16[44,256,128]{2,1,0:T(8,128)(2,1)} fusion(bf16[256,256,128]{2,1,0:T(8,128)(2,1)} %refs_2_.5, s32[]{:T(128)S(6)} %select_n.39), kind=kLoop, calls=%fused_computation.18 | loop fusion | bytes 5767172 | tf_op jit(solution)/shard_map/dynamic_slice | solution.py:359
  4.3 3.0 collective-permute-start
  7.3 6.8 %constant_dynamic-slice_fusion.3 = (bf16[52,256,128]{2,1,0:T(8,128)(2,1)}, bf16[52,256,128]{2,1,0:T(8,128)(2,1)}) fusion(bf16[256,256,128]{2,1,0:T(8,128)(2,1)} %refs_2_.5, s32[]{:T(128)S(6)} %select_n.47, s32[]{:T(128)S(6)} %select_n.46), kind=kLoop, calls=%fused_computation.11 | loop fusion | bytes 13631496 | tf_op jit(solution)/shard_map/dynamic_slice | solution.py:359
  18.1 52.8 %collective-permute-done.refs_3_.refs_6_ = bf16[44,256,128]{2,1,0:T(8,128)(2,1)} collective-permute-done((bf16[44,256,128]{2,1,0:T(8,128)(2,1)}, bf16[44,256,128]{2,1,0:T(8,128)(2,1)}, u32[]{:S(2)}, u32[]{:S(2)}) %collective-permute-start) | collective-permute-done | bytes 2883616 | tf_op jit(solution)/shard_map/ppermute | solution.py:349
  70.9 13.5 %all_to_all.25 = f32[8,16,256]{2,1,0:T(8,128)S(1)} all-to-all(f32[8,16,256]{2,1,0:T(8,128)S(1)} %broadcast_in_dim.8), channel_id=1, replica_groups=mesh['aux'=8,'vir'=4] {'aux'}, dimensions={0} | all-to-all | bytes 262144 | tf_op jit(solution)/shard_map/all_to_all | solution.py:329
  86.0 60.0 %collective-permute-done.1 = f32[1,129,256]{2,1,0:T(8,128)S(1)} collective-permute-done((f32[1,129,256]{2,1,0:T(8,128)S(1)}, f32[1,129,256]{2,1,0:T(8,128)S(1)}, u32[]{:S(2)}, u32[]{:S(2)}) %collective-permute-start.1) | collective-permute-done | bytes 132128 | tf_op jit(solution)/shard_map/ppermute | solution.py:349
  154.1 4.0 %shard_map.59 = bf16[32,128,128]{2,1,0:T(8,128)(2,1)} custom-call(bf16[128,256]{1,0:T(8,128)(2,1)} %slice_bitcast_fusion.xt_ref, bf16[256,256,128]{2,1,0:T(8,128)(2,1)} %refs_2_.5), custom_call_target="tpu_custom_call" | custom-call | tf_op jit(solution)/shard_map/pallas_call | solution.py:216
  158.1 7.0 %copy-done = bf16[256,256,128]{2,1,0:T(8,128)(2,1)S(1)} copy-done((bf16[256,256,128]{2,1,0:T(8,128)(2,1)S(1)}, bf16[256,256,128]{2,1,0:T(8,128)(2,1)}, u32[]{:S(2)}) %copy-start) | copy-done | bytes 16777240
  166.1 9.1 %shard_map.60.refs_1_ = f32[1024,128]{1,0:T(8,128)S(1)} custom-call(s32[7]{0:T(128)S(1)} %stack.39.order_ref, bf16[4,128,256]{2,1,0:T(8,128)(2,1)S(1)} %copy-done.6, bf16[256,256,128]{2,1,0:T(8,128)(2,1)S(1)} %copy-done, bf16[52,256,128]{2,1,0:T(8,128)(2,1)S(1)} %collective-permute-done.3.refs_2_.refs_3_.refs_5_, ...), custom_call_target="tpu_custom_call" | custom-call | tf_op jit(solution)/shard_map/pallas_call | solution.py:184
  182.3 12.3 %collective-permute-done.7 = bf16[16,128,128]{2,1,0:T(8,128)(2,1)S(1)} collective-permute-done((bf16[16,128,128]{2,1,0:T(8,128)(2,1)S(1)}, bf16[16,128,128]{2,1,0:T(8,128)(2,1)S(1)}, u32[]{:S(2)}, u32[]{:S(2)}) %collective-permute-start.7) | collective-permute-done | bytes 524320 | tf_op jit(solution)/shard_map/ppermute | solution.py:349
  197.0 5.8 %copy-done.1 = bf16[256,256,128]{2,1,0:T(8,128)(2,1)S(1)} copy-done((bf16[256,256,128]{2,1,0:T(8,128)(2,1)S(1)}, bf16[256,256,128]{2,1,0:T(8,128)(2,1)}, u32[]{:S(2)}) %copy-start.1) | copy-done | bytes 16777240
  203.7 3.0 shard_map.61.carry_ref
  207.6 5.7 %shard_map.62.refs_1_ = f32[1024,128]{1,0:T(8,128)} custom-call(s32[7]{0:T(128)} %copy-done.15, bf16[16,128,128]{2,1,0:T(8,128)(2,1)} %copy-done.24, bf16[16,128,128]{2,1,0:T(8,128)(2,1)} %collective-permute-done.8.other_ref, bf16[256,256,128]{2,1,0:T(8,128)(2,1)} %refs_2_.5, f32[1024,128]{1,0:T(8,128)} %copy-done.12), custom_call_target="tpu_custom_call" | custom-call | tf_op jit(solution)/shard_map/pallas_call | solution.py:261
  213.3 5.8 %copy-done.2 = bf16[256,256,128]{2,1,0:T(8,128)(2,1)S(1)} copy-done((bf16[256,256,128]{2,1,0:T(8,128)(2,1)S(1)}, bf16[256,256,128]{2,1,0:T(8,128)(2,1)}, u32[]{:S(2)}) %copy-start.2) | copy-done | bytes 16777240
  220.1 2.6 shard_map.63
  222.8 16.5 %all_to_all.26.terms_ref = bf16[32,16,256]{2,1,0:T(8,128)(2,1)} all-to-all(bf16[32,16,256]{2,1,0:T(8,128)(2,1)S(1)} %bitcast.22), channel_id=1, replica_groups=mesh['aux'=8,'vir'=4] {'aux','vir'}, dimensions={0} | all-to-all | bytes 524288 | tf_op jit(solution)/shard_map/all_to_all | solution.py:439
  250.3 4.1 %all-to-all-done.2.refs_0_ = bf16[32,16,256]{2,1,0:T(8,128)(2,1)S(1)} async-done(((bf16[32,16,256]{2,1,0:T(8,128)(2,1)}), bf16[32,16,256]{2,1,0:T(8,128)(2,1)S(1)}, u32[]{:S(2)}, u32[]{:S(2)}) %all-to-all-start.2) | async-done | bytes 262176 | tf_op jit(solution)/shard_map/all_to_all | solution.py:447
  255.1 11.2 %shard_map.65 = (f32[1024,128]{1,0:T(8,128)}, f32[16,256]{1,0:T(8,128)}, f32[1,128]{1,0:T(1,128)}, bf16[4,128,256]{2,1,0:T(8,128)(2,1)}) custom-call(s32[7]{0:T(128)} %copy-done.15, bf16[32,16,256]{2,1,0:T(8,128)(2,1)} %copy-done.31, f32[4,128,256]{2,1,0:T(8,128)} %slice.22.refs_1_, f32[4,1,256]{2,1,0:T(1,128)} %pad_maximum_fusion.2.refs_2_, ...), custom_call_target="tpu_custom_call" | custom-call | flops 4294967296 | bytes 16777216 | tf_op jit(solution)/shard_map/pallas_call | solution.py:184
  266.4 6.8 %collective-permute-done.14.refs_5_ = bf16[8,256,128]{2,1,0:T(8,128)(2,1)S(1)} collective-permute-done((bf16[8,256,128]{2,1,0:T(8,128)(2,1)S(1)}, bf16[8,256,128]{2,1,0:T(8,128)(2,1)S(1)}, u32[]{:S(2)}, u32[]{:S(2)}) %collective-permute-start.14) | collective-permute-done | bytes 524320 | tf_op jit(solution)/shard_map/ppermute | solution.py:349
  273.2 5.8 %copy-done.3 = bf16[256,256,128]{2,1,0:T(8,128)(2,1)S(1)} copy-done((bf16[256,256,128]{2,1,0:T(8,128)(2,1)S(1)}, bf16[256,256,128]{2,1,0:T(8,128)(2,1)}, u32[]{:S(2)}) %copy-start.3) | copy-done | bytes 16777240
  281.0 2.7 shard_map.66
  283.7 4.6 %all-to-all-start.3 = ((bf16[32,16,256]{2,1,0:T(8,128)(2,1)}), bf16[32,16,256]{2,1,0:T(8,128)(2,1)S(1)}, u32[]{:S(2)}, u32[]{:S(2)}) async-start(bf16[32,16,256]{2,1,0:T(8,128)(2,1)} %bitcast.14), calls=%async_computation.3 | async-start | bytes 524288 | tf_op jit(solution)/shard_map/all_to_all | solution.py:439
  288.5 10.4 %all-to-all-done.3.terms_ref = bf16[32,16,256]{2,1,0:T(8,128)(2,1)S(1)} async-done(((bf16[32,16,256]{2,1,0:T(8,128)(2,1)}), bf16[32,16,256]{2,1,0:T(8,128)(2,1)S(1)}, u32[]{:S(2)}, u32[]{:S(2)}) %all-to-all-start.3) | async-done | bytes 262176 | tf_op jit(solution)/shard_map/all_to_all | solution.py:439
  300.3 9.4 %all_to_all.27.sums_ref = f32[32,1,128]{2,1,0:T(1,128)} all-to-all(f32[32,1,128]{2,1,0:T(1,128)S(1)} %get-tuple-element.56), channel_id=1, replica_groups=mesh['aux'=8,'vir'=4] {'aux','vir'}, dimensions={0} | all-to-all | bytes 32768 | tf_op jit(solution)/shard_map/all_to_all | solution.py:454
  (114 shorter events, 43.8 us)
Async XLA Ops:
  4.3 66.6 %collective-permute-start = (bf16[44,256,128]{2,1,0:T(8,128)(2,1)}, bf16[44,256,128]{2,1,0:T(8,128)(2,1)}, u32[]{:S(2)}, u32[]{:S(2)}) collective-permute-start(bf16[44,256,128]{2,1,0:T(8,128)(2,1)} %constant_dynamic-slice_fusion.10), channel_id=1, source_target_pairs={{0,2},{1,3},{2,0},{3,1},{4,6},{5,7},{6,4},{7,5},{8,10},{9,11},{10,... | collective-permute-start | bytes 8650760 | tf_op jit(solution)/shard_map/ppermute | solution.py:349
  7.3 63.6 %copy-start.32 = (f32[1,256,16]{1,2,0:T(8,128)S(1)}, f32[1,256,16]{1,2,0:T(8,128)}, u32[]{:S(2)}) copy-start(f32[1,256,16]{1,2,0:T(8,128)} %param.5) | copy-start | bytes 49156
  7.3 77.1 %copy-start.33 = (f32[256]{0:T(256)S(1)}, f32[256]{0:T(256)}, u32[]{:S(2)}) copy-start(f32[256]{0:T(256)} %param.7) | copy-start | bytes 3076
  14.1 144.1 %collective-permute-start.3 = (bf16[52,256,128]{2,1,0:T(8,128)(2,1)}, bf16[52,256,128]{2,1,0:T(8,128)(2,1)S(1)}, u32[]{:S(2)}, u32[]{:S(2)}) collective-permute-start(bf16[52,256,128]{2,1,0:T(8,128)(2,1)} %get-tuple-element.64), channel_id=1, source_target_pairs={{0,1},{1,0},{2,3},{3,2},{4,5},{5,4},{6,7},{7,6},{8,9},{9,8},{10,11... | collective-permute-start | bytes 10223624 | tf_op jit(solution)/shard_map/ppermute | solution.py:349
  14.1 144.1 %collective-permute-start.4 = (bf16[52,256,128]{2,1,0:T(8,128)(2,1)}, bf16[52,256,128]{2,1,0:T(8,128)(2,1)}, u32[]{:S(2)}, u32[]{:S(2)}) collective-permute-start(bf16[52,256,128]{2,1,0:T(8,128)(2,1)} %get-tuple-element.63), channel_id=1, source_target_pairs={{0,3},{1,2},{2,1},{3,0},{4,7},{5,6},{6,5},{7,4},{8,11},{9,10},{10,... | collective-permute-start | bytes 10223624 | tf_op jit(solution)/shard_map/ppermute | solution.py:349
  84.4 61.6 %collective-permute-start.1 = (f32[1,129,256]{2,1,0:T(8,128)S(1)}, f32[1,129,256]{2,1,0:T(8,128)S(1)}, u32[]{:S(2)}, u32[]{:S(2)}) collective-permute-start(f32[1,129,256]{2,1,0:T(8,128)S(1)} %maximum_bitcast_fusion), channel_id=1, source_target_pairs={{0,2},{1,3},{2,0},{3,1},{4,6},{5,7},{6,4},{7,5},{8,10},{9,11},{10,... | collective-permute-start | bytes 396296 | tf_op jit(solution)/shard_map/ppermute | solution.py:349
  147.4 1.9 collective-permute-start.2
  147.4 49.5 %copy-start.15 = (s32[7]{0:T(128)}, s32[7]{0:T(128)S(1)}, u32[]{:S(2)}) copy-start(s32[7]{0:T(128)S(1)} %stack.39.order_ref) | copy-start | bytes 88
  147.5 29.4 %collective-permute-start.5 = (bf16[8,256,128]{2,1,0:T(8,128)(2,1)}, bf16[8,256,128]{2,1,0:T(8,128)(2,1)}, u32[]{:S(2)}, u32[]{:S(2)}) collective-permute-start(bf16[8,256,128]{2,1,0:T(8,128)(2,1)} %constant_dynamic-slice_fusion.9), channel_id=1, source_target_pairs={{0,2},{1,3},{2,0},{3,1},{4,6},{5,7},{6,4},{7,5},{8,10},{9,11},{10,... | collective-permute-start | bytes 1572872 | tf_op jit(solution)/shard_map/ppermute | solution.py:349
  158.1 38.8 %copy-start.4 = (bf16[52,256,128]{2,1,0:T(8,128)(2,1)}, bf16[52,256,128]{2,1,0:T(8,128)(2,1)S(1)}, u32[]{:S(2)}) copy-start(bf16[52,256,128]{2,1,0:T(8,128)(2,1)S(1)} %collective-permute-done.3.refs_2_.refs_3_.refs_5_) | copy-start | bytes 10223620
  176.8 2.3 collective-permute-start.6
  180.4 14.1 %collective-permute-start.7 = (bf16[16,128,128]{2,1,0:T(8,128)(2,1)S(1)}, bf16[16,128,128]{2,1,0:T(8,128)(2,1)S(1)}, u32[]{:S(2)}, u32[]{:S(2)}) collective-permute-start(bf16[16,128,128]{2,1,0:T(8,128)(2,1)S(1)} %add_convert_fusion.1), channel_id=1, source_target_pairs={{0,2},{1,3},{2,0},{3,1},{4,6},{5,7},{6,4},{7,5},{8,10},{9,11},{10,... | collective-permute-start | bytes 1572872 | tf_op jit(solution)/shard_map/ppermute | solution.py:349
  194.7 12.9 %collective-permute-start.8 = (bf16[16,128,128]{2,1,0:T(8,128)(2,1)S(1)}, bf16[16,128,128]{2,1,0:T(8,128)(2,1)}, u32[]{:S(2)}, u32[]{:S(2)}) collective-permute-start(bf16[16,128,128]{2,1,0:T(8,128)(2,1)S(1)} %add_convert_fusion.mine_ref), channel_id=1, source_target_pairs={{0,1},{1,0},{2,3},{3,2},{4,5},{5,4},{6,7},{7,6},{8,9},{9,8},{10,11... | collective-permute-start | bytes 1572872 | tf_op jit(solution)/shard_map/ppermute | solution.py:349
  194.8 18.5 %collective-permute-start.10 = (bf16[4,256,128]{2,1,0:T(8,128)(2,1)}, bf16[4,256,128]{2,1,0:T(8,128)(2,1)}, u32[]{:S(2)}, u32[]{:S(2)}) collective-permute-start(bf16[4,256,128]{2,1,0:T(8,128)(2,1)} %get-tuple-element.47), channel_id=1, source_target_pairs={{0,2},{1,3},{2,0},{3,1},{4,6},{5,7},{6,4},{7,5},{8,10},{9,11},{10,... | collective-permute-start | bytes 786440 | tf_op jit(solution)/shard_map/ppermute | solution.py:349
  196.5 16.8 %collective-permute-start.11 = (bf16[4,256,128]{2,1,0:T(8,128)(2,1)}, bf16[4,256,128]{2,1,0:T(8,128)(2,1)}, u32[]{:S(2)}, u32[]{:S(2)}) collective-permute-start(bf16[4,256,128]{2,1,0:T(8,128)(2,1)} %get-tuple-element.48), channel_id=1, source_target_pairs={{0,3},{1,2},{2,1},{3,0},{4,7},{5,6},{6,5},{7,4},{8,11},{9,10},{10,... | collective-permute-start | bytes 786440 | tf_op jit(solution)/shard_map/ppermute | solution.py:349
  196.6 16.7 %collective-permute-start.9 = (bf16[4,256,128]{2,1,0:T(8,128)(2,1)}, bf16[4,256,128]{2,1,0:T(8,128)(2,1)}, u32[]{:S(2)}, u32[]{:S(2)}) collective-permute-start(bf16[4,256,128]{2,1,0:T(8,128)(2,1)} %get-tuple-element.46), channel_id=1, source_target_pairs={{0,1},{1,0},{2,3},{3,2},{4,5},{5,4},{6,7},{7,6},{8,9},{9,8},{10,11... | collective-permute-start | bytes 786440 | tf_op jit(solution)/shard_map/ppermute | solution.py:349
  222.8 26.8 %copy-start.26 = (f32[1,129,256]{2,1,0:T(8,128)S(1)}, f32[1,129,256]{2,1,0:T(8,128)}, u32[]{:S(2)}) copy-start(f32[1,129,256]{2,1,0:T(8,128)} %copy-done.25) | copy-start | bytes 396292
  222.8 26.8 %copy-start.28 = (f32[1,129,256]{2,1,0:T(8,128)S(1)}, f32[1,129,256]{2,1,0:T(8,128)}, u32[]{:S(2)}) copy-start(f32[1,129,256]{2,1,0:T(8,128)} %copy-done.27) | copy-start | bytes 396292
  222.8 26.8 %copy-start.30 = (f32[1,129,256]{2,1,0:T(8,128)S(1)}, f32[1,129,256]{2,1,0:T(8,128)}, u32[]{:S(2)}) copy-start(f32[1,129,256]{2,1,0:T(8,128)} %copy-done.29) | copy-start | bytes 396292
  241.1 13.3 %all-to-all-start.2 = ((bf16[32,16,256]{2,1,0:T(8,128)(2,1)}), bf16[32,16,256]{2,1,0:T(8,128)(2,1)S(1)}, u32[]{:S(2)}, u32[]{:S(2)}) async-start(bf16[32,16,256]{2,1,0:T(8,128)(2,1)} %shard_map.64), calls=%async_computation.2 | async-start | bytes 524288 | tf_op jit(solution)/shard_map/all_to_all | solution.py:447
  246.2 20.2 %collective-permute-start.12 = (bf16[8,256,128]{2,1,0:T(8,128)(2,1)}, bf16[8,256,128]{2,1,0:T(8,128)(2,1)S(1)}, u32[]{:S(2)}, u32[]{:S(2)}) collective-permute-start(bf16[8,256,128]{2,1,0:T(8,128)(2,1)} %get-tuple-element.62), channel_id=1, source_target_pairs={{0,1},{1,0},{2,3},{3,2},{4,5},{5,4},{6,7},{7,6},{8,9},{9,8},{10,11... | collective-permute-start | bytes 1572872 | tf_op jit(solution)/shard_map/ppermute | solution.py:349
  246.3 20.1 %collective-permute-start.13 = (bf16[8,256,128]{2,1,0:T(8,128)(2,1)}, bf16[8,256,128]{2,1,0:T(8,128)(2,1)S(1)}, u32[]{:S(2)}, u32[]{:S(2)}) collective-permute-start(bf16[8,256,128]{2,1,0:T(8,128)(2,1)} %get-tuple-element.61), channel_id=1, source_target_pairs={{0,2},{1,3},{2,0},{3,1},{4,6},{5,7},{6,4},{7,5},{8,10},{9,11},{10,... | collective-permute-start | bytes 1572872 | tf_op jit(solution)/shard_map/ppermute | solution.py:349
  248.0 25.2 %collective-permute-start.14 = (bf16[8,256,128]{2,1,0:T(8,128)(2,1)S(1)}, bf16[8,256,128]{2,1,0:T(8,128)(2,1)S(1)}, u32[]{:S(2)}, u32[]{:S(2)}) collective-permute-start(bf16[8,256,128]{2,1,0:T(8,128)(2,1)S(1)} %get-tuple-element.60), channel_id=1, source_target_pairs={{0,3},{1,2},{2,1},{3,0},{4,7},{5,6},{6,5},{7,4},{8,11},{9,10},{10,... | collective-permute-start | bytes 1572872 | tf_op jit(solution)/shard_map/ppermute | solution.py:349
  283.7 15.2 %all-to-all-start.3 = ((bf16[32,16,256]{2,1,0:T(8,128)(2,1)}), bf16[32,16,256]{2,1,0:T(8,128)(2,1)S(1)}, u32[]{:S(2)}, u32[]{:S(2)}) async-start(bf16[32,16,256]{2,1,0:T(8,128)(2,1)} %bitcast.14), calls=%async_computation.3 | async-start | bytes 524288 | tf_op jit(solution)/shard_map/all_to_all | solution.py:439
  (28 other events, 181.9 us)

commit v9 on v7

--- a/solution.py
+++ b/solution.py
@@ -182,7 +182,7 @@
             pltpu.VMEM((len(blocks), nv, size, width, occ), jnp.bfloat16),
             pltpu.SemaphoreType.DMA((len(blocks), nv)),
         ],
-        compiler_params=pltpu.CompilerParams(vmem_limit_bytes=(58 if stepping else 24) * 2**20),
+        compiler_params=pltpu.CompilerParams(vmem_limit_bytes=46 * 2**20),
         cost_estimate=pl.CostEstimate(flops=0, bytes_accessed=0, transcendentals=0),
     )(order, *first, *([carry] if carried else []), *arrays)
 
@@ -190,30 +190,30 @@
 def share_sums(terms, trial, gap):
     count = terms.shape[0]
 
-    def body(terms_ref, trial_ref, gap_ref, diff_ref, scaled_ref, sums_ref):
+    def body(terms_ref, trial_ref, gap_ref, ratios_ref, sums_ref):
         coupling = jnp.sum(terms_ref[...].astype(jnp.float32), axis=0)
         diff, scaled, sums = five_sums(trial_ref[...], gap_ref[...], coupling)
-        diff_ref[...] = diff
-        scaled_ref[...] = scaled
+        ratios_ref[0] = diff
+        ratios_ref[1] = scaled
         lane = lax.broadcasted_iota(jnp.int32, (1, 128), 1)
         row = jnp.zeros((1, 128), jnp.float32)
         for at, value in enumerate(sums):
             row = jnp.where(lane == at, value, row)
         sums_ref[...] = jnp.broadcast_to(row[None], sums_ref.shape)
 
-    like = jax.ShapeDtypeStruct(trial.shape, jnp.float32)
+    ratios = jax.ShapeDtypeStruct((2, *trial.shape), jnp.float32)
     return pl.pallas_call(
         body,
-        out_shape=(like, like, jax.ShapeDtypeStruct((count, 1, 128), jnp.float32)),
+        out_shape=(ratios, jax.ShapeDtypeStruct((count, 1, 128), jnp.float32)),
         compiler_params=pltpu.CompilerParams(vmem_limit_bytes=24 * 2**20),
     )(terms, trial, gap)
 
 
-def step_share(diff, scaled, all_sums, before, total):
-    def body(diff_ref, scaled_ref, sums_ref, before_ref, next_ref, shifts_ref):
+def step_share(ratios, all_sums, before, total):
+    def body(ratios_ref, sums_ref, before_ref, next_ref, shifts_ref):
         row = jnp.sum(sums_ref[...], axis=0)
         fresh, shift = finish(
-            diff_ref[...], scaled_ref[...], [row[:, at : at + 1] for at in range(5)], total
+            ratios_ref[0], ratios_ref[1], [row[:, at : at + 1] for at in range(5)], total
         )
         next_ref[...] = fresh
         shifts_ref[...] = jnp.concatenate([before_ref[:, :1], shift], axis=1)
@@ -221,10 +221,10 @@
     return pl.pallas_call(
         body,
         out_shape=(
-            jax.ShapeDtypeStruct(diff.shape, jnp.float32),
+            jax.ShapeDtypeStruct(ratios.shape[1:], jnp.float32),
             jax.ShapeDtypeStruct((1, 2), jnp.float32),
         ),
-    )(diff, scaled, all_sums, before)
+    )(ratios, all_sums, before)
 
 
 def share_copies(terms):
@@ -334,9 +334,9 @@
     copies = share_copies(sum_terms(partial))
     first = [lax.all_to_all(copies, EVERY, 0, 0, tiled=True), trial, state[:, occ:], occ_energy[:, None]]
     partial, trial_own, before = call(first, blocks, None, na)
-    diff, scaled, sums = share_sums(sum_terms(partial), trial_own, gap_own)
+    ratios, sums = share_sums(sum_terms(partial), trial_own, gap_own)
     sums = lax.all_to_all(sums, EVERY, 0, 0, tiled=True)
-    fresh, shifts = step_share(diff, scaled, sums, before, total)
+    fresh, shifts = step_share(ratios, sums, before, total)
     return (fresh.T[None], shifts.T)
 
 

time: 268 us -> 266 us (level)
  local copies, waits for them, and re-layouts: 26.8 us -> 18.6 us
  waiting for transfers between devices: 155 us -> 162 us
    unnamed x48 -> x34, local copies, waits for them, and re-layouts: 8.73 us -> 1.95 us
    ppermute x11, waiting for transfers between devices: 136 us -> 141 us  [send(): lax.ppermute(value, 'vir', [(one, partner(one, k)) for one in range(nv)])]
  transfers between devices with their start and end apart: 13 -> 13, of which waited for: 8 -> 8; matrix products, arithmetic and copies ran while one was open for 6% -> 5% of each run, Pallas kernels for 4% -> 5%
where the time goes in v9:
time: 266 us; the launch traced here: 265 us
  waiting for transfers between devices  162 us (61%)
  blocking collectives  39.6 us (15%)
  Pallas kernels  29.2 us (11%)
  local copies, waits for them, and re-layouts  18.6 us (7%)
  starting transfers between devices  15.3 us (6%)
    ppermute x11, waiting for transfers between devices, send(): lax.ppermute(value, 'vir', [(one, partner(one, k)) for one in range(nv)])  141 us
    pallas_call x4, Pallas kernels, contract(): pl.pallas_call(body, in_specs=[pl.BlockSpec(memory_space=pltpu.SMEM)] + [...  25.6 us
    all_to_all x1, blocking collectives, sum_terms(): lax.all_to_all(partial.reshape(count, share, width), EVERY, 0, 0, tiled=T...  16.6 us
    dynamic_slice x4, local copies, waits for them, and re-layouts, piece(): lax.dynamic_slice_in_dim(whole, partner(vir_at, k) * own + low, high - lo...  15.3 us
    all_to_all x1, blocking collectives, spread(): return lax.all_to_all(copies, axes, 0, 0, tiled=True)  13.5 us
    all_to_all x1, waiting for transfers between devices, sum_terms(): lax.all_to_all(partial.reshape(count, share, width), EVERY, 0, 0, tiled=T...  10.4 us
    all_to_all x1, waiting for transfers between devices, local(): lax.all_to_all(copies, EVERY, 0, 0, tiled=True)  10.4 us
    ppermute x11, starting transfers between devices, send(): lax.ppermute(value, 'vir', [(one, partner(one, k)) for one in range(nv)])  10.1 us
  transfers between devices with their start and end apart: 13, of which 8 were waited for; matrix products, arithmetic and copies ran while one was open for 5% of the time, Pallas kernels for 5%

profile of v9, /device:TPU:0, one launch (start us, length us, event | category | flops | bytes accessed | tf_op | source)
XLA Modules:
  0.0 265.5 jit_solution(14487267489405890772)
XLA Ops:
  0.6 4.0 %constant_dynamic-slice_fusion.8 = bf16[48,256,128]{2,1,0:T(8,128)(2,1)} fusion(bf16[256,256,128]{2,1,0:T(8,128)(2,1)} %refs_4_.1, s32[]{:T(128)S(6)} %select_n.30), kind=kLoop, calls=%fused_computation.13 | loop fusion | bytes 6291460 | tf_op jit(solution)/shard_map/dynamic_slice | solution.py:270
  4.6 3.0 %collective-permute-start = (bf16[48,256,128]{2,1,0:T(8,128)(2,1)}, bf16[48,256,128]{2,1,0:T(8,128)(2,1)S(1)}, u32[]{:S(2)}, u32[]{:S(2)}) collective-permute-start(bf16[48,256,128]{2,1,0:T(8,128)(2,1)} %constant_dynamic-slice_fusion.8), channel_id=1, source_target_pairs={{0,2},{1,3},{2,0},{3,1},{4,6},{5,7},{6,4},{7,5},{8,10},{9,11},{10,... | collective-permute-start | bytes 9437192 | tf_op jit(solution)/shard_map/ppermute | solution.py:260
  7.6 6.3 %constant_dynamic-slice_fusion = (bf16[48,256,128]{2,1,0:T(8,128)(2,1)}, bf16[48,256,128]{2,1,0:T(8,128)(2,1)}) fusion(bf16[256,256,128]{2,1,0:T(8,128)(2,1)} %refs_4_.1, s32[]{:T(128)S(6)} %select_n.38, s32[]{:T(128)S(6)} %select_n.37), kind=kLoop, calls=%fused_computation.5 | loop fusion | bytes 12582920 | tf_op jit(solution)/shard_map/dynamic_slice | solution.py:270
  14.0 2.1 constant_dynamic-slice_fusion.2
  16.0 3.0 %constant_dynamic-slice_fusion.5 = (bf16[12,256,128]{2,1,0:T(8,128)(2,1)}, bf16[12,256,128]{2,1,0:T(8,128)(2,1)}, bf16[12,256,128]{2,1,0:T(8,128)(2,1)}) fusion(bf16[256,256,128]{2,1,0:T(8,128)(2,1)} %refs_4_.1, s32[]{:T(128)S(6)} %select_n.33, s32[]{:T(128)S(6)} %select_n.32, s32[]{:T(128)S(6)} %select_n.31), kind=kLoop, calls=%fused_computation.10 | loop fusion | bytes 4718604 | tf_op jit(solution)/shard_map/dynamic_slice | solution.py:270
  19.1 57.6 %collective-permute-done.refs_3_.refs_6_ = bf16[48,256,128]{2,1,0:T(8,128)(2,1)S(1)} collective-permute-done((bf16[48,256,128]{2,1,0:T(8,128)(2,1)}, bf16[48,256,128]{2,1,0:T(8,128)(2,1)S(1)}, u32[]{:S(2)}, u32[]{:S(2)}) %collective-permute-start) | collective-permute-done | bytes 3145760 | tf_op jit(solution)/shard_map/ppermute | solution.py:260
  76.7 13.5 %all_to_all.25 = f32[8,16,256]{2,1,0:T(8,128)S(1)} all-to-all(f32[8,16,256]{2,1,0:T(8,128)S(1)} %broadcast_in_dim.8), channel_id=1, replica_groups=mesh['aux'=8,'vir'=4] {'aux'}, dimensions={0} | all-to-all | bytes 262144 | tf_op jit(solution)/shard_map/all_to_all | solution.py:240
  91.8 54.5 %collective-permute-done.1 = f32[1,129,256]{2,1,0:T(8,128)S(1)} collective-permute-done((f32[1,129,256]{2,1,0:T(8,128)S(1)}, f32[1,129,256]{2,1,0:T(8,128)S(1)}, u32[]{:S(2)}, u32[]{:S(2)}) %collective-permute-start.1) | collective-permute-done | bytes 132128 | tf_op jit(solution)/shard_map/ppermute | solution.py:260
  146.9 1.7 collective-permute-start.6
  151.5 8.1 %shard_map.59.refs_1_ = f32[1024,128]{1,0:T(8,128)S(1)} custom-call(s32[6]{0:T(128)S(1)} %stack.35.order_ref, bf16[4,128,256]{2,1,0:T(8,128)(2,1)S(1)} %slice.20.refs_0_, bf16[256,256,128]{2,1,0:T(8,128)(2,1)} %refs_4_.1, bf16[48,256,128]{2,1,0:T(8,128)(2,1)} %collective-permute-done.3.refs_2_.refs_5_, ...), custom_call_target="tpu_custom_call" | custom-call | tf_op jit(solution)/shard_map/pallas_call | solution.py:172
  162.0 5.6 %collective-permute-done.6.refs_4_.refs_9_ = bf16[12,256,128]{2,1,0:T(8,128)(2,1)} collective-permute-done((bf16[12,256,128]{2,1,0:T(8,128)(2,1)}, bf16[12,256,128]{2,1,0:T(8,128)(2,1)}, u32[]{:S(2)}, u32[]{:S(2)}) %collective-permute-start.6) | collective-permute-done | bytes 786464 | tf_op jit(solution)/shard_map/ppermute | solution.py:260
  167.6 16.1 %collective-permute-done.7.refs_5_.refs_10_ = bf16[12,256,128]{2,1,0:T(8,128)(2,1)} collective-permute-done((bf16[12,256,128]{2,1,0:T(8,128)(2,1)}, bf16[12,256,128]{2,1,0:T(8,128)(2,1)}, u32[]{:S(2)}, u32[]{:S(2)}) %collective-permute-start.7) | collective-permute-done | bytes 786464 | tf_op jit(solution)/shard_map/ppermute | solution.py:260
  183.7 3.9 %shard_map.60.refs_1_ = f32[1024,128]{1,0:T(8,128)S(1)} custom-call(s32[6]{0:T(128)S(1)} %stack.35.order_ref, bf16[4,128,256]{2,1,0:T(8,128)(2,1)S(1)} %slice.20.refs_0_, f32[1024,128]{1,0:T(8,128)S(1)} %shard_map.59.refs_1_, bf16[256,256,128]{2,1,0:T(8,128)(2,1)} %refs_4_.1, bf16[12,256,128]{2,1,0:T(8,128)(2,1)} %collective-permute-done.5.refs_3_.refs_8_, ...), custom_call_target="tpu_custom_call" | custom-call | tf_op jit(solution)/shard_map/pallas_call | solution.py:172
  189.2 5.5 %collective-permute-done.9.refs_4_.refs_12_ = bf16[4,256,128]{2,1,0:T(8,128)(2,1)S(1)} collective-permute-done((bf16[4,256,128]{2,1,0:T(8,128)(2,1)S(1)}, bf16[4,256,128]{2,1,0:T(8,128)(2,1)S(1)}, u32[]{:S(2)}, u32[]{:S(2)}) %collective-permute-start.9) | collective-permute-done | bytes 262176 | tf_op jit(solution)/shard_map/ppermute | solution.py:260
  194.7 2.5 shard_map.61
  197.2 16.6 %all_to_all.26.terms_ref = bf16[32,16,256]{2,1,0:T(8,128)(2,1)} all-to-all(bf16[32,16,256]{2,1,0:T(8,128)(2,1)S(1)} %bitcast.19), channel_id=1, replica_groups=mesh['aux'=8,'vir'=4] {'aux','vir'}, dimensions={0} | all-to-all | bytes 524288 | tf_op jit(solution)/shard_map/all_to_all | solution.py:331
  213.8 1.7 shard_map.62
  215.5 2.6 all-to-all-start.2
  218.3 10.4 %all-to-all-done.2.refs_0_ = bf16[32,16,256]{2,1,0:T(8,128)(2,1)S(1)} async-done(((bf16[32,16,256]{2,1,0:T(8,128)(2,1)}), bf16[32,16,256]{2,1,0:T(8,128)(2,1)S(1)}, u32[]{:S(2)}, u32[]{:S(2)}) %all-to-all-start.2) | async-done | bytes 262176 | tf_op jit(solution)/shard_map/all_to_all | solution.py:335
  228.6 11.1 %shard_map.63 = (bf16[8,4,16,256]{3,2,1,0:T(8,128)(2,1)}, f32[16,256]{1,0:T(8,128)S(1)}, f32[1,128]{1,0:T(1,128)S(1)}) custom-call(s32[6]{0:T(128)S(1)} %stack.35.order_ref, bf16[32,16,256]{2,1,0:T(8,128)(2,1)S(1)} %all-to-all-done.2.refs_0_, f32[4,128,256]{2,1,0:T(8,128)S(1)} %slice.18.refs_1_, f32[4,1,256]{2,1,0:T(1,128)S(1)} %pad_maximum_fusion.2.refs_2_, ...), custom_call_target="tpu_custom_call" | custom-call | tf_op jit(solution)/shard_map/pallas_call | solution.py:172
  240.3 2.6 all-to-all-start.3
  243.1 10.4 %all-to-all-done.3.terms_ref = bf16[32,16,256]{2,1,0:T(8,128)(2,1)S(1)} async-done(((bf16[32,16,256]{2,1,0:T(8,128)(2,1)}), bf16[32,16,256]{2,1,0:T(8,128)(2,1)S(1)}, u32[]{:S(2)}, u32[]{:S(2)}) %all-to-all-start.3) | async-done | bytes 262176 | tf_op jit(solution)/shard_map/all_to_all | solution.py:331
  254.3 9.5 %all_to_all.27.sums_ref = f32[32,1,128]{2,1,0:T(1,128)} all-to-all(f32[32,1,128]{2,1,0:T(1,128)S(1)} %get-tuple-element.42), channel_id=1, replica_groups=mesh['aux'=8,'vir'=4] {'aux','vir'}, dimensions={0} | all-to-all | bytes 32768 | tf_op jit(solution)/shard_map/all_to_all | solution.py:338
  263.8 1.7 shard_map.65
  (62 shorter events, 10.6 us)
Async XLA Ops:
  4.6 72.1 %collective-permute-start = (bf16[48,256,128]{2,1,0:T(8,128)(2,1)}, bf16[48,256,128]{2,1,0:T(8,128)(2,1)S(1)}, u32[]{:S(2)}, u32[]{:S(2)}) collective-permute-start(bf16[48,256,128]{2,1,0:T(8,128)(2,1)} %constant_dynamic-slice_fusion.8), channel_id=1, source_target_pairs={{0,2},{1,3},{2,0},{3,1},{4,6},{5,7},{6,4},{7,5},{8,10},{9,11},{10,... | collective-permute-start | bytes 9437192 | tf_op jit(solution)/shard_map/ppermute | solution.py:260
  13.8 136.9 %collective-permute-start.3 = (bf16[48,256,128]{2,1,0:T(8,128)(2,1)}, bf16[48,256,128]{2,1,0:T(8,128)(2,1)}, u32[]{:S(2)}, u32[]{:S(2)}) collective-permute-start(bf16[48,256,128]{2,1,0:T(8,128)(2,1)} %get-tuple-element.47), channel_id=1, source_target_pairs={{0,1},{1,0},{2,3},{3,2},{4,5},{5,4},{6,7},{7,6},{8,9},{9,8},{10,11... | collective-permute-start | bytes 9437192 | tf_op jit(solution)/shard_map/ppermute | solution.py:260
  13.8 137.7 %collective-permute-start.4 = (bf16[48,256,128]{2,1,0:T(8,128)(2,1)}, bf16[48,256,128]{2,1,0:T(8,128)(2,1)}, u32[]{:S(2)}, u32[]{:S(2)}) collective-permute-start(bf16[48,256,128]{2,1,0:T(8,128)(2,1)} %get-tuple-element.46), channel_id=1, source_target_pairs={{0,3},{1,2},{2,1},{3,0},{4,7},{5,6},{6,5},{7,4},{8,11},{9,10},{10,... | collective-permute-start | bytes 9437192 | tf_op jit(solution)/shard_map/ppermute | solution.py:260
  13.9 62.8 %copy-start.14 = (f32[1,256,16]{1,2,0:T(8,128)S(1)}, f32[1,256,16]{1,2,0:T(8,128)}, u32[]{:S(2)}) copy-start(f32[1,256,16]{1,2,0:T(8,128)} %param.5) | copy-start | bytes 49156
  14.0 76.3 %copy-start.15 = (f32[256]{0:T(256)S(1)}, f32[256]{0:T(256)}, u32[]{:S(2)}) copy-start(f32[256]{0:T(256)} %param.7) | copy-start | bytes 3076
  76.7 83.0 %copy-start = (bf16[48,256,128]{2,1,0:T(8,128)(2,1)}, bf16[48,256,128]{2,1,0:T(8,128)(2,1)S(1)}, u32[]{:S(2)}) copy-start(bf16[48,256,128]{2,1,0:T(8,128)(2,1)S(1)} %collective-permute-done.refs_3_.refs_6_) | copy-start | bytes 9437188
  90.2 56.0 %collective-permute-start.1 = (f32[1,129,256]{2,1,0:T(8,128)S(1)}, f32[1,129,256]{2,1,0:T(8,128)S(1)}, u32[]{:S(2)}, u32[]{:S(2)}) collective-permute-start(f32[1,129,256]{2,1,0:T(8,128)S(1)} %maximum_bitcast_fusion), channel_id=1, source_target_pairs={{0,2},{1,3},{2,0},{3,1},{4,6},{5,7},{6,4},{7,5},{8,10},{9,11},{10,... | collective-permute-start | bytes 396296 | tf_op jit(solution)/shard_map/ppermute | solution.py:260
  146.3 2.3 collective-permute-start.2
  146.4 14.2 %collective-permute-start.5 = (bf16[12,256,128]{2,1,0:T(8,128)(2,1)}, bf16[12,256,128]{2,1,0:T(8,128)(2,1)}, u32[]{:S(2)}, u32[]{:S(2)}) collective-permute-start(bf16[12,256,128]{2,1,0:T(8,128)(2,1)} %get-tuple-element.33), channel_id=1, source_target_pairs={{0,1},{1,0},{2,3},{3,2},{4,5},{5,4},{6,7},{7,6},{8,9},{9,8},{10,11... | collective-permute-start | bytes 2359304 | tf_op jit(solution)/shard_map/ppermute | solution.py:260
  146.9 20.7 %collective-permute-start.6 = (bf16[12,256,128]{2,1,0:T(8,128)(2,1)}, bf16[12,256,128]{2,1,0:T(8,128)(2,1)}, u32[]{:S(2)}, u32[]{:S(2)}) collective-permute-start(bf16[12,256,128]{2,1,0:T(8,128)(2,1)} %get-tuple-element.34), channel_id=1, source_target_pairs={{0,2},{1,3},{2,0},{3,1},{4,6},{5,7},{6,4},{7,5},{8,10},{9,11},{10,... | collective-permute-start | bytes 2359304 | tf_op jit(solution)/shard_map/ppermute | solution.py:260
  148.6 35.1 %collective-permute-start.7 = (bf16[12,256,128]{2,1,0:T(8,128)(2,1)}, bf16[12,256,128]{2,1,0:T(8,128)(2,1)}, u32[]{:S(2)}, u32[]{:S(2)}) collective-permute-start(bf16[12,256,128]{2,1,0:T(8,128)(2,1)} %get-tuple-element.35), channel_id=1, source_target_pairs={{0,3},{1,2},{2,1},{3,0},{4,7},{5,6},{6,5},{7,4},{8,11},{9,10},{10,... | collective-permute-start | bytes 2359304 | tf_op jit(solution)/shard_map/ppermute | solution.py:260
  150.7 9.0 %copy-start.13 = (bf16[4,256,128]{2,1,0:T(8,128)(2,1)S(1)}, bf16[4,256,128]{2,1,0:T(8,128)(2,1)}, u32[]{:S(2)}) copy-start(bf16[4,256,128]{2,1,0:T(8,128)(2,1)} %get-tuple-element.38) | copy-start | bytes 786436
  150.7 9.9 %copy-start.12 = (bf16[4,256,128]{2,1,0:T(8,128)(2,1)S(1)}, bf16[4,256,128]{2,1,0:T(8,128)(2,1)}, u32[]{:S(2)}) copy-start(bf16[4,256,128]{2,1,0:T(8,128)(2,1)} %get-tuple-element.36) | copy-start | bytes 786436
  150.8 9.9 %copy-start.11 = (bf16[4,256,128]{2,1,0:T(8,128)(2,1)S(1)}, bf16[4,256,128]{2,1,0:T(8,128)(2,1)}, u32[]{:S(2)}) copy-start(bf16[4,256,128]{2,1,0:T(8,128)(2,1)} %get-tuple-element.37) | copy-start | bytes 786436
  159.7 29.5 %collective-permute-start.10 = (bf16[4,256,128]{2,1,0:T(8,128)(2,1)S(1)}, bf16[4,256,128]{2,1,0:T(8,128)(2,1)S(1)}, u32[]{:S(2)}, u32[]{:S(2)}) collective-permute-start(bf16[4,256,128]{2,1,0:T(8,128)(2,1)S(1)} %copy-done.13), channel_id=1, source_target_pairs={{0,3},{1,2},{2,1},{3,0},{4,7},{5,6},{6,5},{7,4},{8,11},{9,10},{10,... | collective-permute-start | bytes 786440 | tf_op jit(solution)/shard_map/ppermute | solution.py:260
  160.6 28.6 %collective-permute-start.8 = (bf16[4,256,128]{2,1,0:T(8,128)(2,1)S(1)}, bf16[4,256,128]{2,1,0:T(8,128)(2,1)S(1)}, u32[]{:S(2)}, u32[]{:S(2)}) collective-permute-start(bf16[4,256,128]{2,1,0:T(8,128)(2,1)S(1)} %copy-done.12), channel_id=1, source_target_pairs={{0,1},{1,0},{2,3},{3,2},{4,5},{5,4},{6,7},{7,6},{8,9},{9,8},{10,11... | collective-permute-start | bytes 786440 | tf_op jit(solution)/shard_map/ppermute | solution.py:260
  160.6 34.1 %collective-permute-start.9 = (bf16[4,256,128]{2,1,0:T(8,128)(2,1)S(1)}, bf16[4,256,128]{2,1,0:T(8,128)(2,1)S(1)}, u32[]{:S(2)}, u32[]{:S(2)}) collective-permute-start(bf16[4,256,128]{2,1,0:T(8,128)(2,1)S(1)} %copy-done.11), channel_id=1, source_target_pairs={{0,2},{1,3},{2,0},{3,1},{4,6},{5,7},{6,4},{7,5},{8,10},{9,11},{10,... | collective-permute-start | bytes 786440 | tf_op jit(solution)/shard_map/ppermute | solution.py:260
  187.6 30.5 %copy-start.16 = (f32[128]{0:T(128)S(1)}, f32[128]{0:T(128)}, u32[]{:S(2)}) copy-start(f32[128]{0:T(128)} %param.6) | copy-start | bytes 1540
  187.6 30.6 %copy-start.4 = (f32[4,129,256]{2,1,0:T(8,128)S(1)}, f32[4,129,256]{2,1,0:T(8,128)}, u32[]{:S(2)}) copy-start(f32[4,129,256]{2,1,0:T(8,128)} %copy-done.3) | copy-start | bytes 1585156
  187.6 30.6 %copy-start.6 = (f32[1,129,256]{2,1,0:T(8,128)S(1)}, f32[1,129,256]{2,1,0:T(8,128)}, u32[]{:S(2)}) copy-start(f32[1,129,256]{2,1,0:T(8,128)} %copy-done.5) | copy-start | bytes 396292
  187.6 30.6 %copy-start.8 = (f32[1,129,256]{2,1,0:T(8,128)S(1)}, f32[1,129,256]{2,1,0:T(8,128)}, u32[]{:S(2)}) copy-start(f32[1,129,256]{2,1,0:T(8,128)} %copy-done.7) | copy-start | bytes 396292
  187.6 30.6 %copy-start.10 = (f32[1,129,256]{2,1,0:T(8,128)S(1)}, f32[1,129,256]{2,1,0:T(8,128)}, u32[]{:S(2)}) copy-start(f32[1,129,256]{2,1,0:T(8,128)} %copy-done.9) | copy-start | bytes 396292
  215.5 13.2 %all-to-all-start.2 = ((bf16[32,16,256]{2,1,0:T(8,128)(2,1)}), bf16[32,16,256]{2,1,0:T(8,128)(2,1)S(1)}, u32[]{:S(2)}, u32[]{:S(2)}) async-start(bf16[32,16,256]{2,1,0:T(8,128)(2,1)} %shard_map.62), calls=%async_computation.2 | async-start | bytes 524288 | tf_op jit(solution)/shard_map/all_to_all | solution.py:335
  240.3 13.2 %all-to-all-start.3 = ((bf16[32,16,256]{2,1,0:T(8,128)(2,1)}), bf16[32,16,256]{2,1,0:T(8,128)(2,1)S(1)}, u32[]{:S(2)}, u32[]{:S(2)}) async-start(bf16[32,16,256]{2,1,0:T(8,128)(2,1)} %bitcast.12), calls=%async_computation.3 | async-start | bytes 524288 | tf_op jit(solution)/shard_map/all_to_all | solution.py:331
  (6 other events, 8.6 us)

commit v10 on v9

--- a/solution.py
+++ b/solution.py
@@ -235,6 +235,32 @@
     return pl.pallas_call(body, out_shape=jax.ShapeDtypeStruct(terms.shape, jnp.bfloat16))(terms)
 
 
+def cut_out(whole, start, count):
+    parts = 4
+    rows = count // parts
+
+    def body(start_ref, whole_ref, out_ref, sems):
+        copies = []
+        for n in range(parts):
+            place = pl.ds(start_ref[0] + n * rows, rows)
+            copies.append(
+                pltpu.make_async_copy(whole_ref.at[place], out_ref.at[pl.ds(n * rows, rows)], sems.at[n])
+            )
+        for copy in copies:
+            copy.start()
+        for copy in copies:
+            copy.wait()
+
+    return pl.pallas_call(
+        body,
+        in_specs=[pl.BlockSpec(memory_space=pltpu.SMEM), pl.BlockSpec(memory_space=pltpu.HBM)],
+        out_specs=pl.BlockSpec(memory_space=pltpu.VMEM),
+        out_shape=jax.ShapeDtypeStruct((count, *whole.shape[1:]), whole.dtype),
+        scratch_shapes=[pltpu.SemaphoreType.DMA((parts,))],
+        compiler_params=pltpu.CompilerParams(vmem_limit_bytes=46 * 2**20),
+    )(start.astype(jnp.int32)[None], whole)
+
+
 def spread(share, count, axes=EVERY):
     copies = jnp.broadcast_to(share[None], (count,) + share.shape)
     return lax.all_to_all(copies, axes, 0, 0, tiled=True)
@@ -280,11 +306,14 @@
 
     marks = [0, own]
     if cut_up:
-        marks = [0, 12 * unit, 15 * unit, own]
+        marks = [0, 9 * unit, 15 * unit, own]
     far = [k for k in range(nv) if k > 1] + [1]
     later_factors = factors
     for n, k in enumerate(far):
-        cut = piece(k, *marks[:2], later_factors)
+        if cut_up and n == 0:
+            cut = cut_out(factors, partner(vir_at, k) * own, marks[1])
+        else:
+            cut = piece(k, *marks[:2], later_factors)
         if cut_up and n == 0:
             later_factors, cut = lax.optimization_barrier((factors, cut))
         exchange(k, *marks[:2], cut)
@@ -318,14 +347,18 @@
         low, high, end = marks[1:]
         for k, cut in enumerate(later[0]):
             exchange(far[k], low, high, cut)
-        blocks = [[(n * 4 * unit, (n + 1) * 4 * unit)] for n in range(3)]
+        parts = [(n * low // 4, (n + 1) * low // 4) for n in range(4)]
+        middle = (low + high) // 2
         last_block = [[(high, end)]]
-        (carry,) = call([xt], blocks)
+        (carry,) = call([xt], [[part] for part in parts])
         cuts, carry = lax.optimization_barrier((later[1], carry))
         for k, cut in zip(far, cuts):
             exchange(k, high, end, cut)
-        (carry,) = call([xt], [[(low, high)]], carry)
-        blocks.append([(low, high), (high, end)])
+        (carry,) = call([xt], [[(low, middle)], [(middle, high)]], carry)
+        blocks = []
+        for start in range(0, own, 4 * unit):
+            points = [start] + [m for m in marks if start < m < start + 4 * unit] + [start + 4 * unit]
+            blocks.append(list(zip(points, points[1:])))
 
     def sum_terms(partial):
         return lax.all_to_all(partial.reshape(count, share, width), EVERY, 0, 0, tiled=True)

time: 266 us -> 265 us (level)
  local copies, waits for them, and re-layouts: 18.6 us -> 14 us
  Pallas kernels: 29.2 us -> 33 us
    dynamic_slice x4 -> x3, local copies, waits for them, and re-layouts: 15.3 us -> 11.8 us  [piece(): lax.dynamic_slice_in_dim(whole, partner(vir_at, k) * own + low, high - lo...]
    pallas_call x0 -> x1, Pallas kernels: none -> 3.09 us  [cut_out(): pl.pallas_call(body, in_specs=[pl.BlockSpec(memory_space=pltpu.SMEM), pl....]
where the time goes in v10:
time: 265 us
  waiting for transfers between devices  162 us (61%)
  blocking collectives  39.4 us (15%)
  Pallas kernels  33 us (12%)
  starting transfers between devices  15.3 us (6%)
  local copies, waits for them, and re-layouts  14 us (5%)
    ppermute x11, waiting for transfers between devices, send(): lax.ppermute(value, 'vir', [(one, partner(one, k)) for one in range(nv)])  141 us
    pallas_call x4, Pallas kernels, contract(): pl.pallas_call(body, in_specs=[pl.BlockSpec(memory_space=pltpu.SMEM)] + [...  26.4 us
    all_to_all x1, blocking collectives, sum_terms(): lax.all_to_all(partial.reshape(count, share, width), EVERY, 0, 0, tiled=T...  16.6 us
    all_to_all x1, blocking collectives, spread(): return lax.all_to_all(copies, axes, 0, 0, tiled=True)  13.5 us
    dynamic_slice x3, local copies, waits for them, and re-layouts, piece(): lax.dynamic_slice_in_dim(whole, partner(vir_at, k) * own + low, high - lo...  11.8 us
    all_to_all x1, waiting for transfers between devices, sum_terms(): lax.all_to_all(partial.reshape(count, share, width), EVERY, 0, 0, tiled=T...  10.4 us
    all_to_all x1, waiting for transfers between devices, local(): lax.all_to_all(copies, EVERY, 0, 0, tiled=True)  10.4 us
    ppermute x11, starting transfers between devices, send(): lax.ppermute(value, 'vir', [(one, partner(one, k)) for one in range(nv)])  10.1 us
  transfers between devices with their start and end apart: 13, of which 8 were waited for; matrix products, arithmetic and copies ran while one was open for 5% of the time, Pallas kernels for 5%

profile of v10, /device:TPU:0, one launch (start us, length us, event | category | flops | bytes accessed | tf_op | source)
XLA Modules:
  0.0 264.6 jit_solution(1630492872701769519)
XLA Ops:
  0.6 3.1 %shard_map.59 = bf16[36,256,128]{2,1,0:T(8,128)(2,1)} custom-call(s32[1]{0:T(128)} %bitcast.5.start_ref, bf16[256,256,128]{2,1,0:T(8,128)(2,1)} %refs_4_.1), custom_call_target="tpu_custom_call" | custom-call | tf_op jit(solution)/shard_map/pallas_call | solution.py:254
  3.7 3.0 %collective-permute-start = (bf16[36,256,128]{2,1,0:T(8,128)(2,1)}, bf16[36,256,128]{2,1,0:T(8,128)(2,1)S(1)}, u32[]{:S(2)}, u32[]{:S(2)}) collective-permute-start(bf16[36,256,128]{2,1,0:T(8,128)(2,1)} %shard_map.59), channel_id=1, source_target_pairs={{0,2},{1,3},{2,0},{3,1},{4,6},{5,7},{6,4},{7,5},{8,10},{9,11},{10,... | collective-permute-start | bytes 7077896 | tf_op jit(solution)/shard_map/ppermute | solution.py:286
  6.8 5.1 %constant_dynamic-slice_fusion = (bf16[36,256,128]{2,1,0:T(8,128)(2,1)}, bf16[36,256,128]{2,1,0:T(8,128)(2,1)}) fusion(bf16[256,256,128]{2,1,0:T(8,128)(2,1)} %refs_4_.1, s32[]{:T(128)S(6)} %select_n.34, s32[]{:T(128)S(6)} %select_n.33), kind=kLoop, calls=%fused_computation.5 | loop fusion | bytes 9437192 | tf_op jit(solution)/shard_map/dynamic_slice | solution.py:296
  12.0 2.0 constant_dynamic-slice_fusion.2
  14.1 4.7 %constant_dynamic-slice_fusion.5 = (bf16[24,256,128]{2,1,0:T(8,128)(2,1)}, bf16[24,256,128]{2,1,0:T(8,128)(2,1)}, bf16[24,256,128]{2,1,0:T(8,128)(2,1)}) fusion(bf16[256,256,128]{2,1,0:T(8,128)(2,1)} %refs_4_.1, s32[]{:T(128)S(6)} %select_n.29, s32[]{:T(128)S(6)} %select_n.28, s32[]{:T(128)S(6)} %select_n.27), kind=kLoop, calls=%fused_computation.10 | loop fusion | bytes 9437196 | tf_op jit(solution)/shard_map/dynamic_slice | solution.py:296
  18.7 40.3 %collective-permute-done.refs_3_.refs_6_ = bf16[36,256,128]{2,1,0:T(8,128)(2,1)S(1)} collective-permute-done((bf16[36,256,128]{2,1,0:T(8,128)(2,1)}, bf16[36,256,128]{2,1,0:T(8,128)(2,1)S(1)}, u32[]{:S(2)}, u32[]{:S(2)}) %collective-permute-start) | collective-permute-done | bytes 2359328 | tf_op jit(solution)/shard_map/ppermute | solution.py:286
  59.1 13.5 %all_to_all.25 = f32[8,16,256]{2,1,0:T(8,128)S(1)} all-to-all(f32[8,16,256]{2,1,0:T(8,128)S(1)} %broadcast_in_dim.21), channel_id=1, replica_groups=mesh['aux'=8,'vir'=4] {'aux'}, dimensions={0} | all-to-all | bytes 262144 | tf_op jit(solution)/shard_map/all_to_all | solution.py:266
  74.2 37.6 %collective-permute-done.1 = f32[1,129,256]{2,1,0:T(8,128)S(1)} collective-permute-done((f32[1,129,256]{2,1,0:T(8,128)S(1)}, f32[1,129,256]{2,1,0:T(8,128)S(1)}, u32[]{:S(2)}, u32[]{:S(2)}) %collective-permute-start.1) | collective-permute-done | bytes 132128 | tf_op jit(solution)/shard_map/ppermute | solution.py:286
  112.4 1.7 collective-permute-start.6
  115.7 7.4 %shard_map.60.refs_1_ = f32[1024,128]{1,0:T(8,128)S(1)} custom-call(s32[6]{0:T(128)S(1)} %stack.35.order_ref, bf16[4,128,256]{2,1,0:T(8,128)(2,1)S(1)} %slice.20.refs_0_, bf16[256,256,128]{2,1,0:T(8,128)(2,1)} %refs_4_.1, bf16[36,256,128]{2,1,0:T(8,128)(2,1)} %collective-permute-done.3.refs_2_.refs_5_, ...), custom_call_target="tpu_custom_call" | custom-call | tf_op jit(solution)/shard_map/pallas_call | solution.py:172
  125.4 24.5 %collective-permute-done.6.refs_4_.refs_9_ = bf16[24,256,128]{2,1,0:T(8,128)(2,1)} collective-permute-done((bf16[24,256,128]{2,1,0:T(8,128)(2,1)}, bf16[24,256,128]{2,1,0:T(8,128)(2,1)}, u32[]{:S(2)}, u32[]{:S(2)}) %collective-permute-start.6) | collective-permute-done | bytes 1572896 | tf_op jit(solution)/shard_map/ppermute | solution.py:286
  149.9 33.0 %collective-permute-done.7.refs_5_.refs_10_ = bf16[24,256,128]{2,1,0:T(8,128)(2,1)} collective-permute-done((bf16[24,256,128]{2,1,0:T(8,128)(2,1)}, bf16[24,256,128]{2,1,0:T(8,128)(2,1)}, u32[]{:S(2)}, u32[]{:S(2)}) %collective-permute-start.7) | collective-permute-done | bytes 1572896 | tf_op jit(solution)/shard_map/ppermute | solution.py:286
  182.9 5.4 %shard_map.61.refs_1_ = f32[1024,128]{1,0:T(8,128)S(1)} custom-call(s32[6]{0:T(128)S(1)} %stack.35.order_ref, bf16[4,128,256]{2,1,0:T(8,128)(2,1)S(1)} %slice.20.refs_0_, f32[1024,128]{1,0:T(8,128)S(1)} %shard_map.60.refs_1_, bf16[256,256,128]{2,1,0:T(8,128)(2,1)} %refs_4_.1, bf16[24,256,128]{2,1,0:T(8,128)(2,1)} %collective-permute-done.5.refs_3_.refs_8_, ...), custom_call_target="tpu_custom_call" | custom-call | tf_op jit(solution)/shard_map/pallas_call | solution.py:172
  188.4 5.5 %collective-permute-done.9.refs_4_.refs_12_ = bf16[4,256,128]{2,1,0:T(8,128)(2,1)S(1)} collective-permute-done((bf16[4,256,128]{2,1,0:T(8,128)(2,1)S(1)}, bf16[4,256,128]{2,1,0:T(8,128)(2,1)S(1)}, u32[]{:S(2)}, u32[]{:S(2)}) %collective-permute-start.9) | collective-permute-done | bytes 262176 | tf_op jit(solution)/shard_map/ppermute | solution.py:286
  193.9 2.5 shard_map.62
  196.4 16.6 %all_to_all.26.terms_ref = bf16[32,16,256]{2,1,0:T(8,128)(2,1)} all-to-all(bf16[32,16,256]{2,1,0:T(8,128)(2,1)S(1)} %bitcast.20), channel_id=1, replica_groups=mesh['aux'=8,'vir'=4] {'aux','vir'}, dimensions={0} | all-to-all | bytes 524288 | tf_op jit(solution)/shard_map/all_to_all | solution.py:364
  213.0 1.7 shard_map.63
  214.7 2.6 all-to-all-start.2
  217.5 10.4 %all-to-all-done.2.refs_0_ = bf16[32,16,256]{2,1,0:T(8,128)(2,1)S(1)} async-done(((bf16[32,16,256]{2,1,0:T(8,128)(2,1)}), bf16[32,16,256]{2,1,0:T(8,128)(2,1)S(1)}, u32[]{:S(2)}, u32[]{:S(2)}) %all-to-all-start.2) | async-done | bytes 262176 | tf_op jit(solution)/shard_map/all_to_all | solution.py:368
  227.9 11.1 %shard_map.64 = (bf16[8,4,16,256]{3,2,1,0:T(8,128)(2,1)}, f32[16,256]{1,0:T(8,128)S(1)}, f32[1,128]{1,0:T(1,128)S(1)}) custom-call(s32[6]{0:T(128)S(1)} %stack.35.order_ref, bf16[32,16,256]{2,1,0:T(8,128)(2,1)S(1)} %all-to-all-done.2.refs_0_, f32[4,128,256]{2,1,0:T(8,128)S(1)} %slice.18.refs_1_, f32[4,1,256]{2,1,0:T(1,128)S(1)} %pad_maximum_fusion.2.refs_2_, ...), custom_call_target="tpu_custom_call" | custom-call | tf_op jit(solution)/shard_map/pallas_call | solution.py:172
  239.6 2.6 all-to-all-start.3
  242.3 10.4 %all-to-all-done.3.terms_ref = bf16[32,16,256]{2,1,0:T(8,128)(2,1)S(1)} async-done(((bf16[32,16,256]{2,1,0:T(8,128)(2,1)}), bf16[32,16,256]{2,1,0:T(8,128)(2,1)S(1)}, u32[]{:S(2)}, u32[]{:S(2)}) %all-to-all-start.3) | async-done | bytes 262176 | tf_op jit(solution)/shard_map/all_to_all | solution.py:364
  253.6 9.3 %all_to_all.27.sums_ref = f32[32,1,128]{2,1,0:T(1,128)} all-to-all(f32[32,1,128]{2,1,0:T(1,128)S(1)} %get-tuple-element.42), channel_id=1, replica_groups=mesh['aux'=8,'vir'=4] {'aux','vir'}, dimensions={0} | all-to-all | bytes 32768 | tf_op jit(solution)/shard_map/all_to_all | solution.py:371
  262.9 1.7 shard_map.66
  (54 shorter events, 7.9 us)
Async XLA Ops:
  3.7 55.3 %collective-permute-start = (bf16[36,256,128]{2,1,0:T(8,128)(2,1)}, bf16[36,256,128]{2,1,0:T(8,128)(2,1)S(1)}, u32[]{:S(2)}, u32[]{:S(2)}) collective-permute-start(bf16[36,256,128]{2,1,0:T(8,128)(2,1)} %shard_map.59), channel_id=1, source_target_pairs={{0,2},{1,3},{2,0},{3,1},{4,6},{5,7},{6,4},{7,5},{8,10},{9,11},{10,... | collective-permute-start | bytes 7077896 | tf_op jit(solution)/shard_map/ppermute | solution.py:286
  11.9 103.3 %collective-permute-start.3 = (bf16[36,256,128]{2,1,0:T(8,128)(2,1)}, bf16[36,256,128]{2,1,0:T(8,128)(2,1)}, u32[]{:S(2)}, u32[]{:S(2)}) collective-permute-start(bf16[36,256,128]{2,1,0:T(8,128)(2,1)} %get-tuple-element.47), channel_id=1, source_target_pairs={{0,1},{1,0},{2,3},{3,2},{4,5},{5,4},{6,7},{7,6},{8,9},{9,8},{10,11... | collective-permute-start | bytes 7077896 | tf_op jit(solution)/shard_map/ppermute | solution.py:286
  11.9 103.8 %collective-permute-start.4 = (bf16[36,256,128]{2,1,0:T(8,128)(2,1)}, bf16[36,256,128]{2,1,0:T(8,128)(2,1)}, u32[]{:S(2)}, u32[]{:S(2)}) collective-permute-start(bf16[36,256,128]{2,1,0:T(8,128)(2,1)} %get-tuple-element.46), channel_id=1, source_target_pairs={{0,3},{1,2},{2,1},{3,0},{4,7},{5,6},{6,5},{7,4},{8,11},{9,10},{10,... | collective-permute-start | bytes 7077896 | tf_op jit(solution)/shard_map/ppermute | solution.py:286
  14.1 45.0 %copy-start.10 = (f32[1,256,16]{1,2,0:T(8,128)S(1)}, f32[1,256,16]{1,2,0:T(8,128)}, u32[]{:S(2)}) copy-start(f32[1,256,16]{1,2,0:T(8,128)} %param.5) | copy-start | bytes 49156
  14.1 58.5 %copy-start.11 = (f32[256]{0:T(256)S(1)}, f32[256]{0:T(256)}, u32[]{:S(2)}) copy-start(f32[256]{0:T(256)} %param.7) | copy-start | bytes 3076
  59.1 64.1 %copy-start = (bf16[36,256,128]{2,1,0:T(8,128)(2,1)}, bf16[36,256,128]{2,1,0:T(8,128)(2,1)S(1)}, u32[]{:S(2)}) copy-start(bf16[36,256,128]{2,1,0:T(8,128)(2,1)S(1)} %collective-permute-done.refs_3_.refs_6_) | copy-start | bytes 7077892
  72.6 39.2 %collective-permute-start.1 = (f32[1,129,256]{2,1,0:T(8,128)S(1)}, f32[1,129,256]{2,1,0:T(8,128)S(1)}, u32[]{:S(2)}, u32[]{:S(2)}) collective-permute-start(f32[1,129,256]{2,1,0:T(8,128)S(1)} %maximum_bitcast_fusion), channel_id=1, source_target_pairs={{0,2},{1,3},{2,0},{3,1},{4,6},{5,7},{6,4},{7,5},{8,10},{9,11},{10,... | collective-permute-start | bytes 396296 | tf_op jit(solution)/shard_map/ppermute | solution.py:286
  111.8 2.3 collective-permute-start.2
  111.9 12.4 %collective-permute-start.5 = (bf16[24,256,128]{2,1,0:T(8,128)(2,1)}, bf16[24,256,128]{2,1,0:T(8,128)(2,1)}, u32[]{:S(2)}, u32[]{:S(2)}) collective-permute-start(bf16[24,256,128]{2,1,0:T(8,128)(2,1)} %get-tuple-element.33), channel_id=1, source_target_pairs={{0,1},{1,0},{2,3},{3,2},{4,5},{5,4},{6,7},{7,6},{8,9},{9,8},{10,11... | collective-permute-start | bytes 4718600 | tf_op jit(solution)/shard_map/ppermute | solution.py:286
  112.4 37.6 %collective-permute-start.6 = (bf16[24,256,128]{2,1,0:T(8,128)(2,1)}, bf16[24,256,128]{2,1,0:T(8,128)(2,1)}, u32[]{:S(2)}, u32[]{:S(2)}) collective-permute-start(bf16[24,256,128]{2,1,0:T(8,128)(2,1)} %get-tuple-element.34), channel_id=1, source_target_pairs={{0,2},{1,3},{2,0},{3,1},{4,6},{5,7},{6,4},{7,5},{8,10},{9,11},{10,... | collective-permute-start | bytes 4718600 | tf_op jit(solution)/shard_map/ppermute | solution.py:286
  114.1 68.8 %collective-permute-start.7 = (bf16[24,256,128]{2,1,0:T(8,128)(2,1)}, bf16[24,256,128]{2,1,0:T(8,128)(2,1)}, u32[]{:S(2)}, u32[]{:S(2)}) collective-permute-start(bf16[24,256,128]{2,1,0:T(8,128)(2,1)} %get-tuple-element.35), channel_id=1, source_target_pairs={{0,3},{1,2},{2,1},{3,0},{4,7},{5,6},{6,5},{7,4},{8,11},{9,10},{10,... | collective-permute-start | bytes 4718600 | tf_op jit(solution)/shard_map/ppermute | solution.py:286
  115.0 0.7 copy-start.5
  115.0 0.7 copy-start.3
  115.1 8.1 %copy-start.9 = (bf16[4,256,128]{2,1,0:T(8,128)(2,1)S(1)}, bf16[4,256,128]{2,1,0:T(8,128)(2,1)}, u32[]{:S(2)}) copy-start(bf16[4,256,128]{2,1,0:T(8,128)(2,1)} %get-tuple-element.38) | copy-start | bytes 786436
  115.1 9.1 %copy-start.8 = (bf16[4,256,128]{2,1,0:T(8,128)(2,1)S(1)}, bf16[4,256,128]{2,1,0:T(8,128)(2,1)}, u32[]{:S(2)}) copy-start(bf16[4,256,128]{2,1,0:T(8,128)(2,1)} %get-tuple-element.36) | copy-start | bytes 786436
  115.1 9.1 %copy-start.7 = (bf16[4,256,128]{2,1,0:T(8,128)(2,1)S(1)}, bf16[4,256,128]{2,1,0:T(8,128)(2,1)}, u32[]{:S(2)}) copy-start(bf16[4,256,128]{2,1,0:T(8,128)(2,1)} %get-tuple-element.37) | copy-start | bytes 786436
  123.2 65.2 %collective-permute-start.10 = (bf16[4,256,128]{2,1,0:T(8,128)(2,1)S(1)}, bf16[4,256,128]{2,1,0:T(8,128)(2,1)S(1)}, u32[]{:S(2)}, u32[]{:S(2)}) collective-permute-start(bf16[4,256,128]{2,1,0:T(8,128)(2,1)S(1)} %copy-done.9), channel_id=1, source_target_pairs={{0,3},{1,2},{2,1},{3,0},{4,7},{5,6},{6,5},{7,4},{8,11},{9,10},{10,... | collective-permute-start | bytes 786440 | tf_op jit(solution)/shard_map/ppermute | solution.py:286
  124.2 64.2 %collective-permute-start.8 = (bf16[4,256,128]{2,1,0:T(8,128)(2,1)S(1)}, bf16[4,256,128]{2,1,0:T(8,128)(2,1)S(1)}, u32[]{:S(2)}, u32[]{:S(2)}) collective-permute-start(bf16[4,256,128]{2,1,0:T(8,128)(2,1)S(1)} %copy-done.8), channel_id=1, source_target_pairs={{0,1},{1,0},{2,3},{3,2},{4,5},{5,4},{6,7},{7,6},{8,9},{9,8},{10,11... | collective-permute-start | bytes 786440 | tf_op jit(solution)/shard_map/ppermute | solution.py:286
  124.2 69.7 %collective-permute-start.9 = (bf16[4,256,128]{2,1,0:T(8,128)(2,1)S(1)}, bf16[4,256,128]{2,1,0:T(8,128)(2,1)S(1)}, u32[]{:S(2)}, u32[]{:S(2)}) collective-permute-start(bf16[4,256,128]{2,1,0:T(8,128)(2,1)S(1)} %copy-done.7), channel_id=1, source_target_pairs={{0,2},{1,3},{2,0},{3,1},{4,6},{5,7},{6,4},{7,5},{8,10},{9,11},{10,... | collective-permute-start | bytes 786440 | tf_op jit(solution)/shard_map/ppermute | solution.py:286
  188.3 29.0 %copy-start.12 = (f32[128]{0:T(128)S(1)}, f32[128]{0:T(128)}, u32[]{:S(2)}) copy-start(f32[128]{0:T(128)} %param.6) | copy-start | bytes 1540
  196.4 21.1 %copy-start.4 = (f32[1,129,256]{2,1,0:T(8,128)S(1)}, f32[1,129,256]{2,1,0:T(8,128)}, u32[]{:S(2)}) copy-start(f32[1,129,256]{2,1,0:T(8,128)} %copy-done.3) | copy-start | bytes 396292
  196.4 21.1 %copy-start.6 = (f32[1,129,256]{2,1,0:T(8,128)S(1)}, f32[1,129,256]{2,1,0:T(8,128)}, u32[]{:S(2)}) copy-start(f32[1,129,256]{2,1,0:T(8,128)} %copy-done.5) | copy-start | bytes 396292
  214.7 13.2 %all-to-all-start.2 = ((bf16[32,16,256]{2,1,0:T(8,128)(2,1)}), bf16[32,16,256]{2,1,0:T(8,128)(2,1)S(1)}, u32[]{:S(2)}, u32[]{:S(2)}) async-start(bf16[32,16,256]{2,1,0:T(8,128)(2,1)} %shard_map.63), calls=%async_computation.2 | async-start | bytes 524288 | tf_op jit(solution)/shard_map/all_to_all | solution.py:368
  239.6 13.2 %all-to-all-start.3 = ((bf16[32,16,256]{2,1,0:T(8,128)(2,1)}), bf16[32,16,256]{2,1,0:T(8,128)(2,1)S(1)}, u32[]{:S(2)}, u32[]{:S(2)}) async-start(bf16[32,16,256]{2,1,0:T(8,128)(2,1)} %bitcast.13), calls=%async_computation.3 | async-start | bytes 524288 | tf_op jit(solution)/shard_map/all_to_all | solution.py:364
  (2 other events, 1.2 us)

commit v11 on v10

--- a/solution.py
+++ b/solution.py
@@ -79,8 +79,8 @@
     acc_ref[...] = carry_ref[...] if carried else jnp.zeros_like(acc_ref)
     if stepping:
         shares_ref, trial_ref, vir_ref, occ_ref = first_refs
-        own_ref, shift_ref = out_refs[1:]
-        share = own_ref.shape[0]
+        own_ref = out_refs[1]
+        share = own_ref.shape[0] - 1
         coupling = jnp.concatenate(
             [
                 shares_ref[r * nv + order_ref[k]].astype(jnp.float32)
@@ -92,7 +92,7 @@
         gap = jnp.concatenate([vir_ref[k] - occ_ref[...] for k in range(nv)], axis=0)
         diff, scaled, sums = five_sums(trial_ref[...].reshape(nv * occ, width), gap, coupling)
         fresh, shift = finish(diff, scaled, sums, total)
-        shift_ref[...] = jnp.broadcast_to(shift, shift_ref.shape)
+        own_ref[share:, :] = jnp.broadcast_to(shift, (1, width))
         for k in range(nv):
             rows = fresh[k * occ : (k + 1) * occ]
             xt_ref[:, k * width : (k + 1) * width] = rows.astype(jnp.bfloat16)
@@ -100,7 +100,7 @@
         for r in range(1, occ // share):
             rows = fresh[r * share : (r + 1) * share]
             mine = jnp.where(order_ref[nv + 1] == r, rows, mine)
-        own_ref[...] = mine
+        own_ref[:share, :] = mine
     else:
         for k in range(nv):
             xt_ref[:, k * width : (k + 1) * width] = first_refs[0][k]
@@ -163,8 +163,7 @@
     else:
         out = [jax.ShapeDtypeStruct((aux_count, nv, occ // aux_count, width), jnp.bfloat16)]
     if stepping:
-        out.append(jax.ShapeDtypeStruct((occ // aux_count, width), jnp.float32))
-        out.append(jax.ShapeDtypeStruct((1, 128), jnp.float32))
+        out.append(jax.ShapeDtypeStruct((occ // aux_count + 1, width), jnp.float32))
     in_vmem, in_hbm = pl.BlockSpec(memory_space=pltpu.VMEM), pl.BlockSpec(memory_space=pltpu.HBM)
     body = functools.partial(
         contract_body, nv, placed, size, own, carried, stepping, nv * width * occ
@@ -192,16 +191,18 @@
 
     def body(terms_ref, trial_ref, gap_ref, ratios_ref, sums_ref):
         coupling = jnp.sum(terms_ref[...].astype(jnp.float32), axis=0)
-        diff, scaled, sums = five_sums(trial_ref[...], gap_ref[...], coupling)
+        share = gap_ref.shape[0]
+        diff, scaled, sums = five_sums(trial_ref[:share, :], gap_ref[...], coupling)
         ratios_ref[0] = diff
         ratios_ref[1] = scaled
+        ratios_ref[2] = jnp.broadcast_to(trial_ref[share:, :], diff.shape)
         lane = lax.broadcasted_iota(jnp.int32, (1, 128), 1)
         row = jnp.zeros((1, 128), jnp.float32)
         for at, value in enumerate(sums):
             row = jnp.where(lane == at, value, row)
         sums_ref[...] = jnp.broadcast_to(row[None], sums_ref.shape)
 
-    ratios = jax.ShapeDtypeStruct((2, *trial.shape), jnp.float32)
+    ratios = jax.ShapeDtypeStruct((3, *gap.shape), jnp.float32)
     return pl.pallas_call(
         body,
         out_shape=(ratios, jax.ShapeDtypeStruct((count, 1, 128), jnp.float32)),
@@ -209,14 +210,14 @@
     )(terms, trial, gap)
 
 
-def step_share(ratios, all_sums, before, total):
-    def body(ratios_ref, sums_ref, before_ref, next_ref, shifts_ref):
+def step_share(ratios, all_sums, total):
+    def body(ratios_ref, sums_ref, next_ref, shifts_ref):
         row = jnp.sum(sums_ref[...], axis=0)
         fresh, shift = finish(
             ratios_ref[0], ratios_ref[1], [row[:, at : at + 1] for at in range(5)], total
         )
         next_ref[...] = fresh
-        shifts_ref[...] = jnp.concatenate([before_ref[:, :1], shift], axis=1)
+        shifts_ref[...] = jnp.concatenate([ratios_ref[2, :1, :1], shift], axis=1)
 
     return pl.pallas_call(
         body,
@@ -224,7 +225,7 @@
             jax.ShapeDtypeStruct(ratios.shape[1:], jnp.float32),
             jax.ShapeDtypeStruct((1, 2), jnp.float32),
         ),
-    )(ratios, all_sums, before)
+    )(ratios, all_sums)
 
 
 def share_copies(terms):
@@ -351,7 +352,7 @@
         middle = (low + high) // 2
         last_block = [[(high, end)]]
         (carry,) = call([xt], [[part] for part in parts])
-        cuts, carry = lax.optimization_barrier((later[1], carry))
+        cuts, carry = after_newest(2, later[1], carry)
         for k, cut in zip(far, cuts):
             exchange(k, high, end, cut)
         (carry,) = call([xt], [[(low, middle)], [(middle, high)]], carry)
@@ -366,10 +367,10 @@
     (partial,) = call([xt], last_block, carry, na)
     copies = share_copies(sum_terms(partial))
     first = [lax.all_to_all(copies, EVERY, 0, 0, tiled=True), trial, state[:, occ:], occ_energy[:, None]]
-    partial, trial_own, before = call(first, blocks, None, na)
+    partial, trial_own = call(first, blocks, None, na)
     ratios, sums = share_sums(sum_terms(partial), trial_own, gap_own)
     sums = lax.all_to_all(sums, EVERY, 0, 0, tiled=True)
-    fresh, shifts = step_share(ratios, sums, before, total)
+    fresh, shifts = step_share(ratios, sums, total)
     return (fresh.T[None], shifts.T)
 
 

time: 265 us -> 265 us (level)
  no operation moved by 1% of the time
where the time goes in v11:
time: 265 us; the launch traced here: 264 us
  waiting for transfers between devices  162 us (61%)
  blocking collectives  39.5 us (15%)
  Pallas kernels  33.1 us (12%)
  starting transfers between devices  15.2 us (6%)
  local copies, waits for them, and re-layouts  12.8 us (5%)
    ppermute x11, waiting for transfers between devices, send(): lax.ppermute(value, 'vir', [(one, partner(one, k)) for one in range(nv)])  142 us
    pallas_call x4, Pallas kernels, contract(): pl.pallas_call(body, in_specs=[pl.BlockSpec(memory_space=pltpu.SMEM)] + [...  26.4 us
    all_to_all x1, blocking collectives, sum_terms(): lax.all_to_all(partial.reshape(count, share, width), EVERY, 0, 0, tiled=T...  16.6 us
    all_to_all x1, blocking collectives, spread(): return lax.all_to_all(copies, axes, 0, 0, tiled=True)  13.5 us
    dynamic_slice x3, local copies, waits for them, and re-layouts, piece(): lax.dynamic_slice_in_dim(whole, partner(vir_at, k) * own + low, high - lo...  11.8 us
    all_to_all x1, waiting for transfers between devices, sum_terms(): lax.all_to_all(partial.reshape(count, share, width), EVERY, 0, 0, tiled=T...  10.4 us
    all_to_all x1, waiting for transfers between devices, local(): lax.all_to_all(copies, EVERY, 0, 0, tiled=True)  10.4 us
    ppermute x11, starting transfers between devices, send(): lax.ppermute(value, 'vir', [(one, partner(one, k)) for one in range(nv)])  10 us
  transfers between devices with their start and end apart: 13, of which 8 were waited for; matrix products, arithmetic and copies ran while one was open for 5% of the time, Pallas kernels for 5%

profile of v11, /device:TPU:0, one launch (start us, length us, event | category | flops | bytes accessed | tf_op | source)
XLA Modules:
  0.0 264.0 jit_solution(11807888459893211285)
XLA Ops:
  0.6 3.1 %shard_map.59 = bf16[36,256,128]{2,1,0:T(8,128)(2,1)} custom-call(s32[1]{0:T(128)} %bitcast.5.start_ref, bf16[256,256,128]{2,1,0:T(8,128)(2,1)} %refs_4_.1), custom_call_target="tpu_custom_call" | custom-call | tf_op jit(solution)/shard_map/pallas_call | solution.py:255
  3.7 3.0 %collective-permute-start = (bf16[36,256,128]{2,1,0:T(8,128)(2,1)}, bf16[36,256,128]{2,1,0:T(8,128)(2,1)S(1)}, u32[]{:S(2)}, u32[]{:S(2)}) collective-permute-start(bf16[36,256,128]{2,1,0:T(8,128)(2,1)} %shard_map.59), channel_id=1, source_target_pairs={{0,2},{1,3},{2,0},{3,1},{4,6},{5,7},{6,4},{7,5},{8,10},{9,11},{10,... | collective-permute-start | bytes 7077896 | tf_op jit(solution)/shard_map/ppermute | solution.py:287
  6.8 5.1 %constant_dynamic-slice_fusion = (bf16[36,256,128]{2,1,0:T(8,128)(2,1)}, bf16[36,256,128]{2,1,0:T(8,128)(2,1)}) fusion(bf16[256,256,128]{2,1,0:T(8,128)(2,1)} %refs_4_.1, s32[]{:T(128)S(6)} %select_n.34, s32[]{:T(128)S(6)} %select_n.33), kind=kLoop, calls=%fused_computation.5 | loop fusion | bytes 9437192 | tf_op jit(solution)/shard_map/dynamic_slice | solution.py:297
  12.0 2.0 constant_dynamic-slice_fusion.2
  14.0 4.7 %constant_dynamic-slice_fusion.5 = (bf16[24,256,128]{2,1,0:T(8,128)(2,1)}, bf16[24,256,128]{2,1,0:T(8,128)(2,1)}, bf16[24,256,128]{2,1,0:T(8,128)(2,1)}) fusion(bf16[256,256,128]{2,1,0:T(8,128)(2,1)} %refs_4_.1, s32[]{:T(128)S(6)} %select_n.29, s32[]{:T(128)S(6)} %select_n.28, s32[]{:T(128)S(6)} %select_n.27), kind=kLoop, calls=%fused_computation.10 | loop fusion | bytes 9437196 | tf_op jit(solution)/shard_map/dynamic_slice | solution.py:297
  18.7 40.3 %collective-permute-done.refs_3_.refs_6_ = bf16[36,256,128]{2,1,0:T(8,128)(2,1)S(1)} collective-permute-done((bf16[36,256,128]{2,1,0:T(8,128)(2,1)}, bf16[36,256,128]{2,1,0:T(8,128)(2,1)S(1)}, u32[]{:S(2)}, u32[]{:S(2)}) %collective-permute-start) | collective-permute-done | bytes 2359328 | tf_op jit(solution)/shard_map/ppermute | solution.py:287
  59.1 13.5 %all_to_all.25 = f32[8,16,256]{2,1,0:T(8,128)S(1)} all-to-all(f32[8,16,256]{2,1,0:T(8,128)S(1)} %broadcast_in_dim.21), channel_id=1, replica_groups=mesh['aux'=8,'vir'=4] {'aux'}, dimensions={0} | all-to-all | bytes 262144 | tf_op jit(solution)/shard_map/all_to_all | solution.py:267
  74.1 37.6 %collective-permute-done.1 = f32[1,129,256]{2,1,0:T(8,128)S(1)} collective-permute-done((f32[1,129,256]{2,1,0:T(8,128)S(1)}, f32[1,129,256]{2,1,0:T(8,128)S(1)}, u32[]{:S(2)}, u32[]{:S(2)}) %collective-permute-start.1) | collective-permute-done | bytes 132128 | tf_op jit(solution)/shard_map/ppermute | solution.py:287
  111.9 1.8 collective-permute-start.5
  115.1 7.4 %shard_map.60.refs_1_ = f32[1024,128]{1,0:T(8,128)S(1)} custom-call(s32[6]{0:T(128)S(1)} %stack.35.order_ref, bf16[4,128,256]{2,1,0:T(8,128)(2,1)S(1)} %slice.20.refs_0_, bf16[256,256,128]{2,1,0:T(8,128)(2,1)} %refs_4_.1, bf16[36,256,128]{2,1,0:T(8,128)(2,1)} %collective-permute-done.3.refs_2_.refs_5_, ...), custom_call_target="tpu_custom_call" | custom-call | tf_op jit(solution)/shard_map/pallas_call | solution.py:171
  122.6 26.8 %collective-permute-done.5.refs_4_.refs_9_ = bf16[24,256,128]{2,1,0:T(8,128)(2,1)} collective-permute-done((bf16[24,256,128]{2,1,0:T(8,128)(2,1)}, bf16[24,256,128]{2,1,0:T(8,128)(2,1)}, u32[]{:S(2)}, u32[]{:S(2)}) %collective-permute-start.5) | collective-permute-done | bytes 1572896 | tf_op jit(solution)/shard_map/ppermute | solution.py:287
  151.6 30.8 %collective-permute-done.7.refs_5_.refs_10_ = bf16[24,256,128]{2,1,0:T(8,128)(2,1)} collective-permute-done((bf16[24,256,128]{2,1,0:T(8,128)(2,1)}, bf16[24,256,128]{2,1,0:T(8,128)(2,1)}, u32[]{:S(2)}, u32[]{:S(2)}) %collective-permute-start.7) | collective-permute-done | bytes 1572896 | tf_op jit(solution)/shard_map/ppermute | solution.py:287
  182.4 5.4 %shard_map.61.refs_1_ = f32[1024,128]{1,0:T(8,128)S(1)} custom-call(s32[6]{0:T(128)S(1)} %stack.35.order_ref, bf16[4,128,256]{2,1,0:T(8,128)(2,1)S(1)} %slice.20.refs_0_, f32[1024,128]{1,0:T(8,128)S(1)} %shard_map.60.refs_1_, bf16[256,256,128]{2,1,0:T(8,128)(2,1)} %refs_4_.1, bf16[24,256,128]{2,1,0:T(8,128)(2,1)} %collective-permute-done.6.refs_3_.refs_8_, ...), custom_call_target="tpu_custom_call" | custom-call | tf_op jit(solution)/shard_map/pallas_call | solution.py:171
  187.9 5.9 %collective-permute-done.9.refs_4_.refs_12_ = bf16[4,256,128]{2,1,0:T(8,128)(2,1)S(1)} collective-permute-done((bf16[4,256,128]{2,1,0:T(8,128)(2,1)S(1)}, bf16[4,256,128]{2,1,0:T(8,128)(2,1)S(1)}, u32[]{:S(2)}, u32[]{:S(2)}) %collective-permute-start.9) | collective-permute-done | bytes 262176 | tf_op jit(solution)/shard_map/ppermute | solution.py:287
  193.8 2.5 shard_map.62
  196.3 16.6 %all_to_all.26.terms_ref = bf16[32,16,256]{2,1,0:T(8,128)(2,1)} all-to-all(bf16[32,16,256]{2,1,0:T(8,128)(2,1)S(1)} %bitcast.20), channel_id=1, replica_groups=mesh['aux'=8,'vir'=4] {'aux','vir'}, dimensions={0} | all-to-all | bytes 524288 | tf_op jit(solution)/shard_map/all_to_all | solution.py:365
  212.9 1.7 shard_map.63
  214.6 2.6 all-to-all-start.2
  217.4 10.4 %all-to-all-done.2.refs_0_ = bf16[32,16,256]{2,1,0:T(8,128)(2,1)S(1)} async-done(((bf16[32,16,256]{2,1,0:T(8,128)(2,1)}), bf16[32,16,256]{2,1,0:T(8,128)(2,1)S(1)}, u32[]{:S(2)}, u32[]{:S(2)}) %all-to-all-start.2) | async-done | bytes 262176 | tf_op jit(solution)/shard_map/all_to_all | solution.py:369
  227.8 11.1 %shard_map.64 = (bf16[8,4,16,256]{3,2,1,0:T(8,128)(2,1)}, f32[17,256]{1,0:T(8,128)S(1)}) custom-call(s32[6]{0:T(128)S(1)} %stack.35.order_ref, bf16[32,16,256]{2,1,0:T(8,128)(2,1)S(1)} %all-to-all-done.2.refs_0_, f32[4,128,256]{2,1,0:T(8,128)S(1)} %slice.18.refs_1_, f32[4,1,256]{2,1,0:T(1,128)S(1)} %pad_maximum_fusion.2.refs_2_, f32[128,1]{1,0:T(8,128)S(1)} %copy.6.refs_3_, ...), custom_call_target="tpu_custom_call" | custom-call | tf_op jit(solution)/shard_map/pallas_call | solution.py:171
  238.9 2.6 all-to-all-start.3
  241.7 10.4 %all-to-all-done.3.terms_ref = bf16[32,16,256]{2,1,0:T(8,128)(2,1)S(1)} async-done(((bf16[32,16,256]{2,1,0:T(8,128)(2,1)}), bf16[32,16,256]{2,1,0:T(8,128)(2,1)S(1)}, u32[]{:S(2)}, u32[]{:S(2)}) %all-to-all-start.3) | async-done | bytes 262176 | tf_op jit(solution)/shard_map/all_to_all | solution.py:365
  252.9 9.4 %all_to_all.27.sums_ref = f32[32,1,128]{2,1,0:T(1,128)} all-to-all(f32[32,1,128]{2,1,0:T(1,128)S(1)} %get-tuple-element.43), channel_id=1, replica_groups=mesh['aux'=8,'vir'=4] {'aux','vir'}, dimensions={0} | all-to-all | bytes 32768 | tf_op jit(solution)/shard_map/all_to_all | solution.py:372
  262.3 1.7 shard_map.66
  (44 shorter events, 6.6 us)
Async XLA Ops:
  3.7 55.3 %collective-permute-start = (bf16[36,256,128]{2,1,0:T(8,128)(2,1)}, bf16[36,256,128]{2,1,0:T(8,128)(2,1)S(1)}, u32[]{:S(2)}, u32[]{:S(2)}) collective-permute-start(bf16[36,256,128]{2,1,0:T(8,128)(2,1)} %shard_map.59), channel_id=1, source_target_pairs={{0,2},{1,3},{2,0},{3,1},{4,6},{5,7},{6,4},{7,5},{8,10},{9,11},{10,... | collective-permute-start | bytes 7077896 | tf_op jit(solution)/shard_map/ppermute | solution.py:287
  11.8 103.3 %collective-permute-start.3 = (bf16[36,256,128]{2,1,0:T(8,128)(2,1)}, bf16[36,256,128]{2,1,0:T(8,128)(2,1)}, u32[]{:S(2)}, u32[]{:S(2)}) collective-permute-start(bf16[36,256,128]{2,1,0:T(8,128)(2,1)} %get-tuple-element.47), channel_id=1, source_target_pairs={{0,1},{1,0},{2,3},{3,2},{4,5},{5,4},{6,7},{7,6},{8,9},{9,8},{10,11... | collective-permute-start | bytes 7077896 | tf_op jit(solution)/shard_map/ppermute | solution.py:287
  11.8 103.3 %collective-permute-start.4 = (bf16[36,256,128]{2,1,0:T(8,128)(2,1)}, bf16[36,256,128]{2,1,0:T(8,128)(2,1)}, u32[]{:S(2)}, u32[]{:S(2)}) collective-permute-start(bf16[36,256,128]{2,1,0:T(8,128)(2,1)} %get-tuple-element.46), channel_id=1, source_target_pairs={{0,3},{1,2},{2,1},{3,0},{4,7},{5,6},{6,5},{7,4},{8,11},{9,10},{10,... | collective-permute-start | bytes 7077896 | tf_op jit(solution)/shard_map/ppermute | solution.py:287
  14.0 45.0 %copy-start.5 = (f32[1,256,16]{1,2,0:T(8,128)S(1)}, f32[1,256,16]{1,2,0:T(8,128)}, u32[]{:S(2)}) copy-start(f32[1,256,16]{1,2,0:T(8,128)} %param.5) | copy-start | bytes 49156
  14.0 58.5 %copy-start.6 = (f32[256]{0:T(256)S(1)}, f32[256]{0:T(256)}, u32[]{:S(2)}) copy-start(f32[256]{0:T(256)} %param.7) | copy-start | bytes 3076
  59.0 63.5 %copy-start = (bf16[36,256,128]{2,1,0:T(8,128)(2,1)}, bf16[36,256,128]{2,1,0:T(8,128)(2,1)S(1)}, u32[]{:S(2)}) copy-start(bf16[36,256,128]{2,1,0:T(8,128)(2,1)S(1)} %collective-permute-done.refs_3_.refs_6_) | copy-start | bytes 7077892
  72.6 39.2 %collective-permute-start.1 = (f32[1,129,256]{2,1,0:T(8,128)S(1)}, f32[1,129,256]{2,1,0:T(8,128)S(1)}, u32[]{:S(2)}, u32[]{:S(2)}) collective-permute-start(f32[1,129,256]{2,1,0:T(8,128)S(1)} %maximum_bitcast_fusion), channel_id=1, source_target_pairs={{0,2},{1,3},{2,0},{3,1},{4,6},{5,7},{6,4},{7,5},{8,10},{9,11},{10,... | collective-permute-start | bytes 396296 | tf_op jit(solution)/shard_map/ppermute | solution.py:287
  111.8 2.0 collective-permute-start.2
  111.9 37.6 %collective-permute-start.5 = (bf16[24,256,128]{2,1,0:T(8,128)(2,1)}, bf16[24,256,128]{2,1,0:T(8,128)(2,1)}, u32[]{:S(2)}, u32[]{:S(2)}) collective-permute-start(bf16[24,256,128]{2,1,0:T(8,128)(2,1)} %get-tuple-element.32), channel_id=1, source_target_pairs={{0,2},{1,3},{2,0},{3,1},{4,6},{5,7},{6,4},{7,5},{8,10},{9,11},{10,... | collective-permute-start | bytes 4718600 | tf_op jit(solution)/shard_map/ppermute | solution.py:287
  113.7 37.9 %collective-permute-start.6 = (bf16[24,256,128]{2,1,0:T(8,128)(2,1)}, bf16[24,256,128]{2,1,0:T(8,128)(2,1)}, u32[]{:S(2)}, u32[]{:S(2)}) collective-permute-start(bf16[24,256,128]{2,1,0:T(8,128)(2,1)} %get-tuple-element.34), channel_id=1, source_target_pairs={{0,1},{1,0},{2,3},{3,2},{4,5},{5,4},{6,7},{7,6},{8,9},{9,8},{10,11... | collective-permute-start | bytes 4718600 | tf_op jit(solution)/shard_map/ppermute | solution.py:287
  113.8 68.6 %collective-permute-start.7 = (bf16[24,256,128]{2,1,0:T(8,128)(2,1)}, bf16[24,256,128]{2,1,0:T(8,128)(2,1)}, u32[]{:S(2)}, u32[]{:S(2)}) collective-permute-start(bf16[24,256,128]{2,1,0:T(8,128)(2,1)} %get-tuple-element.36), channel_id=1, source_target_pairs={{0,3},{1,2},{2,1},{3,0},{4,7},{5,6},{6,5},{7,4},{8,11},{9,10},{10,... | collective-permute-start | bytes 4718600 | tf_op jit(solution)/shard_map/ppermute | solution.py:287
  115.1 34.4 %copy-start.4 = (bf16[4,256,128]{2,1,0:T(8,128)(2,1)S(1)}, bf16[4,256,128]{2,1,0:T(8,128)(2,1)}, u32[]{:S(2)}) copy-start(bf16[4,256,128]{2,1,0:T(8,128)(2,1)} %get-tuple-element.39) | copy-start | bytes 786436
  115.1 34.9 %copy-start.3 = (bf16[4,256,128]{2,1,0:T(8,128)(2,1)S(1)}, bf16[4,256,128]{2,1,0:T(8,128)(2,1)}, u32[]{:S(2)}) copy-start(bf16[4,256,128]{2,1,0:T(8,128)(2,1)} %get-tuple-element.37) | copy-start | bytes 786436
  115.1 36.2 %copy-start.2 = (bf16[4,256,128]{2,1,0:T(8,128)(2,1)S(1)}, bf16[4,256,128]{2,1,0:T(8,128)(2,1)}, u32[]{:S(2)}) copy-start(bf16[4,256,128]{2,1,0:T(8,128)(2,1)} %get-tuple-element.38) | copy-start | bytes 786436
  149.4 38.5 %collective-permute-start.10 = (bf16[4,256,128]{2,1,0:T(8,128)(2,1)S(1)}, bf16[4,256,128]{2,1,0:T(8,128)(2,1)S(1)}, u32[]{:S(2)}, u32[]{:S(2)}) collective-permute-start(bf16[4,256,128]{2,1,0:T(8,128)(2,1)S(1)} %copy-done.4), channel_id=1, source_target_pairs={{0,3},{1,2},{2,1},{3,0},{4,7},{5,6},{6,5},{7,4},{8,11},{9,10},{10,... | collective-permute-start | bytes 786440 | tf_op jit(solution)/shard_map/ppermute | solution.py:287
  150.0 37.9 %collective-permute-start.8 = (bf16[4,256,128]{2,1,0:T(8,128)(2,1)S(1)}, bf16[4,256,128]{2,1,0:T(8,128)(2,1)S(1)}, u32[]{:S(2)}, u32[]{:S(2)}) collective-permute-start(bf16[4,256,128]{2,1,0:T(8,128)(2,1)S(1)} %copy-done.3), channel_id=1, source_target_pairs={{0,1},{1,0},{2,3},{3,2},{4,5},{5,4},{6,7},{7,6},{8,9},{9,8},{10,11... | collective-permute-start | bytes 786440 | tf_op jit(solution)/shard_map/ppermute | solution.py:287
  151.3 42.5 %collective-permute-start.9 = (bf16[4,256,128]{2,1,0:T(8,128)(2,1)S(1)}, bf16[4,256,128]{2,1,0:T(8,128)(2,1)S(1)}, u32[]{:S(2)}, u32[]{:S(2)}) collective-permute-start(bf16[4,256,128]{2,1,0:T(8,128)(2,1)S(1)} %copy-done.2), channel_id=1, source_target_pairs={{0,2},{1,3},{2,0},{3,1},{4,6},{5,7},{6,4},{7,5},{8,10},{9,11},{10,... | collective-permute-start | bytes 786440 | tf_op jit(solution)/shard_map/ppermute | solution.py:287
  187.8 29.4 %copy-start.7 = (f32[128]{0:T(128)S(1)}, f32[128]{0:T(128)}, u32[]{:S(2)}) copy-start(f32[128]{0:T(128)} %param.6) | copy-start | bytes 1540
  214.6 13.2 %all-to-all-start.2 = ((bf16[32,16,256]{2,1,0:T(8,128)(2,1)}), bf16[32,16,256]{2,1,0:T(8,128)(2,1)S(1)}, u32[]{:S(2)}, u32[]{:S(2)}) async-start(bf16[32,16,256]{2,1,0:T(8,128)(2,1)} %shard_map.63), calls=%async_computation.2 | async-start | bytes 524288 | tf_op jit(solution)/shard_map/all_to_all | solution.py:369
  238.9 13.2 %all-to-all-start.3 = ((bf16[32,16,256]{2,1,0:T(8,128)(2,1)}), bf16[32,16,256]{2,1,0:T(8,128)(2,1)S(1)}, u32[]{:S(2)}, u32[]{:S(2)}) async-start(bf16[32,16,256]{2,1,0:T(8,128)(2,1)} %bitcast.13), calls=%async_computation.3 | async-start | bytes 524288 | tf_op jit(solution)/shard_map/all_to_all | solution.py:365
  252.3 0.6 copy-start.1

commit v12 on v11

--- a/solution.py
+++ b/solution.py
@@ -237,7 +237,7 @@
 
 
 def cut_out(whole, start, count):
-    parts = 4
+    parts = next(n for n in (12, 9, 8, 4, 2, 1) if count % n == 0)
     rows = count // parts
 
     def body(start_ref, whole_ref, out_ref, sems):

time: 265 us -> 265 us (level)
  no operation moved by 1% of the time
where the time goes in v12:
time: 265 us; the launch traced here: 264 us
  waiting for transfers between devices  162 us (61%)
  blocking collectives  39.5 us (15%)
  Pallas kernels  33.2 us (13%)
  starting transfers between devices  15.2 us (6%)
  local copies, waits for them, and re-layouts  12.8 us (5%)
    ppermute x11, waiting for transfers between devices, send(): lax.ppermute(value, 'vir', [(one, partner(one, k)) for one in range(nv)])  142 us
    pallas_call x4, Pallas kernels, contract(): pl.pallas_call(body, in_specs=[pl.BlockSpec(memory_space=pltpu.SMEM)] + [...  26.4 us
    all_to_all x1, blocking collectives, sum_terms(): lax.all_to_all(partial.reshape(count, share, width), EVERY, 0, 0, tiled=T...  16.6 us
    all_to_all x1, blocking collectives, spread(): return lax.all_to_all(copies, axes, 0, 0, tiled=True)  13.5 us
    dynamic_slice x3, local copies, waits for them, and re-layouts, piece(): lax.dynamic_slice_in_dim(whole, partner(vir_at, k) * own + low, high - lo...  11.8 us
    all_to_all x1, waiting for transfers between devices, sum_terms(): lax.all_to_all(partial.reshape(count, share, width), EVERY, 0, 0, tiled=T...  10.4 us
    all_to_all x1, waiting for transfers between devices, local(): lax.all_to_all(copies, EVERY, 0, 0, tiled=True)  10.4 us
    ppermute x11, starting transfers between devices, send(): lax.ppermute(value, 'vir', [(one, partner(one, k)) for one in range(nv)])  10 us
  transfers between devices with their start and end apart: 13, of which 8 were waited for; matrix products, arithmetic and copies ran while one was open for 5% of the time, Pallas kernels for 5%

profile of v12, /device:TPU:0, one launch (start us, length us, event | category | flops | bytes accessed | tf_op | source)
XLA Modules:
  0.0 264.2 jit_solution(14756823482493515447)
XLA Ops:
  0.6 3.2 %shard_map.59 = bf16[36,256,128]{2,1,0:T(8,128)(2,1)} custom-call(s32[1]{0:T(128)} %bitcast.5.start_ref, bf16[256,256,128]{2,1,0:T(8,128)(2,1)} %refs_4_.1), custom_call_target="tpu_custom_call" | custom-call | tf_op jit(solution)/shard_map/pallas_call | solution.py:255
  3.9 3.0 %collective-permute-start = (bf16[36,256,128]{2,1,0:T(8,128)(2,1)}, bf16[36,256,128]{2,1,0:T(8,128)(2,1)S(1)}, u32[]{:S(2)}, u32[]{:S(2)}) collective-permute-start(bf16[36,256,128]{2,1,0:T(8,128)(2,1)} %shard_map.59), channel_id=1, source_target_pairs={{0,2},{1,3},{2,0},{3,1},{4,6},{5,7},{6,4},{7,5},{8,10},{9,11},{10,... | collective-permute-start | bytes 7077896 | tf_op jit(solution)/shard_map/ppermute | solution.py:287
  6.9 5.1 %constant_dynamic-slice_fusion = (bf16[36,256,128]{2,1,0:T(8,128)(2,1)}, bf16[36,256,128]{2,1,0:T(8,128)(2,1)}) fusion(bf16[256,256,128]{2,1,0:T(8,128)(2,1)} %refs_4_.1, s32[]{:T(128)S(6)} %select_n.34, s32[]{:T(128)S(6)} %select_n.33), kind=kLoop, calls=%fused_computation.5 | loop fusion | bytes 9437192 | tf_op jit(solution)/shard_map/dynamic_slice | solution.py:297
  12.2 2.0 constant_dynamic-slice_fusion.2
  14.2 4.7 %constant_dynamic-slice_fusion.5 = (bf16[24,256,128]{2,1,0:T(8,128)(2,1)}, bf16[24,256,128]{2,1,0:T(8,128)(2,1)}, bf16[24,256,128]{2,1,0:T(8,128)(2,1)}) fusion(bf16[256,256,128]{2,1,0:T(8,128)(2,1)} %refs_4_.1, s32[]{:T(128)S(6)} %select_n.29, s32[]{:T(128)S(6)} %select_n.28, s32[]{:T(128)S(6)} %select_n.27), kind=kLoop, calls=%fused_computation.10 | loop fusion | bytes 9437196 | tf_op jit(solution)/shard_map/dynamic_slice | solution.py:297
  18.9 40.3 %collective-permute-done.refs_3_.refs_6_ = bf16[36,256,128]{2,1,0:T(8,128)(2,1)S(1)} collective-permute-done((bf16[36,256,128]{2,1,0:T(8,128)(2,1)}, bf16[36,256,128]{2,1,0:T(8,128)(2,1)S(1)}, u32[]{:S(2)}, u32[]{:S(2)}) %collective-permute-start) | collective-permute-done | bytes 2359328 | tf_op jit(solution)/shard_map/ppermute | solution.py:287
  59.2 13.5 %all_to_all.25 = f32[8,16,256]{2,1,0:T(8,128)S(1)} all-to-all(f32[8,16,256]{2,1,0:T(8,128)S(1)} %broadcast_in_dim.21), channel_id=1, replica_groups=mesh['aux'=8,'vir'=4] {'aux'}, dimensions={0} | all-to-all | bytes 262144 | tf_op jit(solution)/shard_map/all_to_all | solution.py:267
  74.3 37.6 %collective-permute-done.1 = f32[1,129,256]{2,1,0:T(8,128)S(1)} collective-permute-done((f32[1,129,256]{2,1,0:T(8,128)S(1)}, f32[1,129,256]{2,1,0:T(8,128)S(1)}, u32[]{:S(2)}, u32[]{:S(2)}) %collective-permute-start.1) | collective-permute-done | bytes 132128 | tf_op jit(solution)/shard_map/ppermute | solution.py:287
  112.0 1.8 collective-permute-start.5
  115.3 7.4 %shard_map.60.refs_1_ = f32[1024,128]{1,0:T(8,128)S(1)} custom-call(s32[6]{0:T(128)S(1)} %stack.35.order_ref, bf16[4,128,256]{2,1,0:T(8,128)(2,1)S(1)} %slice.20.refs_0_, bf16[256,256,128]{2,1,0:T(8,128)(2,1)} %refs_4_.1, bf16[36,256,128]{2,1,0:T(8,128)(2,1)} %collective-permute-done.3.refs_2_.refs_5_, ...), custom_call_target="tpu_custom_call" | custom-call | tf_op jit(solution)/shard_map/pallas_call | solution.py:171
  122.8 26.8 %collective-permute-done.5.refs_4_.refs_9_ = bf16[24,256,128]{2,1,0:T(8,128)(2,1)} collective-permute-done((bf16[24,256,128]{2,1,0:T(8,128)(2,1)}, bf16[24,256,128]{2,1,0:T(8,128)(2,1)}, u32[]{:S(2)}, u32[]{:S(2)}) %collective-permute-start.5) | collective-permute-done | bytes 1572896 | tf_op jit(solution)/shard_map/ppermute | solution.py:287
  151.8 30.8 %collective-permute-done.7.refs_5_.refs_10_ = bf16[24,256,128]{2,1,0:T(8,128)(2,1)} collective-permute-done((bf16[24,256,128]{2,1,0:T(8,128)(2,1)}, bf16[24,256,128]{2,1,0:T(8,128)(2,1)}, u32[]{:S(2)}, u32[]{:S(2)}) %collective-permute-start.7) | collective-permute-done | bytes 1572896 | tf_op jit(solution)/shard_map/ppermute | solution.py:287
  182.6 5.4 %shard_map.61.refs_1_ = f32[1024,128]{1,0:T(8,128)S(1)} custom-call(s32[6]{0:T(128)S(1)} %stack.35.order_ref, bf16[4,128,256]{2,1,0:T(8,128)(2,1)S(1)} %slice.20.refs_0_, f32[1024,128]{1,0:T(8,128)S(1)} %shard_map.60.refs_1_, bf16[256,256,128]{2,1,0:T(8,128)(2,1)} %refs_4_.1, bf16[24,256,128]{2,1,0:T(8,128)(2,1)} %collective-permute-done.6.refs_3_.refs_8_, ...), custom_call_target="tpu_custom_call" | custom-call | tf_op jit(solution)/shard_map/pallas_call | solution.py:171
  188.1 5.9 %collective-permute-done.9.refs_4_.refs_12_ = bf16[4,256,128]{2,1,0:T(8,128)(2,1)S(1)} collective-permute-done((bf16[4,256,128]{2,1,0:T(8,128)(2,1)S(1)}, bf16[4,256,128]{2,1,0:T(8,128)(2,1)S(1)}, u32[]{:S(2)}, u32[]{:S(2)}) %collective-permute-start.9) | collective-permute-done | bytes 262176 | tf_op jit(solution)/shard_map/ppermute | solution.py:287
  194.0 2.5 shard_map.62
  196.5 16.6 %all_to_all.26.terms_ref = bf16[32,16,256]{2,1,0:T(8,128)(2,1)} all-to-all(bf16[32,16,256]{2,1,0:T(8,128)(2,1)S(1)} %bitcast.20), channel_id=1, replica_groups=mesh['aux'=8,'vir'=4] {'aux','vir'}, dimensions={0} | all-to-all | bytes 524288 | tf_op jit(solution)/shard_map/all_to_all | solution.py:365
  213.0 1.7 shard_map.63
  214.7 2.6 all-to-all-start.2
  217.5 10.4 %all-to-all-done.2.refs_0_ = bf16[32,16,256]{2,1,0:T(8,128)(2,1)S(1)} async-done(((bf16[32,16,256]{2,1,0:T(8,128)(2,1)}), bf16[32,16,256]{2,1,0:T(8,128)(2,1)S(1)}, u32[]{:S(2)}, u32[]{:S(2)}) %all-to-all-start.2) | async-done | bytes 262176 | tf_op jit(solution)/shard_map/all_to_all | solution.py:369
  227.9 11.1 %shard_map.64 = (bf16[8,4,16,256]{3,2,1,0:T(8,128)(2,1)}, f32[17,256]{1,0:T(8,128)S(1)}) custom-call(s32[6]{0:T(128)S(1)} %stack.35.order_ref, bf16[32,16,256]{2,1,0:T(8,128)(2,1)S(1)} %all-to-all-done.2.refs_0_, f32[4,128,256]{2,1,0:T(8,128)S(1)} %slice.18.refs_1_, f32[4,1,256]{2,1,0:T(1,128)S(1)} %pad_maximum_fusion.2.refs_2_, f32[128,1]{1,0:T(8,128)S(1)} %copy.6.refs_3_, ...), custom_call_target="tpu_custom_call" | custom-call | tf_op jit(solution)/shard_map/pallas_call | solution.py:171
  239.1 2.6 all-to-all-start.3
  241.8 10.4 %all-to-all-done.3.terms_ref = bf16[32,16,256]{2,1,0:T(8,128)(2,1)S(1)} async-done(((bf16[32,16,256]{2,1,0:T(8,128)(2,1)}), bf16[32,16,256]{2,1,0:T(8,128)(2,1)S(1)}, u32[]{:S(2)}, u32[]{:S(2)}) %all-to-all-start.3) | async-done | bytes 262176 | tf_op jit(solution)/shard_map/all_to_all | solution.py:365
  253.1 9.4 %all_to_all.27.sums_ref = f32[32,1,128]{2,1,0:T(1,128)} all-to-all(f32[32,1,128]{2,1,0:T(1,128)S(1)} %get-tuple-element.43), channel_id=1, replica_groups=mesh['aux'=8,'vir'=4] {'aux','vir'}, dimensions={0} | all-to-all | bytes 32768 | tf_op jit(solution)/shard_map/all_to_all | solution.py:372
  262.5 1.7 shard_map.66
  (44 shorter events, 6.6 us)
Async XLA Ops:
  3.9 55.3 %collective-permute-start = (bf16[36,256,128]{2,1,0:T(8,128)(2,1)}, bf16[36,256,128]{2,1,0:T(8,128)(2,1)S(1)}, u32[]{:S(2)}, u32[]{:S(2)}) collective-permute-start(bf16[36,256,128]{2,1,0:T(8,128)(2,1)} %shard_map.59), channel_id=1, source_target_pairs={{0,2},{1,3},{2,0},{3,1},{4,6},{5,7},{6,4},{7,5},{8,10},{9,11},{10,... | collective-permute-start | bytes 7077896 | tf_op jit(solution)/shard_map/ppermute | solution.py:287
  12.0 103.3 %collective-permute-start.3 = (bf16[36,256,128]{2,1,0:T(8,128)(2,1)}, bf16[36,256,128]{2,1,0:T(8,128)(2,1)}, u32[]{:S(2)}, u32[]{:S(2)}) collective-permute-start(bf16[36,256,128]{2,1,0:T(8,128)(2,1)} %get-tuple-element.47), channel_id=1, source_target_pairs={{0,1},{1,0},{2,3},{3,2},{4,5},{5,4},{6,7},{7,6},{8,9},{9,8},{10,11... | collective-permute-start | bytes 7077896 | tf_op jit(solution)/shard_map/ppermute | solution.py:287
  12.0 103.3 %collective-permute-start.4 = (bf16[36,256,128]{2,1,0:T(8,128)(2,1)}, bf16[36,256,128]{2,1,0:T(8,128)(2,1)}, u32[]{:S(2)}, u32[]{:S(2)}) collective-permute-start(bf16[36,256,128]{2,1,0:T(8,128)(2,1)} %get-tuple-element.46), channel_id=1, source_target_pairs={{0,3},{1,2},{2,1},{3,0},{4,7},{5,6},{6,5},{7,4},{8,11},{9,10},{10,... | collective-permute-start | bytes 7077896 | tf_op jit(solution)/shard_map/ppermute | solution.py:287
  14.2 45.0 %copy-start.5 = (f32[1,256,16]{1,2,0:T(8,128)S(1)}, f32[1,256,16]{1,2,0:T(8,128)}, u32[]{:S(2)}) copy-start(f32[1,256,16]{1,2,0:T(8,128)} %param.5) | copy-start | bytes 49156
  14.2 58.5 %copy-start.6 = (f32[256]{0:T(256)S(1)}, f32[256]{0:T(256)}, u32[]{:S(2)}) copy-start(f32[256]{0:T(256)} %param.7) | copy-start | bytes 3076
  59.2 63.5 %copy-start = (bf16[36,256,128]{2,1,0:T(8,128)(2,1)}, bf16[36,256,128]{2,1,0:T(8,128)(2,1)S(1)}, u32[]{:S(2)}) copy-start(bf16[36,256,128]{2,1,0:T(8,128)(2,1)S(1)} %collective-permute-done.refs_3_.refs_6_) | copy-start | bytes 7077892
  72.7 39.2 %collective-permute-start.1 = (f32[1,129,256]{2,1,0:T(8,128)S(1)}, f32[1,129,256]{2,1,0:T(8,128)S(1)}, u32[]{:S(2)}, u32[]{:S(2)}) collective-permute-start(f32[1,129,256]{2,1,0:T(8,128)S(1)} %maximum_bitcast_fusion), channel_id=1, source_target_pairs={{0,2},{1,3},{2,0},{3,1},{4,6},{5,7},{6,4},{7,5},{8,10},{9,11},{10,... | collective-permute-start | bytes 396296 | tf_op jit(solution)/shard_map/ppermute | solution.py:287
  111.9 2.0 collective-permute-start.2
  112.0 37.6 %collective-permute-start.5 = (bf16[24,256,128]{2,1,0:T(8,128)(2,1)}, bf16[24,256,128]{2,1,0:T(8,128)(2,1)}, u32[]{:S(2)}, u32[]{:S(2)}) collective-permute-start(bf16[24,256,128]{2,1,0:T(8,128)(2,1)} %get-tuple-element.32), channel_id=1, source_target_pairs={{0,2},{1,3},{2,0},{3,1},{4,6},{5,7},{6,4},{7,5},{8,10},{9,11},{10,... | collective-permute-start | bytes 4718600 | tf_op jit(solution)/shard_map/ppermute | solution.py:287
  113.8 37.9 %collective-permute-start.6 = (bf16[24,256,128]{2,1,0:T(8,128)(2,1)}, bf16[24,256,128]{2,1,0:T(8,128)(2,1)}, u32[]{:S(2)}, u32[]{:S(2)}) collective-permute-start(bf16[24,256,128]{2,1,0:T(8,128)(2,1)} %get-tuple-element.34), channel_id=1, source_target_pairs={{0,1},{1,0},{2,3},{3,2},{4,5},{5,4},{6,7},{7,6},{8,9},{9,8},{10,11... | collective-permute-start | bytes 4718600 | tf_op jit(solution)/shard_map/ppermute | solution.py:287
  114.0 68.6 %collective-permute-start.7 = (bf16[24,256,128]{2,1,0:T(8,128)(2,1)}, bf16[24,256,128]{2,1,0:T(8,128)(2,1)}, u32[]{:S(2)}, u32[]{:S(2)}) collective-permute-start(bf16[24,256,128]{2,1,0:T(8,128)(2,1)} %get-tuple-element.36), channel_id=1, source_target_pairs={{0,3},{1,2},{2,1},{3,0},{4,7},{5,6},{6,5},{7,4},{8,11},{9,10},{10,... | collective-permute-start | bytes 4718600 | tf_op jit(solution)/shard_map/ppermute | solution.py:287
  115.2 34.4 %copy-start.4 = (bf16[4,256,128]{2,1,0:T(8,128)(2,1)S(1)}, bf16[4,256,128]{2,1,0:T(8,128)(2,1)}, u32[]{:S(2)}) copy-start(bf16[4,256,128]{2,1,0:T(8,128)(2,1)} %get-tuple-element.39) | copy-start | bytes 786436
  115.3 34.9 %copy-start.3 = (bf16[4,256,128]{2,1,0:T(8,128)(2,1)S(1)}, bf16[4,256,128]{2,1,0:T(8,128)(2,1)}, u32[]{:S(2)}) copy-start(bf16[4,256,128]{2,1,0:T(8,128)(2,1)} %get-tuple-element.37) | copy-start | bytes 786436
  115.3 36.2 %copy-start.2 = (bf16[4,256,128]{2,1,0:T(8,128)(2,1)S(1)}, bf16[4,256,128]{2,1,0:T(8,128)(2,1)}, u32[]{:S(2)}) copy-start(bf16[4,256,128]{2,1,0:T(8,128)(2,1)} %get-tuple-element.38) | copy-start | bytes 786436
  149.6 38.5 %collective-permute-start.10 = (bf16[4,256,128]{2,1,0:T(8,128)(2,1)S(1)}, bf16[4,256,128]{2,1,0:T(8,128)(2,1)S(1)}, u32[]{:S(2)}, u32[]{:S(2)}) collective-permute-start(bf16[4,256,128]{2,1,0:T(8,128)(2,1)S(1)} %copy-done.4), channel_id=1, source_target_pairs={{0,3},{1,2},{2,1},{3,0},{4,7},{5,6},{6,5},{7,4},{8,11},{9,10},{10,... | collective-permute-start | bytes 786440 | tf_op jit(solution)/shard_map/ppermute | solution.py:287
  150.2 37.9 %collective-permute-start.8 = (bf16[4,256,128]{2,1,0:T(8,128)(2,1)S(1)}, bf16[4,256,128]{2,1,0:T(8,128)(2,1)S(1)}, u32[]{:S(2)}, u32[]{:S(2)}) collective-permute-start(bf16[4,256,128]{2,1,0:T(8,128)(2,1)S(1)} %copy-done.3), channel_id=1, source_target_pairs={{0,1},{1,0},{2,3},{3,2},{4,5},{5,4},{6,7},{7,6},{8,9},{9,8},{10,11... | collective-permute-start | bytes 786440 | tf_op jit(solution)/shard_map/ppermute | solution.py:287
  151.5 42.5 %collective-permute-start.9 = (bf16[4,256,128]{2,1,0:T(8,128)(2,1)S(1)}, bf16[4,256,128]{2,1,0:T(8,128)(2,1)S(1)}, u32[]{:S(2)}, u32[]{:S(2)}) collective-permute-start(bf16[4,256,128]{2,1,0:T(8,128)(2,1)S(1)} %copy-done.2), channel_id=1, source_target_pairs={{0,2},{1,3},{2,0},{3,1},{4,6},{5,7},{6,4},{7,5},{8,10},{9,11},{10,... | collective-permute-start | bytes 786440 | tf_op jit(solution)/shard_map/ppermute | solution.py:287
  187.9 29.4 %copy-start.7 = (f32[128]{0:T(128)S(1)}, f32[128]{0:T(128)}, u32[]{:S(2)}) copy-start(f32[128]{0:T(128)} %param.6) | copy-start | bytes 1540
  214.7 13.2 %all-to-all-start.2 = ((bf16[32,16,256]{2,1,0:T(8,128)(2,1)}), bf16[32,16,256]{2,1,0:T(8,128)(2,1)S(1)}, u32[]{:S(2)}, u32[]{:S(2)}) async-start(bf16[32,16,256]{2,1,0:T(8,128)(2,1)} %shard_map.63), calls=%async_computation.2 | async-start | bytes 524288 | tf_op jit(solution)/shard_map/all_to_all | solution.py:369
  239.1 13.2 %all-to-all-start.3 = ((bf16[32,16,256]{2,1,0:T(8,128)(2,1)}), bf16[32,16,256]{2,1,0:T(8,128)(2,1)S(1)}, u32[]{:S(2)}, u32[]{:S(2)}) async-start(bf16[32,16,256]{2,1,0:T(8,128)(2,1)} %bitcast.13), calls=%async_computation.3 | async-start | bytes 524288 | tf_op jit(solution)/shard_map/all_to_all | solution.py:365
  252.5 0.6 copy-start.1

commit v13 on v11

--- a/solution.py
+++ b/solution.py
@@ -357,8 +357,9 @@
             exchange(k, high, end, cut)
         (carry,) = call([xt], [[(low, middle)], [(middle, high)]], carry)
         blocks = []
-        for start in range(0, own, 4 * unit):
-            points = [start] + [m for m in marks if start < m < start + 4 * unit] + [start + 4 * unit]
+        for start in range(0, own, 8 * unit):
+            stop = start + 8 * unit
+            points = [start] + [m for m in marks if start < m < stop] + [stop]
             blocks.append(list(zip(points, points[1:])))
 
     def sum_terms(partial):

time: 265 us -> 265 us (level)
  no operation moved by 1% of the time
where the time goes in v13:
time: 265 us
  waiting for transfers between devices  162 us (61%)
  blocking collectives  39.5 us (15%)
  Pallas kernels  33.9 us (13%)
  starting transfers between devices  15.2 us (6%)
  local copies, waits for them, and re-layouts  12.8 us (5%)
    ppermute x11, waiting for transfers between devices, send(): lax.ppermute(value, 'vir', [(one, partner(one, k)) for one in range(nv)])  142 us
    pallas_call x4, Pallas kernels, contract(): pl.pallas_call(body, in_specs=[pl.BlockSpec(memory_space=pltpu.SMEM)] + [...  27.3 us
    all_to_all x1, blocking collectives, sum_terms(): lax.all_to_all(partial.reshape(count, share, width), EVERY, 0, 0, tiled=T...  16.6 us
    all_to_all x1, blocking collectives, spread(): return lax.all_to_all(copies, axes, 0, 0, tiled=True)  13.5 us
    dynamic_slice x3, local copies, waits for them, and re-layouts, piece(): lax.dynamic_slice_in_dim(whole, partner(vir_at, k) * own + low, high - lo...  11.8 us
    all_to_all x1, waiting for transfers between devices, sum_terms(): lax.all_to_all(partial.reshape(count, share, width), EVERY, 0, 0, tiled=T...  10.4 us
    all_to_all x1, waiting for transfers between devices, local(): lax.all_to_all(copies, EVERY, 0, 0, tiled=True)  10.4 us
    ppermute x11, starting transfers between devices, send(): lax.ppermute(value, 'vir', [(one, partner(one, k)) for one in range(nv)])  10 us
  transfers between devices with their start and end apart: 13, of which 8 were waited for; matrix products, arithmetic and copies ran while one was open for 5% of the time, Pallas kernels for 5%

profile of v13, /device:TPU:0, one launch (start us, length us, event | category | flops | bytes accessed | tf_op | source)
XLA Modules:
  0.0 264.9 jit_solution(18124787850315869434)
XLA Ops:
  0.6 3.1 %shard_map.59 = bf16[36,256,128]{2,1,0:T(8,128)(2,1)} custom-call(s32[1]{0:T(128)} %bitcast.5.start_ref, bf16[256,256,128]{2,1,0:T(8,128)(2,1)} %refs_4_.1), custom_call_target="tpu_custom_call" | custom-call | tf_op jit(solution)/shard_map/pallas_call | solution.py:255
  3.7 3.0 %collective-permute-start = (bf16[36,256,128]{2,1,0:T(8,128)(2,1)}, bf16[36,256,128]{2,1,0:T(8,128)(2,1)S(1)}, u32[]{:S(2)}, u32[]{:S(2)}) collective-permute-start(bf16[36,256,128]{2,1,0:T(8,128)(2,1)} %shard_map.59), channel_id=1, source_target_pairs={{0,2},{1,3},{2,0},{3,1},{4,6},{5,7},{6,4},{7,5},{8,10},{9,11},{10,... | collective-permute-start | bytes 7077896 | tf_op jit(solution)/shard_map/ppermute | solution.py:287
  6.8 5.1 %constant_dynamic-slice_fusion = (bf16[36,256,128]{2,1,0:T(8,128)(2,1)}, bf16[36,256,128]{2,1,0:T(8,128)(2,1)}) fusion(bf16[256,256,128]{2,1,0:T(8,128)(2,1)} %refs_4_.1, s32[]{:T(128)S(6)} %select_n.34, s32[]{:T(128)S(6)} %select_n.33), kind=kLoop, calls=%fused_computation.5 | loop fusion | bytes 9437192 | tf_op jit(solution)/shard_map/dynamic_slice | solution.py:297
  12.0 2.0 constant_dynamic-slice_fusion.2
  14.0 4.7 %constant_dynamic-slice_fusion.5 = (bf16[24,256,128]{2,1,0:T(8,128)(2,1)}, bf16[24,256,128]{2,1,0:T(8,128)(2,1)}, bf16[24,256,128]{2,1,0:T(8,128)(2,1)}) fusion(bf16[256,256,128]{2,1,0:T(8,128)(2,1)} %refs_4_.1, s32[]{:T(128)S(6)} %select_n.29, s32[]{:T(128)S(6)} %select_n.28, s32[]{:T(128)S(6)} %select_n.27), kind=kLoop, calls=%fused_computation.10 | loop fusion | bytes 9437196 | tf_op jit(solution)/shard_map/dynamic_slice | solution.py:297
  18.7 40.3 %collective-permute-done.refs_3_.refs_6_ = bf16[36,256,128]{2,1,0:T(8,128)(2,1)S(1)} collective-permute-done((bf16[36,256,128]{2,1,0:T(8,128)(2,1)}, bf16[36,256,128]{2,1,0:T(8,128)(2,1)S(1)}, u32[]{:S(2)}, u32[]{:S(2)}) %collective-permute-start) | collective-permute-done | bytes 2359328 | tf_op jit(solution)/shard_map/ppermute | solution.py:287
  59.1 13.5 %all_to_all.25 = f32[8,16,256]{2,1,0:T(8,128)S(1)} all-to-all(f32[8,16,256]{2,1,0:T(8,128)S(1)} %broadcast_in_dim.21), channel_id=1, replica_groups=mesh['aux'=8,'vir'=4] {'aux'}, dimensions={0} | all-to-all | bytes 262144 | tf_op jit(solution)/shard_map/all_to_all | solution.py:267
  74.1 37.6 %collective-permute-done.1 = f32[1,129,256]{2,1,0:T(8,128)S(1)} collective-permute-done((f32[1,129,256]{2,1,0:T(8,128)S(1)}, f32[1,129,256]{2,1,0:T(8,128)S(1)}, u32[]{:S(2)}, u32[]{:S(2)}) %collective-permute-start.1) | collective-permute-done | bytes 132128 | tf_op jit(solution)/shard_map/ppermute | solution.py:287
  111.9 1.8 collective-permute-start.5
  115.1 7.4 %shard_map.60.refs_1_ = f32[1024,128]{1,0:T(8,128)S(1)} custom-call(s32[6]{0:T(128)S(1)} %stack.35.order_ref, bf16[4,128,256]{2,1,0:T(8,128)(2,1)S(1)} %slice.20.refs_0_, bf16[256,256,128]{2,1,0:T(8,128)(2,1)} %refs_4_.1, bf16[36,256,128]{2,1,0:T(8,128)(2,1)} %collective-permute-done.3.refs_2_.refs_5_, ...), custom_call_target="tpu_custom_call" | custom-call | tf_op jit(solution)/shard_map/pallas_call | solution.py:171
  122.6 26.8 %collective-permute-done.5.refs_4_.refs_9_ = bf16[24,256,128]{2,1,0:T(8,128)(2,1)} collective-permute-done((bf16[24,256,128]{2,1,0:T(8,128)(2,1)}, bf16[24,256,128]{2,1,0:T(8,128)(2,1)}, u32[]{:S(2)}, u32[]{:S(2)}) %collective-permute-start.5) | collective-permute-done | bytes 1572896 | tf_op jit(solution)/shard_map/ppermute | solution.py:287
  151.6 30.8 %collective-permute-done.7.refs_5_.refs_10_ = bf16[24,256,128]{2,1,0:T(8,128)(2,1)} collective-permute-done((bf16[24,256,128]{2,1,0:T(8,128)(2,1)}, bf16[24,256,128]{2,1,0:T(8,128)(2,1)}, u32[]{:S(2)}, u32[]{:S(2)}) %collective-permute-start.7) | collective-permute-done | bytes 1572896 | tf_op jit(solution)/shard_map/ppermute | solution.py:287
  182.4 5.4 %shard_map.61.refs_1_ = f32[1024,128]{1,0:T(8,128)S(1)} custom-call(s32[6]{0:T(128)S(1)} %stack.35.order_ref, bf16[4,128,256]{2,1,0:T(8,128)(2,1)S(1)} %slice.20.refs_0_, f32[1024,128]{1,0:T(8,128)S(1)} %shard_map.60.refs_1_, bf16[256,256,128]{2,1,0:T(8,128)(2,1)} %refs_4_.1, bf16[24,256,128]{2,1,0:T(8,128)(2,1)} %collective-permute-done.6.refs_3_.refs_8_, ...), custom_call_target="tpu_custom_call" | custom-call | tf_op jit(solution)/shard_map/pallas_call | solution.py:171
  187.9 5.9 %collective-permute-done.9.refs_4_.refs_12_ = bf16[4,256,128]{2,1,0:T(8,128)(2,1)S(1)} collective-permute-done((bf16[4,256,128]{2,1,0:T(8,128)(2,1)S(1)}, bf16[4,256,128]{2,1,0:T(8,128)(2,1)S(1)}, u32[]{:S(2)}, u32[]{:S(2)}) %collective-permute-start.9) | collective-permute-done | bytes 262176 | tf_op jit(solution)/shard_map/ppermute | solution.py:287
  193.8 2.5 shard_map.62
  196.3 16.6 %all_to_all.26.terms_ref = bf16[32,16,256]{2,1,0:T(8,128)(2,1)} all-to-all(bf16[32,16,256]{2,1,0:T(8,128)(2,1)S(1)} %bitcast.20), channel_id=1, replica_groups=mesh['aux'=8,'vir'=4] {'aux','vir'}, dimensions={0} | all-to-all | bytes 524288 | tf_op jit(solution)/shard_map/all_to_all | solution.py:366
  212.9 1.7 shard_map.63
  214.6 2.6 all-to-all-start.2
  217.4 10.4 %all-to-all-done.2.refs_0_ = bf16[32,16,256]{2,1,0:T(8,128)(2,1)S(1)} async-done(((bf16[32,16,256]{2,1,0:T(8,128)(2,1)}), bf16[32,16,256]{2,1,0:T(8,128)(2,1)S(1)}, u32[]{:S(2)}, u32[]{:S(2)}) %all-to-all-start.2) | async-done | bytes 262176 | tf_op jit(solution)/shard_map/all_to_all | solution.py:370
  227.8 12.0 %shard_map.64 = (bf16[8,4,16,256]{3,2,1,0:T(8,128)(2,1)}, f32[17,256]{1,0:T(8,128)S(1)}) custom-call(s32[6]{0:T(128)S(1)} %stack.35.order_ref, bf16[32,16,256]{2,1,0:T(8,128)(2,1)S(1)} %all-to-all-done.2.refs_0_, f32[4,128,256]{2,1,0:T(8,128)S(1)} %slice.18.refs_1_, f32[4,1,256]{2,1,0:T(1,128)S(1)} %pad_maximum_fusion.2.refs_2_, f32[128,1]{1,0:T(8,128)S(1)} %copy.6.refs_3_, ...), custom_call_target="tpu_custom_call" | custom-call | tf_op jit(solution)/shard_map/pallas_call | solution.py:171
  239.8 2.6 all-to-all-start.3
  242.5 10.4 %all-to-all-done.3.terms_ref = bf16[32,16,256]{2,1,0:T(8,128)(2,1)S(1)} async-done(((bf16[32,16,256]{2,1,0:T(8,128)(2,1)}), bf16[32,16,256]{2,1,0:T(8,128)(2,1)S(1)}, u32[]{:S(2)}, u32[]{:S(2)}) %all-to-all-start.3) | async-done | bytes 262176 | tf_op jit(solution)/shard_map/all_to_all | solution.py:366
  253.8 9.4 %all_to_all.27.sums_ref = f32[32,1,128]{2,1,0:T(1,128)} all-to-all(f32[32,1,128]{2,1,0:T(1,128)S(1)} %get-tuple-element.43), channel_id=1, replica_groups=mesh['aux'=8,'vir'=4] {'aux','vir'}, dimensions={0} | all-to-all | bytes 32768 | tf_op jit(solution)/shard_map/all_to_all | solution.py:373
  263.2 1.7 shard_map.66
  (44 shorter events, 6.6 us)
Async XLA Ops:
  3.7 55.3 %collective-permute-start = (bf16[36,256,128]{2,1,0:T(8,128)(2,1)}, bf16[36,256,128]{2,1,0:T(8,128)(2,1)S(1)}, u32[]{:S(2)}, u32[]{:S(2)}) collective-permute-start(bf16[36,256,128]{2,1,0:T(8,128)(2,1)} %shard_map.59), channel_id=1, source_target_pairs={{0,2},{1,3},{2,0},{3,1},{4,6},{5,7},{6,4},{7,5},{8,10},{9,11},{10,... | collective-permute-start | bytes 7077896 | tf_op jit(solution)/shard_map/ppermute | solution.py:287
  11.8 103.3 %collective-permute-start.3 = (bf16[36,256,128]{2,1,0:T(8,128)(2,1)}, bf16[36,256,128]{2,1,0:T(8,128)(2,1)}, u32[]{:S(2)}, u32[]{:S(2)}) collective-permute-start(bf16[36,256,128]{2,1,0:T(8,128)(2,1)} %get-tuple-element.47), channel_id=1, source_target_pairs={{0,1},{1,0},{2,3},{3,2},{4,5},{5,4},{6,7},{7,6},{8,9},{9,8},{10,11... | collective-permute-start | bytes 7077896 | tf_op jit(solution)/shard_map/ppermute | solution.py:287
  11.8 103.3 %collective-permute-start.4 = (bf16[36,256,128]{2,1,0:T(8,128)(2,1)}, bf16[36,256,128]{2,1,0:T(8,128)(2,1)}, u32[]{:S(2)}, u32[]{:S(2)}) collective-permute-start(bf16[36,256,128]{2,1,0:T(8,128)(2,1)} %get-tuple-element.46), channel_id=1, source_target_pairs={{0,3},{1,2},{2,1},{3,0},{4,7},{5,6},{6,5},{7,4},{8,11},{9,10},{10,... | collective-permute-start | bytes 7077896 | tf_op jit(solution)/shard_map/ppermute | solution.py:287
  14.0 45.0 %copy-start.5 = (f32[1,256,16]{1,2,0:T(8,128)S(1)}, f32[1,256,16]{1,2,0:T(8,128)}, u32[]{:S(2)}) copy-start(f32[1,256,16]{1,2,0:T(8,128)} %param.5) | copy-start | bytes 49156
  14.0 58.5 %copy-start.6 = (f32[256]{0:T(256)S(1)}, f32[256]{0:T(256)}, u32[]{:S(2)}) copy-start(f32[256]{0:T(256)} %param.7) | copy-start | bytes 3076
  59.0 63.5 %copy-start = (bf16[36,256,128]{2,1,0:T(8,128)(2,1)}, bf16[36,256,128]{2,1,0:T(8,128)(2,1)S(1)}, u32[]{:S(2)}) copy-start(bf16[36,256,128]{2,1,0:T(8,128)(2,1)S(1)} %collective-permute-done.refs_3_.refs_6_) | copy-start | bytes 7077892
  72.6 39.2 %collective-permute-start.1 = (f32[1,129,256]{2,1,0:T(8,128)S(1)}, f32[1,129,256]{2,1,0:T(8,128)S(1)}, u32[]{:S(2)}, u32[]{:S(2)}) collective-permute-start(f32[1,129,256]{2,1,0:T(8,128)S(1)} %maximum_bitcast_fusion), channel_id=1, source_target_pairs={{0,2},{1,3},{2,0},{3,1},{4,6},{5,7},{6,4},{7,5},{8,10},{9,11},{10,... | collective-permute-start | bytes 396296 | tf_op jit(solution)/shard_map/ppermute | solution.py:287
  111.8 2.0 collective-permute-start.2
  111.9 37.6 %collective-permute-start.5 = (bf16[24,256,128]{2,1,0:T(8,128)(2,1)}, bf16[24,256,128]{2,1,0:T(8,128)(2,1)}, u32[]{:S(2)}, u32[]{:S(2)}) collective-permute-start(bf16[24,256,128]{2,1,0:T(8,128)(2,1)} %get-tuple-element.32), channel_id=1, source_target_pairs={{0,2},{1,3},{2,0},{3,1},{4,6},{5,7},{6,4},{7,5},{8,10},{9,11},{10,... | collective-permute-start | bytes 4718600 | tf_op jit(solution)/shard_map/ppermute | solution.py:287
  113.7 37.9 %collective-permute-start.6 = (bf16[24,256,128]{2,1,0:T(8,128)(2,1)}, bf16[24,256,128]{2,1,0:T(8,128)(2,1)}, u32[]{:S(2)}, u32[]{:S(2)}) collective-permute-start(bf16[24,256,128]{2,1,0:T(8,128)(2,1)} %get-tuple-element.34), channel_id=1, source_target_pairs={{0,1},{1,0},{2,3},{3,2},{4,5},{5,4},{6,7},{7,6},{8,9},{9,8},{10,11... | collective-permute-start | bytes 4718600 | tf_op jit(solution)/shard_map/ppermute | solution.py:287
  113.8 68.6 %collective-permute-start.7 = (bf16[24,256,128]{2,1,0:T(8,128)(2,1)}, bf16[24,256,128]{2,1,0:T(8,128)(2,1)}, u32[]{:S(2)}, u32[]{:S(2)}) collective-permute-start(bf16[24,256,128]{2,1,0:T(8,128)(2,1)} %get-tuple-element.36), channel_id=1, source_target_pairs={{0,3},{1,2},{2,1},{3,0},{4,7},{5,6},{6,5},{7,4},{8,11},{9,10},{10,... | collective-permute-start | bytes 4718600 | tf_op jit(solution)/shard_map/ppermute | solution.py:287
  115.1 34.4 %copy-start.4 = (bf16[4,256,128]{2,1,0:T(8,128)(2,1)S(1)}, bf16[4,256,128]{2,1,0:T(8,128)(2,1)}, u32[]{:S(2)}) copy-start(bf16[4,256,128]{2,1,0:T(8,128)(2,1)} %get-tuple-element.39) | copy-start | bytes 786436
  115.1 34.9 %copy-start.3 = (bf16[4,256,128]{2,1,0:T(8,128)(2,1)S(1)}, bf16[4,256,128]{2,1,0:T(8,128)(2,1)}, u32[]{:S(2)}) copy-start(bf16[4,256,128]{2,1,0:T(8,128)(2,1)} %get-tuple-element.37) | copy-start | bytes 786436
  115.1 36.2 %copy-start.2 = (bf16[4,256,128]{2,1,0:T(8,128)(2,1)S(1)}, bf16[4,256,128]{2,1,0:T(8,128)(2,1)}, u32[]{:S(2)}) copy-start(bf16[4,256,128]{2,1,0:T(8,128)(2,1)} %get-tuple-element.38) | copy-start | bytes 786436
  149.4 38.5 %collective-permute-start.10 = (bf16[4,256,128]{2,1,0:T(8,128)(2,1)S(1)}, bf16[4,256,128]{2,1,0:T(8,128)(2,1)S(1)}, u32[]{:S(2)}, u32[]{:S(2)}) collective-permute-start(bf16[4,256,128]{2,1,0:T(8,128)(2,1)S(1)} %copy-done.4), channel_id=1, source_target_pairs={{0,3},{1,2},{2,1},{3,0},{4,7},{5,6},{6,5},{7,4},{8,11},{9,10},{10,... | collective-permute-start | bytes 786440 | tf_op jit(solution)/shard_map/ppermute | solution.py:287
  150.0 37.9 %collective-permute-start.8 = (bf16[4,256,128]{2,1,0:T(8,128)(2,1)S(1)}, bf16[4,256,128]{2,1,0:T(8,128)(2,1)S(1)}, u32[]{:S(2)}, u32[]{:S(2)}) collective-permute-start(bf16[4,256,128]{2,1,0:T(8,128)(2,1)S(1)} %copy-done.3), channel_id=1, source_target_pairs={{0,1},{1,0},{2,3},{3,2},{4,5},{5,4},{6,7},{7,6},{8,9},{9,8},{10,11... | collective-permute-start | bytes 786440 | tf_op jit(solution)/shard_map/ppermute | solution.py:287
  151.3 42.5 %collective-permute-start.9 = (bf16[4,256,128]{2,1,0:T(8,128)(2,1)S(1)}, bf16[4,256,128]{2,1,0:T(8,128)(2,1)S(1)}, u32[]{:S(2)}, u32[]{:S(2)}) collective-permute-start(bf16[4,256,128]{2,1,0:T(8,128)(2,1)S(1)} %copy-done.2), channel_id=1, source_target_pairs={{0,2},{1,3},{2,0},{3,1},{4,6},{5,7},{6,4},{7,5},{8,10},{9,11},{10,... | collective-permute-start | bytes 786440 | tf_op jit(solution)/shard_map/ppermute | solution.py:287
  187.8 29.4 %copy-start.7 = (f32[128]{0:T(128)S(1)}, f32[128]{0:T(128)}, u32[]{:S(2)}) copy-start(f32[128]{0:T(128)} %param.6) | copy-start | bytes 1540
  214.6 13.2 %all-to-all-start.2 = ((bf16[32,16,256]{2,1,0:T(8,128)(2,1)}), bf16[32,16,256]{2,1,0:T(8,128)(2,1)S(1)}, u32[]{:S(2)}, u32[]{:S(2)}) async-start(bf16[32,16,256]{2,1,0:T(8,128)(2,1)} %shard_map.63), calls=%async_computation.2 | async-start | bytes 524288 | tf_op jit(solution)/shard_map/all_to_all | solution.py:370
  239.8 13.2 %all-to-all-start.3 = ((bf16[32,16,256]{2,1,0:T(8,128)(2,1)}), bf16[32,16,256]{2,1,0:T(8,128)(2,1)S(1)}, u32[]{:S(2)}, u32[]{:S(2)}) async-start(bf16[32,16,256]{2,1,0:T(8,128)(2,1)} %bitcast.13), calls=%async_computation.3 | async-start | bytes 524288 | tf_op jit(solution)/shard_map/all_to_all | solution.py:366
  253.2 0.6 copy-start.1

commit v14 on v11

--- a/solution.py
+++ b/solution.py
@@ -309,17 +309,21 @@
     if cut_up:
         marks = [0, 9 * unit, 15 * unit, own]
     far = [k for k in range(nv) if k > 1] + [1]
+    first = {k: marks[1] for k in far}
+    if cut_up:
+        first[2] = 6 * unit
     later_factors = factors
     for n, k in enumerate(far):
         if cut_up and n == 0:
-            cut = cut_out(factors, partner(vir_at, k) * own, marks[1])
+            cut = cut_out(factors, partner(vir_at, k) * own, first[k])
         else:
-            cut = piece(k, *marks[:2], later_factors)
+            cut = piece(k, 0, first[k], later_factors)
         if cut_up and n == 0:
             later_factors, cut = lax.optimization_barrier((factors, cut))
-        exchange(k, *marks[:2], cut)
+        exchange(k, 0, first[k], cut)
     if cut_up:
-        later = [[piece(k, low, high, later_factors) for k in far] for low, high in zip(marks[1:], marks[2:])]
+        later = [[piece(k, first[k], marks[2], later_factors) for k in far]]
+        later += [[piece(k, marks[2], own, later_factors) for k in far]]
         later, trials = lax.optimization_barrier((later, *after_newest(2, trials)))
 
     gathered = spread(trials[0].T, na, "aux").reshape(occ, width)
@@ -345,17 +349,17 @@
     carry = None
     blocks = last_block = [[(0, own)]]
     if cut_up:
-        low, high, end = marks[1:]
-        for k, cut in enumerate(later[0]):
-            exchange(far[k], low, high, cut)
-        parts = [(n * low // 4, (n + 1) * low // 4) for n in range(4)]
-        middle = (low + high) // 2
+        low, (high, end) = first[2], marks[2:]
+        for k, cut in zip(far, later[0]):
+            exchange(k, first[k], high, cut)
         last_block = [[(high, end)]]
-        (carry,) = call([xt], [[part] for part in parts])
+        (carry,) = call([xt], [[(0, low // 2)], [(low // 2, low)]])
         cuts, carry = after_newest(2, later[1], carry)
         for k, cut in zip(far, cuts):
             exchange(k, high, end, cut)
-        (carry,) = call([xt], [[(low, middle)], [(middle, high)]], carry)
+        parts = [(low + n * (high - low) // 3, low + (n + 1) * (high - low) // 3) for n in range(3)]
+        (carry,) = call([xt], [[part] for part in parts], carry)
+        marks.insert(1, low)
         blocks = []
         for start in range(0, own, 4 * unit):
             points = [start] + [m for m in marks if start < m < start + 4 * unit] + [start + 4 * unit]

time: 265 us -> 265 us (level)
  transfers between devices with their start and end apart: 13 -> 13, of which waited for: 8 -> 7; matrix products, arithmetic and copies ran while one was open for 5% -> 5% of each run, Pallas kernels for 5% -> 5%
where the time goes in v14:
time: 265 us
  waiting for transfers between devices  164 us (62%)
  blocking collectives  39 us (15%)
  Pallas kernels  32.2 us (12%)
  starting transfers between devices  15 us (6%)
  local copies, waits for them, and re-layouts  13.1 us (5%)
    ppermute x11, waiting for transfers between devices, send(): lax.ppermute(value, 'vir', [(one, partner(one, k)) for one in range(nv)])  143 us
    pallas_call x4, Pallas kernels, contract(): pl.pallas_call(body, in_specs=[pl.BlockSpec(memory_space=pltpu.SMEM)] + [...  26.1 us
    all_to_all x1, blocking collectives, sum_terms(): lax.all_to_all(partial.reshape(count, share, width), EVERY, 0, 0, tiled=T...  16.6 us
    all_to_all x1, blocking collectives, spread(): return lax.all_to_all(copies, axes, 0, 0, tiled=True)  12.9 us
    dynamic_slice x3, local copies, waits for them, and re-layouts, piece(): lax.dynamic_slice_in_dim(whole, partner(vir_at, k) * own + low, high - lo...  12.2 us
    all_to_all x1, waiting for transfers between devices, sum_terms(): lax.all_to_all(partial.reshape(count, share, width), EVERY, 0, 0, tiled=T...  10.4 us
    all_to_all x1, waiting for transfers between devices, local(): lax.all_to_all(copies, EVERY, 0, 0, tiled=True)  10.4 us
    ppermute x11, starting transfers between devices, send(): lax.ppermute(value, 'vir', [(one, partner(one, k)) for one in range(nv)])  9.79 us
  transfers between devices with their start and end apart: 13, of which 7 were waited for; matrix products, arithmetic and copies ran while one was open for 5% of the time, Pallas kernels for 5%

profile of v14, /device:TPU:0, one launch (start us, length us, event | category | flops | bytes accessed | tf_op | source)
XLA Modules:
  0.0 264.6 jit_solution(14237936939939613544)
XLA Ops:
  0.6 2.5 shard_map.59
  3.2 3.0 %collective-permute-start = (bf16[24,256,128]{2,1,0:T(8,128)(2,1)}, bf16[24,256,128]{2,1,0:T(8,128)(2,1)}, u32[]{:S(2)}, u32[]{:S(2)}) collective-permute-start(bf16[24,256,128]{2,1,0:T(8,128)(2,1)} %shard_map.59), channel_id=1, source_target_pairs={{0,2},{1,3},{2,0},{3,1},{4,6},{5,7},{6,4},{7,5},{8,10},{9,11},{10,... | collective-permute-start | bytes 4718600 | tf_op jit(solution)/shard_map/ppermute | solution.py:287
  6.2 6.2 %constant_dynamic-slice_fusion = (bf16[36,256,128]{2,1,0:T(8,128)(2,1)}, bf16[36,256,128]{2,1,0:T(8,128)(2,1)}, bf16[36,256,128]{2,1,0:T(8,128)(2,1)}) fusion(bf16[256,256,128]{2,1,0:T(8,128)(2,1)} %refs_4_.1, s32[]{:T(128)S(6)} %select_n.34, s32[]{:T(128)S(6)} %select_n.33, s32[]{:T(128)S(6)} %select_n.27), kind=kLoop, calls=%fused_computation.5 | loop fusion | bytes 14155788 | tf_op jit(solution)/shard_map/dynamic_slice | solution.py:297
  12.6 2.0 constant_dynamic-slice_fusion.2
  14.6 3.9 %constant_dynamic-slice_fusion.5 = (bf16[24,256,128]{2,1,0:T(8,128)(2,1)}, bf16[24,256,128]{2,1,0:T(8,128)(2,1)}) fusion(bf16[256,256,128]{2,1,0:T(8,128)(2,1)} %refs_4_.1, s32[]{:T(128)S(6)} %select_n.29, s32[]{:T(128)S(6)} %select_n.28), kind=kLoop, calls=%fused_computation.10 | loop fusion | bytes 6291464 | tf_op jit(solution)/shard_map/dynamic_slice | solution.py:297
  18.5 23.2 %collective-permute-done.refs_3_.refs_6_ = bf16[24,256,128]{2,1,0:T(8,128)(2,1)} collective-permute-done((bf16[24,256,128]{2,1,0:T(8,128)(2,1)}, bf16[24,256,128]{2,1,0:T(8,128)(2,1)}, u32[]{:S(2)}, u32[]{:S(2)}) %collective-permute-start) | collective-permute-done | bytes 1572896 | tf_op jit(solution)/shard_map/ppermute | solution.py:287
  41.8 2.1 collective-permute-start.5
  43.8 12.9 %all_to_all.25 = f32[8,16,256]{2,1,0:T(8,128)S(1)} all-to-all(f32[8,16,256]{2,1,0:T(8,128)S(1)} %broadcast_in_dim.21), channel_id=1, replica_groups=mesh['aux'=8,'vir'=4] {'aux'}, dimensions={0} | all-to-all | bytes 262144 | tf_op jit(solution)/shard_map/all_to_all | solution.py:267
  57.4 87.6 %collective-permute-done.1 = f32[1,129,256]{2,1,0:T(8,128)S(1)} collective-permute-done((f32[1,129,256]{2,1,0:T(8,128)S(1)}, f32[1,129,256]{2,1,0:T(8,128)S(1)}, u32[]{:S(2)}, u32[]{:S(2)}) %collective-permute-start.1) | collective-permute-done | bytes 132128 | tf_op jit(solution)/shard_map/ppermute | solution.py:287
  146.6 1.5 collective-permute-start.7
  148.3 5.6 %shard_map.60.refs_1_ = f32[1024,128]{1,0:T(8,128)S(1)} custom-call(s32[6]{0:T(128)S(1)} %stack.35.order_ref, bf16[4,128,256]{2,1,0:T(8,128)(2,1)S(1)} %slice.20.refs_0_, bf16[256,256,128]{2,1,0:T(8,128)(2,1)} %refs_4_.1, bf16[36,256,128]{2,1,0:T(8,128)(2,1)} %collective-permute-done.3.refs_2_.refs_3_.refs_5_, ...), custom_call_target="tpu_custom_call" | custom-call | tf_op jit(solution)/shard_map/pallas_call | solution.py:171
  155.9 27.4 %collective-permute-done.7.refs_7_.refs_10_ = bf16[24,256,128]{2,1,0:T(8,128)(2,1)} collective-permute-done((bf16[24,256,128]{2,1,0:T(8,128)(2,1)}, bf16[24,256,128]{2,1,0:T(8,128)(2,1)}, u32[]{:S(2)}, u32[]{:S(2)}) %collective-permute-start.7) | collective-permute-done | bytes 1572896 | tf_op jit(solution)/shard_map/ppermute | solution.py:287
  183.3 6.9 %shard_map.61.refs_1_ = f32[1024,128]{1,0:T(8,128)S(1)} custom-call(s32[6]{0:T(128)S(1)} %stack.35.order_ref, bf16[4,128,256]{2,1,0:T(8,128)(2,1)S(1)} %slice.20.refs_0_, f32[1024,128]{1,0:T(8,128)S(1)} %shard_map.60.refs_1_, bf16[256,256,128]{2,1,0:T(8,128)(2,1)} %refs_4_.1, bf16[36,256,128]{2,1,0:T(8,128)(2,1)} %collective-permute-done.3.refs_2_.refs_3_.refs_5_, ...), custom_call_target="tpu_custom_call" | custom-call | tf_op jit(solution)/shard_map/pallas_call | solution.py:171
  190.2 4.2 %collective-permute-done.10.refs_5_.refs_13_ = bf16[4,256,128]{2,1,0:T(8,128)(2,1)S(1)} collective-permute-done((bf16[4,256,128]{2,1,0:T(8,128)(2,1)S(1)}, bf16[4,256,128]{2,1,0:T(8,128)(2,1)S(1)}, u32[]{:S(2)}, u32[]{:S(2)}) %collective-permute-start.10) | collective-permute-done | bytes 262176 | tf_op jit(solution)/shard_map/ppermute | solution.py:287
  194.4 2.5 shard_map.62
  196.9 16.6 %all_to_all.26.terms_ref = bf16[32,16,256]{2,1,0:T(8,128)(2,1)} all-to-all(bf16[32,16,256]{2,1,0:T(8,128)(2,1)S(1)} %bitcast.20), channel_id=1, replica_groups=mesh['aux'=8,'vir'=4] {'aux','vir'}, dimensions={0} | all-to-all | bytes 524288 | tf_op jit(solution)/shard_map/all_to_all | solution.py:369
  213.5 1.7 shard_map.63
  215.2 2.6 all-to-all-start.2
  217.9 10.4 %all-to-all-done.2.refs_0_ = bf16[32,16,256]{2,1,0:T(8,128)(2,1)S(1)} async-done(((bf16[32,16,256]{2,1,0:T(8,128)(2,1)}), bf16[32,16,256]{2,1,0:T(8,128)(2,1)S(1)}, u32[]{:S(2)}, u32[]{:S(2)}) %all-to-all-start.2) | async-done | bytes 262176 | tf_op jit(solution)/shard_map/all_to_all | solution.py:373
  228.4 11.1 %shard_map.64 = (bf16[8,4,16,256]{3,2,1,0:T(8,128)(2,1)}, f32[17,256]{1,0:T(8,128)S(1)}) custom-call(s32[6]{0:T(128)S(1)} %stack.35.order_ref, bf16[32,16,256]{2,1,0:T(8,128)(2,1)S(1)} %all-to-all-done.2.refs_0_, f32[4,128,256]{2,1,0:T(8,128)S(1)} %slice.18.refs_1_, f32[4,1,256]{2,1,0:T(1,128)S(1)} %pad_maximum_fusion.2.refs_2_, f32[128,1]{1,0:T(8,128)S(1)} %copy.6.refs_3_, ...), custom_call_target="tpu_custom_call" | custom-call | tf_op jit(solution)/shard_map/pallas_call | solution.py:171
  239.5 2.6 all-to-all-start.3
  242.3 10.4 %all-to-all-done.3.terms_ref = bf16[32,16,256]{2,1,0:T(8,128)(2,1)S(1)} async-done(((bf16[32,16,256]{2,1,0:T(8,128)(2,1)}), bf16[32,16,256]{2,1,0:T(8,128)(2,1)S(1)}, u32[]{:S(2)}, u32[]{:S(2)}) %all-to-all-start.3) | async-done | bytes 262176 | tf_op jit(solution)/shard_map/all_to_all | solution.py:369
  253.5 9.4 %all_to_all.27.sums_ref = f32[32,1,128]{2,1,0:T(1,128)} all-to-all(f32[32,1,128]{2,1,0:T(1,128)S(1)} %get-tuple-element.43), channel_id=1, replica_groups=mesh['aux'=8,'vir'=4] {'aux','vir'}, dimensions={0} | all-to-all | bytes 32768 | tf_op jit(solution)/shard_map/all_to_all | solution.py:376
  262.9 1.7 shard_map.66
  (44 shorter events, 5.6 us)
Async XLA Ops:
  3.2 38.6 %collective-permute-start = (bf16[24,256,128]{2,1,0:T(8,128)(2,1)}, bf16[24,256,128]{2,1,0:T(8,128)(2,1)}, u32[]{:S(2)}, u32[]{:S(2)}) collective-permute-start(bf16[24,256,128]{2,1,0:T(8,128)(2,1)} %shard_map.59), channel_id=1, source_target_pairs={{0,2},{1,3},{2,0},{3,1},{4,6},{5,7},{6,4},{7,5},{8,10},{9,11},{10,... | collective-permute-start | bytes 4718600 | tf_op jit(solution)/shard_map/ppermute | solution.py:287
  12.5 135.8 %collective-permute-start.4 = (bf16[36,256,128]{2,1,0:T(8,128)(2,1)}, bf16[36,256,128]{2,1,0:T(8,128)(2,1)S(1)}, u32[]{:S(2)}, u32[]{:S(2)}) collective-permute-start(bf16[36,256,128]{2,1,0:T(8,128)(2,1)} %get-tuple-element.46), channel_id=1, source_target_pairs={{0,3},{1,2},{2,1},{3,0},{4,7},{5,6},{6,5},{7,4},{8,11},{9,10},{10,... | collective-permute-start | bytes 7077896 | tf_op jit(solution)/shard_map/ppermute | solution.py:287
  12.5 135.8 %collective-permute-start.3 = (bf16[36,256,128]{2,1,0:T(8,128)(2,1)}, bf16[36,256,128]{2,1,0:T(8,128)(2,1)}, u32[]{:S(2)}, u32[]{:S(2)}) collective-permute-start(bf16[36,256,128]{2,1,0:T(8,128)(2,1)} %get-tuple-element.47), channel_id=1, source_target_pairs={{0,1},{1,0},{2,3},{3,2},{4,5},{5,4},{6,7},{7,6},{8,9},{9,8},{10,11... | collective-permute-start | bytes 7077896 | tf_op jit(solution)/shard_map/ppermute | solution.py:287
  14.6 29.2 %copy-start.5 = (f32[1,256,16]{1,2,0:T(8,128)S(1)}, f32[1,256,16]{1,2,0:T(8,128)}, u32[]{:S(2)}) copy-start(f32[1,256,16]{1,2,0:T(8,128)} %param.5) | copy-start | bytes 49156
  14.6 42.1 %copy-start.6 = (f32[256]{0:T(256)S(1)}, f32[256]{0:T(256)}, u32[]{:S(2)}) copy-start(f32[256]{0:T(256)} %param.7) | copy-start | bytes 3076
  41.8 112.2 %collective-permute-start.5 = (bf16[36,256,128]{2,1,0:T(8,128)(2,1)}, bf16[36,256,128]{2,1,0:T(8,128)(2,1)}, u32[]{:S(2)}, u32[]{:S(2)}) collective-permute-start(bf16[36,256,128]{2,1,0:T(8,128)(2,1)} %get-tuple-element.32), channel_id=1, source_target_pairs={{0,2},{1,3},{2,0},{3,1},{4,6},{5,7},{6,4},{7,5},{8,10},{9,11},{10,... | collective-permute-start | bytes 7077896 | tf_op jit(solution)/shard_map/ppermute | solution.py:287
  56.8 88.1 %collective-permute-start.1 = (f32[1,129,256]{2,1,0:T(8,128)S(1)}, f32[1,129,256]{2,1,0:T(8,128)S(1)}, u32[]{:S(2)}, u32[]{:S(2)}) collective-permute-start(f32[1,129,256]{2,1,0:T(8,128)S(1)} %maximum_bitcast_fusion), channel_id=1, source_target_pairs={{0,2},{1,3},{2,0},{3,1},{4,6},{5,7},{6,4},{7,5},{8,10},{9,11},{10,... | collective-permute-start | bytes 396296 | tf_op jit(solution)/shard_map/ppermute | solution.py:287
  145.0 1.6 collective-permute-start.2
  145.0 10.9 %collective-permute-start.6 = (bf16[24,256,128]{2,1,0:T(8,128)(2,1)}, bf16[24,256,128]{2,1,0:T(8,128)(2,1)}, u32[]{:S(2)}, u32[]{:S(2)}) collective-permute-start(bf16[24,256,128]{2,1,0:T(8,128)(2,1)} %get-tuple-element.35), channel_id=1, source_target_pairs={{0,1},{1,0},{2,3},{3,2},{4,5},{5,4},{6,7},{7,6},{8,9},{9,8},{10,11... | collective-permute-start | bytes 4718600 | tf_op jit(solution)/shard_map/ppermute | solution.py:287
  146.6 36.7 %collective-permute-start.7 = (bf16[24,256,128]{2,1,0:T(8,128)(2,1)}, bf16[24,256,128]{2,1,0:T(8,128)(2,1)}, u32[]{:S(2)}, u32[]{:S(2)}) collective-permute-start(bf16[24,256,128]{2,1,0:T(8,128)(2,1)} %get-tuple-element.36), channel_id=1, source_target_pairs={{0,3},{1,2},{2,1},{3,0},{4,7},{5,6},{6,5},{7,4},{8,11},{9,10},{10,... | collective-permute-start | bytes 4718600 | tf_op jit(solution)/shard_map/ppermute | solution.py:287
  148.2 5.7 %copy-start.4 = (bf16[4,256,128]{2,1,0:T(8,128)(2,1)S(1)}, bf16[4,256,128]{2,1,0:T(8,128)(2,1)}, u32[]{:S(2)}) copy-start(bf16[4,256,128]{2,1,0:T(8,128)(2,1)} %get-tuple-element.37) | copy-start | bytes 786436
  148.3 6.2 %copy-start.3 = (bf16[4,256,128]{2,1,0:T(8,128)(2,1)S(1)}, bf16[4,256,128]{2,1,0:T(8,128)(2,1)}, u32[]{:S(2)}) copy-start(bf16[4,256,128]{2,1,0:T(8,128)(2,1)} %get-tuple-element.38) | copy-start | bytes 786436
  148.3 6.4 %copy-start.2 = (bf16[4,256,128]{2,1,0:T(8,128)(2,1)S(1)}, bf16[4,256,128]{2,1,0:T(8,128)(2,1)}, u32[]{:S(2)}) copy-start(bf16[4,256,128]{2,1,0:T(8,128)(2,1)} %get-tuple-element.39) | copy-start | bytes 786436
  148.3 5.6 %copy-start = (bf16[36,256,128]{2,1,0:T(8,128)(2,1)}, bf16[36,256,128]{2,1,0:T(8,128)(2,1)S(1)}, u32[]{:S(2)}) copy-start(bf16[36,256,128]{2,1,0:T(8,128)(2,1)S(1)} %collective-permute-done.4.refs_4_.refs_5_.refs_7_) | copy-start | bytes 7077892
  154.0 36.2 %collective-permute-start.8 = (bf16[4,256,128]{2,1,0:T(8,128)(2,1)S(1)}, bf16[4,256,128]{2,1,0:T(8,128)(2,1)S(1)}, u32[]{:S(2)}, u32[]{:S(2)}) collective-permute-start(bf16[4,256,128]{2,1,0:T(8,128)(2,1)S(1)} %copy-done.4), channel_id=1, source_target_pairs={{0,1},{1,0},{2,3},{3,2},{4,5},{5,4},{6,7},{7,6},{8,9},{9,8},{10,11... | collective-permute-start | bytes 786440 | tf_op jit(solution)/shard_map/ppermute | solution.py:287
  154.4 35.7 %collective-permute-start.9 = (bf16[4,256,128]{2,1,0:T(8,128)(2,1)S(1)}, bf16[4,256,128]{2,1,0:T(8,128)(2,1)S(1)}, u32[]{:S(2)}, u32[]{:S(2)}) collective-permute-start(bf16[4,256,128]{2,1,0:T(8,128)(2,1)S(1)} %copy-done.3), channel_id=1, source_target_pairs={{0,2},{1,3},{2,0},{3,1},{4,6},{5,7},{6,4},{7,5},{8,10},{9,11},{10,... | collective-permute-start | bytes 786440 | tf_op jit(solution)/shard_map/ppermute | solution.py:287
  154.7 39.7 %collective-permute-start.10 = (bf16[4,256,128]{2,1,0:T(8,128)(2,1)S(1)}, bf16[4,256,128]{2,1,0:T(8,128)(2,1)S(1)}, u32[]{:S(2)}, u32[]{:S(2)}) collective-permute-start(bf16[4,256,128]{2,1,0:T(8,128)(2,1)S(1)} %copy-done.2), channel_id=1, source_target_pairs={{0,3},{1,2},{2,1},{3,0},{4,7},{5,6},{6,5},{7,4},{8,11},{9,10},{10,... | collective-permute-start | bytes 786440 | tf_op jit(solution)/shard_map/ppermute | solution.py:287
  190.1 27.6 %copy-start.7 = (f32[128]{0:T(128)S(1)}, f32[128]{0:T(128)}, u32[]{:S(2)}) copy-start(f32[128]{0:T(128)} %param.6) | copy-start | bytes 1540
  215.2 13.2 %all-to-all-start.2 = ((bf16[32,16,256]{2,1,0:T(8,128)(2,1)}), bf16[32,16,256]{2,1,0:T(8,128)(2,1)S(1)}, u32[]{:S(2)}, u32[]{:S(2)}) async-start(bf16[32,16,256]{2,1,0:T(8,128)(2,1)} %shard_map.63), calls=%async_computation.2 | async-start | bytes 524288 | tf_op jit(solution)/shard_map/all_to_all | solution.py:373
  239.5 13.2 %all-to-all-start.3 = ((bf16[32,16,256]{2,1,0:T(8,128)(2,1)}), bf16[32,16,256]{2,1,0:T(8,128)(2,1)S(1)}, u32[]{:S(2)}, u32[]{:S(2)}) async-start(bf16[32,16,256]{2,1,0:T(8,128)(2,1)} %bitcast.13), calls=%async_computation.3 | async-start | bytes 524288 | tf_op jit(solution)/shard_map/all_to_all | solution.py:369
  252.9 0.6 copy-start.1

commit v15 on v11

--- a/solution.py
+++ b/solution.py
@@ -307,7 +307,7 @@
 
     marks = [0, own]
     if cut_up:
-        marks = [0, 9 * unit, 15 * unit, own]
+        marks = [0, 9 * unit, own - unit // 2, own]
     far = [k for k in range(nv) if k > 1] + [1]
     later_factors = factors
     for n, k in enumerate(far):

time: 265 us -> 279 us (1.053)
  waiting for transfers between devices: 162 us -> 184 us
  blocking collectives: 39.5 us -> 25.2 us
  starting transfers between devices: 15.2 us -> 20.6 us
    ppermute x11, waiting for transfers between devices: 142 us -> 163 us  [send(): lax.ppermute(value, 'vir', [(one, partner(one, k)) for one in range(nv)])]
    all_to_all x1 -> x0, blocking collectives: 13.5 us -> none  [spread(): return lax.all_to_all(copies, axes, 0, 0, tiled=True)]
    all_to_all x0 -> x1, starting transfers between devices: none -> 6.03 us  [spread(): return lax.all_to_all(copies, axes, 0, 0, tiled=True)]
  transfers between devices with their start and end apart: 13 -> 14, of which waited for: 8 -> 8; matrix products, arithmetic and copies ran while one was open for 5% -> 4% of each run, Pallas kernels for 5% -> 5%
where the time goes in v15:
time: 279 us; the launch traced here: 278 us
  waiting for transfers between devices  184 us (66%)
  Pallas kernels  33.4 us (12%)
  blocking collectives  25.2 us (9%)
  starting transfers between devices  20.6 us (7%)
  local copies, waits for them, and re-layouts  13.5 us (5%)
    ppermute x11, waiting for transfers between devices, send(): lax.ppermute(value, 'vir', [(one, partner(one, k)) for one in range(nv)])  163 us
    pallas_call x4, Pallas kernels, contract(): pl.pallas_call(body, in_specs=[pl.BlockSpec(memory_space=pltpu.SMEM)] + [...  26.8 us
    all_to_all x1, blocking collectives, sum_terms(): lax.all_to_all(partial.reshape(count, share, width), EVERY, 0, 0, tiled=T...  15.9 us
    dynamic_slice x3, local copies, waits for them, and re-layouts, piece(): lax.dynamic_slice_in_dim(whole, partner(vir_at, k) * own + low, high - lo...  11.8 us
    all_to_all x1, waiting for transfers between devices, sum_terms(): lax.all_to_all(partial.reshape(count, share, width), EVERY, 0, 0, tiled=T...  10.4 us
    all_to_all x1, waiting for transfers between devices, local(): lax.all_to_all(copies, EVERY, 0, 0, tiled=True)  10.4 us
    ppermute x11, starting transfers between devices, send(): lax.ppermute(value, 'vir', [(one, partner(one, k)) for one in range(nv)])  9.35 us
    all_to_all x1, blocking collectives, local(): sums = lax.all_to_all(sums, EVERY, 0, 0, tiled=True)  9.32 us
  transfers between devices with their start and end apart: 14, of which 8 were waited for; matrix products, arithmetic and copies ran while one was open for 4% of the time, Pallas kernels for 5%

profile of v15, /device:TPU:0, one launch (start us, length us, event | category | flops | bytes accessed | tf_op | source)
XLA Modules:
  0.0 278.1 jit_solution(1774994631065240760)
XLA Ops:
  0.6 3.1 %shard_map.59 = bf16[36,256,128]{2,1,0:T(8,128)(2,1)} custom-call(s32[1]{0:T(128)} %bitcast.5.start_ref, bf16[256,256,128]{2,1,0:T(8,128)(2,1)} %refs_4_.1), custom_call_target="tpu_custom_call" | custom-call | tf_op jit(solution)/shard_map/pallas_call | solution.py:255
  3.7 3.0 %collective-permute-start = (bf16[36,256,128]{2,1,0:T(8,128)(2,1)}, bf16[36,256,128]{2,1,0:T(8,128)(2,1)S(1)}, u32[]{:S(2)}, u32[]{:S(2)}) collective-permute-start(bf16[36,256,128]{2,1,0:T(8,128)(2,1)} %shard_map.59), channel_id=1, source_target_pairs={{0,2},{1,3},{2,0},{3,1},{4,6},{5,7},{6,4},{7,5},{8,10},{9,11},{10,... | collective-permute-start | bytes 7077896 | tf_op jit(solution)/shard_map/ppermute | solution.py:287
  6.7 1.8 constant_dynamic-slice_fusion.2
  8.5 4.9 %constant_dynamic-slice_fusion.5 = (bf16[26,256,128]{2,1,0:T(8,128)(2,1)}, bf16[26,256,128]{2,1,0:T(8,128)(2,1)}, bf16[26,256,128]{2,1,0:T(8,128)(2,1)}) fusion(bf16[256,256,128]{2,1,0:T(8,128)(2,1)} %refs_4_.1, s32[]{:T(128)S(6)} %select_n.29, s32[]{:T(128)S(6)} %select_n.28, s32[]{:T(128)S(6)} %select_n.27), kind=kLoop, calls=%fused_computation.10 | loop fusion | bytes 10223628 | tf_op jit(solution)/shard_map/dynamic_slice | solution.py:297
  13.4 44.8 %collective-permute-done.refs_3_.refs_6_ = bf16[36,256,128]{2,1,0:T(8,128)(2,1)S(1)} collective-permute-done((bf16[36,256,128]{2,1,0:T(8,128)(2,1)}, bf16[36,256,128]{2,1,0:T(8,128)(2,1)S(1)}, u32[]{:S(2)}, u32[]{:S(2)}) %collective-permute-start) | collective-permute-done | bytes 2359328 | tf_op jit(solution)/shard_map/ppermute | solution.py:287
  58.9 6.0 %all-to-all-start = ((f32[8,16,256]{2,1,0:T(8,128)}), f32[8,16,256]{2,1,0:T(8,128)S(1)}, u32[]{:S(2)}, u32[]{:S(2)}) async-start(f32[8,16,256]{2,1,0:T(8,128)} %broadcast_in_dim.21), calls=%async_computation | async-start | bytes 262144 | tf_op jit(solution)/shard_map/all_to_all | solution.py:267
  64.9 5.1 %constant_dynamic-slice_fusion = (bf16[36,256,128]{2,1,0:T(8,128)(2,1)}, bf16[36,256,128]{2,1,0:T(8,128)(2,1)}) fusion(bf16[256,256,128]{2,1,0:T(8,128)(2,1)} %refs_4_.1, s32[]{:T(128)S(6)} %select_n.34, s32[]{:T(128)S(6)} %select_n.33), kind=kLoop, calls=%fused_computation.5 | loop fusion | bytes 9437192 | tf_op jit(solution)/shard_map/dynamic_slice | solution.py:297
  70.0 1.6 collective-permute-start.3
  72.3 1.6 collective-permute-start.1
  73.9 52.9 %collective-permute-done.1 = f32[1,129,256]{2,1,0:T(8,128)S(1)} collective-permute-done((f32[1,129,256]{2,1,0:T(8,128)S(1)}, f32[1,129,256]{2,1,0:T(8,128)S(1)}, u32[]{:S(2)}, u32[]{:S(2)}) %collective-permute-start.1) | collective-permute-done | bytes 132128 | tf_op jit(solution)/shard_map/ppermute | solution.py:287
  129.3 7.4 %shard_map.60.refs_1_ = f32[1024,128]{1,0:T(8,128)S(1)} custom-call(s32[6]{0:T(128)S(1)} %stack.35.order_ref, bf16[4,128,256]{2,1,0:T(8,128)(2,1)S(1)} %slice.20.refs_0_, bf16[256,256,128]{2,1,0:T(8,128)(2,1)} %refs_4_.1, bf16[36,256,128]{2,1,0:T(8,128)(2,1)} %collective-permute-done.3.refs_2_.refs_5_, ...), custom_call_target="tpu_custom_call" | custom-call | tf_op jit(solution)/shard_map/pallas_call | solution.py:171
  136.8 30.5 %collective-permute-done.5.refs_4_.refs_9_ = bf16[26,256,128]{2,1,0:T(8,128)(2,1)} collective-permute-done((bf16[26,256,128]{2,1,0:T(8,128)(2,1)}, bf16[26,256,128]{2,1,0:T(8,128)(2,1)}, u32[]{:S(2)}, u32[]{:S(2)}) %collective-permute-start.5) | collective-permute-done | bytes 1703968 | tf_op jit(solution)/shard_map/ppermute | solution.py:287
  169.1 33.7 %collective-permute-done.7.refs_5_.refs_10_ = bf16[26,256,128]{2,1,0:T(8,128)(2,1)} collective-permute-done((bf16[26,256,128]{2,1,0:T(8,128)(2,1)}, bf16[26,256,128]{2,1,0:T(8,128)(2,1)}, u32[]{:S(2)}, u32[]{:S(2)}) %collective-permute-start.7) | collective-permute-done | bytes 1703968 | tf_op jit(solution)/shard_map/ppermute | solution.py:287
  202.9 5.8 %shard_map.61.refs_1_ = f32[1024,128]{1,0:T(8,128)S(1)} custom-call(s32[6]{0:T(128)S(1)} %stack.35.order_ref, bf16[4,128,256]{2,1,0:T(8,128)(2,1)S(1)} %slice.20.refs_0_, f32[1024,128]{1,0:T(8,128)S(1)} %shard_map.60.refs_1_, bf16[256,256,128]{2,1,0:T(8,128)(2,1)} %refs_4_.1, bf16[26,256,128]{2,1,0:T(8,128)(2,1)} %collective-permute-done.6.refs_3_.refs_8_, ...), custom_call_target="tpu_custom_call" | custom-call | tf_op jit(solution)/shard_map/pallas_call | solution.py:171
  208.8 2.3 shard_map.62
  211.1 15.9 %all_to_all.25.terms_ref = bf16[32,16,256]{2,1,0:T(8,128)(2,1)} all-to-all(bf16[32,16,256]{2,1,0:T(8,128)(2,1)S(1)} %bitcast.20), channel_id=1, replica_groups=mesh['aux'=8,'vir'=4] {'aux','vir'}, dimensions={0} | all-to-all | bytes 524288 | tf_op jit(solution)/shard_map/all_to_all | solution.py:365
  227.0 1.7 shard_map.63
  228.7 2.6 all-to-all-start.2
  231.5 10.4 %all-to-all-done.2.refs_0_ = bf16[32,16,256]{2,1,0:T(8,128)(2,1)S(1)} async-done(((bf16[32,16,256]{2,1,0:T(8,128)(2,1)}), bf16[32,16,256]{2,1,0:T(8,128)(2,1)S(1)}, u32[]{:S(2)}, u32[]{:S(2)}) %all-to-all-start.2) | async-done | bytes 262176 | tf_op jit(solution)/shard_map/all_to_all | solution.py:369
  241.9 11.1 %shard_map.64 = (bf16[8,4,16,256]{3,2,1,0:T(8,128)(2,1)}, f32[17,256]{1,0:T(8,128)S(1)}) custom-call(s32[6]{0:T(128)S(1)} %stack.35.order_ref, bf16[32,16,256]{2,1,0:T(8,128)(2,1)S(1)} %all-to-all-done.2.refs_0_, f32[4,128,256]{2,1,0:T(8,128)S(1)} %slice.18.refs_1_, f32[4,1,256]{2,1,0:T(1,128)S(1)} %pad_maximum_fusion.2.refs_2_, f32[128,1]{1,0:T(8,128)S(1)} %copy.6.refs_3_, ...), custom_call_target="tpu_custom_call" | custom-call | tf_op jit(solution)/shard_map/pallas_call | solution.py:171
  253.1 2.6 all-to-all-start.3
  255.8 10.4 %all-to-all-done.3.terms_ref = bf16[32,16,256]{2,1,0:T(8,128)(2,1)S(1)} async-done(((bf16[32,16,256]{2,1,0:T(8,128)(2,1)}), bf16[32,16,256]{2,1,0:T(8,128)(2,1)S(1)}, u32[]{:S(2)}, u32[]{:S(2)}) %all-to-all-start.3) | async-done | bytes 262176 | tf_op jit(solution)/shard_map/all_to_all | solution.py:365
  267.1 9.3 %all_to_all.26.sums_ref = f32[32,1,128]{2,1,0:T(1,128)} all-to-all(f32[32,1,128]{2,1,0:T(1,128)S(1)} %get-tuple-element.43), channel_id=1, replica_groups=mesh['aux'=8,'vir'=4] {'aux','vir'}, dimensions={0} | all-to-all | bytes 32768 | tf_op jit(solution)/shard_map/all_to_all | solution.py:372
  276.4 1.7 shard_map.66
  (45 shorter events, 6.8 us)
Async XLA Ops:
  3.7 54.5 %collective-permute-start = (bf16[36,256,128]{2,1,0:T(8,128)(2,1)}, bf16[36,256,128]{2,1,0:T(8,128)(2,1)S(1)}, u32[]{:S(2)}, u32[]{:S(2)}) collective-permute-start(bf16[36,256,128]{2,1,0:T(8,128)(2,1)} %shard_map.59), channel_id=1, source_target_pairs={{0,2},{1,3},{2,0},{3,1},{4,6},{5,7},{6,4},{7,5},{8,10},{9,11},{10,... | collective-permute-start | bytes 7077896 | tf_op jit(solution)/shard_map/ppermute | solution.py:287
  8.5 49.7 %copy-start.5 = (f32[1,256,16]{1,2,0:T(8,128)S(1)}, f32[1,256,16]{1,2,0:T(8,128)}, u32[]{:S(2)}) copy-start(f32[1,256,16]{1,2,0:T(8,128)} %param.5) | copy-start | bytes 49156
  58.2 71.2 %copy-start = (bf16[36,256,128]{2,1,0:T(8,128)(2,1)}, bf16[36,256,128]{2,1,0:T(8,128)(2,1)S(1)}, u32[]{:S(2)}) copy-start(bf16[36,256,128]{2,1,0:T(8,128)(2,1)S(1)} %collective-permute-done.refs_3_.refs_6_) | copy-start | bytes 7077892
  58.9 13.4 %all-to-all-start = ((f32[8,16,256]{2,1,0:T(8,128)}), f32[8,16,256]{2,1,0:T(8,128)S(1)}, u32[]{:S(2)}, u32[]{:S(2)}) async-start(f32[8,16,256]{2,1,0:T(8,128)} %broadcast_in_dim.21), calls=%async_computation | async-start | bytes 262144 | tf_op jit(solution)/shard_map/all_to_all | solution.py:267
  64.9 7.3 %copy-start.6 = (f32[256]{0:T(256)S(1)}, f32[256]{0:T(256)}, u32[]{:S(2)}) copy-start(f32[256]{0:T(256)} %param.7) | copy-start | bytes 3076
  70.0 59.3 %collective-permute-start.4 = (bf16[36,256,128]{2,1,0:T(8,128)(2,1)}, bf16[36,256,128]{2,1,0:T(8,128)(2,1)}, u32[]{:S(2)}, u32[]{:S(2)}) collective-permute-start(bf16[36,256,128]{2,1,0:T(8,128)(2,1)} %get-tuple-element.46), channel_id=1, source_target_pairs={{0,3},{1,2},{2,1},{3,0},{4,7},{5,6},{6,5},{7,4},{8,11},{9,10},{10,... | collective-permute-start | bytes 7077896 | tf_op jit(solution)/shard_map/ppermute | solution.py:287
  70.0 59.3 %collective-permute-start.3 = (bf16[36,256,128]{2,1,0:T(8,128)(2,1)}, bf16[36,256,128]{2,1,0:T(8,128)(2,1)}, u32[]{:S(2)}, u32[]{:S(2)}) collective-permute-start(bf16[36,256,128]{2,1,0:T(8,128)(2,1)} %get-tuple-element.47), channel_id=1, source_target_pairs={{0,1},{1,0},{2,3},{3,2},{4,5},{5,4},{6,7},{7,6},{8,9},{9,8},{10,11... | collective-permute-start | bytes 7077896 | tf_op jit(solution)/shard_map/ppermute | solution.py:287
  72.3 54.5 %collective-permute-start.1 = (f32[1,129,256]{2,1,0:T(8,128)S(1)}, f32[1,129,256]{2,1,0:T(8,128)S(1)}, u32[]{:S(2)}, u32[]{:S(2)}) collective-permute-start(f32[1,129,256]{2,1,0:T(8,128)S(1)} %maximum_bitcast_fusion), channel_id=1, source_target_pairs={{0,2},{1,3},{2,0},{3,1},{4,6},{5,7},{6,4},{7,5},{8,10},{9,11},{10,... | collective-permute-start | bytes 396296 | tf_op jit(solution)/shard_map/ppermute | solution.py:287
  126.8 1.6 collective-permute-start.2
  126.9 40.4 %collective-permute-start.5 = (bf16[26,256,128]{2,1,0:T(8,128)(2,1)}, bf16[26,256,128]{2,1,0:T(8,128)(2,1)}, u32[]{:S(2)}, u32[]{:S(2)}) collective-permute-start(bf16[26,256,128]{2,1,0:T(8,128)(2,1)} %get-tuple-element.32), channel_id=1, source_target_pairs={{0,2},{1,3},{2,0},{3,1},{4,6},{5,7},{6,4},{7,5},{8,10},{9,11},{10,... | collective-permute-start | bytes 5111816 | tf_op jit(solution)/shard_map/ppermute | solution.py:287
  127.3 41.9 %collective-permute-start.6 = (bf16[26,256,128]{2,1,0:T(8,128)(2,1)}, bf16[26,256,128]{2,1,0:T(8,128)(2,1)}, u32[]{:S(2)}, u32[]{:S(2)}) collective-permute-start(bf16[26,256,128]{2,1,0:T(8,128)(2,1)} %get-tuple-element.34), channel_id=1, source_target_pairs={{0,1},{1,0},{2,3},{3,2},{4,5},{5,4},{6,7},{7,6},{8,9},{9,8},{10,11... | collective-permute-start | bytes 5111816 | tf_op jit(solution)/shard_map/ppermute | solution.py:287
  128.4 74.4 %collective-permute-start.7 = (bf16[26,256,128]{2,1,0:T(8,128)(2,1)}, bf16[26,256,128]{2,1,0:T(8,128)(2,1)}, u32[]{:S(2)}, u32[]{:S(2)}) collective-permute-start(bf16[26,256,128]{2,1,0:T(8,128)(2,1)} %get-tuple-element.36), channel_id=1, source_target_pairs={{0,3},{1,2},{2,1},{3,0},{4,7},{5,6},{6,5},{7,4},{8,11},{9,10},{10,... | collective-permute-start | bytes 5111816 | tf_op jit(solution)/shard_map/ppermute | solution.py:287
  129.3 38.0 %copy-start.4 = (bf16[2,256,128]{2,1,0:T(8,128)(2,1)S(1)}, bf16[2,256,128]{2,1,0:T(8,128)(2,1)}, u32[]{:S(2)}) copy-start(bf16[2,256,128]{2,1,0:T(8,128)(2,1)} %get-tuple-element.37) | copy-start | bytes 393220
  129.3 38.0 %copy-start.3 = (bf16[2,256,128]{2,1,0:T(8,128)(2,1)S(1)}, bf16[2,256,128]{2,1,0:T(8,128)(2,1)}, u32[]{:S(2)}) copy-start(bf16[2,256,128]{2,1,0:T(8,128)(2,1)} %get-tuple-element.38) | copy-start | bytes 393220
  129.3 38.4 %copy-start.2 = (bf16[2,256,128]{2,1,0:T(8,128)(2,1)S(1)}, bf16[2,256,128]{2,1,0:T(8,128)(2,1)}, u32[]{:S(2)}) copy-start(bf16[2,256,128]{2,1,0:T(8,128)(2,1)} %get-tuple-element.39) | copy-start | bytes 393220
  167.3 41.5 %collective-permute-start.8 = (bf16[2,256,128]{2,1,0:T(8,128)(2,1)S(1)}, bf16[2,256,128]{2,1,0:T(8,128)(2,1)S(1)}, u32[]{:S(2)}, u32[]{:S(2)}) collective-permute-start(bf16[2,256,128]{2,1,0:T(8,128)(2,1)S(1)} %copy-done.4), channel_id=1, source_target_pairs={{0,1},{1,0},{2,3},{3,2},{4,5},{5,4},{6,7},{7,6},{8,9},{9,8},{10,11... | collective-permute-start | bytes 393224 | tf_op jit(solution)/shard_map/ppermute | solution.py:287
  167.3 41.5 %collective-permute-start.9 = (bf16[2,256,128]{2,1,0:T(8,128)(2,1)S(1)}, bf16[2,256,128]{2,1,0:T(8,128)(2,1)S(1)}, u32[]{:S(2)}, u32[]{:S(2)}) collective-permute-start(bf16[2,256,128]{2,1,0:T(8,128)(2,1)S(1)} %copy-done.3), channel_id=1, source_target_pairs={{0,2},{1,3},{2,0},{3,1},{4,6},{5,7},{6,4},{7,5},{8,10},{9,11},{10,... | collective-permute-start | bytes 393224 | tf_op jit(solution)/shard_map/ppermute | solution.py:287
  167.7 41.1 %collective-permute-start.10 = (bf16[2,256,128]{2,1,0:T(8,128)(2,1)S(1)}, bf16[2,256,128]{2,1,0:T(8,128)(2,1)S(1)}, u32[]{:S(2)}, u32[]{:S(2)}) collective-permute-start(bf16[2,256,128]{2,1,0:T(8,128)(2,1)S(1)} %copy-done.2), channel_id=1, source_target_pairs={{0,3},{1,2},{2,1},{3,0},{4,7},{5,6},{6,5},{7,4},{8,11},{9,10},{10,... | collective-permute-start | bytes 393224 | tf_op jit(solution)/shard_map/ppermute | solution.py:287
  208.7 22.6 %copy-start.7 = (f32[128]{0:T(128)S(1)}, f32[128]{0:T(128)}, u32[]{:S(2)}) copy-start(f32[128]{0:T(128)} %param.6) | copy-start | bytes 1540
  228.7 13.2 %all-to-all-start.2 = ((bf16[32,16,256]{2,1,0:T(8,128)(2,1)}), bf16[32,16,256]{2,1,0:T(8,128)(2,1)S(1)}, u32[]{:S(2)}, u32[]{:S(2)}) async-start(bf16[32,16,256]{2,1,0:T(8,128)(2,1)} %shard_map.63), calls=%async_computation.2 | async-start | bytes 524288 | tf_op jit(solution)/shard_map/all_to_all | solution.py:369
  253.1 13.2 %all-to-all-start.3 = ((bf16[32,16,256]{2,1,0:T(8,128)(2,1)}), bf16[32,16,256]{2,1,0:T(8,128)(2,1)S(1)}, u32[]{:S(2)}, u32[]{:S(2)}) async-start(bf16[32,16,256]{2,1,0:T(8,128)(2,1)} %bitcast.13), calls=%async_computation.3 | async-start | bytes 524288 | tf_op jit(solution)/shard_map/all_to_all | solution.py:365
  266.5 0.6 copy-start.1
